TPU v7x, 32 devices: a whole 2x2x4 slice. The times are simulated.
32 devices in a mesh: slab: 8 (over z, y), mode: 4 (over x, core).
Axes of the slice: x: 2, y: 2, z: 4, core: 2. Of those that a mesh axis runs over, the one named last changes fastest.
Arguments:
- incoming_occupation: float32 [256, 64, 16, 128], P('mode', 'slab'), may hold values from 0.25 to 1.75
- crystal_kelvin_given: float32 [64, 16, 128], P('slab'), may hold values from 0.5 to 1.5
- generating_region_flag: int32 [64, 16, 128], P('slab'), may hold values 0 or 1
- ordinate_label_array: int32 [256], P('mode'), may hold values from 0 to 255, each once
- spectral_group_velocity: float32 [8], replicated, may hold values from 0.5 to 1
- spectral_scatter_rate: float32 [8], replicated, may hold values from 0.0003 to 0.03
- spectral_storage_factor: float32 [8], replicated, may hold values from 0.5 to 2
- spectral_quartic_threshold: float32 [8], replicated, may hold values from 0.4 to 1
- spectral_generation_rate: float32 [8], replicated, may hold values from 0.005 to 0.05
Outputs:
- energy_out: float32 [256, 64, 16, 128], P('mode', 'slab')
- temp_out: float32 [64, 16, 128], P('slab')
Inputs may be any that keep to these rules, and one draw needn't show every extreme that they name: `ordinate_label_array`: each of the 256 mode numbers stands in exactly one slot.
All inputs are finite; a program needn't handle non-finite values. No bound on the sum of `generating_region_flag` on one device may be relied on, other than what follows from the above.
Results may differ from a plain program's by a relative error of at most 0.0003.
Values sent between devices are 32-bit elements; how exact they have to be, the bound alone decides.
No kernel may reach another device: no remote copies, remote signals or barrier semaphores. Data moves between devices by JAX's collectives and lax.ppermute only.
A program may use at most 128 MiB of HBM per device.

v0:
```python
import math

import jax
import jax.numpy as jnp
from jax import lax
from jax.sharding import PartitionSpec as P

FREQ_GROUPS = 8
DIRS = 32
ITERS = 3
NEWTON = 4


PSEUDO_RATE = 0.03


def shifted(array, axis, by):
    size = lax.axis_size(axis)
    pairs = [(i, i + by) for i in range(size) if 0 <= i + by < size]
    return lax.ppermute(array, axis, pairs)


def spectral_entry(indicator_matrix, values):
    return jnp.sum(indicator_matrix * values[None, :], axis=1)


def broadcast_spectral(values):
    return values[:, None, None, None]


def entry_amounts(
    gathered_entries,
    spectral_group_velocity,
    spectral_scatter_rate,
    spectral_storage_factor,
    spectral_quartic_threshold,
    spectral_generation_rate,
):
    spectral_ordinal = gathered_entries // DIRS
    direction = gathered_entries % DIRS
    indicator_matrix = (
        spectral_ordinal[:, None] == jnp.arange(FREQ_GROUPS, dtype=jnp.int32)[None, :]
    ).astype(spectral_group_velocity.dtype)
    group_speed = spectral_entry(indicator_matrix, spectral_group_velocity)
    relax_rate = spectral_entry(indicator_matrix, spectral_scatter_rate)
    heat_scale = spectral_entry(indicator_matrix, spectral_storage_factor)
    threshold_factor = spectral_entry(indicator_matrix, spectral_quartic_threshold)
    source_rate = spectral_entry(indicator_matrix, spectral_generation_rate)
    polar_level = direction % 4
    cosine = jnp.where(
        polar_level == 0,
        0.99995,
        jnp.where(polar_level == 1, 0.9999, jnp.where(polar_level == 2, -0.9999, -0.99995)),
    ).astype(spectral_group_velocity.dtype)
    sine_part = jnp.sqrt(1.0 - cosine * cosine)
    azimuth = ((direction // 4).astype(spectral_group_velocity.dtype) + 0.5) * (
        2.0 * math.pi / (DIRS // 4)
    )
    velocity_x = group_speed * cosine
    velocity_y = group_speed * sine_part * jnp.cos(azimuth)
    velocity_z = group_speed * sine_part * jnp.sin(azimuth)
    diagonal = (
        jnp.abs(velocity_x) + jnp.abs(velocity_y) + jnp.abs(velocity_z) + relax_rate + PSEUDO_RATE
    )
    decay_ratio = jnp.abs(velocity_x) / diagonal
    wall_value = heat_scale * (1.0 + 1.0 / (4.0 * threshold_factor**3))
    return (
        velocity_x,
        velocity_y,
        velocity_z,
        relax_rate,
        heat_scale,
        threshold_factor,
        source_rate,
        diagonal,
        decay_ratio,
        wall_value,
    )


def transport_forcing(mode_group_internal, crystal_kelvin, generating_region_flag, entry_location):
    velocity_y = entry_location[1]
    velocity_z = entry_location[2]
    upwind_y = jnp.where(
        broadcast_spectral(velocity_y) > 0,
        jnp.roll(mode_group_internal, 1, 2),
        jnp.roll(mode_group_internal, -1, 2),
    )
    upwind_z = jnp.where(
        broadcast_spectral(velocity_z) > 0,
        jnp.roll(mode_group_internal, 1, 3),
        jnp.roll(mode_group_internal, -1, 3),
    )
    conservation_residual = broadcast_spectral(entry_location[4]) * (
        crystal_kelvin + crystal_kelvin**4 / (4.0 * broadcast_spectral(entry_location[5]) ** 3)
    )
    heating = broadcast_spectral(entry_location[6]) * generating_region_flag.astype(
        mode_group_internal.dtype
    )
    gathered = (
        PSEUDO_RATE * mode_group_internal
        + broadcast_spectral(entry_location[3]) * conservation_residual
        + heating
    )
    gathered = (
        gathered
        + broadcast_spectral(jnp.abs(velocity_y)) * upwind_y
        + broadcast_spectral(jnp.abs(velocity_z)) * upwind_z
    )
    return gathered / broadcast_spectral(entry_location[7])


def root_finding_correction(
    volumetric_internal, crystal_kelvin, spectral_storage_factor, spectral_quartic_threshold
):
    for newton_step in range(NEWTON):
        third_power_kelvin = crystal_kelvin**3
        present_iterate = -volumetric_internal
        residual_derivative = jnp.zeros_like(volumetric_internal)
        for spectral_ordinal in range(FREQ_GROUPS):
            threshold_third_power = spectral_quartic_threshold[spectral_ordinal] ** 3
            present_iterate = present_iterate + spectral_storage_factor[spectral_ordinal] * (
                crystal_kelvin + crystal_kelvin * third_power_kelvin / (4.0 * threshold_third_power)
            )
            residual_derivative = residual_derivative + spectral_storage_factor[
                spectral_ordinal
            ] * (1.0 + third_power_kelvin / threshold_third_power)
        crystal_kelvin = crystal_kelvin - present_iterate / residual_derivative
    return crystal_kelvin


def local(
    incoming_occupation,
    crystal_kelvin_given,
    generating_region_flag,
    ordinate_label_array,
    spectral_group_velocity,
    spectral_scatter_rate,
    spectral_storage_factor,
    spectral_quartic_threshold,
    spectral_generation_rate,
):
    entry_location = entry_amounts(
        ordinate_label_array,
        spectral_group_velocity,
        spectral_scatter_rate,
        spectral_storage_factor,
        spectral_quartic_threshold,
        spectral_generation_rate,
    )
    slot_count, depth_x, width_y, width_z = incoming_occupation.shape
    slab_count = lax.axis_size("slab")
    slab_index = lax.axis_index("slab")
    forward = broadcast_spectral(entry_location[0]) > 0
    forward_plane = (entry_location[0] > 0)[:, None, None]
    decay_ratio = entry_location[8]
    position = jnp.arange(depth_x, dtype=jnp.int32)
    distance = (position[:, None] - position[None, :]).astype(jnp.float32)
    lower_part = (position[:, None] >= position[None, :])[None, :, :]
    kernel = jnp.where(
        lower_part,
        jnp.power(decay_ratio[:, None, None], jnp.maximum(distance, 0.0)[None, :, :]),
        0.0,
    )
    carried = jnp.power(decay_ratio[:, None], (position + 1).astype(jnp.float32)[None, :])[
        :, :, None, None
    ]
    composite = jnp.power(decay_ratio, float(depth_x))[:, None, None]
    wall_plane = entry_location[9][:, None, None] * jnp.ones(
        (slot_count, width_y, width_z), jnp.float32
    )
    mode_group_internal = incoming_occupation
    crystal_kelvin = crystal_kelvin_given
    for iteration in range(ITERS):
        equilibrium_reemission = transport_forcing(
            mode_group_internal, crystal_kelvin, generating_region_flag, entry_location
        )
        flipped = jnp.where(forward, equilibrium_reemission, equilibrium_reemission[:, ::-1])
        local_sweep = jnp.einsum("mij,mjyz->miyz", kernel, flipped, precision=lax.Precision.HIGHEST)
        outgoing = local_sweep[:, depth_x - 1]

        def relay(sweep_step, twofold_result):
            sent_up = shifted(composite * twofold_result[0] + outgoing, "slab", 1)
            sent_down = shifted(composite * twofold_result[1] + outgoing, "slab", -1)
            return (
                jnp.where(slab_index == 0, wall_plane, sent_up),
                jnp.where(slab_index == slab_count - 1, wall_plane, sent_down),
            )

        into_up, into_down = lax.fori_loop(0, slab_count - 1, relay, (wall_plane, wall_plane))
        incoming = jnp.where(forward_plane, into_up, into_down)
        swept_energy = local_sweep + carried * incoming[:, None]
        mode_group_internal = jnp.where(forward, swept_energy, swept_energy[:, ::-1])
        partial_value = jnp.sum(mode_group_internal, axis=0) / DIRS
        volumetric_internal = lax.psum(partial_value, "mode")
        crystal_kelvin = root_finding_correction(
            volumetric_internal, crystal_kelvin, spectral_storage_factor, spectral_quartic_threshold
        )
    return (mode_group_internal, crystal_kelvin)


def solution(mesh):
    return jax.shard_map(
        local,
        mesh=mesh,
        in_specs=(
            P("mode", "slab", None, None),
            P("slab", None, None),
            P("slab", None, None),
            P("mode"),
            P(),
            P(),
            P(),
            P(),
            P(),
        ),
        out_specs=(P("mode", "slab", None, None), P("slab", None, None)),
        check_vma=False,
    )
```

profile of v0, /device:TPU:0, one launch (start us, length us, event | category | flops | bytes accessed | tf_op | source)
XLA Modules:
  0.0 935.6 jit_solution(12650063234319625436)
XLA Ops:
  34.2 9.7 %fusion.35 = f32[64,8,16,128]{3,1,2,0:T(8,128)} fusion(f32[64,8,16,1]{3,1,2,0:T(8,128)S(1)} %copy.84, f32[64,8,16,127]{3,1,2,0:T(8,128)S(1)} %copy.85, f32[64,8,16,127]{3,1,2,0:T(8,128)S(1)} %copy.86, f32[64,8,16,1]{3,1,2,0:T(8,128)S(1)} %copy.87, f32[64,8,1,128]{3,1,2,0:T(8,128)S(1)} %copy.88, f32[64,8,15,128]{3,1,2,0:T(8,128)S(1)} %copy.89, ...), kind=kLoop, calls=%fused_computation.59 | loop fusion | flops 19922944 | bytes 25364352 | tf_op jit(solution)/shard_map/div | solution.py:110
  43.9 6.7 rev.18
  50.6 6.2 fusion.31
  59.7 209.5 %while.45 = (s32[]{:T(128)}, f32[64,16,128]{2,1,0:T(8,128)S(1)}, f32[64,16,128]{2,1,0:T(8,128)S(1)}, pred[]{:T(512)}, f32[64,1,1]{0,2,1:T(1,128)S(1)}, /*index=5...) while((s32[]{:T(128)}, f32[64,16,128]{2,1,0:T(8,128)S(1)}, ...), condition=%wide.region_6.7_spmd.clone, body=%wide.region_5.6_spmd.clone.sunk | while | flops 786434 | bytes 11010763 | solution.py:190
  66.8 9.9 %collective-permute-done = f32[64,16,128]{2,1,0:T(8,128)S(1)} collective-permute-done((f32[64,16,128]{2,1,0:T(8,128)S(1)}, f32[64,16,128]{2,1,0:T(8,128)S(1)}, u32[]{:S(2)}, u32[]{:S(2)}) %collective-permute-start) | collective-permute-done | bytes 524320 | tf_op jit(solution)/shard_map/while/body/eval_jaxpr/ppermute | solution.py:20
  76.7 11.4 %collective-permute-done.1 = f32[64,16,128]{2,1,0:T(8,128)S(1)} collective-permute-done((f32[64,16,128]{2,1,0:T(8,128)S(1)}, f32[64,16,128]{2,1,0:T(8,128)S(1)}, u32[]{:S(2)}, u32[]{:S(2)}) %collective-permute-start.1) | collective-permute-done | bytes 524320 | tf_op jit(solution)/shard_map/while/body/eval_jaxpr/ppermute | solution.py:20
  96.6 10.1 %collective-permute-done = f32[64,16,128]{2,1,0:T(8,128)S(1)} collective-permute-done((f32[64,16,128]{2,1,0:T(8,128)S(1)}, f32[64,16,128]{2,1,0:T(8,128)S(1)}, u32[]{:S(2)}, u32[]{:S(2)}) %collective-permute-start) | collective-permute-done | bytes 524320 | tf_op jit(solution)/shard_map/while/body/eval_jaxpr/ppermute | solution.py:20
  106.7 11.4 %collective-permute-done.1 = f32[64,16,128]{2,1,0:T(8,128)S(1)} collective-permute-done((f32[64,16,128]{2,1,0:T(8,128)S(1)}, f32[64,16,128]{2,1,0:T(8,128)S(1)}, u32[]{:S(2)}, u32[]{:S(2)}) %collective-permute-start.1) | collective-permute-done | bytes 524320 | tf_op jit(solution)/shard_map/while/body/eval_jaxpr/ppermute | solution.py:20
  126.6 10.1 %collective-permute-done = f32[64,16,128]{2,1,0:T(8,128)S(1)} collective-permute-done((f32[64,16,128]{2,1,0:T(8,128)S(1)}, f32[64,16,128]{2,1,0:T(8,128)S(1)}, u32[]{:S(2)}, u32[]{:S(2)}) %collective-permute-start) | collective-permute-done | bytes 524320 | tf_op jit(solution)/shard_map/while/body/eval_jaxpr/ppermute | solution.py:20
  136.8 11.4 %collective-permute-done.1 = f32[64,16,128]{2,1,0:T(8,128)S(1)} collective-permute-done((f32[64,16,128]{2,1,0:T(8,128)S(1)}, f32[64,16,128]{2,1,0:T(8,128)S(1)}, u32[]{:S(2)}, u32[]{:S(2)}) %collective-permute-start.1) | collective-permute-done | bytes 524320 | tf_op jit(solution)/shard_map/while/body/eval_jaxpr/ppermute | solution.py:20
  156.6 10.1 %collective-permute-done = f32[64,16,128]{2,1,0:T(8,128)S(1)} collective-permute-done((f32[64,16,128]{2,1,0:T(8,128)S(1)}, f32[64,16,128]{2,1,0:T(8,128)S(1)}, u32[]{:S(2)}, u32[]{:S(2)}) %collective-permute-start) | collective-permute-done | bytes 524320 | tf_op jit(solution)/shard_map/while/body/eval_jaxpr/ppermute | solution.py:20
  166.8 11.4 %collective-permute-done.1 = f32[64,16,128]{2,1,0:T(8,128)S(1)} collective-permute-done((f32[64,16,128]{2,1,0:T(8,128)S(1)}, f32[64,16,128]{2,1,0:T(8,128)S(1)}, u32[]{:S(2)}, u32[]{:S(2)}) %collective-permute-start.1) | collective-permute-done | bytes 524320 | tf_op jit(solution)/shard_map/while/body/eval_jaxpr/ppermute | solution.py:20
  186.7 10.1 %collective-permute-done = f32[64,16,128]{2,1,0:T(8,128)S(1)} collective-permute-done((f32[64,16,128]{2,1,0:T(8,128)S(1)}, f32[64,16,128]{2,1,0:T(8,128)S(1)}, u32[]{:S(2)}, u32[]{:S(2)}) %collective-permute-start) | collective-permute-done | bytes 524320 | tf_op jit(solution)/shard_map/while/body/eval_jaxpr/ppermute | solution.py:20
  196.8 11.4 %collective-permute-done.1 = f32[64,16,128]{2,1,0:T(8,128)S(1)} collective-permute-done((f32[64,16,128]{2,1,0:T(8,128)S(1)}, f32[64,16,128]{2,1,0:T(8,128)S(1)}, u32[]{:S(2)}, u32[]{:S(2)}) %collective-permute-start.1) | collective-permute-done | bytes 524320 | tf_op jit(solution)/shard_map/while/body/eval_jaxpr/ppermute | solution.py:20
  216.7 10.1 %collective-permute-done = f32[64,16,128]{2,1,0:T(8,128)S(1)} collective-permute-done((f32[64,16,128]{2,1,0:T(8,128)S(1)}, f32[64,16,128]{2,1,0:T(8,128)S(1)}, u32[]{:S(2)}, u32[]{:S(2)}) %collective-permute-start) | collective-permute-done | bytes 524320 | tf_op jit(solution)/shard_map/while/body/eval_jaxpr/ppermute | solution.py:20
  226.8 11.4 %collective-permute-done.1 = f32[64,16,128]{2,1,0:T(8,128)S(1)} collective-permute-done((f32[64,16,128]{2,1,0:T(8,128)S(1)}, f32[64,16,128]{2,1,0:T(8,128)S(1)}, u32[]{:S(2)}, u32[]{:S(2)}) %collective-permute-start.1) | collective-permute-done | bytes 524320 | tf_op jit(solution)/shard_map/while/body/eval_jaxpr/ppermute | solution.py:20
  246.7 10.1 %collective-permute-done = f32[64,16,128]{2,1,0:T(8,128)S(1)} collective-permute-done((f32[64,16,128]{2,1,0:T(8,128)S(1)}, f32[64,16,128]{2,1,0:T(8,128)S(1)}, u32[]{:S(2)}, u32[]{:S(2)}) %collective-permute-start) | collective-permute-done | bytes 524320 | tf_op jit(solution)/shard_map/while/body/eval_jaxpr/ppermute | solution.py:20
  256.9 11.4 %collective-permute-done.1 = f32[64,16,128]{2,1,0:T(8,128)S(1)} collective-permute-done((f32[64,16,128]{2,1,0:T(8,128)S(1)}, f32[64,16,128]{2,1,0:T(8,128)S(1)}, u32[]{:S(2)}, u32[]{:S(2)}) %collective-permute-start.1) | collective-permute-done | bytes 524320 | tf_op jit(solution)/shard_map/while/body/eval_jaxpr/ppermute | solution.py:20
  274.0 6.7 rev.19
  286.6 8.2 fusion.455
  320.0 6.3 multiply_multiply_fusion.12
  326.3 13.9 %fusion.34 = f32[64,8,16,128]{3,1,2,0:T(8,128)} fusion(f32[64,8,16,1]{3,1,2,0:T(8,128)} %get-tuple-element.436, f32[64,8,16,127]{3,1,2,0:T(8,128)} %get-tuple-element.438, f32[64,8,16,127]{3,1,2,0:T(8,128)} %get-tuple-element.437, f32[64,8,16,1]{3,1,2,0:T(8,128)} %get-tuple-element.435, f32[64,8,1,128]{3,1,2,0:T(8,128)S(1)} %get-tuple-element.432, ...), kind=kLoop, calls=%fused_computation.58 | loop fusion | flops 19922944 | bytes 25364352 | tf_op jit(solution)/shard_map/div | solution.py:110
  340.2 6.7 rev.20
  346.9 6.2 fusion.29
  355.9 210.1 %while.46 = (s32[]{:T(128)}, f32[64,16,128]{2,1,0:T(8,128)S(1)}, f32[64,16,128]{2,1,0:T(8,128)S(1)}, pred[]{:T(512)}, f32[64,1,1]{0,2,1:T(1,128)S(1)}, /*index=5...) while((s32[]{:T(128)}, f32[64,16,128]{2,1,0:T(8,128)S(1)}, ...), condition=%wide.region_10.11_spmd.clone, body=%wide.region_9.10_spmd.clone.sunk | while | flops 786434 | bytes 11010763 | solution.py:190
  363.4 10.1 %collective-permute-done.2 = f32[64,16,128]{2,1,0:T(8,128)S(1)} collective-permute-done((f32[64,16,128]{2,1,0:T(8,128)S(1)}, f32[64,16,128]{2,1,0:T(8,128)S(1)}, u32[]{:S(2)}, u32[]{:S(2)}) %collective-permute-start.2) | collective-permute-done | bytes 524320 | tf_op jit(solution)/shard_map/while/body/eval_jaxpr/ppermute | solution.py:20
  373.5 11.4 %collective-permute-done.3 = f32[64,16,128]{2,1,0:T(8,128)S(1)} collective-permute-done((f32[64,16,128]{2,1,0:T(8,128)S(1)}, f32[64,16,128]{2,1,0:T(8,128)S(1)}, u32[]{:S(2)}, u32[]{:S(2)}) %collective-permute-start.3) | collective-permute-done | bytes 524320 | tf_op jit(solution)/shard_map/while/body/eval_jaxpr/ppermute | solution.py:20
  393.4 10.1 %collective-permute-done.2 = f32[64,16,128]{2,1,0:T(8,128)S(1)} collective-permute-done((f32[64,16,128]{2,1,0:T(8,128)S(1)}, f32[64,16,128]{2,1,0:T(8,128)S(1)}, u32[]{:S(2)}, u32[]{:S(2)}) %collective-permute-start.2) | collective-permute-done | bytes 524320 | tf_op jit(solution)/shard_map/while/body/eval_jaxpr/ppermute | solution.py:20
  403.6 11.4 %collective-permute-done.3 = f32[64,16,128]{2,1,0:T(8,128)S(1)} collective-permute-done((f32[64,16,128]{2,1,0:T(8,128)S(1)}, f32[64,16,128]{2,1,0:T(8,128)S(1)}, u32[]{:S(2)}, u32[]{:S(2)}) %collective-permute-start.3) | collective-permute-done | bytes 524320 | tf_op jit(solution)/shard_map/while/body/eval_jaxpr/ppermute | solution.py:20
  423.5 10.1 %collective-permute-done.2 = f32[64,16,128]{2,1,0:T(8,128)S(1)} collective-permute-done((f32[64,16,128]{2,1,0:T(8,128)S(1)}, f32[64,16,128]{2,1,0:T(8,128)S(1)}, u32[]{:S(2)}, u32[]{:S(2)}) %collective-permute-start.2) | collective-permute-done | bytes 524320 | tf_op jit(solution)/shard_map/while/body/eval_jaxpr/ppermute | solution.py:20
  433.6 11.4 %collective-permute-done.3 = f32[64,16,128]{2,1,0:T(8,128)S(1)} collective-permute-done((f32[64,16,128]{2,1,0:T(8,128)S(1)}, f32[64,16,128]{2,1,0:T(8,128)S(1)}, u32[]{:S(2)}, u32[]{:S(2)}) %collective-permute-start.3) | collective-permute-done | bytes 524320 | tf_op jit(solution)/shard_map/while/body/eval_jaxpr/ppermute | solution.py:20
  453.5 10.1 %collective-permute-done.2 = f32[64,16,128]{2,1,0:T(8,128)S(1)} collective-permute-done((f32[64,16,128]{2,1,0:T(8,128)S(1)}, f32[64,16,128]{2,1,0:T(8,128)S(1)}, u32[]{:S(2)}, u32[]{:S(2)}) %collective-permute-start.2) | collective-permute-done | bytes 524320 | tf_op jit(solution)/shard_map/while/body/eval_jaxpr/ppermute | solution.py:20
  463.6 11.4 %collective-permute-done.3 = f32[64,16,128]{2,1,0:T(8,128)S(1)} collective-permute-done((f32[64,16,128]{2,1,0:T(8,128)S(1)}, f32[64,16,128]{2,1,0:T(8,128)S(1)}, u32[]{:S(2)}, u32[]{:S(2)}) %collective-permute-start.3) | collective-permute-done | bytes 524320 | tf_op jit(solution)/shard_map/while/body/eval_jaxpr/ppermute | solution.py:20
  483.5 10.1 %collective-permute-done.2 = f32[64,16,128]{2,1,0:T(8,128)S(1)} collective-permute-done((f32[64,16,128]{2,1,0:T(8,128)S(1)}, f32[64,16,128]{2,1,0:T(8,128)S(1)}, u32[]{:S(2)}, u32[]{:S(2)}) %collective-permute-start.2) | collective-permute-done | bytes 524320 | tf_op jit(solution)/shard_map/while/body/eval_jaxpr/ppermute | solution.py:20
  493.7 11.4 %collective-permute-done.3 = f32[64,16,128]{2,1,0:T(8,128)S(1)} collective-permute-done((f32[64,16,128]{2,1,0:T(8,128)S(1)}, f32[64,16,128]{2,1,0:T(8,128)S(1)}, u32[]{:S(2)}, u32[]{:S(2)}) %collective-permute-start.3) | collective-permute-done | bytes 524320 | tf_op jit(solution)/shard_map/while/body/eval_jaxpr/ppermute | solution.py:20
  513.5 10.1 %collective-permute-done.2 = f32[64,16,128]{2,1,0:T(8,128)S(1)} collective-permute-done((f32[64,16,128]{2,1,0:T(8,128)S(1)}, f32[64,16,128]{2,1,0:T(8,128)S(1)}, u32[]{:S(2)}, u32[]{:S(2)}) %collective-permute-start.2) | collective-permute-done | bytes 524320 | tf_op jit(solution)/shard_map/while/body/eval_jaxpr/ppermute | solution.py:20
  523.7 11.4 %collective-permute-done.3 = f32[64,16,128]{2,1,0:T(8,128)S(1)} collective-permute-done((f32[64,16,128]{2,1,0:T(8,128)S(1)}, f32[64,16,128]{2,1,0:T(8,128)S(1)}, u32[]{:S(2)}, u32[]{:S(2)}) %collective-permute-start.3) | collective-permute-done | bytes 524320 | tf_op jit(solution)/shard_map/while/body/eval_jaxpr/ppermute | solution.py:20
  543.6 10.1 %collective-permute-done.2 = f32[64,16,128]{2,1,0:T(8,128)S(1)} collective-permute-done((f32[64,16,128]{2,1,0:T(8,128)S(1)}, f32[64,16,128]{2,1,0:T(8,128)S(1)}, u32[]{:S(2)}, u32[]{:S(2)}) %collective-permute-start.2) | collective-permute-done | bytes 524320 | tf_op jit(solution)/shard_map/while/body/eval_jaxpr/ppermute | solution.py:20
  553.7 11.4 %collective-permute-done.3 = f32[64,16,128]{2,1,0:T(8,128)S(1)} collective-permute-done((f32[64,16,128]{2,1,0:T(8,128)S(1)}, f32[64,16,128]{2,1,0:T(8,128)S(1)}, u32[]{:S(2)}, u32[]{:S(2)}) %collective-permute-start.3) | collective-permute-done | bytes 524320 | tf_op jit(solution)/shard_map/while/body/eval_jaxpr/ppermute | solution.py:20
  570.8 6.7 rev.21
  596.7 32.3 %all-reduce.6.cloned.1.call-done = f32[8,16,128]{2,0,1:T(8,128)} async-done(((f32[8,16,128]{2,0,1:T(8,128)}), f32[8,16,128]{2,0,1:T(8,128)}) %all-reduce.6.cloned.1.call-update) | async-done | bytes 65552 | tf_op jit(solution)/shard_map/psum | solution.py:195
  629.0 6.3 multiply_multiply_fusion.10
  635.3 14.0 %fusion.33 = f32[64,8,16,128]{3,1,2,0:T(8,128)} fusion(f32[64,8,16,1]{3,1,2,0:T(8,128)} %get-tuple-element.428, f32[64,8,16,127]{3,1,2,0:T(8,128)} %get-tuple-element.430, f32[64,8,16,127]{3,1,2,0:T(8,128)} %get-tuple-element.429, f32[64,8,16,1]{3,1,2,0:T(8,128)} %get-tuple-element.427, f32[64,8,1,128]{3,1,2,0:T(8,128)S(1)} %get-tuple-element.424, ...), kind=kLoop, calls=%fused_computation.57 | loop fusion | flops 19922944 | bytes 25364352 | tf_op jit(solution)/shard_map/div | solution.py:110
  649.3 6.6 rev.22
  655.9 6.2 fusion.27
  664.9 207.0 %while.47 = (s32[]{:T(128)}, f32[64,16,128]{2,1,0:T(8,128)S(1)}, f32[64,16,128]{2,1,0:T(8,128)S(1)}, pred[]{:T(512)}, f32[64,1,1]{0,2,1:T(1,128)S(1)}, /*index=5...) while((s32[]{:T(128)}, f32[64,16,128]{2,1,0:T(8,128)S(1)}, ...), condition=%wide.region_14.15_spmd.clone, body=%wide.region_13.14_spmd.clone.sunk | while | flops 786434 | bytes 11010763 | solution.py:190
  671.0 8.4 collective-permute-done.4
  679.4 11.4 %collective-permute-done.5 = f32[64,16,128]{2,1,0:T(8,128)S(1)} collective-permute-done((f32[64,16,128]{2,1,0:T(8,128)S(1)}, f32[64,16,128]{2,1,0:T(8,128)S(1)}, u32[]{:S(2)}, u32[]{:S(2)}) %collective-permute-start.5) | collective-permute-done | bytes 524320 | tf_op jit(solution)/shard_map/while/body/eval_jaxpr/ppermute | solution.py:20
  693.2 6.1 collective-permute-start.5
  699.3 10.1 %collective-permute-done.4 = f32[64,16,128]{2,1,0:T(8,128)S(1)} collective-permute-done((f32[64,16,128]{2,1,0:T(8,128)S(1)}, f32[64,16,128]{2,1,0:T(8,128)S(1)}, u32[]{:S(2)}, u32[]{:S(2)}) %collective-permute-start.4) | collective-permute-done | bytes 524320 | tf_op jit(solution)/shard_map/while/body/eval_jaxpr/ppermute | solution.py:20
  709.4 11.4 %collective-permute-done.5 = f32[64,16,128]{2,1,0:T(8,128)S(1)} collective-permute-done((f32[64,16,128]{2,1,0:T(8,128)S(1)}, f32[64,16,128]{2,1,0:T(8,128)S(1)}, u32[]{:S(2)}, u32[]{:S(2)}) %collective-permute-start.5) | collective-permute-done | bytes 524320 | tf_op jit(solution)/shard_map/while/body/eval_jaxpr/ppermute | solution.py:20
  729.3 10.1 %collective-permute-done.4 = f32[64,16,128]{2,1,0:T(8,128)S(1)} collective-permute-done((f32[64,16,128]{2,1,0:T(8,128)S(1)}, f32[64,16,128]{2,1,0:T(8,128)S(1)}, u32[]{:S(2)}, u32[]{:S(2)}) %collective-permute-start.4) | collective-permute-done | bytes 524320 | tf_op jit(solution)/shard_map/while/body/eval_jaxpr/ppermute | solution.py:20
  739.5 11.4 %collective-permute-done.5 = f32[64,16,128]{2,1,0:T(8,128)S(1)} collective-permute-done((f32[64,16,128]{2,1,0:T(8,128)S(1)}, f32[64,16,128]{2,1,0:T(8,128)S(1)}, u32[]{:S(2)}, u32[]{:S(2)}) %collective-permute-start.5) | collective-permute-done | bytes 524320 | tf_op jit(solution)/shard_map/while/body/eval_jaxpr/ppermute | solution.py:20
  759.4 10.1 %collective-permute-done.4 = f32[64,16,128]{2,1,0:T(8,128)S(1)} collective-permute-done((f32[64,16,128]{2,1,0:T(8,128)S(1)}, f32[64,16,128]{2,1,0:T(8,128)S(1)}, u32[]{:S(2)}, u32[]{:S(2)}) %collective-permute-start.4) | collective-permute-done | bytes 524320 | tf_op jit(solution)/shard_map/while/body/eval_jaxpr/ppermute | solution.py:20
  769.5 11.4 %collective-permute-done.5 = f32[64,16,128]{2,1,0:T(8,128)S(1)} collective-permute-done((f32[64,16,128]{2,1,0:T(8,128)S(1)}, f32[64,16,128]{2,1,0:T(8,128)S(1)}, u32[]{:S(2)}, u32[]{:S(2)}) %collective-permute-start.5) | collective-permute-done | bytes 524320 | tf_op jit(solution)/shard_map/while/body/eval_jaxpr/ppermute | solution.py:20
  789.4 10.1 %collective-permute-done.4 = f32[64,16,128]{2,1,0:T(8,128)S(1)} collective-permute-done((f32[64,16,128]{2,1,0:T(8,128)S(1)}, f32[64,16,128]{2,1,0:T(8,128)S(1)}, u32[]{:S(2)}, u32[]{:S(2)}) %collective-permute-start.4) | collective-permute-done | bytes 524320 | tf_op jit(solution)/shard_map/while/body/eval_jaxpr/ppermute | solution.py:20
  799.5 11.4 %collective-permute-done.5 = f32[64,16,128]{2,1,0:T(8,128)S(1)} collective-permute-done((f32[64,16,128]{2,1,0:T(8,128)S(1)}, f32[64,16,128]{2,1,0:T(8,128)S(1)}, u32[]{:S(2)}, u32[]{:S(2)}) %collective-permute-start.5) | collective-permute-done | bytes 524320 | tf_op jit(solution)/shard_map/while/body/eval_jaxpr/ppermute | solution.py:20
  819.4 10.1 %collective-permute-done.4 = f32[64,16,128]{2,1,0:T(8,128)S(1)} collective-permute-done((f32[64,16,128]{2,1,0:T(8,128)S(1)}, f32[64,16,128]{2,1,0:T(8,128)S(1)}, u32[]{:S(2)}, u32[]{:S(2)}) %collective-permute-start.4) | collective-permute-done | bytes 524320 | tf_op jit(solution)/shard_map/while/body/eval_jaxpr/ppermute | solution.py:20
  829.6 11.4 %collective-permute-done.5 = f32[64,16,128]{2,1,0:T(8,128)S(1)} collective-permute-done((f32[64,16,128]{2,1,0:T(8,128)S(1)}, f32[64,16,128]{2,1,0:T(8,128)S(1)}, u32[]{:S(2)}, u32[]{:S(2)}) %collective-permute-start.5) | collective-permute-done | bytes 524320 | tf_op jit(solution)/shard_map/while/body/eval_jaxpr/ppermute | solution.py:20
  849.4 10.1 %collective-permute-done.4 = f32[64,16,128]{2,1,0:T(8,128)S(1)} collective-permute-done((f32[64,16,128]{2,1,0:T(8,128)S(1)}, f32[64,16,128]{2,1,0:T(8,128)S(1)}, u32[]{:S(2)}, u32[]{:S(2)}) %collective-permute-start.4) | collective-permute-done | bytes 524320 | tf_op jit(solution)/shard_map/while/body/eval_jaxpr/ppermute | solution.py:20
  859.6 11.4 %collective-permute-done.5 = f32[64,16,128]{2,1,0:T(8,128)S(1)} collective-permute-done((f32[64,16,128]{2,1,0:T(8,128)S(1)}, f32[64,16,128]{2,1,0:T(8,128)S(1)}, u32[]{:S(2)}, u32[]{:S(2)}) %collective-permute-start.5) | collective-permute-done | bytes 524320 | tf_op jit(solution)/shard_map/while/body/eval_jaxpr/ppermute | solution.py:20
  876.7 6.7 rev.23
  894.5 27.5 %all-reduce.8.cloned.1.call-done = f32[8,16,128]{2,0,1:T(8,128)} async-done(((f32[8,16,128]{2,0,1:T(8,128)}), f32[8,16,128]{2,0,1:T(8,128)}) %all-reduce.8.cloned.1.call-update) | async-done | bytes 65552 | tf_op jit(solution)/shard_map/psum | solution.py:195
  921.9 6.3 divide_subtract_fusion
  (221 shorter events, 265.6 us)
Async XLA Ops:
  7.2 312.8 %all-reduce.4.cloned.1.call-start = ((), (), s32[]{:S(2)}) async-start(), calls=%async_computation | async-start | bytes 131072 | tf_op jit(solution)/shard_map/psum | solution.py:195
  7.2 5.2 copy-start.2
  16.2 3.4 copy-start.18
  16.2 3.5 copy-start.12
  19.7 2.2 copy-start.7
  25.8 2.4 copy-start.6
  30.0 3.8 copy-start.11
  30.1 3.9 copy-start.13
  30.1 3.9 copy-start.14
  30.1 3.9 copy-start.15
  30.1 3.9 copy-start.16
  30.1 3.9 copy-start.17
  56.8 2.0 copy-start.3
  59.9 16.8 %collective-permute-start = (f32[64,16,128]{2,1,0:T(8,128)S(1)}, f32[64,16,128]{2,1,0:T(8,128)S(1)}, u32[]{:S(2)}, u32[]{:S(2)}) collective-permute-start(f32[64,16,128]{2,1,0:T(8,128)S(1)} %get-tuple-element.614), channel_id=1, source_target_pairs={{4,0},{8,4},{12,8},{16,12},{20,16},{24,20},{28,24},{5,1},{9,5},{13... | collective-permute-start | bytes 1572872 | tf_op jit(solution)/shard_map/while/body/eval_jaxpr/ppermute | solution.py:20
  61.2 26.9 %collective-permute-start.1 = (f32[64,16,128]{2,1,0:T(8,128)S(1)}, f32[64,16,128]{2,1,0:T(8,128)S(1)}, u32[]{:S(2)}, u32[]{:S(2)}) collective-permute-start(f32[64,16,128]{2,1,0:T(8,128)S(1)} %get-tuple-element.615), channel_id=1, source_target_pairs={{0,4},{4,8},{8,12},{12,16},{16,20},{20,24},{24,28},{1,5},{5,9},{9,... | collective-permute-start | bytes 1572872 | tf_op jit(solution)/shard_map/while/body/eval_jaxpr/ppermute | solution.py:20
  88.1 0.8 copy-start.8
  89.2 17.5 %collective-permute-start = (f32[64,16,128]{2,1,0:T(8,128)S(1)}, f32[64,16,128]{2,1,0:T(8,128)S(1)}, u32[]{:S(2)}, u32[]{:S(2)}) collective-permute-start(f32[64,16,128]{2,1,0:T(8,128)S(1)} %get-tuple-element.614), channel_id=1, source_target_pairs={{4,0},{8,4},{12,8},{16,12},{20,16},{24,20},{28,24},{5,1},{9,5},{13... | collective-permute-start | bytes 1572872 | tf_op jit(solution)/shard_map/while/body/eval_jaxpr/ppermute | solution.py:20
  90.5 27.6 %collective-permute-start.1 = (f32[64,16,128]{2,1,0:T(8,128)S(1)}, f32[64,16,128]{2,1,0:T(8,128)S(1)}, u32[]{:S(2)}, u32[]{:S(2)}) collective-permute-start(f32[64,16,128]{2,1,0:T(8,128)S(1)} %get-tuple-element.615), channel_id=1, source_target_pairs={{0,4},{4,8},{8,12},{12,16},{16,20},{20,24},{24,28},{1,5},{5,9},{9,... | collective-permute-start | bytes 1572872 | tf_op jit(solution)/shard_map/while/body/eval_jaxpr/ppermute | solution.py:20
  119.2 17.5 %collective-permute-start = (f32[64,16,128]{2,1,0:T(8,128)S(1)}, f32[64,16,128]{2,1,0:T(8,128)S(1)}, u32[]{:S(2)}, u32[]{:S(2)}) collective-permute-start(f32[64,16,128]{2,1,0:T(8,128)S(1)} %get-tuple-element.614), channel_id=1, source_target_pairs={{4,0},{8,4},{12,8},{16,12},{20,16},{24,20},{28,24},{5,1},{9,5},{13... | collective-permute-start | bytes 1572872 | tf_op jit(solution)/shard_map/while/body/eval_jaxpr/ppermute | solution.py:20
  120.5 27.6 %collective-permute-start.1 = (f32[64,16,128]{2,1,0:T(8,128)S(1)}, f32[64,16,128]{2,1,0:T(8,128)S(1)}, u32[]{:S(2)}, u32[]{:S(2)}) collective-permute-start(f32[64,16,128]{2,1,0:T(8,128)S(1)} %get-tuple-element.615), channel_id=1, source_target_pairs={{0,4},{4,8},{8,12},{12,16},{16,20},{20,24},{24,28},{1,5},{5,9},{9,... | collective-permute-start | bytes 1572872 | tf_op jit(solution)/shard_map/while/body/eval_jaxpr/ppermute | solution.py:20
  149.3 17.5 %collective-permute-start = (f32[64,16,128]{2,1,0:T(8,128)S(1)}, f32[64,16,128]{2,1,0:T(8,128)S(1)}, u32[]{:S(2)}, u32[]{:S(2)}) collective-permute-start(f32[64,16,128]{2,1,0:T(8,128)S(1)} %get-tuple-element.614), channel_id=1, source_target_pairs={{4,0},{8,4},{12,8},{16,12},{20,16},{24,20},{28,24},{5,1},{9,5},{13... | collective-permute-start | bytes 1572872 | tf_op jit(solution)/shard_map/while/body/eval_jaxpr/ppermute | solution.py:20
  150.6 27.6 %collective-permute-start.1 = (f32[64,16,128]{2,1,0:T(8,128)S(1)}, f32[64,16,128]{2,1,0:T(8,128)S(1)}, u32[]{:S(2)}, u32[]{:S(2)}) collective-permute-start(f32[64,16,128]{2,1,0:T(8,128)S(1)} %get-tuple-element.615), channel_id=1, source_target_pairs={{0,4},{4,8},{8,12},{12,16},{16,20},{20,24},{24,28},{1,5},{5,9},{9,... | collective-permute-start | bytes 1572872 | tf_op jit(solution)/shard_map/while/body/eval_jaxpr/ppermute | solution.py:20
  179.3 17.5 %collective-permute-start = (f32[64,16,128]{2,1,0:T(8,128)S(1)}, f32[64,16,128]{2,1,0:T(8,128)S(1)}, u32[]{:S(2)}, u32[]{:S(2)}) collective-permute-start(f32[64,16,128]{2,1,0:T(8,128)S(1)} %get-tuple-element.614), channel_id=1, source_target_pairs={{4,0},{8,4},{12,8},{16,12},{20,16},{24,20},{28,24},{5,1},{9,5},{13... | collective-permute-start | bytes 1572872 | tf_op jit(solution)/shard_map/while/body/eval_jaxpr/ppermute | solution.py:20
  180.6 27.6 %collective-permute-start.1 = (f32[64,16,128]{2,1,0:T(8,128)S(1)}, f32[64,16,128]{2,1,0:T(8,128)S(1)}, u32[]{:S(2)}, u32[]{:S(2)}) collective-permute-start(f32[64,16,128]{2,1,0:T(8,128)S(1)} %get-tuple-element.615), channel_id=1, source_target_pairs={{0,4},{4,8},{8,12},{12,16},{16,20},{20,24},{24,28},{1,5},{5,9},{9,... | collective-permute-start | bytes 1572872 | tf_op jit(solution)/shard_map/while/body/eval_jaxpr/ppermute | solution.py:20
  209.3 17.5 %collective-permute-start = (f32[64,16,128]{2,1,0:T(8,128)S(1)}, f32[64,16,128]{2,1,0:T(8,128)S(1)}, u32[]{:S(2)}, u32[]{:S(2)}) collective-permute-start(f32[64,16,128]{2,1,0:T(8,128)S(1)} %get-tuple-element.614), channel_id=1, source_target_pairs={{4,0},{8,4},{12,8},{16,12},{20,16},{24,20},{28,24},{5,1},{9,5},{13... | collective-permute-start | bytes 1572872 | tf_op jit(solution)/shard_map/while/body/eval_jaxpr/ppermute | solution.py:20
  210.6 27.6 %collective-permute-start.1 = (f32[64,16,128]{2,1,0:T(8,128)S(1)}, f32[64,16,128]{2,1,0:T(8,128)S(1)}, u32[]{:S(2)}, u32[]{:S(2)}) collective-permute-start(f32[64,16,128]{2,1,0:T(8,128)S(1)} %get-tuple-element.615), channel_id=1, source_target_pairs={{0,4},{4,8},{8,12},{12,16},{16,20},{20,24},{24,28},{1,5},{5,9},{9,... | collective-permute-start | bytes 1572872 | tf_op jit(solution)/shard_map/while/body/eval_jaxpr/ppermute | solution.py:20
  239.3 17.5 %collective-permute-start = (f32[64,16,128]{2,1,0:T(8,128)S(1)}, f32[64,16,128]{2,1,0:T(8,128)S(1)}, u32[]{:S(2)}, u32[]{:S(2)}) collective-permute-start(f32[64,16,128]{2,1,0:T(8,128)S(1)} %get-tuple-element.614), channel_id=1, source_target_pairs={{4,0},{8,4},{12,8},{16,12},{20,16},{24,20},{28,24},{5,1},{9,5},{13... | collective-permute-start | bytes 1572872 | tf_op jit(solution)/shard_map/while/body/eval_jaxpr/ppermute | solution.py:20
  240.6 27.6 %collective-permute-start.1 = (f32[64,16,128]{2,1,0:T(8,128)S(1)}, f32[64,16,128]{2,1,0:T(8,128)S(1)}, u32[]{:S(2)}, u32[]{:S(2)}) collective-permute-start(f32[64,16,128]{2,1,0:T(8,128)S(1)} %get-tuple-element.615), channel_id=1, source_target_pairs={{0,4},{4,8},{8,12},{12,16},{16,20},{20,24},{24,28},{1,5},{5,9},{9,... | collective-permute-start | bytes 1572872 | tf_op jit(solution)/shard_map/while/body/eval_jaxpr/ppermute | solution.py:20
  286.6 342.5 %all-reduce.6.cloned.1.call-start = ((), (), s32[]{:S(2)}) async-start(), calls=%async_computation.1 | async-start | bytes 131072 | tf_op jit(solution)/shard_map/psum | solution.py:195
  286.6 8.2 copy-start
  353.1 2.0 copy-start.5
  356.1 17.4 %collective-permute-start.2 = (f32[64,16,128]{2,1,0:T(8,128)S(1)}, f32[64,16,128]{2,1,0:T(8,128)S(1)}, u32[]{:S(2)}, u32[]{:S(2)}) collective-permute-start(f32[64,16,128]{2,1,0:T(8,128)S(1)} %get-tuple-element.626), channel_id=1, source_target_pairs={{4,0},{8,4},{12,8},{16,12},{20,16},{24,20},{28,24},{5,1},{9,5},{13... | collective-permute-start | bytes 1572872 | tf_op jit(solution)/shard_map/while/body/eval_jaxpr/ppermute | solution.py:20
  357.4 27.5 %collective-permute-start.3 = (f32[64,16,128]{2,1,0:T(8,128)S(1)}, f32[64,16,128]{2,1,0:T(8,128)S(1)}, u32[]{:S(2)}, u32[]{:S(2)}) collective-permute-start(f32[64,16,128]{2,1,0:T(8,128)S(1)} %get-tuple-element.627), channel_id=1, source_target_pairs={{0,4},{4,8},{8,12},{12,16},{16,20},{20,24},{24,28},{1,5},{5,9},{9,... | collective-permute-start | bytes 1572872 | tf_op jit(solution)/shard_map/while/body/eval_jaxpr/ppermute | solution.py:20
  384.9 0.8 copy-start.9
  386.0 17.5 %collective-permute-start.2 = (f32[64,16,128]{2,1,0:T(8,128)S(1)}, f32[64,16,128]{2,1,0:T(8,128)S(1)}, u32[]{:S(2)}, u32[]{:S(2)}) collective-permute-start(f32[64,16,128]{2,1,0:T(8,128)S(1)} %get-tuple-element.626), channel_id=1, source_target_pairs={{4,0},{8,4},{12,8},{16,12},{20,16},{24,20},{28,24},{5,1},{9,5},{13... | collective-permute-start | bytes 1572872 | tf_op jit(solution)/shard_map/while/body/eval_jaxpr/ppermute | solution.py:20
  387.3 27.6 %collective-permute-start.3 = (f32[64,16,128]{2,1,0:T(8,128)S(1)}, f32[64,16,128]{2,1,0:T(8,128)S(1)}, u32[]{:S(2)}, u32[]{:S(2)}) collective-permute-start(f32[64,16,128]{2,1,0:T(8,128)S(1)} %get-tuple-element.627), channel_id=1, source_target_pairs={{0,4},{4,8},{8,12},{12,16},{16,20},{20,24},{24,28},{1,5},{5,9},{9,... | collective-permute-start | bytes 1572872 | tf_op jit(solution)/shard_map/while/body/eval_jaxpr/ppermute | solution.py:20
  414.9 0.8 copy-start.9
  416.1 17.5 %collective-permute-start.2 = (f32[64,16,128]{2,1,0:T(8,128)S(1)}, f32[64,16,128]{2,1,0:T(8,128)S(1)}, u32[]{:S(2)}, u32[]{:S(2)}) collective-permute-start(f32[64,16,128]{2,1,0:T(8,128)S(1)} %get-tuple-element.626), channel_id=1, source_target_pairs={{4,0},{8,4},{12,8},{16,12},{20,16},{24,20},{28,24},{5,1},{9,5},{13... | collective-permute-start | bytes 1572872 | tf_op jit(solution)/shard_map/while/body/eval_jaxpr/ppermute | solution.py:20
  417.4 27.6 %collective-permute-start.3 = (f32[64,16,128]{2,1,0:T(8,128)S(1)}, f32[64,16,128]{2,1,0:T(8,128)S(1)}, u32[]{:S(2)}, u32[]{:S(2)}) collective-permute-start(f32[64,16,128]{2,1,0:T(8,128)S(1)} %get-tuple-element.627), channel_id=1, source_target_pairs={{0,4},{4,8},{8,12},{12,16},{16,20},{20,24},{24,28},{1,5},{5,9},{9,... | collective-permute-start | bytes 1572872 | tf_op jit(solution)/shard_map/while/body/eval_jaxpr/ppermute | solution.py:20
  446.1 17.5 %collective-permute-start.2 = (f32[64,16,128]{2,1,0:T(8,128)S(1)}, f32[64,16,128]{2,1,0:T(8,128)S(1)}, u32[]{:S(2)}, u32[]{:S(2)}) collective-permute-start(f32[64,16,128]{2,1,0:T(8,128)S(1)} %get-tuple-element.626), channel_id=1, source_target_pairs={{4,0},{8,4},{12,8},{16,12},{20,16},{24,20},{28,24},{5,1},{9,5},{13... | collective-permute-start | bytes 1572872 | tf_op jit(solution)/shard_map/while/body/eval_jaxpr/ppermute | solution.py:20
  447.4 27.6 %collective-permute-start.3 = (f32[64,16,128]{2,1,0:T(8,128)S(1)}, f32[64,16,128]{2,1,0:T(8,128)S(1)}, u32[]{:S(2)}, u32[]{:S(2)}) collective-permute-start(f32[64,16,128]{2,1,0:T(8,128)S(1)} %get-tuple-element.627), channel_id=1, source_target_pairs={{0,4},{4,8},{8,12},{12,16},{16,20},{20,24},{24,28},{1,5},{5,9},{9,... | collective-permute-start | bytes 1572872 | tf_op jit(solution)/shard_map/while/body/eval_jaxpr/ppermute | solution.py:20
  476.1 17.5 %collective-permute-start.2 = (f32[64,16,128]{2,1,0:T(8,128)S(1)}, f32[64,16,128]{2,1,0:T(8,128)S(1)}, u32[]{:S(2)}, u32[]{:S(2)}) collective-permute-start(f32[64,16,128]{2,1,0:T(8,128)S(1)} %get-tuple-element.626), channel_id=1, source_target_pairs={{4,0},{8,4},{12,8},{16,12},{20,16},{24,20},{28,24},{5,1},{9,5},{13... | collective-permute-start | bytes 1572872 | tf_op jit(solution)/shard_map/while/body/eval_jaxpr/ppermute | solution.py:20
  477.4 27.6 %collective-permute-start.3 = (f32[64,16,128]{2,1,0:T(8,128)S(1)}, f32[64,16,128]{2,1,0:T(8,128)S(1)}, u32[]{:S(2)}, u32[]{:S(2)}) collective-permute-start(f32[64,16,128]{2,1,0:T(8,128)S(1)} %get-tuple-element.627), channel_id=1, source_target_pairs={{0,4},{4,8},{8,12},{12,16},{16,20},{20,24},{24,28},{1,5},{5,9},{9,... | collective-permute-start | bytes 1572872 | tf_op jit(solution)/shard_map/while/body/eval_jaxpr/ppermute | solution.py:20
  506.1 17.5 %collective-permute-start.2 = (f32[64,16,128]{2,1,0:T(8,128)S(1)}, f32[64,16,128]{2,1,0:T(8,128)S(1)}, u32[]{:S(2)}, u32[]{:S(2)}) collective-permute-start(f32[64,16,128]{2,1,0:T(8,128)S(1)} %get-tuple-element.626), channel_id=1, source_target_pairs={{4,0},{8,4},{12,8},{16,12},{20,16},{24,20},{28,24},{5,1},{9,5},{13... | collective-permute-start | bytes 1572872 | tf_op jit(solution)/shard_map/while/body/eval_jaxpr/ppermute | solution.py:20
  507.4 27.6 %collective-permute-start.3 = (f32[64,16,128]{2,1,0:T(8,128)S(1)}, f32[64,16,128]{2,1,0:T(8,128)S(1)}, u32[]{:S(2)}, u32[]{:S(2)}) collective-permute-start(f32[64,16,128]{2,1,0:T(8,128)S(1)} %get-tuple-element.627), channel_id=1, source_target_pairs={{0,4},{4,8},{8,12},{12,16},{16,20},{20,24},{24,28},{1,5},{5,9},{9,... | collective-permute-start | bytes 1572872 | tf_op jit(solution)/shard_map/while/body/eval_jaxpr/ppermute | solution.py:20
  536.2 17.5 %collective-permute-start.2 = (f32[64,16,128]{2,1,0:T(8,128)S(1)}, f32[64,16,128]{2,1,0:T(8,128)S(1)}, u32[]{:S(2)}, u32[]{:S(2)}) collective-permute-start(f32[64,16,128]{2,1,0:T(8,128)S(1)} %get-tuple-element.626), channel_id=1, source_target_pairs={{4,0},{8,4},{12,8},{16,12},{20,16},{24,20},{28,24},{5,1},{9,5},{13... | collective-permute-start | bytes 1572872 | tf_op jit(solution)/shard_map/while/body/eval_jaxpr/ppermute | solution.py:20
  537.5 27.6 %collective-permute-start.3 = (f32[64,16,128]{2,1,0:T(8,128)S(1)}, f32[64,16,128]{2,1,0:T(8,128)S(1)}, u32[]{:S(2)}, u32[]{:S(2)}) collective-permute-start(f32[64,16,128]{2,1,0:T(8,128)S(1)} %get-tuple-element.627), channel_id=1, source_target_pairs={{0,4},{4,8},{8,12},{12,16},{16,20},{20,24},{24,28},{1,5},{5,9},{9,... | collective-permute-start | bytes 1572872 | tf_op jit(solution)/shard_map/while/body/eval_jaxpr/ppermute | solution.py:20
  581.4 9.8 %copy-start.1 = (f32[64,8,16,128]{3,1,2,0:T(8,128)}, f32[64,8,16,128]{3,1,2,0:T(8,128)S(1)}, u32[]{:S(2)}) copy-start(f32[64,8,16,128]{3,1,2,0:T(8,128)S(1)} %get-tuple-element.396) | copy-start | bytes 12582916
  595.6 326.4 %all-reduce.8.cloned.1.call-start = ((), (), s32[]{:S(2)}) async-start(), calls=%async_computation.2 | async-start | bytes 131072 | tf_op jit(solution)/shard_map/psum | solution.py:195
  662.1 2.0 copy-start.4
  665.1 14.3 %collective-permute-start.4 = (f32[64,16,128]{2,1,0:T(8,128)S(1)}, f32[64,16,128]{2,1,0:T(8,128)S(1)}, u32[]{:S(2)}, u32[]{:S(2)}) collective-permute-start(f32[64,16,128]{2,1,0:T(8,128)S(1)} %get-tuple-element.638), channel_id=1, source_target_pairs={{4,0},{8,4},{12,8},{16,12},{20,16},{24,20},{28,24},{5,1},{9,5},{13... | collective-permute-start | bytes 1572872 | tf_op jit(solution)/shard_map/while/body/eval_jaxpr/ppermute | solution.py:20
  666.4 24.4 %collective-permute-start.5 = (f32[64,16,128]{2,1,0:T(8,128)S(1)}, f32[64,16,128]{2,1,0:T(8,128)S(1)}, u32[]{:S(2)}, u32[]{:S(2)}) collective-permute-start(f32[64,16,128]{2,1,0:T(8,128)S(1)} %get-tuple-element.639), channel_id=1, source_target_pairs={{0,4},{4,8},{8,12},{12,16},{16,20},{20,24},{24,28},{1,5},{5,9},{9,... | collective-permute-start | bytes 1572872 | tf_op jit(solution)/shard_map/while/body/eval_jaxpr/ppermute | solution.py:20
  691.9 17.5 %collective-permute-start.4 = (f32[64,16,128]{2,1,0:T(8,128)S(1)}, f32[64,16,128]{2,1,0:T(8,128)S(1)}, u32[]{:S(2)}, u32[]{:S(2)}) collective-permute-start(f32[64,16,128]{2,1,0:T(8,128)S(1)} %get-tuple-element.638), channel_id=1, source_target_pairs={{4,0},{8,4},{12,8},{16,12},{20,16},{24,20},{28,24},{5,1},{9,5},{13... | collective-permute-start | bytes 1572872 | tf_op jit(solution)/shard_map/while/body/eval_jaxpr/ppermute | solution.py:20
  693.2 27.6 %collective-permute-start.5 = (f32[64,16,128]{2,1,0:T(8,128)S(1)}, f32[64,16,128]{2,1,0:T(8,128)S(1)}, u32[]{:S(2)}, u32[]{:S(2)}) collective-permute-start(f32[64,16,128]{2,1,0:T(8,128)S(1)} %get-tuple-element.639), channel_id=1, source_target_pairs={{0,4},{4,8},{8,12},{12,16},{16,20},{20,24},{24,28},{1,5},{5,9},{9,... | collective-permute-start | bytes 1572872 | tf_op jit(solution)/shard_map/while/body/eval_jaxpr/ppermute | solution.py:20
  721.9 17.5 %collective-permute-start.4 = (f32[64,16,128]{2,1,0:T(8,128)S(1)}, f32[64,16,128]{2,1,0:T(8,128)S(1)}, u32[]{:S(2)}, u32[]{:S(2)}) collective-permute-start(f32[64,16,128]{2,1,0:T(8,128)S(1)} %get-tuple-element.638), channel_id=1, source_target_pairs={{4,0},{8,4},{12,8},{16,12},{20,16},{24,20},{28,24},{5,1},{9,5},{13... | collective-permute-start | bytes 1572872 | tf_op jit(solution)/shard_map/while/body/eval_jaxpr/ppermute | solution.py:20
  723.2 27.6 %collective-permute-start.5 = (f32[64,16,128]{2,1,0:T(8,128)S(1)}, f32[64,16,128]{2,1,0:T(8,128)S(1)}, u32[]{:S(2)}, u32[]{:S(2)}) collective-permute-start(f32[64,16,128]{2,1,0:T(8,128)S(1)} %get-tuple-element.639), channel_id=1, source_target_pairs={{0,4},{4,8},{8,12},{12,16},{16,20},{20,24},{24,28},{1,5},{5,9},{9,... | collective-permute-start | bytes 1572872 | tf_op jit(solution)/shard_map/while/body/eval_jaxpr/ppermute | solution.py:20
  752.0 17.5 %collective-permute-start.4 = (f32[64,16,128]{2,1,0:T(8,128)S(1)}, f32[64,16,128]{2,1,0:T(8,128)S(1)}, u32[]{:S(2)}, u32[]{:S(2)}) collective-permute-start(f32[64,16,128]{2,1,0:T(8,128)S(1)} %get-tuple-element.638), channel_id=1, source_target_pairs={{4,0},{8,4},{12,8},{16,12},{20,16},{24,20},{28,24},{5,1},{9,5},{13... | collective-permute-start | bytes 1572872 | tf_op jit(solution)/shard_map/while/body/eval_jaxpr/ppermute | solution.py:20
  753.3 27.6 %collective-permute-start.5 = (f32[64,16,128]{2,1,0:T(8,128)S(1)}, f32[64,16,128]{2,1,0:T(8,128)S(1)}, u32[]{:S(2)}, u32[]{:S(2)}) collective-permute-start(f32[64,16,128]{2,1,0:T(8,128)S(1)} %get-tuple-element.639), channel_id=1, source_target_pairs={{0,4},{4,8},{8,12},{12,16},{16,20},{20,24},{24,28},{1,5},{5,9},{9,... | collective-permute-start | bytes 1572872 | tf_op jit(solution)/shard_map/while/body/eval_jaxpr/ppermute | solution.py:20
  782.0 17.5 %collective-permute-start.4 = (f32[64,16,128]{2,1,0:T(8,128)S(1)}, f32[64,16,128]{2,1,0:T(8,128)S(1)}, u32[]{:S(2)}, u32[]{:S(2)}) collective-permute-start(f32[64,16,128]{2,1,0:T(8,128)S(1)} %get-tuple-element.638), channel_id=1, source_target_pairs={{4,0},{8,4},{12,8},{16,12},{20,16},{24,20},{28,24},{5,1},{9,5},{13... | collective-permute-start | bytes 1572872 | tf_op jit(solution)/shard_map/while/body/eval_jaxpr/ppermute | solution.py:20
  783.3 27.6 %collective-permute-start.5 = (f32[64,16,128]{2,1,0:T(8,128)S(1)}, f32[64,16,128]{2,1,0:T(8,128)S(1)}, u32[]{:S(2)}, u32[]{:S(2)}) collective-permute-start(f32[64,16,128]{2,1,0:T(8,128)S(1)} %get-tuple-element.639), channel_id=1, source_target_pairs={{0,4},{4,8},{8,12},{12,16},{16,20},{20,24},{24,28},{1,5},{5,9},{9,... | collective-permute-start | bytes 1572872 | tf_op jit(solution)/shard_map/while/body/eval_jaxpr/ppermute | solution.py:20
  812.0 17.5 %collective-permute-start.4 = (f32[64,16,128]{2,1,0:T(8,128)S(1)}, f32[64,16,128]{2,1,0:T(8,128)S(1)}, u32[]{:S(2)}, u32[]{:S(2)}) collective-permute-start(f32[64,16,128]{2,1,0:T(8,128)S(1)} %get-tuple-element.638), channel_id=1, source_target_pairs={{4,0},{8,4},{12,8},{16,12},{20,16},{24,20},{28,24},{5,1},{9,5},{13... | collective-permute-start | bytes 1572872 | tf_op jit(solution)/shard_map/while/body/eval_jaxpr/ppermute | solution.py:20
  813.3 27.6 %collective-permute-start.5 = (f32[64,16,128]{2,1,0:T(8,128)S(1)}, f32[64,16,128]{2,1,0:T(8,128)S(1)}, u32[]{:S(2)}, u32[]{:S(2)}) collective-permute-start(f32[64,16,128]{2,1,0:T(8,128)S(1)} %get-tuple-element.639), channel_id=1, source_target_pairs={{0,4},{4,8},{8,12},{12,16},{16,20},{20,24},{24,28},{1,5},{5,9},{9,... | collective-permute-start | bytes 1572872 | tf_op jit(solution)/shard_map/while/body/eval_jaxpr/ppermute | solution.py:20
  842.0 17.5 %collective-permute-start.4 = (f32[64,16,128]{2,1,0:T(8,128)S(1)}, f32[64,16,128]{2,1,0:T(8,128)S(1)}, u32[]{:S(2)}, u32[]{:S(2)}) collective-permute-start(f32[64,16,128]{2,1,0:T(8,128)S(1)} %get-tuple-element.638), channel_id=1, source_target_pairs={{4,0},{8,4},{12,8},{16,12},{20,16},{24,20},{28,24},{5,1},{9,5},{13... | collective-permute-start | bytes 1572872 | tf_op jit(solution)/shard_map/while/body/eval_jaxpr/ppermute | solution.py:20
  843.3 27.6 %collective-permute-start.5 = (f32[64,16,128]{2,1,0:T(8,128)S(1)}, f32[64,16,128]{2,1,0:T(8,128)S(1)}, u32[]{:S(2)}, u32[]{:S(2)}) collective-permute-start(f32[64,16,128]{2,1,0:T(8,128)S(1)} %get-tuple-element.639), channel_id=1, source_target_pairs={{0,4},{4,8},{8,12},{12,16},{16,20},{20,24},{24,28},{1,5},{5,9},{9,... | collective-permute-start | bytes 1572872 | tf_op jit(solution)/shard_map/while/body/eval_jaxpr/ppermute | solution.py:20
  (18 other events, 14.3 us)
Sparse Core Ops, SparseCore 0:
  286.7 33.2 all-reduce.3
  595.7 33.2 all-reduce.5
  889.5 32.4 all-reduce.7
where the time goes:
time: 948 us; the launch traced here: 936 us
  waiting for transfers between devices  510 us (54%)
  starting transfers between devices  153 us (16%)
  local copies, waits for them, and re-layouts  130 us (14%)
  other arithmetic  93.3 us (10%)
  between operations  29.6 us (3%)
  matrix products  18.5 us (2%)
    ppermute x42, waiting for transfers between devices, shifted(): return lax.ppermute(array, axis, pairs)  450 us
    ppermute x42, starting transfers between devices, shifted(): return lax.ppermute(array, axis, pairs)  153 us
    psum x3, waiting for transfers between devices, local(): volumetric_internal = lax.psum(partial_value, 'mode')  59.9 us
    div x3, other arithmetic, transport_forcing(): return gathered / broadcast_spectral(entry_location[7])  37.6 us
    slice x6, local copies, waits for them, and re-layouts, transport_forcing(): jnp.roll(mode_group_internal, 1, 3)  31.7 us
    unnamed x42, local copies, waits for them, and re-layouts  25.9 us
    rev x3, local copies, waits for them, and re-layouts, local(): swept_energy[:, ::-1]  20.2 us
    rev x3, local copies, waits for them, and re-layouts, local(): equilibrium_reemission[:, ::-1]  20.1 us
  transfers between devices with their start and end apart: 45, of which 45 were waited for; matrix products, arithmetic and copies ran while one was open for 3% of the time, Pallas kernels for 0%

commit v1 on v0

v1 whole, which is shorter than its diff:
```python
import functools
import math

import jax
import jax.numpy as jnp
import numpy as np
from jax import lax
from jax.experimental import pallas as pl
from jax.experimental.pallas import tpu as pltpu
from jax.sharding import PartitionSpec as P

FREQ_GROUPS = 8
DIRS = 32
ITERS = 3
NEWTON = 4
PSEUDO_RATE = 0.03

SELF, UPY, UPZ, THERM, QUART, HEAT, RATIO, COMPOSITE, WALL = range(9)
FORWARD, SHIFT_Y, SHIFT_Z = range(3)

SMEM = pl.BlockSpec(memory_space=pltpu.SMEM)


def slot_tables(labels, speed, rate, storage, threshold, generation, depth, width_y, width_z):
    band = labels // DIRS
    direction = labels % DIRS
    of_band = (band[None, :] == jnp.arange(FREQ_GROUPS, dtype=jnp.int32)[:, None]).astype(jnp.float32)
    speed, rate, storage, threshold, generation = (
        jnp.sum(of_band * value[:, None], axis=0)
        for value in (speed, rate, storage, threshold, generation)
    )
    polar = direction % 4
    cosine = jnp.where((polar == 0) | (polar == 3), np.float32(0.99995), np.float32(0.9999))
    sine = jnp.sqrt(1.0 - cosine * cosine)
    azimuth = ((direction // 4).astype(jnp.float32) + 0.5) * (2.0 * math.pi / (DIRS // 4))
    vy = speed * sine * jnp.cos(azimuth)
    vz = speed * sine * jnp.sin(azimuth)
    vx = speed * cosine
    diagonal = vx + jnp.abs(vy) + jnp.abs(vz) + rate + PSEUDO_RATE
    quartic = 1.0 / (4.0 * threshold**3)
    ratio = vx / diagonal
    composite = ratio
    for _ in range(int(math.log2(depth))):
        composite = composite * composite
    therm = rate * storage / diagonal
    floats = jnp.stack(
        [
            PSEUDO_RATE / diagonal,
            jnp.abs(vy) / diagonal,
            jnp.abs(vz) / diagonal,
            therm,
            therm * quartic,
            generation / diagonal,
            ratio,
            composite,
            storage * (1.0 + quartic),
        ]
    )
    ints = jnp.stack(
        [
            (polar < 2).astype(jnp.int32),
            jnp.where(vy > 0, 1, width_y - 1).astype(jnp.int32),
            jnp.where(vz > 0, 1, width_z - 1).astype(jnp.int32),
        ]
    )
    return floats, ints


def newton(density, kelvin, linear, quart):
    for _ in range(NEWTON):
        cube = kelvin * kelvin * kelvin
        residual = linear * kelvin + quart * (kelvin * cube) - density
        kelvin = kelvin - residual / (linear + 4.0 * quart * cube)
    return kelvin


def sweep_body(block, depth, floats, ints, first, energy, incoming, kelvin, quartic, heat, swept, outgoing):
    base = pl.program_id(0) * block

    def one_slot(i, carry):
        s = base + i
        forward = ints[FORWARD, s]
        start = jnp.where(forward == 1, 0, depth - 1)
        step = jnp.where(forward == 1, 1, -1)
        shift_y, shift_z = ints[SHIFT_Y, s], ints[SHIFT_Z, s]
        c_self, c_y, c_z = floats[SELF, s], floats[UPY, s], floats[UPZ, s]
        c_t, c_q, c_h = floats[THERM, s], floats[QUART, s], floats[HEAT, s]
        ratio = floats[RATIO, s]
        total = None
        fading = None if first else incoming[i]
        for j in range(depth):
            x = start + step * j
            value = energy[i, x]
            if not first:
                fading = ratio * fading
                value = value + fading
            source = (
                c_self * value
                + c_y * pltpu.roll(value, shift_y, 0)
                + c_z * pltpu.roll(value, shift_z, 1)
                + c_t * kelvin[x]
                + c_q * quartic[x]
                + c_h * heat[x]
            )
            total = source if total is None else ratio * total + source
            swept[i, x] = total
        outgoing[i] = total
        return carry

    lax.fori_loop(0, block, one_slot, 0)


def first_kernel(block, depth, floats, ints, energy, kelvin, flag, swept, outgoing, quartic, heat):
    @pl.when(pl.program_id(0) == 0)
    def _():
        square = kelvin[...] * kelvin[...]
        quartic[...] = square * square
        heat[...] = flag[...].astype(jnp.float32)

    sweep_body(block, depth, floats, ints, True, energy, None, kelvin, quartic, heat, swept, outgoing)


def next_kernel(
    block, depth, parts, floats, ints, sums, energy, incoming, before, flag, *rest
):
    densities, (swept, outgoing, kelvin, quartic, heat) = rest[:parts], rest[parts:]

    @pl.when(pl.program_id(0) == 0)
    def _():
        now = newton(add_up(densities) * (1.0 / DIRS), before[...], sums[0], sums[1])
        kelvin[...] = now
        square = now * now
        quartic[...] = square * square
        heat[...] = flag[...].astype(jnp.float32)

    sweep_body(block, depth, floats, ints, False, energy, incoming, kelvin, quartic, heat, swept, outgoing)


def add_up(refs):
    values = [ref[...] for ref in refs]
    while len(values) > 1:
        values = [a + b for a, b in zip(values[::2], values[1::2])]
    return values[0]


def density_kernel(block, depth, final, floats, ints, swept, incoming, *outs):
    density = outs[-1]

    @pl.when(pl.program_id(0) == 0)
    def _():
        density[...] = jnp.zeros_like(density)

    base = pl.program_id(0) * block

    def one_slot(i, carry):
        s = base + i
        forward = ints[FORWARD, s]
        start = jnp.where(forward == 1, 0, depth - 1)
        step = jnp.where(forward == 1, 1, -1)
        ratio = floats[RATIO, s]
        fading = incoming[i]
        for j in range(depth):
            x = start + step * j
            fading = ratio * fading
            value = swept[i, x] + fading
            if final:
                outs[0][i, x] = value
            density[x] += value
        return carry

    lax.fori_loop(0, block, one_slot, 0)


def newton_kernel(sums, before, *rest):
    densities, kelvin = rest[:-1], rest[-1]
    kelvin[...] = newton(add_up(densities) * (1.0 / DIRS), before[...], sums[0], sums[1])


def scan_kernel(own, slabs, home, floats, ints, outgoing, incoming):
    base = home[0] * own

    def one_slot(i, carry):
        s = base + i
        forward = ints[FORWARD, s]
        start = jnp.where(forward == 1, 0, slabs - 1)
        step = jnp.where(forward == 1, 1, -1)
        composite = floats[COMPOSITE, s]
        entering = jnp.full(outgoing.shape[2:], floats[WALL, s], jnp.float32)
        for j in range(slabs):
            k = start + step * j
            incoming[k, i] = entering
            if j < slabs - 1:
                entering = composite * entering + outgoing[k, i]
        return carry

    lax.fori_loop(0, own, one_slot, 0)


def local(incoming_occupation, crystal_kelvin_given, generating_region_flag, labels, speed, rate, storage, threshold, generation):
    slots, depth, width_y, width_z = incoming_occupation.shape
    slabs, modes = lax.axis_size("slab"), lax.axis_size("mode")
    own = slots // slabs
    block = 8
    grid = (slots // block,)
    plane = (width_y, width_z)
    home = lax.axis_index("slab").astype(jnp.int32).reshape(1)
    floats, ints = slot_tables(labels, speed, rate, storage, threshold, generation, depth, width_y, width_z)
    sums = jnp.stack([jnp.sum(storage), jnp.sum(storage / (4.0 * threshold**3))])

    slot_block = pl.BlockSpec((block, depth, *plane), lambda i: (i, 0, 0, 0))
    face_block = pl.BlockSpec((block, *plane), lambda i: (i, 0, 0))
    cells = pl.BlockSpec((depth, *plane), lambda i: (0, 0, 0))
    energy_shape = jax.ShapeDtypeStruct((slots, depth, *plane), jnp.float32)
    face_shape = jax.ShapeDtypeStruct((slots, *plane), jnp.float32)
    cell_shape = jax.ShapeDtypeStruct((depth, *plane), jnp.float32)
    cell_scratch = pltpu.VMEM((depth, *plane), jnp.float32)
    params = pltpu.CompilerParams(vmem_limit_bytes=40 * 1024 * 1024)

    def exchange(outgoing):
        gathered = lax.all_to_all(outgoing.reshape(slabs, own, *plane), "slab", 0, 0)
        incoming = pl.pallas_call(
            functools.partial(scan_kernel, own, slabs),
            in_specs=[SMEM, SMEM, SMEM, pl.BlockSpec(memory_space=pltpu.VMEM)],
            out_specs=pl.BlockSpec(memory_space=pltpu.VMEM),
            out_shape=jax.ShapeDtypeStruct((slabs, own, *plane), jnp.float32),
            compiler_params=params,
            name="slab_scan",
        )(home, floats, ints, gathered)
        return lax.all_to_all(incoming, "slab", 0, 0).reshape(slots, *plane)

    def spread(density):
        return [density] + [
            lax.ppermute(density, "mode", [(i, i ^ by) for i in range(modes)]) for by in range(1, modes)
        ]

    kelvin = crystal_kelvin_given
    swept, outgoing = pl.pallas_call(
        functools.partial(first_kernel, block, depth),
        grid=grid,
        in_specs=[SMEM, SMEM, slot_block, cells, cells],
        out_specs=[slot_block, face_block],
        out_shape=[energy_shape, face_shape],
        scratch_shapes=[cell_scratch, cell_scratch],
        compiler_params=params,
        name="first_sweep",
    )(floats, ints, incoming_occupation, kelvin, generating_region_flag)
    for _ in range(ITERS - 1):
        incoming = exchange(outgoing)
        density = pl.pallas_call(
            functools.partial(density_kernel, block, depth, False),
            grid=grid,
            in_specs=[SMEM, SMEM, slot_block, face_block],
            out_specs=cells,
            out_shape=cell_shape,
            compiler_params=params,
            name="density",
        )(floats, ints, swept, incoming)
        swept, outgoing, kelvin = pl.pallas_call(
            functools.partial(next_kernel, block, depth, modes),
            grid=grid,
            in_specs=[SMEM, SMEM, SMEM, slot_block, face_block, cells, cells] + [cells] * modes,
            out_specs=[slot_block, face_block, cells],
            out_shape=[energy_shape, face_shape, cell_shape],
            scratch_shapes=[cell_scratch, cell_scratch],
            compiler_params=params,
            name="next_sweep",
        )(floats, ints, sums, swept, incoming, kelvin, generating_region_flag, *spread(density))
    incoming = exchange(outgoing)
    energy, density = pl.pallas_call(
        functools.partial(density_kernel, block, depth, True),
        grid=grid,
        in_specs=[SMEM, SMEM, slot_block, face_block],
        out_specs=[slot_block, cells],
        out_shape=[energy_shape, cell_shape],
        compiler_params=params,
        name="final_energy",
    )(floats, ints, swept, incoming)
    kelvin = pl.pallas_call(
        newton_kernel,
        in_specs=[SMEM] + [pl.BlockSpec(memory_space=pltpu.VMEM)] * (modes + 1),
        out_specs=pl.BlockSpec(memory_space=pltpu.VMEM),
        out_shape=cell_shape,
        compiler_params=params,
        name="final_kelvin",
    )(sums, kelvin, *spread(density))
    return energy, kelvin


def solution(mesh):
    return jax.shard_map(
        local,
        mesh=mesh,
        in_specs=(
            P("mode", "slab", None, None),
            P("slab", None, None),
            P("slab", None, None),
            P("mode"),
            P(),
            P(),
            P(),
            P(),
            P(),
        ),
        out_specs=(P("mode", "slab", None, None), P("slab", None, None)),
        check_vma=False,
    )
```

time: 948 us -> 178 us (0.19); the launches traced: 936 us -> 177 us
  waiting for transfers between devices: 510 us -> 38.2 us
  starting transfers between devices: 153 us -> 16.7 us
  local copies, waits for them, and re-layouts: 130 us -> 8.13 us
  other arithmetic: 93.3 us -> 4.17 us
  blocking collectives: 0 us -> 71.2 us
  Pallas kernels: 0 us -> 38 us
  between operations: 29.6 us -> 0.78 us
  matrix products: 18.5 us -> 0 us
    ppermute x42 -> x9, waiting for transfers between devices: 450 us -> 9.69 us  [spread(): lax.ppermute(density, 'mode', [(i, i ^ by) for i in range(modes)])]
    ppermute x42 -> x9, starting transfers between devices: 153 us -> 5.7 us  [spread(): lax.ppermute(density, 'mode', [(i, i ^ by) for i in range(modes)])]
    all_to_all x0 -> x4, blocking collectives: none -> 71.2 us  [the longest x2 36.1 us: exchange(): lax.all_to_all(outgoing.reshape(slabs, own, *plane), 'slab', 0, 0)]
    psum x3 -> x0, waiting for transfers between devices: 59.9 us -> none  [local(): volumetric_internal = lax.psum(partial_value, 'mode')]
    slice x17 -> x0, local copies, waits for them, and re-layouts: 46.5 us -> none  [the longest x6 31.7 us: transport_forcing(): jnp.roll(mode_group_internal, 1, 3)]
    rev x6 -> x0, local copies, waits for them, and re-layouts: 40.2 us -> none  [the longest x3 20.2 us: local(): swept_energy[:, ::-1]]
    div x6 -> x0, other arithmetic: 39.5 us -> none  [the longest x3 37.6 us: transport_forcing(): return gathered / broadcast_spectral(entry_location[7])]
    pallas_call x0 -> x10, Pallas kernels: none -> 38 us  [the longest x2 15 us: local(): pl.pallas_call(functools.partial(next_kernel, block, depth, modes), grid=...]
  transfers between devices with their start and end apart: 45 -> 11, of which waited for: 45 -> 8; matrix products, arithmetic and copies ran while one was open for 3% -> 1% of each run, Pallas kernels for 0% -> 0%
where the time goes in v1:
time: 178 us; the launch traced here: 177 us
  blocking collectives  71.2 us (40%)
  waiting for transfers between devices  38.2 us (21%)
  Pallas kernels  38 us (21%)
  starting transfers between devices  16.7 us (9%)
  local copies, waits for them, and re-layouts  8.13 us (5%)
  other arithmetic  4.17 us (2%)
    all_to_all x2, blocking collectives, exchange(): lax.all_to_all(outgoing.reshape(slabs, own, *plane), 'slab', 0, 0)  36.1 us
    all_to_all x2, blocking collectives, exchange(): return lax.all_to_all(incoming, 'slab', 0, 0).reshape(slots, *plane)  35.1 us
    pallas_call x2, Pallas kernels, local(): pl.pallas_call(functools.partial(next_kernel, block, depth, modes), grid=...  15 us
    all_to_all x1, waiting for transfers between devices, exchange(): lax.all_to_all(outgoing.reshape(slabs, own, *plane), 'slab', 0, 0)  14.5 us
    all_to_all x1, waiting for transfers between devices, exchange(): return lax.all_to_all(incoming, 'slab', 0, 0).reshape(slots, *plane)  14.1 us
    ppermute x9, waiting for transfers between devices, spread(): lax.ppermute(density, 'mode', [(i, i ^ by) for i in range(modes)])  9.69 us
    unnamed x20, local copies, waits for them, and re-layouts  8.09 us
    pallas_call x1, Pallas kernels, local(): pl.pallas_call(functools.partial(first_kernel, block, depth), grid=grid,...  7.93 us
  transfers between devices with their start and end apart: 11, of which 8 were waited for; matrix products, arithmetic and copies ran while one was open for 1% of the time, Pallas kernels for 0%

profile of v1, /device:TPU:0, one launch (start us, length us, event | category | flops | bytes accessed | tf_op | source)
XLA Modules:
  0.0 177.3 jit_solution(14248747258690817527)
XLA Ops:
  0.6 0.0 copy-start.8
  0.6 0.0 copy-start.9
  0.7 0.7 fusion.7
  1.3 0.7 and_select_fusion.3
  2.0 0.8 select_reduce_fusion
  2.8 0.1 fusion.8
  3.0 0.0 copy-start.3
  3.0 2.2 %copy-done.3 = f32[64,8,16,128]{3,2,1,0:T(8,128)S(1)} copy-done((f32[64,8,16,128]{3,2,1,0:T(8,128)S(1)}, f32[64,8,16,128]{3,2,1,0:T(8,128)}, u32[]{:S(2)}) %copy-start.3) | copy-done | bytes 4194328
  5.2 0.0 copy-start.4
  5.2 0.8 copy-done.4
  6.1 0.0 copy-start.6
  6.1 0.8 copy-done.6
  6.9 7.9 %first_sweep.1 = (f32[64,8,16,128]{3,2,1,0:T(8,128)S(1)}, f32[64,16,128]{2,1,0:T(8,128)}) custom-call(f32[9,64]{1,0:T(8,128)S(1)} %stack.60.floats, s32[3,64]{1,0:T(4,128)S(1)} %pad_add_fusion.ints, f32[64,8,16,128]{3,2,1,0:T(8,128)S(1)} %copy-done.3, f32[8,16,128]{2,1,0:T(8,128)S(1)} %copy-done.6, s32[8,16,128]{2,1,0:T(8,128)S(1)} %copy-done.4), custom_call_target="tpu_custom_call" | custom-call | tf_op jit(solution)/shard_map/first_sweep/pallas_call | solution.py:237
  14.8 0.0 copy-start
  14.8 2.0 %copy-done = f32[64,8,16,128]{3,2,1,0:T(8,128)} copy-done((f32[64,8,16,128]{3,2,1,0:T(8,128)}, f32[64,8,16,128]{3,2,1,0:T(8,128)S(1)}, u32[]{:S(2)}) %copy-start) | copy-done | bytes 4194328
  16.8 0.0 copy-start.5
  16.8 0.0 copy-start.7
  16.8 7.4 %all-to-all-start = ((f32[8,8,16,128]{3,2,1,0:T(8,128)}), f32[8,8,16,128]{3,2,1,0:T(8,128)S(1)}, u32[]{:S(2)}, u32[]{:S(2)}) async-start(f32[8,8,16,128]{3,2,1,0:T(8,128)} %bitcast.16), calls=%async_computation | async-start | bytes 1048576 | tf_op jit(solution)/shard_map/all_to_all | solution.py:220
  24.3 14.5 %all-to-all-done.outgoing = f32[8,8,16,128]{3,2,1,0:T(8,128)S(1)} async-done(((f32[8,8,16,128]{3,2,1,0:T(8,128)}), f32[8,8,16,128]{3,2,1,0:T(8,128)S(1)}, u32[]{:S(2)}, u32[]{:S(2)}) %all-to-all-start) | async-done | bytes 524320 | tf_op jit(solution)/shard_map/all_to_all | solution.py:220
  38.7 1.7 slab_scan.3
  40.4 3.6 %all-to-all-start.1 = ((f32[8,8,16,128]{3,2,1,0:T(8,128)}), f32[8,8,16,128]{3,2,1,0:T(8,128)S(1)}, u32[]{:S(2)}, u32[]{:S(2)}) async-start(f32[8,8,16,128]{3,2,1,0:T(8,128)} %slab_scan.3), calls=%async_computation.1 | async-start | bytes 1048576 | tf_op jit(solution)/shard_map/all_to_all | solution.py:229
  44.1 0.0 copy-done.8
  44.1 0.0 copy-done.9
  44.1 0.6 fusion.12
  44.7 14.1 %all-to-all-done.1 = f32[8,8,16,128]{3,2,1,0:T(8,128)S(1)} async-done(((f32[8,8,16,128]{3,2,1,0:T(8,128)}), f32[8,8,16,128]{3,2,1,0:T(8,128)S(1)}, u32[]{:S(2)}, u32[]{:S(2)}) %all-to-all-start.1) | async-done | bytes 524320 | tf_op jit(solution)/shard_map/all_to_all | solution.py:229
  58.7 0.0 copy-start.1
  58.7 2.2 %copy-done.1 = f32[64,8,16,128]{3,2,1,0:T(8,128)S(1)} copy-done((f32[64,8,16,128]{3,2,1,0:T(8,128)S(1)}, f32[64,8,16,128]{3,2,1,0:T(8,128)}, u32[]{:S(2)}) %copy-start.1) | copy-done | bytes 4194328
  60.9 0.0 copy-start.2
  60.9 2.6 %density.2.rest_0_ = f32[8,16,128]{2,1,0:T(8,128)S(1)} custom-call(f32[9,64]{1,0:T(8,128)S(1)} %stack.60.floats, s32[3,64]{1,0:T(4,128)S(1)} %pad_add_fusion.ints, f32[64,8,16,128]{3,2,1,0:T(8,128)S(1)} %copy-done.1, f32[64,16,128]{2,1,0:T(8,128)S(1)} %bitcast.33), custom_call_target="tpu_custom_call" | custom-call | tf_op jit(solution)/shard_map/density/pallas_call | solution.py:249
  63.6 0.1 collective-permute-start.2
  63.6 1.6 collective-permute-start.1
  65.2 0.3 collective-permute-start
  65.5 1.3 pad_maximum_fusion.sums
  66.8 1.2 collective-permute-done.2.rest_3_
  68.0 1.5 collective-permute-done.1.rest_2_
  69.4 0.0 collective-permute-done.rest_1_
  69.4 0.0 copy-done.5
  69.4 0.0 copy-done.7
  69.4 0.0 copy-done.2
  69.4 7.5 %next_sweep.2 = (f32[64,8,16,128]{3,2,1,0:T(8,128)S(1)}, f32[64,16,128]{2,1,0:T(8,128)S(1)}, f32[8,16,128]{2,1,0:T(8,128)S(1)}) custom-call(f32[9,64]{1,0:T(8,128)S(1)} %stack.60.floats, s32[3,64]{1,0:T(4,128)S(1)} %pad_add_fusion.ints, f32[2]{0:T(128)S(1)} %pad_maximum_fusion.sums, f32[64,8,16,128]{3,2,1,0:T(8,128)S(1)} %copy-done.2, ...), custom_call_target="tpu_custom_call" | custom-call | tf_op jit(solution)/shard_map/next_sweep/pallas_call | solution.py:258
  77.0 18.0 %all_to_all.30.outgoing = f32[8,8,16,128]{3,2,1,0:T(8,128)S(1)} all-to-all(f32[8,8,16,128]{3,2,1,0:T(8,128)S(1)} %bitcast.39), channel_id=1, replica_groups=mesh['slab'=8,'mode'=4] {'slab'}, dimensions={0} | all-to-all | bytes 1048576 | tf_op jit(solution)/shard_map/all_to_all | solution.py:220
  94.9 0.9 slab_scan.4
  95.8 17.5 %all_to_all.31 = f32[8,8,16,128]{3,2,1,0:T(8,128)S(1)} all-to-all(f32[8,8,16,128]{3,2,1,0:T(8,128)S(1)} %slab_scan.4), channel_id=1, replica_groups=mesh['slab'=8,'mode'=4] {'slab'}, dimensions={0} | all-to-all | bytes 1048576 | tf_op jit(solution)/shard_map/all_to_all | solution.py:229
  113.3 2.6 %density.3.rest_0_ = f32[8,16,128]{2,1,0:T(8,128)S(1)} custom-call(f32[9,64]{1,0:T(8,128)S(1)} %stack.60.floats, s32[3,64]{1,0:T(4,128)S(1)} %pad_add_fusion.ints, f32[64,8,16,128]{3,2,1,0:T(8,128)S(1)} %get-tuple-element.14.swept.energy, f32[64,16,128]{2,1,0:T(8,128)S(1)} %bitcast.35), custom_call_target="tpu_custom_call" | custom-call | tf_op jit(solution)/shard_map/density/pallas_call | solution.py:249
  116.0 0.1 collective-permute-start.5
  116.1 1.6 collective-permute-start.4
  117.7 0.2 collective-permute-start.3
  117.9 2.4 %collective-permute-done.5.rest_3_ = f32[8,16,128]{2,1,0:T(8,128)S(1)} collective-permute-done((f32[8,16,128]{2,1,0:T(8,128)S(1)}, f32[8,16,128]{2,1,0:T(8,128)S(1)}, u32[]{:S(2)}, u32[]{:S(2)}) %collective-permute-start.5) | collective-permute-done | bytes 65568 | tf_op jit(solution)/shard_map/ppermute | solution.py:233
  120.3 1.5 collective-permute-done.4.rest_2_
  121.8 0.0 collective-permute-done.3.rest_1_
  121.8 7.5 %next_sweep.3 = (f32[64,8,16,128]{3,2,1,0:T(8,128)S(1)}, f32[64,16,128]{2,1,0:T(8,128)S(1)}, f32[8,16,128]{2,1,0:T(8,128)S(1)}) custom-call(f32[9,64]{1,0:T(8,128)S(1)} %stack.60.floats, s32[3,64]{1,0:T(4,128)S(1)} %pad_add_fusion.ints, f32[2]{0:T(128)S(1)} %pad_maximum_fusion.sums, f32[64,8,16,128]{3,2,1,0:T(8,128)S(1)} %get-tuple-element.14.swept.energy, ...), custom_call_target="tpu_custom_call" | custom-call | tf_op jit(solution)/shard_map/next_sweep/pallas_call | solution.py:258
  129.3 18.1 %all_to_all.32.outgoing = f32[8,8,16,128]{3,2,1,0:T(8,128)S(1)} all-to-all(f32[8,8,16,128]{3,2,1,0:T(8,128)S(1)} %bitcast.38), channel_id=1, replica_groups=mesh['slab'=8,'mode'=4] {'slab'}, dimensions={0} | all-to-all | bytes 1048576 | tf_op jit(solution)/shard_map/all_to_all | solution.py:220
  147.4 0.9 slab_scan.5
  148.3 17.6 %all_to_all.33 = f32[8,8,16,128]{3,2,1,0:T(8,128)S(1)} all-to-all(f32[8,8,16,128]{3,2,1,0:T(8,128)S(1)} %slab_scan.5), channel_id=1, replica_groups=mesh['slab'=8,'mode'=4] {'slab'}, dimensions={0} | all-to-all | bytes 1048576 | tf_op jit(solution)/shard_map/all_to_all | solution.py:229
  165.9 5.1 %final_energy.1 = (f32[64,8,16,128]{3,2,1,0:T(8,128)}, f32[8,16,128]{2,1,0:T(8,128)S(1)}) custom-call(f32[9,64]{1,0:T(8,128)S(1)} %stack.60.floats, s32[3,64]{1,0:T(4,128)S(1)} %pad_add_fusion.ints, f32[64,8,16,128]{3,2,1,0:T(8,128)S(1)} %get-tuple-element.17.swept, f32[64,16,128]{2,1,0:T(8,128)S(1)} %bitcast.37), custom_call_target="tpu_custom_call" | custom-call | tf_op jit(solution)/shard_map/final_energy/pallas_call | solution.py:269
  171.0 0.0 collective-permute-start.8
  171.0 0.9 collective-permute-start.7
  171.9 0.9 collective-permute-start.6
  172.9 2.3 %collective-permute-done.8.rest_3_ = f32[8,16,128]{2,1,0:T(8,128)S(1)} collective-permute-done((f32[8,16,128]{2,1,0:T(8,128)S(1)}, f32[8,16,128]{2,1,0:T(8,128)S(1)}, u32[]{:S(2)}, u32[]{:S(2)}) %collective-permute-start.8) | collective-permute-done | bytes 65568 | tf_op jit(solution)/shard_map/ppermute | solution.py:233
  175.1 0.8 collective-permute-done.7.rest_2_
  176.0 0.0 collective-permute-done.6.rest_1_
  176.0 1.3 final_kelvin.1
  (6 shorter events, 0.1 us)
Async XLA Ops:
  0.6 43.4 %copy-start.8 = (f32[8]{0:T(128)S(1)}, f32[8]{0:T(128)}, u32[]{:S(2)}) copy-start(f32[8]{0:T(128)} %param.16) | copy-start | bytes 100
  0.6 43.4 %copy-start.9 = (f32[8]{0:T(128)S(1)}, f32[8]{0:T(128)}, u32[]{:S(2)}) copy-start(f32[8]{0:T(128)} %param.15) | copy-start | bytes 100
  3.0 2.2 %copy-start.3 = (f32[64,8,16,128]{3,2,1,0:T(8,128)S(1)}, f32[64,8,16,128]{3,2,1,0:T(8,128)}, u32[]{:S(2)}) copy-start(f32[64,8,16,128]{3,2,1,0:T(8,128)} %energy.1) | copy-start | bytes 12582916
  5.2 0.8 copy-start.4
  6.1 0.8 copy-start.6
  14.8 2.0 %copy-start = (f32[64,8,16,128]{3,2,1,0:T(8,128)}, f32[64,8,16,128]{3,2,1,0:T(8,128)S(1)}, u32[]{:S(2)}) copy-start(f32[64,8,16,128]{3,2,1,0:T(8,128)S(1)} %get-tuple-element.12.swept.energy) | copy-start | bytes 12582916
  16.8 52.6 %copy-start.5 = (s32[8,16,128]{2,1,0:T(8,128)S(1)}, s32[8,16,128]{2,1,0:T(8,128)}, u32[]{:S(2)}) copy-start(s32[8,16,128]{2,1,0:T(8,128)} %flag.5) | copy-start | bytes 196612
  16.8 52.6 %copy-start.7 = (f32[8,16,128]{2,1,0:T(8,128)S(1)}, f32[8,16,128]{2,1,0:T(8,128)}, u32[]{:S(2)}) copy-start(f32[8,16,128]{2,1,0:T(8,128)} %before.1) | copy-start | bytes 196612
  16.8 21.9 %all-to-all-start = ((f32[8,8,16,128]{3,2,1,0:T(8,128)}), f32[8,8,16,128]{3,2,1,0:T(8,128)S(1)}, u32[]{:S(2)}, u32[]{:S(2)}) async-start(f32[8,8,16,128]{3,2,1,0:T(8,128)} %bitcast.16), calls=%async_computation | async-start | bytes 1048576 | tf_op jit(solution)/shard_map/all_to_all | solution.py:220
  40.4 18.3 %all-to-all-start.1 = ((f32[8,8,16,128]{3,2,1,0:T(8,128)}), f32[8,8,16,128]{3,2,1,0:T(8,128)S(1)}, u32[]{:S(2)}, u32[]{:S(2)}) async-start(f32[8,8,16,128]{3,2,1,0:T(8,128)} %slab_scan.3), calls=%async_computation.1 | async-start | bytes 1048576 | tf_op jit(solution)/shard_map/all_to_all | solution.py:229
  58.7 2.2 %copy-start.1 = (f32[64,8,16,128]{3,2,1,0:T(8,128)S(1)}, f32[64,8,16,128]{3,2,1,0:T(8,128)}, u32[]{:S(2)}) copy-start(f32[64,8,16,128]{3,2,1,0:T(8,128)} %copy-done) | copy-start | bytes 12582916
  60.9 8.5 %copy-start.2 = (f32[64,8,16,128]{3,2,1,0:T(8,128)S(1)}, f32[64,8,16,128]{3,2,1,0:T(8,128)}, u32[]{:S(2)}) copy-start(f32[64,8,16,128]{3,2,1,0:T(8,128)} %copy-done) | copy-start | bytes 12582916
  63.6 4.4 %collective-permute-start.2 = (f32[8,16,128]{2,1,0:T(8,128)S(1)}, f32[8,16,128]{2,1,0:T(8,128)S(1)}, u32[]{:S(2)}, u32[]{:S(2)}) collective-permute-start(f32[8,16,128]{2,1,0:T(8,128)S(1)} %density.2.rest_0_), channel_id=1, source_target_pairs={{0,3},{1,2},{2,1},{3,0},{4,7},{5,6},{6,5},{7,4},{8,11},{9,10},{10,... | collective-permute-start | bytes 196616 | tf_op jit(solution)/shard_map/ppermute | solution.py:233
  63.6 5.8 %collective-permute-start.1 = (f32[8,16,128]{2,1,0:T(8,128)S(1)}, f32[8,16,128]{2,1,0:T(8,128)S(1)}, u32[]{:S(2)}, u32[]{:S(2)}) collective-permute-start(f32[8,16,128]{2,1,0:T(8,128)S(1)} %density.2.rest_0_), channel_id=1, source_target_pairs={{0,2},{1,3},{2,0},{3,1},{4,6},{5,7},{6,4},{7,5},{8,10},{9,11},{10,... | collective-permute-start | bytes 196616 | tf_op jit(solution)/shard_map/ppermute | solution.py:233
  65.2 4.2 %collective-permute-start = (f32[8,16,128]{2,1,0:T(8,128)S(1)}, f32[8,16,128]{2,1,0:T(8,128)S(1)}, u32[]{:S(2)}, u32[]{:S(2)}) collective-permute-start(f32[8,16,128]{2,1,0:T(8,128)S(1)} %density.2.rest_0_), channel_id=1, source_target_pairs={{0,1},{1,0},{2,3},{3,2},{4,5},{5,4},{6,7},{7,6},{8,9},{9,8},{10,11... | collective-permute-start | bytes 196616 | tf_op jit(solution)/shard_map/ppermute | solution.py:233
  116.0 4.3 %collective-permute-start.5 = (f32[8,16,128]{2,1,0:T(8,128)S(1)}, f32[8,16,128]{2,1,0:T(8,128)S(1)}, u32[]{:S(2)}, u32[]{:S(2)}) collective-permute-start(f32[8,16,128]{2,1,0:T(8,128)S(1)} %density.3.rest_0_), channel_id=1, source_target_pairs={{0,3},{1,2},{2,1},{3,0},{4,7},{5,6},{6,5},{7,4},{8,11},{9,10},{10,... | collective-permute-start | bytes 196616 | tf_op jit(solution)/shard_map/ppermute | solution.py:233
  116.1 5.8 %collective-permute-start.4 = (f32[8,16,128]{2,1,0:T(8,128)S(1)}, f32[8,16,128]{2,1,0:T(8,128)S(1)}, u32[]{:S(2)}, u32[]{:S(2)}) collective-permute-start(f32[8,16,128]{2,1,0:T(8,128)S(1)} %density.3.rest_0_), channel_id=1, source_target_pairs={{0,2},{1,3},{2,0},{3,1},{4,6},{5,7},{6,4},{7,5},{8,10},{9,11},{10,... | collective-permute-start | bytes 196616 | tf_op jit(solution)/shard_map/ppermute | solution.py:233
  117.7 4.1 %collective-permute-start.3 = (f32[8,16,128]{2,1,0:T(8,128)S(1)}, f32[8,16,128]{2,1,0:T(8,128)S(1)}, u32[]{:S(2)}, u32[]{:S(2)}) collective-permute-start(f32[8,16,128]{2,1,0:T(8,128)S(1)} %density.3.rest_0_), channel_id=1, source_target_pairs={{0,1},{1,0},{2,3},{3,2},{4,5},{5,4},{6,7},{7,6},{8,9},{9,8},{10,11... | collective-permute-start | bytes 196616 | tf_op jit(solution)/shard_map/ppermute | solution.py:233
  171.0 4.1 %collective-permute-start.8 = (f32[8,16,128]{2,1,0:T(8,128)S(1)}, f32[8,16,128]{2,1,0:T(8,128)S(1)}, u32[]{:S(2)}, u32[]{:S(2)}) collective-permute-start(f32[8,16,128]{2,1,0:T(8,128)S(1)} %get-tuple-element.21.rest_0_), channel_id=1, source_target_pairs={{0,3},{1,2},{2,1},{3,0},{4,7},{5,6},{6,5},{7,4},{8,11},{9,10},{10,... | collective-permute-start | bytes 196616 | tf_op jit(solution)/shard_map/ppermute | solution.py:233
  171.0 4.9 %collective-permute-start.7 = (f32[8,16,128]{2,1,0:T(8,128)S(1)}, f32[8,16,128]{2,1,0:T(8,128)S(1)}, u32[]{:S(2)}, u32[]{:S(2)}) collective-permute-start(f32[8,16,128]{2,1,0:T(8,128)S(1)} %get-tuple-element.21.rest_0_), channel_id=1, source_target_pairs={{0,2},{1,3},{2,0},{3,1},{4,6},{5,7},{6,4},{7,5},{8,10},{9,11},{10,... | collective-permute-start | bytes 196616 | tf_op jit(solution)/shard_map/ppermute | solution.py:233
  171.9 4.0 %collective-permute-start.6 = (f32[8,16,128]{2,1,0:T(8,128)S(1)}, f32[8,16,128]{2,1,0:T(8,128)S(1)}, u32[]{:S(2)}, u32[]{:S(2)}) collective-permute-start(f32[8,16,128]{2,1,0:T(8,128)S(1)} %get-tuple-element.21.rest_0_), channel_id=1, source_target_pairs={{0,1},{1,0},{2,3},{3,2},{4,5},{5,4},{6,7},{7,6},{8,9},{9,8},{10,11... | collective-permute-start | bytes 196616 | tf_op jit(solution)/shard_map/ppermute | solution.py:233

commit v2 on v1

v2 whole, which is shorter than its diff:
```python
import functools
import math

import jax
import jax.numpy as jnp
import numpy as np
from jax import lax
from jax.experimental import pallas as pl
from jax.experimental.pallas import tpu as pltpu
from jax.sharding import PartitionSpec as P

FREQ_GROUPS = 8
DIRS = 32
ITERS = 3
NEWTON = 4
PSEUDO_RATE = 0.03
GROUP = 4
COSINES = (np.float32(0.99995), np.float32(0.9999))

SELF, UPY, UPZ, RATIO, WALL, FULL, FULL_N, FULL_T, FULL_GROUP = range(9)
FORWARD, SHIFT_Y, SHIFT_Z, EDGE_Y, KIND = range(5)
SLAB, MODE = range(2)

SMEM = pl.BlockSpec(memory_space=pltpu.SMEM)
VMEM = pl.BlockSpec(memory_space=pltpu.VMEM)
PARAMS = pltpu.CompilerParams(vmem_limit_bytes=48 * 1024 * 1024)


def diagonal_of(speed, rate, cosine):
    sine = jnp.sqrt(1.0 - cosine * cosine)
    across = np.float32(math.cos(math.pi / 8) + math.sin(math.pi / 8))
    return speed * (cosine + sine * across) + rate + PSEUDO_RATE


def slot_tables(labels, speed, rate, storage, threshold, slab, slabs, depth, width_y, width_z):
    band = labels // DIRS
    direction = labels % DIRS
    of_band = (band[None, :] == jnp.arange(FREQ_GROUPS, dtype=jnp.int32)[:, None]).astype(jnp.float32)
    speed, rate, storage, threshold = (
        jnp.sum(of_band * value[:, None], axis=0) for value in (speed, rate, storage, threshold)
    )
    polar = direction % 4
    outer = (polar == 0) | (polar == 3)
    forward = polar < 2
    cosine = jnp.where(outer, COSINES[0], COSINES[1])
    sine = jnp.sqrt(1.0 - cosine * cosine)
    azimuth = ((direction // 4).astype(jnp.float32) + 0.5) * (2.0 * math.pi / (DIRS // 4))
    vy = speed * sine * jnp.cos(azimuth)
    vz = speed * sine * jnp.sin(azimuth)
    diagonal = diagonal_of(speed, rate, cosine)
    ratio = speed * cosine / diagonal
    full = lax.integer_pow(ratio, depth)
    at_wall = jnp.where(forward, slab == 0, slab == slabs - 1)
    wall = storage * (1.0 + 1.0 / (4.0 * threshold**3))
    floats = jnp.stack(
        [
            PSEUDO_RATE / diagonal,
            jnp.abs(vy) / diagonal,
            jnp.abs(vz) / diagonal,
            ratio,
            jnp.where(at_wall, wall, 0.0),
            full,
            depth * full,
            (depth * (depth + 1) // 2) * full,
            lax.integer_pow(full, GROUP),
        ]
    )
    ints = jnp.stack(
        [
            forward.astype(jnp.int32),
            jnp.where(vy > 0, 1, 7).astype(jnp.int32),
            jnp.where(vz > 0, 1, width_z - 1).astype(jnp.int32),
            jnp.where(vy > 0, 0, 7).astype(jnp.int32),
            2 * band + jnp.where(outer, 0, 1),
        ]
    )
    x = jnp.arange(slabs * depth, dtype=jnp.int32)[:, None]
    past = jnp.where(forward[None, :], x - (slab * depth + depth - 1), slab * depth - x)
    n = past.astype(jnp.float32)
    weight = jnp.where(past > 0, jnp.power(ratio[None, :], jnp.maximum(n, 0.0)), 0.0)
    return floats, ints, jnp.concatenate([weight, n * weight, (0.5 * n * (n + 1.0)) * weight], axis=1)


def kind_table(speed, rate, storage, threshold, generation):
    rows = []
    for cosine in COSINES:
        diagonal = diagonal_of(speed, rate, cosine)
        therm = rate * storage / diagonal
        rows.append(jnp.stack([therm, therm / (4.0 * threshold**3), generation / diagonal]))
    return jnp.stack(rows, axis=2).reshape(3, 2 * FREQ_GROUPS)


def newton(density, kelvin, linear, quart):
    for _ in range(NEWTON):
        cube = kelvin * kelvin * kelvin
        residual = linear * kelvin + quart * (kelvin * cube) - density
        kelvin = kelvin - residual / (linear + 4.0 * quart * cube)
    return kelvin


def add_up(refs):
    values = [ref[...] for ref in refs]
    while len(values) > 1:
        values = [a + b for a, b in zip(values[::2], values[1::2])]
    return values[0]


def stencil(low, high, c_self, c_y, c_z, shift_y, shift_z, at_edge):
    turned_low, turned_high = pltpu.roll(low, shift_y, 0), pltpu.roll(high, shift_y, 0)
    up_low = jnp.where(at_edge, turned_high, turned_low)
    up_high = jnp.where(at_edge, turned_low, turned_high)
    return (
        c_self * low + c_y * up_low + c_z * pltpu.roll(low, shift_z, 1),
        c_self * high + c_y * up_high + c_z * pltpu.roll(high, shift_z, 1),
    )


def sweep_kernel(which, sizes, *refs):
    block, blocks, depth, width_y, slots, modes, group = sizes
    refs = list(refs)
    take = lambda count: [refs.pop(0) for _ in range(count)]
    meta, floats, ints, kinds, energy, flag, matrix = take(7)
    kelvins = take(1 if which == 1 else modes)
    older = take(which - 1)
    (swept,) = take(1)
    if which == 1:
        stencil_one, stencil_two, quarter = take(3)
    elif which == 2:
        (stencil_one,) = take(1)
    faces = take(group)
    shares = take(modes)
    outgoing, density, sources, kelvin = take(4)
    own = slots // group
    rows = width_y // modes
    step = pl.program_id(0)
    slab, mode = meta[SLAB], meta[MODE]

    @pl.when(step == 0)
    def _():
        if which == 1:
            kelvin[...] = kelvins[0][...]
            for yy in range(rows):
                quarter[:, yy * 128 : (yy + 1) * 128] = kelvin[pl.ds(mode * rows + yy, depth, stride=width_y), :]
        else:
            for by in range(modes):
                for yy in range(rows):
                    y = (mode ^ by) * rows + yy
                    kelvin[pl.ds(y, depth, stride=width_y), :] = kelvins[by][:, yy * 128 : (yy + 1) * 128]
        density[...] = jnp.zeros_like(density)

        def one_cell_row(x, carry):
            at = pl.ds(x * width_y, width_y)
            t = kelvin[at, :]
            square = t * t
            fourth = square * square
            heat = flag[at, :].astype(jnp.float32)
            for kind in range(2 * FREQ_GROUPS):
                sources[kind, at, :] = kinds[0, kind] * t + kinds[1, kind] * fourth + kinds[2, kind] * heat
            return carry

        lax.fori_loop(0, depth, one_cell_row, 0)

    row = lax.broadcasted_iota(jnp.int32, (8, 128), 0)

    def one_slot(i, carry):
        s = step * block + i
        forward = ints[FORWARD, s]
        start = jnp.where(forward == 1, 0, depth - 1)
        stride = jnp.where(forward == 1, 1, -1)
        c_self, c_y, c_z, ratio = floats[SELF, s], floats[UPY, s], floats[UPZ, s], floats[RATIO, s]
        kind = ints[KIND, s]
        at_edge = row == ints[EDGE_Y, s]
        apply = lambda low, high: stencil(low, high, c_self, c_y, c_z, ints[SHIFT_Y, s], ints[SHIFT_Z, s], at_edge)
        total_low = total_high = jnp.full((8, 128), floats[WALL, s], jnp.float32)
        for j in range(depth):
            at = (start + stride * j) * 16
            at_low, at_high = pl.ds(at, 8), pl.ds(at + 8, 8)
            low, high = apply(energy[i, at_low, :], energy[i, at_high, :])
            total_low = ratio * total_low + (low + sources[kind, at_low, :])
            total_high = ratio * total_high + (high + sources[kind, at_high, :])
            swept[i, at_low, :] = total_low
            swept[i, at_high, :] = total_high
            density[at_low, :] += total_low
            density[at_high, :] += total_high
        at_low, at_high = pl.ds(s * 16, 8), pl.ds(s * 16 + 8, 8)
        outgoing[at_low, :] = total_low
        outgoing[at_high, :] = total_high
        if which < ITERS:
            low, high = apply(total_low, total_high)
            stencil_one[at_low, :] = low
            stencil_one[at_high, :] = high
        if which == 1:
            low, high = apply(low, high)
            stencil_two[at_low, :] = low
            stencil_two[at_high, :] = high
        return carry

    lax.fori_loop(0, block, one_slot, 0, unroll=2)

    @pl.when(step == blocks - 1)
    def _():
        face = stencil_two if which == 1 else stencil_one if which == 2 else outgoing
        for by in range(group):
            faces[by][...] = face[pl.ds(((slab % group) ^ by) * own * 16, own * 16), :]
        planes = [outgoing] + older
        home = pl.ds(slab * depth, depth)
        for by in range(modes):
            ys = [(mode ^ by) * rows + yy for yy in range(rows)]
            total = None
            for index, plane in enumerate(planes):
                right = jnp.concatenate([plane[pl.ds(y, slots, stride=width_y), :] for y in ys], axis=1)
                term = jnp.dot(
                    matrix[:, index * slots : (index + 1) * slots],
                    right,
                    precision=lax.Precision.HIGHEST,
                    preferred_element_type=jnp.float32,
                )
                total = term if total is None else total + term
            shares[by][...] = total
            shares[by][home, :] += jnp.concatenate([density[pl.ds(y, depth, stride=width_y), :] for y in ys], axis=1)


def partial_kernel(slabs, depth, modes, meta, *refs):
    shares, outs, total = refs[:modes], refs[modes:-1], refs[-1]
    total[...] = add_up(shares)
    for by in range(slabs):
        outs[by][...] = total[pl.ds((meta[SLAB] ^ by) * depth, depth), :]


def newton_kernel(sums, before, *rest):
    parts, kelvin = rest[:-1], rest[-1]
    kelvin[...] = newton(add_up(parts) * (1.0 / DIRS), before[...], sums[0], sums[1])


def compose_kernel(own, group, earlier, meta, floats, ints, *refs):
    refs = list(refs)
    received, entered = refs[:group], refs[group : group + earlier]
    composite, effective = refs[group + earlier :]
    place = meta[SLAB] % group
    for by in range(group):
        effective[place ^ by] = received[by][...]

    def one_slot(i, carry):
        s = place * own + i
        forward = ints[FORWARD, s]
        start = jnp.where(forward == 1, 0, group - 1)
        stride = jnp.where(forward == 1, 1, -1)
        at = pl.ds(i * 16, 16)
        total = jnp.zeros((16, 128), jnp.float32)
        for j in range(group):
            k = start + stride * j
            value = effective[k, at, :]
            if earlier:
                for back in range(earlier):
                    value += floats[FULL_N + back, s] * entered[earlier - 1 - back][k, at, :]
                effective[k, at, :] = value
            total = floats[FULL, s] * total + value
        composite[at, :] = total
        return carry

    lax.fori_loop(0, own, one_slot, 0)


def enter_kernel(own, group, groups, meta, floats, ints, effective, *refs):
    composites, (entered, *outs, ordered) = refs[:groups], refs[groups:]
    slab = meta[SLAB]
    place, mine = slab % group, slab // group
    for by in range(groups):
        ordered[mine ^ by] = composites[by][...]

    def one_slot(i, carry):
        s = place * own + i
        forward = ints[FORWARD, s]
        start = jnp.where(forward == 1, 0, group - 1)
        stride = jnp.where(forward == 1, 1, -1)
        begin = jnp.where(forward == 1, 0, groups - 1)
        ahead = jnp.where(forward == 1, mine, groups - 1 - mine)
        at = pl.ds(i * 16, 16)
        total = jnp.zeros((16, 128), jnp.float32)
        for g in range(groups - 1):
            later = floats[FULL_GROUP, s] * total + ordered[begin + stride * g, at, :]
            total = jnp.where(g < ahead, later, total)
        for j in range(group):
            k = start + stride * j
            entered[k, at, :] = total
            if j < group - 1:
                total = floats[FULL, s] * total + effective[k, at, :]
        return carry

    lax.fori_loop(0, own, one_slot, 0)
    for by in range(group):
        outs[by][...] = entered[place ^ by]


def final_kernel(block, depth, width_y, own, group, modes, meta, floats, ints, swept, *refs):
    planes = [refs[index * group : (index + 1) * group] for index in range(ITERS)]
    kelvins = refs[ITERS * group : ITERS * group + modes]
    energy, kelvin, *ordered = refs[ITERS * group + modes :]
    step = pl.program_id(0)
    place = meta[SLAB] % group
    rows = width_y // modes

    @pl.when(step == 0)
    def _():
        for index in range(ITERS):
            for by in range(group):
                ordered[index][pl.ds((place ^ by) * own * 16, own * 16), :] = planes[index][by][...]
        for by in range(modes):
            for yy in range(rows):
                y = (meta[MODE] ^ by) * rows + yy
                kelvin[pl.ds(y, depth, stride=width_y), :] = kelvins[by][:, yy * 128 : (yy + 1) * 128]

    def one_slot(i, carry):
        s = step * block + i
        forward = ints[FORWARD, s]
        start = jnp.where(forward == 1, 0, depth - 1)
        stride = jnp.where(forward == 1, 1, -1)
        ratio = floats[RATIO, s]
        at = pl.ds(s * 16, 16)
        first, second, third = (ref[at, :] for ref in ordered)
        for j in range(depth):
            first = ratio * first
            second = ratio * second + first
            third = ratio * third + second
            here = pl.ds((start + stride * j) * 16, 16)
            energy[i, here, :] = swept[i, here, :] + third
        return carry

    lax.fori_loop(0, block, one_slot, 0, unroll=2)


def local(incoming_occupation, crystal_kelvin_given, generating_region_flag, labels, speed, rate, storage, threshold, generation):
    slots, depth, width_y, width_z = incoming_occupation.shape
    slabs, modes = lax.axis_size("slab"), lax.axis_size("mode")
    group, groups = GROUP, slabs // GROUP
    own = slots // group
    lanes = width_y // modes * width_z
    block = 8
    blocks = slots // block
    slab = lax.axis_index("slab").astype(jnp.int32)
    mode = lax.axis_index("mode").astype(jnp.int32)
    meta = jnp.stack([slab, mode])
    floats, ints, matrix = slot_tables(labels, speed, rate, storage, threshold, slab, slabs, depth, width_y, width_z)
    kinds = kind_table(speed, rate, storage, threshold, generation)
    sums = jnp.stack([jnp.sum(storage), jnp.sum(storage / (4.0 * threshold**3))])

    def shape(*dims):
        return jax.ShapeDtypeStruct(dims, jnp.float32)

    def whole(*dims):
        return pl.BlockSpec(dims, lambda i: (0,) * len(dims))

    def swap(array, axis, by):
        size = lax.axis_size(axis)
        return lax.ppermute(array, axis, [(i, i ^ by) for i in range(size)])

    cells = depth * width_y
    slot_block = pl.BlockSpec((block, cells, width_z), lambda i: (i, 0, 0))
    face_rows = own * width_y

    def sweep(which, energy, kelvins, older):
        outs = [(slot_block, shape(slots, cells, width_z))]
        plane = (whole(slots * width_y, width_z), shape(slots * width_y, width_z))
        if which == 1:
            outs += [plane, plane, (whole(depth, lanes), shape(depth, lanes))]
        elif which == 2:
            outs += [plane]
        outs += [(whole(face_rows, width_z), shape(face_rows, width_z))] * group
        outs += [(whole(slabs * depth, lanes), shape(slabs * depth, lanes))] * modes
        results = pl.pallas_call(
            functools.partial(sweep_kernel, which, (block, blocks, depth, width_y, slots, modes, group)),
            grid=(blocks,),
            in_specs=[SMEM] * 4
            + [slot_block, whole(cells, width_z), whole(slabs * depth, ITERS * slots)]
            + [whole(*k.shape) for k in kelvins]
            + [whole(slots * width_y, width_z)] * len(older),
            out_specs=[spec for spec, _ in outs],
            out_shape=[of for _, of in outs],
            scratch_shapes=[
                pltpu.VMEM((slots * width_y, width_z), jnp.float32),
                pltpu.VMEM((cells, width_z), jnp.float32),
                pltpu.VMEM((2 * FREQ_GROUPS, cells, width_z), jnp.float32),
                pltpu.VMEM((cells, width_z), jnp.float32),
            ],
            compiler_params=PARAMS,
            name=f"sweep_{which}",
        )(meta, floats, ints, kinds, energy, flag, matrix, *kelvins, *older)
        return results[: -group - modes], results[-group - modes : -modes], results[-modes:]

    def solve(shares, before):
        shares = [shares[0]] + [swap(shares[by], "mode", by) for by in range(1, modes)]
        parts = pl.pallas_call(
            functools.partial(partial_kernel, slabs, depth, modes),
            in_specs=[SMEM] + [VMEM] * modes,
            out_specs=[VMEM] * slabs,
            out_shape=[shape(depth, lanes)] * slabs,
            scratch_shapes=[pltpu.VMEM((slabs * depth, lanes), jnp.float32)],
            compiler_params=PARAMS,
            name="density_parts",
        )(meta, *shares)
        parts = [parts[0]] + [swap(parts[by], "slab", by) for by in range(1, slabs)]
        quarter = pl.pallas_call(
            newton_kernel,
            in_specs=[SMEM] + [VMEM] * (slabs + 1),
            out_specs=VMEM,
            out_shape=shape(depth, lanes),
            compiler_params=PARAMS,
            name="newton",
        )(sums, before, *parts)
        return quarter, [quarter] + [swap(quarter, "mode", by) for by in range(1, modes)]

    def exchange(faces, before):
        received = [faces[0]] + [swap(faces[by], "slab", by) for by in range(1, group)]
        composite, effective = pl.pallas_call(
            functools.partial(compose_kernel, own, group, len(before)),
            in_specs=[SMEM] * 3 + [VMEM] * (group + len(before)),
            out_specs=[VMEM] * 2,
            out_shape=[shape(face_rows, width_z), shape(group, face_rows, width_z)],
            compiler_params=PARAMS,
            name="compose",
        )(meta, floats, ints, *received, *before)
        composites = [composite] + [swap(composite, "slab", by * group) for by in range(1, groups)]
        entered, *outs = pl.pallas_call(
            functools.partial(enter_kernel, own, group, groups),
            in_specs=[SMEM] * 3 + [VMEM] * (1 + groups),
            out_specs=[VMEM] * (1 + group),
            out_shape=[shape(group, face_rows, width_z)] + [shape(face_rows, width_z)] * group,
            scratch_shapes=[pltpu.VMEM((groups, face_rows, width_z), jnp.float32)],
            compiler_params=PARAMS,
            name="enter",
        )(meta, floats, ints, effective, *composites)
        return entered, [outs[0]] + [swap(outs[by], "slab", by) for by in range(1, group)]

    flag = generating_region_flag.reshape(cells, width_z)
    energy = incoming_occupation.reshape(slots, cells, width_z)
    kelvins = [crystal_kelvin_given.reshape(cells, width_z)]

    (energy, once, twice, quarter), faces, shares = sweep(1, energy, kelvins, [])
    quarter, kelvins = solve(shares, quarter)
    entered_one, planes_one = exchange(faces, [])

    (energy, once_two), faces, shares = sweep(2, energy, kelvins, [once])
    quarter, kelvins = solve(shares, quarter)
    entered_two, planes_two = exchange(faces, [entered_one])

    (energy,), faces, shares = sweep(3, energy, kelvins, [once_two, twice])
    quarter, kelvins = solve(shares, quarter)
    _, planes_three = exchange(faces, [entered_one, entered_two])

    energy, kelvin = pl.pallas_call(
        functools.partial(final_kernel, block, depth, width_y, own, group, modes),
        grid=(blocks,),
        in_specs=[SMEM] * 3
        + [slot_block]
        + [whole(face_rows, width_z)] * (ITERS * group)
        + [whole(depth, lanes)] * modes,
        out_specs=[slot_block, whole(cells, width_z)],
        out_shape=[shape(slots, cells, width_z), shape(cells, width_z)],
        scratch_shapes=[pltpu.VMEM((slots * width_y, width_z), jnp.float32)] * ITERS,
        compiler_params=PARAMS,
        name="final_energy",
    )(meta, floats, ints, energy, *planes_one, *planes_two, *planes_three, *kelvins)
    return energy.reshape(slots, depth, width_y, width_z), kelvin.reshape(depth, width_y, width_z)


def solution(mesh):
    return jax.shard_map(
        local,
        mesh=mesh,
        in_specs=(
            P("mode", "slab", None, None),
            P("slab", None, None),
            P("slab", None, None),
            P("mode"),
            P(),
            P(),
            P(),
            P(),
            P(),
        ),
        out_specs=(P("mode", "slab", None, None), P("slab", None, None)),
        check_vma=False,
    )
```

time: 178 us -> 167 us (0.938)
  blocking collectives: 71.2 us -> 0 us
  starting transfers between devices: 16.7 us -> 70 us
  Pallas kernels: 38 us -> 49.6 us
  local copies, waits for them, and re-layouts: 8.13 us -> 1.93 us
    all_to_all x4 -> x0, blocking collectives: 71.2 us -> none  [the longest x2 36.1 us: exchange(): lax.all_to_all(outgoing.reshape(slabs, own, *plane), 'slab', 0, 0)]
    ppermute x9 -> x60, starting transfers between devices: 5.7 us -> 70 us  [swap(): return lax.ppermute(array, axis, [(i, i ^ by) for i in range(size)])]
    all_to_all x2 -> x0, waiting for transfers between devices: 28.5 us -> none  [the longest x1 14.5 us: exchange(): lax.all_to_all(outgoing.reshape(slabs, own, *plane), 'slab', 0, 0)]
    ppermute x9 -> x60, waiting for transfers between devices: 9.69 us -> 38 us  [swap(): return lax.ppermute(array, axis, [(i, i ^ by) for i in range(size)])]
    pallas_call x10 -> x16, Pallas kernels: 38 us -> 49.6 us  [the longest x3 33.6 us: sweep(): pl.pallas_call(functools.partial(sweep_kernel, which, (block, blocks, dep...]
    all_to_all x2 -> x0, starting transfers between devices: 11 us -> none  [the longest x1 7.41 us: exchange(): lax.all_to_all(outgoing.reshape(slabs, own, *plane), 'slab', 0, 0)]
    unnamed x20 -> x8, local copies, waits for them, and re-layouts: 8.09 us -> 1.69 us
  transfers between devices with their start and end apart: 11 -> 60, of which waited for: 8 -> 21; matrix products, arithmetic and copies ran while one was open for 1% -> 1% of each run, Pallas kernels for 0% -> 19%
where the time goes in v2:
time: 167 us; the launch traced here: 166 us
  starting transfers between devices  70 us (42%)
  Pallas kernels  49.6 us (30%)
  waiting for transfers between devices  38 us (23%)
  other arithmetic  5.41 us (3%)
  local copies, waits for them, and re-layouts  1.93 us (1%)
    ppermute x60, starting transfers between devices, swap(): return lax.ppermute(array, axis, [(i, i ^ by) for i in range(size)])  70 us
    ppermute x60, waiting for transfers between devices, swap(): return lax.ppermute(array, axis, [(i, i ^ by) for i in range(size)])  38 us
    pallas_call x3, Pallas kernels, sweep(): pl.pallas_call(functools.partial(sweep_kernel, which, (block, blocks, dep...  33.6 us
    pallas_call x1, Pallas kernels, local(): pl.pallas_call(functools.partial(final_kernel, block, depth, width_y, own...  5.05 us
    pallas_call x3, Pallas kernels, exchange(): pl.pallas_call(functools.partial(enter_kernel, own, group, groups), in_sp...  4.08 us
    pallas_call x3, Pallas kernels, exchange(): pl.pallas_call(functools.partial(compose_kernel, own, group, len(before))...  3.4 us
  transfers between devices with their start and end apart: 60, of which 21 were waited for; matrix products, arithmetic and copies ran while one was open for 1% of the time, Pallas kernels for 19%

profile of v2, /device:TPU:0, one launch (start us, length us, event | category | flops | bytes accessed | tf_op | source)
XLA Modules:
  0.0 166.0 jit_solution(9625549666429166698)
XLA Ops:
  2.1 0.8 select_reduce_fusion
  3.0 1.4 fusion.23
  5.0 0.8 copy-done.1
  5.9 0.8 copy-done.3
  6.7 12.0 %sweep_1.1 = (f32[64,128,128]{2,1,0:T(8,128)}, f32[1024,128]{1,0:T(8,128)S(1)}, f32[1024,128]{1,0:T(8,128)S(1)}, f32[8,512]{1,0:T(8,128)S(1)}, f32[256,128]{1,0:...) custom-call(s32[2]{0:T(128)S(1)} %pad_add_fusion.refs_0_.meta, ...), custom_call_target="tpu_custom_call" | custom-call | tf_op jit(solution)/shard_map/sweep_1/pallas_call | solution.py:370
  19.2 2.5 %collective-permute-start.1 = (f32[64,512]{1,0:T(8,128)S(1)}, f32[64,512]{1,0:T(8,128)S(1)}, u32[]{:S(2)}, u32[]{:S(2)}) collective-permute-start(f32[64,512]{1,0:T(8,128)S(1)} %get-tuple-element.83), channel_id=1, source_target_pairs={{0,2},{1,3},{2,0},{3,1},{4,6},{5,7},{6,4},{7,5},{8,10},{9,11},{10,... | collective-permute-start | bytes 393224 | tf_op jit(solution)/shard_map/ppermute | solution.py:355
  21.8 4.2 %collective-permute-done.1.refs_2_ = f32[64,512]{1,0:T(8,128)S(1)} collective-permute-done((f32[64,512]{1,0:T(8,128)S(1)}, f32[64,512]{1,0:T(8,128)S(1)}, u32[]{:S(2)}, u32[]{:S(2)}) %collective-permute-start.1) | collective-permute-done | bytes 131104 | tf_op jit(solution)/shard_map/ppermute | solution.py:355
  26.0 2.4 %collective-permute-done.2.refs_3_ = f32[64,512]{1,0:T(8,128)S(1)} collective-permute-done((f32[64,512]{1,0:T(8,128)S(1)}, f32[64,512]{1,0:T(8,128)S(1)}, u32[]{:S(2)}, u32[]{:S(2)}) %collective-permute-start.2) | collective-permute-done | bytes 131104 | tf_op jit(solution)/shard_map/ppermute | solution.py:355
  29.0 1.6 collective-permute-start.3
  30.7 1.6 collective-permute-start.4
  32.6 2.6 %collective-permute-start.6 = (f32[8,512]{1,0:T(8,128)S(1)}, f32[8,512]{1,0:T(8,128)S(1)}, u32[]{:S(2)}, u32[]{:S(2)}) collective-permute-start(f32[8,512]{1,0:T(8,128)S(1)} %get-tuple-element.89), channel_id=1, source_target_pairs={{0,16},{4,20},{8,24},{12,28},{16,0},{20,4},{24,8},{28,12},{1,17},{... | collective-permute-start | bytes 49160 | tf_op jit(solution)/shard_map/ppermute | solution.py:355
  35.2 1.3 collective-permute-start.7
  37.0 1.6 collective-permute-start.27
  38.6 1.4 collective-permute-start.28
  40.0 3.6 %collective-permute-start.8 = (f32[8,512]{1,0:T(8,128)S(1)}, f32[8,512]{1,0:T(8,128)S(1)}, u32[]{:S(2)}, u32[]{:S(2)}) collective-permute-start(f32[8,512]{1,0:T(8,128)S(1)} %get-tuple-element.91), channel_id=1, source_target_pairs={{0,24},{4,28},{8,16},{12,20},{16,8},{20,12},{24,0},{28,4},{1,25},{... | collective-permute-start | bytes 49160 | tf_op jit(solution)/shard_map/ppermute | solution.py:355
  43.7 1.3 pad_maximum_fusion.2.sums
  45.0 2.1 %collective-permute-done.8.rest_6_ = f32[8,512]{1,0:T(8,128)S(1)} collective-permute-done((f32[8,512]{1,0:T(8,128)S(1)}, f32[8,512]{1,0:T(8,128)S(1)}, u32[]{:S(2)}, u32[]{:S(2)}) %collective-permute-start.8) | collective-permute-done | bytes 16416 | tf_op jit(solution)/shard_map/ppermute | solution.py:355
  47.2 2.9 %collective-permute-done.9.rest_7_ = f32[8,512]{1,0:T(8,128)S(1)} collective-permute-done((f32[8,512]{1,0:T(8,128)S(1)}, f32[8,512]{1,0:T(8,128)S(1)}, u32[]{:S(2)}, u32[]{:S(2)}) %collective-permute-start.9) | collective-permute-done | bytes 16416 | tf_op jit(solution)/shard_map/ppermute | solution.py:355
  50.7 1.5 collective-permute-start.11
  52.3 0.9 collective-permute-start.12
  53.2 1.4 collective-permute-done.11.refs_9_
  54.5 0.9 collective-permute-done.12.refs_10_
  55.5 11.1 %sweep_2.1 = (f32[64,128,128]{2,1,0:T(8,128)}, f32[1024,128]{1,0:T(8,128)S(1)}, f32[256,128]{1,0:T(8,128)S(1)}, f32[256,128]{1,0:T(8,128)S(1)}, f32[256,128]{1,0...) custom-call(s32[2]{0:T(128)S(1)} %pad_add_fusion.refs_0_.meta, ...), custom_call_target="tpu_custom_call" | custom-call | tf_op jit(solution)/shard_map/sweep_2/pallas_call | solution.py:370
  66.7 1.1 collective-permute-start.14
  68.4 1.0 compose.3
  69.6 3.5 %collective-permute-done.14.refs_2_ = f32[64,512]{1,0:T(8,128)S(1)} collective-permute-done((f32[64,512]{1,0:T(8,128)S(1)}, f32[64,512]{1,0:T(8,128)S(1)}, u32[]{:S(2)}, u32[]{:S(2)}) %collective-permute-start.14) | collective-permute-done | bytes 131104 | tf_op jit(solution)/shard_map/ppermute | solution.py:355
  73.0 1.7 %collective-permute-done.15.refs_3_ = f32[64,512]{1,0:T(8,128)S(1)} collective-permute-done((f32[64,512]{1,0:T(8,128)S(1)}, f32[64,512]{1,0:T(8,128)S(1)}, u32[]{:S(2)}, u32[]{:S(2)}) %collective-permute-start.15) | collective-permute-done | bytes 131104 | tf_op jit(solution)/shard_map/ppermute | solution.py:355
  75.9 3.0 %collective-permute-start.18 = (f32[8,512]{1,0:T(8,128)S(1)}, f32[8,512]{1,0:T(8,128)S(1)}, u32[]{:S(2)}, u32[]{:S(2)}) collective-permute-start(f32[8,512]{1,0:T(8,128)S(1)} %get-tuple-element.102), channel_id=1, source_target_pairs={{0,12},{4,8},{8,4},{12,0},{16,28},{20,24},{24,20},{28,16},{1,13},{... | collective-permute-start | bytes 49160 | tf_op jit(solution)/shard_map/ppermute | solution.py:355
  79.1 2.6 %collective-permute-start.20 = (f32[8,512]{1,0:T(8,128)S(1)}, f32[8,512]{1,0:T(8,128)S(1)}, u32[]{:S(2)}, u32[]{:S(2)}) collective-permute-start(f32[8,512]{1,0:T(8,128)S(1)} %get-tuple-element.104), channel_id=1, source_target_pairs={{0,20},{4,16},{8,28},{12,24},{16,4},{20,0},{24,12},{28,8},{1,21},{... | collective-permute-start | bytes 49160 | tf_op jit(solution)/shard_map/ppermute | solution.py:355
  82.0 4.5 %collective-permute-start.22 = (f32[8,512]{1,0:T(8,128)S(1)}, f32[8,512]{1,0:T(8,128)S(1)}, u32[]{:S(2)}, u32[]{:S(2)}) collective-permute-start(f32[8,512]{1,0:T(8,128)S(1)} %get-tuple-element.106), channel_id=1, source_target_pairs={{0,28},{4,24},{8,20},{12,16},{16,12},{20,8},{24,4},{28,0},{1,29},{... | collective-permute-start | bytes 49160 | tf_op jit(solution)/shard_map/ppermute | solution.py:355
  87.3 1.2 collective-permute-done.22.rest_7_
  89.1 1.2 collective-permute-start.24
  91.0 1.5 collective-permute-start.33
  92.9 1.6 collective-permute-start.35
  94.5 10.5 %sweep_3.1 = (f32[64,128,128]{2,1,0:T(8,128)}, f32[256,128]{1,0:T(8,128)S(1)}, f32[256,128]{1,0:T(8,128)S(1)}, f32[256,128]{1,0:T(8,128)S(1)}, f32[256,128]{1,0:...) custom-call(s32[2]{0:T(128)S(1)} %pad_add_fusion.refs_0_.meta, ...), custom_call_target="tpu_custom_call" | custom-call | tf_op jit(solution)/shard_map/sweep_3/pallas_call | solution.py:370
  105.0 1.2 collective-permute-start.48
  106.2 1.1 enter.3
  107.3 0.8 collective-permute-start.49
  108.0 1.1 compose.4
  109.2 3.6 %collective-permute-start.36 = (f32[256,128]{1,0:T(8,128)S(1)}, f32[256,128]{1,0:T(8,128)S(1)}, u32[]{:S(2)}, u32[]{:S(2)}) collective-permute-start(f32[256,128]{1,0:T(8,128)S(1)} %get-tuple-element.126.refs_0_), channel_id=1, source_target_pairs={{0,16},{4,20},{8,24},{12,28},{16,0},{20,4},{24,8},{28,12},{1,17},{... | collective-permute-start | bytes 393224 | tf_op jit(solution)/shard_map/ppermute | solution.py:355
  113.3 1.6 collective-permute-start.41
  114.9 1.4 collective-permute-start.42
  117.4 2.3 %collective-permute-done.36.refs_1_ = f32[256,128]{1,0:T(8,128)S(1)} collective-permute-done((f32[256,128]{1,0:T(8,128)S(1)}, f32[256,128]{1,0:T(8,128)S(1)}, u32[]{:S(2)}, u32[]{:S(2)}) %collective-permute-start.36) | collective-permute-done | bytes 131104 | tf_op jit(solution)/shard_map/ppermute | solution.py:355
  119.7 2.0 %collective-permute-start.52 = (f32[8,512]{1,0:T(8,128)S(1)}, f32[8,512]{1,0:T(8,128)S(1)}, u32[]{:S(2)}, u32[]{:S(2)}) collective-permute-start(f32[8,512]{1,0:T(8,128)S(1)} %get-tuple-element.149), channel_id=1, source_target_pairs={{0,12},{4,8},{8,4},{12,0},{16,28},{20,24},{24,20},{28,16},{1,13},{... | collective-permute-start | bytes 49160 | tf_op jit(solution)/shard_map/ppermute | solution.py:355
  122.2 1.6 collective-permute-start.53
  124.3 1.2 collective-permute-start.54
  125.6 1.1 enter.4
  126.7 1.2 compose.5
  127.9 2.7 %collective-permute-start.55 = (f32[8,512]{1,0:T(8,128)S(1)}, f32[8,512]{1,0:T(8,128)S(1)}, u32[]{:S(2)}, u32[]{:S(2)}) collective-permute-start(f32[8,512]{1,0:T(8,128)S(1)} %get-tuple-element.152), channel_id=1, source_target_pairs={{0,24},{4,28},{8,16},{12,20},{16,8},{20,12},{24,0},{28,4},{1,25},{... | collective-permute-start | bytes 49160 | tf_op jit(solution)/shard_map/ppermute | solution.py:355
  130.6 1.4 collective-permute-start.30
  132.0 1.4 collective-permute-start.43
  133.4 3.1 %collective-permute-start.56 = (f32[8,512]{1,0:T(8,128)S(1)}, f32[8,512]{1,0:T(8,128)S(1)}, u32[]{:S(2)}, u32[]{:S(2)}) collective-permute-start(f32[8,512]{1,0:T(8,128)S(1)} %get-tuple-element.153), channel_id=1, source_target_pairs={{0,28},{4,24},{8,20},{12,16},{16,12},{20,8},{24,4},{28,0},{1,29},{... | collective-permute-start | bytes 49160 | tf_op jit(solution)/shard_map/ppermute | solution.py:355
  136.5 4.3 %collective-permute-done.56.rest_7_ = f32[8,512]{1,0:T(8,128)S(1)} collective-permute-done((f32[8,512]{1,0:T(8,128)S(1)}, f32[8,512]{1,0:T(8,128)S(1)}, u32[]{:S(2)}, u32[]{:S(2)}) %collective-permute-start.56) | collective-permute-done | bytes 16416 | tf_op jit(solution)/shard_map/ppermute | solution.py:355
  140.8 1.2 collective-permute-start.37
  142.7 1.2 collective-permute-start.58
  144.6 1.9 %enter.5 = (f32[4,256,128]{2,1,0:T(8,128)}, f32[256,128]{1,0:T(8,128)S(1)}, f32[256,128]{1,0:T(8,128)S(1)}, f32[256,128]{1,0:T(8,128)S(1)}, f32[256,128]{1,0:T(8,128)S(1)}) custom-call(s32[2]{0:T(128)S(1)} %pad_add_fusion.refs_0_.meta, f32[9,64]{1,0:T(8,128)S(1)} %stack.114.refs_1_.floats, s32[5,64]{1,0:T(8,128)S(1)} %stack.121.refs_2_.ints, ...), custom_call_target="tpu_custom_call" | custom-call | tf_op jit(solution)/shard_map/enter/pallas_call | solution.py:423
  147.1 1.6 collective-permute-start.39
  148.7 1.2 collective-permute-start.44
  150.6 1.6 collective-permute-start.46
  152.8 3.1 %collective-permute-done.39.refs_7_ = f32[256,128]{1,0:T(8,128)S(1)} collective-permute-done((f32[256,128]{1,0:T(8,128)S(1)}, f32[256,128]{1,0:T(8,128)S(1)}, u32[]{:S(2)}, u32[]{:S(2)}) %collective-permute-start.39) | collective-permute-done | bytes 131104 | tf_op jit(solution)/shard_map/ppermute | solution.py:355
  155.9 0.9 collective-permute-done.44.refs_9_
  156.7 1.7 %collective-permute-done.45.refs_10_ = f32[256,128]{1,0:T(8,128)S(1)} collective-permute-done((f32[256,128]{1,0:T(8,128)S(1)}, f32[256,128]{1,0:T(8,128)S(1)}, u32[]{:S(2)}, u32[]{:S(2)}) %collective-permute-start.45) | collective-permute-done | bytes 131104 | tf_op jit(solution)/shard_map/ppermute | solution.py:355
  158.4 2.5 %collective-permute-done.46.refs_11_ = f32[256,128]{1,0:T(8,128)S(1)} collective-permute-done((f32[256,128]{1,0:T(8,128)S(1)}, f32[256,128]{1,0:T(8,128)S(1)}, u32[]{:S(2)}, u32[]{:S(2)}) %collective-permute-start.46) | collective-permute-done | bytes 131104 | tf_op jit(solution)/shard_map/ppermute | solution.py:355
  160.9 5.0 %final_energy.1 = (f32[64,128,128]{2,1,0:T(8,128)}, f32[128,128]{1,0:T(8,128)}) custom-call(s32[2]{0:T(128)S(1)} %pad_add_fusion.refs_0_.meta, f32[9,64]{1,0:T(8,128)S(1)} %stack.114.refs_1_.floats, s32[5,64]{1,0:T(8,128)S(1)} %stack.121.refs_2_.ints, f32[64,128,128]{2,1,0:T(8,128)S(1)} %copy-done, f32[256,128]{1,0:T(8,128)S(1)} %get-tuple-element.116.refs_0_, ...), custom_call_target="tpu_custom_call" | custom-call | tf_op jit(solution)/shard_map/final_energy/pallas_call | solution.py:450
  (101 shorter events, 15.9 us)
Async XLA Ops:
  0.6 54.8 %copy-start.2 = (s32[8,16,128]{2,1,0:T(8,128)S(1)}, s32[8,16,128]{2,1,0:T(8,128)}, u32[]{:S(2)}) copy-start(s32[8,16,128]{2,1,0:T(8,128)} %param.11) | copy-start | bytes 196612
  5.0 0.8 copy-start.1
  5.9 0.8 copy-start.3
  18.7 3.1 %collective-permute-start = (f32[64,512]{1,0:T(8,128)S(1)}, f32[64,512]{1,0:T(8,128)S(1)}, u32[]{:S(2)}, u32[]{:S(2)}) collective-permute-start(f32[64,512]{1,0:T(8,128)S(1)} %get-tuple-element.82), channel_id=1, source_target_pairs={{0,1},{1,0},{2,3},{3,2},{4,5},{5,4},{6,7},{7,6},{8,9},{9,8},{10,11... | collective-permute-start | bytes 393224 | tf_op jit(solution)/shard_map/ppermute | solution.py:355
  19.2 6.8 %collective-permute-start.1 = (f32[64,512]{1,0:T(8,128)S(1)}, f32[64,512]{1,0:T(8,128)S(1)}, u32[]{:S(2)}, u32[]{:S(2)}) collective-permute-start(f32[64,512]{1,0:T(8,128)S(1)} %get-tuple-element.83), channel_id=1, source_target_pairs={{0,2},{1,3},{2,0},{3,1},{4,6},{5,7},{6,4},{7,5},{8,10},{9,11},{10,... | collective-permute-start | bytes 393224 | tf_op jit(solution)/shard_map/ppermute | solution.py:355
  21.6 6.8 %collective-permute-start.2 = (f32[64,512]{1,0:T(8,128)S(1)}, f32[64,512]{1,0:T(8,128)S(1)}, u32[]{:S(2)}, u32[]{:S(2)}) collective-permute-start(f32[64,512]{1,0:T(8,128)S(1)} %get-tuple-element.84), channel_id=1, source_target_pairs={{0,3},{1,2},{2,1},{3,0},{4,7},{5,6},{6,5},{7,4},{8,11},{9,10},{10,... | collective-permute-start | bytes 393224 | tf_op jit(solution)/shard_map/ppermute | solution.py:355
  29.0 7.5 %collective-permute-start.3 = (f32[8,512]{1,0:T(8,128)S(1)}, f32[8,512]{1,0:T(8,128)S(1)}, u32[]{:S(2)}, u32[]{:S(2)}) collective-permute-start(f32[8,512]{1,0:T(8,128)S(1)} %get-tuple-element.86), channel_id=1, source_target_pairs={{0,4},{4,0},{8,12},{12,8},{16,20},{20,16},{24,28},{28,24},{1,5},{5... | collective-permute-start | bytes 49160 | tf_op jit(solution)/shard_map/ppermute | solution.py:355
  30.7 6.3 %collective-permute-start.4 = (f32[8,512]{1,0:T(8,128)S(1)}, f32[8,512]{1,0:T(8,128)S(1)}, u32[]{:S(2)}, u32[]{:S(2)}) collective-permute-start(f32[8,512]{1,0:T(8,128)S(1)} %get-tuple-element.87), channel_id=1, source_target_pairs={{0,8},{4,12},{8,0},{12,4},{16,24},{20,28},{24,16},{28,20},{1,9},{5... | collective-permute-start | bytes 49160 | tf_op jit(solution)/shard_map/ppermute | solution.py:355
  32.2 6.4 %collective-permute-start.5 = (f32[8,512]{1,0:T(8,128)S(1)}, f32[8,512]{1,0:T(8,128)S(1)}, u32[]{:S(2)}, u32[]{:S(2)}) collective-permute-start(f32[8,512]{1,0:T(8,128)S(1)} %get-tuple-element.88), channel_id=1, source_target_pairs={{0,12},{4,8},{8,4},{12,0},{16,28},{20,24},{24,20},{28,16},{1,13},{... | collective-permute-start | bytes 49160 | tf_op jit(solution)/shard_map/ppermute | solution.py:355
  32.6 7.4 %collective-permute-start.6 = (f32[8,512]{1,0:T(8,128)S(1)}, f32[8,512]{1,0:T(8,128)S(1)}, u32[]{:S(2)}, u32[]{:S(2)}) collective-permute-start(f32[8,512]{1,0:T(8,128)S(1)} %get-tuple-element.89), channel_id=1, source_target_pairs={{0,16},{4,20},{8,24},{12,28},{16,0},{20,4},{24,8},{28,12},{1,17},{... | collective-permute-start | bytes 49160 | tf_op jit(solution)/shard_map/ppermute | solution.py:355
  35.2 8.4 %collective-permute-start.7 = (f32[8,512]{1,0:T(8,128)S(1)}, f32[8,512]{1,0:T(8,128)S(1)}, u32[]{:S(2)}, u32[]{:S(2)}) collective-permute-start(f32[8,512]{1,0:T(8,128)S(1)} %get-tuple-element.90), channel_id=1, source_target_pairs={{0,20},{4,16},{8,28},{12,24},{16,4},{20,0},{24,12},{28,8},{1,21},{... | collective-permute-start | bytes 49160 | tf_op jit(solution)/shard_map/ppermute | solution.py:355
  36.5 31.3 %collective-permute-start.26 = (f32[256,128]{1,0:T(8,128)S(1)}, f32[256,128]{1,0:T(8,128)S(1)}, u32[]{:S(2)}, u32[]{:S(2)}) collective-permute-start(f32[256,128]{1,0:T(8,128)S(1)} %get-tuple-element.111), channel_id=1, source_target_pairs={{0,4},{4,0},{8,12},{12,8},{16,20},{20,16},{24,28},{28,24},{1,5},{5... | collective-permute-start | bytes 393224 | tf_op jit(solution)/shard_map/ppermute | solution.py:355
  37.0 31.5 %collective-permute-start.27 = (f32[256,128]{1,0:T(8,128)S(1)}, f32[256,128]{1,0:T(8,128)S(1)}, u32[]{:S(2)}, u32[]{:S(2)}) collective-permute-start(f32[256,128]{1,0:T(8,128)S(1)} %get-tuple-element.112), channel_id=1, source_target_pairs={{0,8},{4,12},{8,0},{12,4},{16,24},{20,28},{24,16},{28,20},{1,9},{5... | collective-permute-start | bytes 393224 | tf_op jit(solution)/shard_map/ppermute | solution.py:355
  38.6 29.8 %collective-permute-start.28 = (f32[256,128]{1,0:T(8,128)S(1)}, f32[256,128]{1,0:T(8,128)S(1)}, u32[]{:S(2)}, u32[]{:S(2)}) collective-permute-start(f32[256,128]{1,0:T(8,128)S(1)} %get-tuple-element.113), channel_id=1, source_target_pairs={{0,12},{4,8},{8,4},{12,0},{16,28},{20,24},{24,20},{28,16},{1,13},{... | collective-permute-start | bytes 393224 | tf_op jit(solution)/shard_map/ppermute | solution.py:355
  40.0 7.2 %collective-permute-start.8 = (f32[8,512]{1,0:T(8,128)S(1)}, f32[8,512]{1,0:T(8,128)S(1)}, u32[]{:S(2)}, u32[]{:S(2)}) collective-permute-start(f32[8,512]{1,0:T(8,128)S(1)} %get-tuple-element.91), channel_id=1, source_target_pairs={{0,24},{4,28},{8,16},{12,20},{16,8},{20,12},{24,0},{28,4},{1,25},{... | collective-permute-start | bytes 49160 | tf_op jit(solution)/shard_map/ppermute | solution.py:355
  43.6 6.4 %collective-permute-start.9 = (f32[8,512]{1,0:T(8,128)S(1)}, f32[8,512]{1,0:T(8,128)S(1)}, u32[]{:S(2)}, u32[]{:S(2)}) collective-permute-start(f32[8,512]{1,0:T(8,128)S(1)} %get-tuple-element.92), channel_id=1, source_target_pairs={{0,28},{4,24},{8,20},{12,16},{16,12},{20,8},{24,4},{28,0},{1,29},{... | collective-permute-start | bytes 49160 | tf_op jit(solution)/shard_map/ppermute | solution.py:355
  50.7 1.6 collective-permute-start.10
  50.7 3.8 %collective-permute-start.11 = (f32[8,512]{1,0:T(8,128)S(1)}, f32[8,512]{1,0:T(8,128)S(1)}, u32[]{:S(2)}, u32[]{:S(2)}) collective-permute-start(f32[8,512]{1,0:T(8,128)S(1)} %newton.3.refs_7_.before), channel_id=1, source_target_pairs={{0,2},{1,3},{2,0},{3,1},{4,6},{5,7},{6,4},{7,5},{8,10},{9,11},{10,... | collective-permute-start | bytes 49160 | tf_op jit(solution)/shard_map/ppermute | solution.py:355
  52.3 3.2 %collective-permute-start.12 = (f32[8,512]{1,0:T(8,128)S(1)}, f32[8,512]{1,0:T(8,128)S(1)}, u32[]{:S(2)}, u32[]{:S(2)}) collective-permute-start(f32[8,512]{1,0:T(8,128)S(1)} %newton.3.refs_7_.before), channel_id=1, source_target_pairs={{0,3},{1,2},{2,1},{3,0},{4,7},{5,6},{6,5},{7,4},{8,11},{9,10},{10,... | collective-permute-start | bytes 49160 | tf_op jit(solution)/shard_map/ppermute | solution.py:355
  66.6 3.0 %collective-permute-start.13 = (f32[64,512]{1,0:T(8,128)S(1)}, f32[64,512]{1,0:T(8,128)S(1)}, u32[]{:S(2)}, u32[]{:S(2)}) collective-permute-start(f32[64,512]{1,0:T(8,128)S(1)} %get-tuple-element.96), channel_id=1, source_target_pairs={{0,1},{1,0},{2,3},{3,2},{4,5},{5,4},{6,7},{7,6},{8,9},{9,8},{10,11... | collective-permute-start | bytes 393224 | tf_op jit(solution)/shard_map/ppermute | solution.py:355
  66.7 6.3 %collective-permute-start.14 = (f32[64,512]{1,0:T(8,128)S(1)}, f32[64,512]{1,0:T(8,128)S(1)}, u32[]{:S(2)}, u32[]{:S(2)}) collective-permute-start(f32[64,512]{1,0:T(8,128)S(1)} %get-tuple-element.97), channel_id=1, source_target_pairs={{0,2},{1,3},{2,0},{3,1},{4,6},{5,7},{6,4},{7,5},{8,10},{9,11},{10,... | collective-permute-start | bytes 393224 | tf_op jit(solution)/shard_map/ppermute | solution.py:355
  67.8 6.9 %collective-permute-start.15 = (f32[64,512]{1,0:T(8,128)S(1)}, f32[64,512]{1,0:T(8,128)S(1)}, u32[]{:S(2)}, u32[]{:S(2)}) collective-permute-start(f32[64,512]{1,0:T(8,128)S(1)} %get-tuple-element.98), channel_id=1, source_target_pairs={{0,3},{1,2},{2,1},{3,0},{4,7},{5,6},{6,5},{7,4},{8,11},{9,10},{10,... | collective-permute-start | bytes 393224 | tf_op jit(solution)/shard_map/ppermute | solution.py:355
  69.5 35.5 %collective-permute-start.29 = (f32[256,128]{1,0:T(8,128)S(1)}, f32[256,128]{1,0:T(8,128)S(1)}, u32[]{:S(2)}, u32[]{:S(2)}) collective-permute-start(f32[256,128]{1,0:T(8,128)S(1)} %get-tuple-element.115.refs_0_), channel_id=1, source_target_pairs={{0,16},{4,20},{8,24},{12,28},{16,0},{20,4},{24,8},{28,12},{1,17},{... | collective-permute-start | bytes 393224 | tf_op jit(solution)/shard_map/ppermute | solution.py:355
  75.3 3.8 %collective-permute-start.16 = (f32[8,512]{1,0:T(8,128)S(1)}, f32[8,512]{1,0:T(8,128)S(1)}, u32[]{:S(2)}, u32[]{:S(2)}) collective-permute-start(f32[8,512]{1,0:T(8,128)S(1)} %get-tuple-element.100), channel_id=1, source_target_pairs={{0,4},{4,0},{8,12},{12,8},{16,20},{20,16},{24,28},{28,24},{1,5},{5... | collective-permute-start | bytes 49160 | tf_op jit(solution)/shard_map/ppermute | solution.py:355
  75.9 5.9 %collective-permute-start.17 = (f32[8,512]{1,0:T(8,128)S(1)}, f32[8,512]{1,0:T(8,128)S(1)}, u32[]{:S(2)}, u32[]{:S(2)}) collective-permute-start(f32[8,512]{1,0:T(8,128)S(1)} %get-tuple-element.101), channel_id=1, source_target_pairs={{0,8},{4,12},{8,0},{12,4},{16,24},{20,28},{24,16},{28,20},{1,9},{5... | collective-permute-start | bytes 49160 | tf_op jit(solution)/shard_map/ppermute | solution.py:355
  75.9 6.1 %collective-permute-start.18 = (f32[8,512]{1,0:T(8,128)S(1)}, f32[8,512]{1,0:T(8,128)S(1)}, u32[]{:S(2)}, u32[]{:S(2)}) collective-permute-start(f32[8,512]{1,0:T(8,128)S(1)} %get-tuple-element.102), channel_id=1, source_target_pairs={{0,12},{4,8},{8,4},{12,0},{16,28},{20,24},{24,20},{28,16},{1,13},{... | collective-permute-start | bytes 49160 | tf_op jit(solution)/shard_map/ppermute | solution.py:355
  78.9 7.7 %collective-permute-start.19 = (f32[8,512]{1,0:T(8,128)S(1)}, f32[8,512]{1,0:T(8,128)S(1)}, u32[]{:S(2)}, u32[]{:S(2)}) collective-permute-start(f32[8,512]{1,0:T(8,128)S(1)} %get-tuple-element.103), channel_id=1, source_target_pairs={{0,16},{4,20},{8,24},{12,28},{16,0},{20,4},{24,8},{28,12},{1,17},{... | collective-permute-start | bytes 49160 | tf_op jit(solution)/shard_map/ppermute | solution.py:355
  79.1 7.4 %collective-permute-start.20 = (f32[8,512]{1,0:T(8,128)S(1)}, f32[8,512]{1,0:T(8,128)S(1)}, u32[]{:S(2)}, u32[]{:S(2)}) collective-permute-start(f32[8,512]{1,0:T(8,128)S(1)} %get-tuple-element.104), channel_id=1, source_target_pairs={{0,20},{4,16},{8,28},{12,24},{16,4},{20,0},{24,12},{28,8},{1,21},{... | collective-permute-start | bytes 49160 | tf_op jit(solution)/shard_map/ppermute | solution.py:355
  81.7 5.5 %collective-permute-start.21 = (f32[8,512]{1,0:T(8,128)S(1)}, f32[8,512]{1,0:T(8,128)S(1)}, u32[]{:S(2)}, u32[]{:S(2)}) collective-permute-start(f32[8,512]{1,0:T(8,128)S(1)} %get-tuple-element.105), channel_id=1, source_target_pairs={{0,24},{4,28},{8,16},{12,20},{16,8},{20,12},{24,0},{28,4},{1,25},{... | collective-permute-start | bytes 49160 | tf_op jit(solution)/shard_map/ppermute | solution.py:355
  82.0 6.4 %collective-permute-start.22 = (f32[8,512]{1,0:T(8,128)S(1)}, f32[8,512]{1,0:T(8,128)S(1)}, u32[]{:S(2)}, u32[]{:S(2)}) collective-permute-start(f32[8,512]{1,0:T(8,128)S(1)} %get-tuple-element.106), channel_id=1, source_target_pairs={{0,28},{4,24},{8,20},{12,16},{16,12},{20,8},{24,4},{28,0},{1,29},{... | collective-permute-start | bytes 49160 | tf_op jit(solution)/shard_map/ppermute | solution.py:355
  89.0 3.4 %collective-permute-start.23 = (f32[8,512]{1,0:T(8,128)S(1)}, f32[8,512]{1,0:T(8,128)S(1)}, u32[]{:S(2)}, u32[]{:S(2)}) collective-permute-start(f32[8,512]{1,0:T(8,128)S(1)} %newton.4.refs_7_.before), channel_id=1, source_target_pairs={{0,1},{1,0},{2,3},{3,2},{4,5},{5,4},{6,7},{7,6},{8,9},{9,8},{10,11... | collective-permute-start | bytes 49160 | tf_op jit(solution)/shard_map/ppermute | solution.py:355
  89.1 3.8 %collective-permute-start.24 = (f32[8,512]{1,0:T(8,128)S(1)}, f32[8,512]{1,0:T(8,128)S(1)}, u32[]{:S(2)}, u32[]{:S(2)}) collective-permute-start(f32[8,512]{1,0:T(8,128)S(1)} %newton.4.refs_7_.before), channel_id=1, source_target_pairs={{0,2},{1,3},{2,0},{3,1},{4,6},{5,7},{6,4},{7,5},{8,10},{9,11},{10,... | collective-permute-start | bytes 49160 | tf_op jit(solution)/shard_map/ppermute | solution.py:355
  90.3 4.2 %collective-permute-start.25 = (f32[8,512]{1,0:T(8,128)S(1)}, f32[8,512]{1,0:T(8,128)S(1)}, u32[]{:S(2)}, u32[]{:S(2)}) collective-permute-start(f32[8,512]{1,0:T(8,128)S(1)} %newton.4.refs_7_.before), channel_id=1, source_target_pairs={{0,3},{1,2},{2,1},{3,0},{4,7},{5,6},{6,5},{7,4},{8,11},{9,10},{10,... | collective-permute-start | bytes 49160 | tf_op jit(solution)/shard_map/ppermute | solution.py:355
  91.0 16.3 %collective-permute-start.33 = (f32[256,128]{1,0:T(8,128)S(1)}, f32[256,128]{1,0:T(8,128)S(1)}, u32[]{:S(2)}, u32[]{:S(2)}) collective-permute-start(f32[256,128]{1,0:T(8,128)S(1)} %get-tuple-element.121), channel_id=1, source_target_pairs={{0,4},{4,0},{8,12},{12,8},{16,20},{20,16},{24,28},{28,24},{1,5},{5... | collective-permute-start | bytes 393224 | tf_op jit(solution)/shard_map/ppermute | solution.py:355
  92.5 15.6 %collective-permute-start.34 = (f32[256,128]{1,0:T(8,128)S(1)}, f32[256,128]{1,0:T(8,128)S(1)}, u32[]{:S(2)}, u32[]{:S(2)}) collective-permute-start(f32[256,128]{1,0:T(8,128)S(1)} %get-tuple-element.122), channel_id=1, source_target_pairs={{0,8},{4,12},{8,0},{12,4},{16,24},{20,28},{24,16},{28,20},{1,9},{5... | collective-permute-start | bytes 393224 | tf_op jit(solution)/shard_map/ppermute | solution.py:355
  92.9 15.1 %collective-permute-start.35 = (f32[256,128]{1,0:T(8,128)S(1)}, f32[256,128]{1,0:T(8,128)S(1)}, u32[]{:S(2)}, u32[]{:S(2)}) collective-permute-start(f32[256,128]{1,0:T(8,128)S(1)} %get-tuple-element.123), channel_id=1, source_target_pairs={{0,12},{4,8},{8,4},{12,0},{16,28},{20,24},{24,20},{28,16},{1,13},{... | collective-permute-start | bytes 393224 | tf_op jit(solution)/shard_map/ppermute | solution.py:355
  105.0 56.0 %copy-start = (f32[64,128,128]{2,1,0:T(8,128)S(1)}, f32[64,128,128]{2,1,0:T(8,128)}, u32[]{:S(2)}) copy-start(f32[64,128,128]{2,1,0:T(8,128)} %get-tuple-element.109.swept) | copy-start | bytes 12582916
  105.0 8.3 %collective-permute-start.47 = (f32[64,512]{1,0:T(8,128)S(1)}, f32[64,512]{1,0:T(8,128)S(1)}, u32[]{:S(2)}, u32[]{:S(2)}) collective-permute-start(f32[64,512]{1,0:T(8,128)S(1)} %get-tuple-element.143), channel_id=1, source_target_pairs={{0,1},{1,0},{2,3},{3,2},{4,5},{5,4},{6,7},{7,6},{8,9},{9,8},{10,11... | collective-permute-start | bytes 393224 | tf_op jit(solution)/shard_map/ppermute | solution.py:355
  105.0 9.9 %collective-permute-start.48 = (f32[64,512]{1,0:T(8,128)S(1)}, f32[64,512]{1,0:T(8,128)S(1)}, u32[]{:S(2)}, u32[]{:S(2)}) collective-permute-start(f32[64,512]{1,0:T(8,128)S(1)} %get-tuple-element.144), channel_id=1, source_target_pairs={{0,2},{1,3},{2,0},{3,1},{4,6},{5,7},{6,4},{7,5},{8,10},{9,11},{10,... | collective-permute-start | bytes 393224 | tf_op jit(solution)/shard_map/ppermute | solution.py:355
  107.3 9.0 %collective-permute-start.49 = (f32[64,512]{1,0:T(8,128)S(1)}, f32[64,512]{1,0:T(8,128)S(1)}, u32[]{:S(2)}, u32[]{:S(2)}) collective-permute-start(f32[64,512]{1,0:T(8,128)S(1)} %get-tuple-element.145), channel_id=1, source_target_pairs={{0,3},{1,2},{2,1},{3,0},{4,7},{5,6},{6,5},{7,4},{8,11},{9,10},{10,... | collective-permute-start | bytes 393224 | tf_op jit(solution)/shard_map/ppermute | solution.py:355
  109.2 10.5 %collective-permute-start.36 = (f32[256,128]{1,0:T(8,128)S(1)}, f32[256,128]{1,0:T(8,128)S(1)}, u32[]{:S(2)}, u32[]{:S(2)}) collective-permute-start(f32[256,128]{1,0:T(8,128)S(1)} %get-tuple-element.126.refs_0_), channel_id=1, source_target_pairs={{0,16},{4,20},{8,24},{12,28},{16,0},{20,4},{24,8},{28,12},{1,17},{... | collective-permute-start | bytes 393224 | tf_op jit(solution)/shard_map/ppermute | solution.py:355
  112.8 6.9 %collective-permute-start.40 = (f32[256,128]{1,0:T(8,128)S(1)}, f32[256,128]{1,0:T(8,128)S(1)}, u32[]{:S(2)}, u32[]{:S(2)}) collective-permute-start(f32[256,128]{1,0:T(8,128)S(1)} %get-tuple-element.132), channel_id=1, source_target_pairs={{0,4},{4,0},{8,12},{12,8},{16,20},{20,16},{24,28},{28,24},{1,5},{5... | collective-permute-start | bytes 393224 | tf_op jit(solution)/shard_map/ppermute | solution.py:355
  113.3 8.9 %collective-permute-start.41 = (f32[256,128]{1,0:T(8,128)S(1)}, f32[256,128]{1,0:T(8,128)S(1)}, u32[]{:S(2)}, u32[]{:S(2)}) collective-permute-start(f32[256,128]{1,0:T(8,128)S(1)} %get-tuple-element.133), channel_id=1, source_target_pairs={{0,8},{4,12},{8,0},{12,4},{16,24},{20,28},{24,16},{28,20},{1,9},{5... | collective-permute-start | bytes 393224 | tf_op jit(solution)/shard_map/ppermute | solution.py:355
  114.9 9.4 %collective-permute-start.42 = (f32[256,128]{1,0:T(8,128)S(1)}, f32[256,128]{1,0:T(8,128)S(1)}, u32[]{:S(2)}, u32[]{:S(2)}) collective-permute-start(f32[256,128]{1,0:T(8,128)S(1)} %get-tuple-element.134), channel_id=1, source_target_pairs={{0,12},{4,8},{8,4},{12,0},{16,28},{20,24},{24,20},{28,16},{1,13},{... | collective-permute-start | bytes 393224 | tf_op jit(solution)/shard_map/ppermute | solution.py:355
  116.9 11.0 %collective-permute-start.50 = (f32[8,512]{1,0:T(8,128)S(1)}, f32[8,512]{1,0:T(8,128)S(1)}, u32[]{:S(2)}, u32[]{:S(2)}) collective-permute-start(f32[8,512]{1,0:T(8,128)S(1)} %get-tuple-element.147), channel_id=1, source_target_pairs={{0,4},{4,0},{8,12},{12,8},{16,20},{20,16},{24,28},{28,24},{1,5},{5... | collective-permute-start | bytes 49160 | tf_op jit(solution)/shard_map/ppermute | solution.py:355
  119.7 10.9 %collective-permute-start.51 = (f32[8,512]{1,0:T(8,128)S(1)}, f32[8,512]{1,0:T(8,128)S(1)}, u32[]{:S(2)}, u32[]{:S(2)}) collective-permute-start(f32[8,512]{1,0:T(8,128)S(1)} %get-tuple-element.148), channel_id=1, source_target_pairs={{0,8},{4,12},{8,0},{12,4},{16,24},{20,28},{24,16},{28,20},{1,9},{5... | collective-permute-start | bytes 49160 | tf_op jit(solution)/shard_map/ppermute | solution.py:355
  119.7 12.3 %collective-permute-start.52 = (f32[8,512]{1,0:T(8,128)S(1)}, f32[8,512]{1,0:T(8,128)S(1)}, u32[]{:S(2)}, u32[]{:S(2)}) collective-permute-start(f32[8,512]{1,0:T(8,128)S(1)} %get-tuple-element.149), channel_id=1, source_target_pairs={{0,12},{4,8},{8,4},{12,0},{16,28},{20,24},{24,20},{28,16},{1,13},{... | collective-permute-start | bytes 49160 | tf_op jit(solution)/shard_map/ppermute | solution.py:355
  122.2 9.8 %collective-permute-start.53 = (f32[8,512]{1,0:T(8,128)S(1)}, f32[8,512]{1,0:T(8,128)S(1)}, u32[]{:S(2)}, u32[]{:S(2)}) collective-permute-start(f32[8,512]{1,0:T(8,128)S(1)} %get-tuple-element.150), channel_id=1, source_target_pairs={{0,16},{4,20},{8,24},{12,28},{16,0},{20,4},{24,8},{28,12},{1,17},{... | collective-permute-start | bytes 49160 | tf_op jit(solution)/shard_map/ppermute | solution.py:355
  124.3 9.1 %collective-permute-start.54 = (f32[8,512]{1,0:T(8,128)S(1)}, f32[8,512]{1,0:T(8,128)S(1)}, u32[]{:S(2)}, u32[]{:S(2)}) collective-permute-start(f32[8,512]{1,0:T(8,128)S(1)} %get-tuple-element.151), channel_id=1, source_target_pairs={{0,20},{4,16},{8,28},{12,24},{16,4},{20,0},{24,12},{28,8},{1,21},{... | collective-permute-start | bytes 49160 | tf_op jit(solution)/shard_map/ppermute | solution.py:355
  127.9 8.6 %collective-permute-start.55 = (f32[8,512]{1,0:T(8,128)S(1)}, f32[8,512]{1,0:T(8,128)S(1)}, u32[]{:S(2)}, u32[]{:S(2)}) collective-permute-start(f32[8,512]{1,0:T(8,128)S(1)} %get-tuple-element.152), channel_id=1, source_target_pairs={{0,24},{4,28},{8,16},{12,20},{16,8},{20,12},{24,0},{28,4},{1,25},{... | collective-permute-start | bytes 49160 | tf_op jit(solution)/shard_map/ppermute | solution.py:355
  130.6 12.0 %collective-permute-start.30 = (f32[256,128]{1,0:T(8,128)S(1)}, f32[256,128]{1,0:T(8,128)S(1)}, u32[]{:S(2)}, u32[]{:S(2)}) collective-permute-start(f32[256,128]{1,0:T(8,128)S(1)} %get-tuple-element.117), channel_id=1, source_target_pairs={{0,4},{4,0},{8,12},{12,8},{16,20},{20,16},{24,28},{28,24},{1,5},{5... | collective-permute-start | bytes 393224 | tf_op jit(solution)/shard_map/ppermute | solution.py:355
  132.0 10.7 %collective-permute-start.31 = (f32[256,128]{1,0:T(8,128)S(1)}, f32[256,128]{1,0:T(8,128)S(1)}, u32[]{:S(2)}, u32[]{:S(2)}) collective-permute-start(f32[256,128]{1,0:T(8,128)S(1)} %get-tuple-element.118), channel_id=1, source_target_pairs={{0,8},{4,12},{8,0},{12,4},{16,24},{20,28},{24,16},{28,20},{1,9},{5... | collective-permute-start | bytes 393224 | tf_op jit(solution)/shard_map/ppermute | solution.py:355
  132.0 11.9 %collective-permute-start.43 = (f32[256,128]{1,0:T(8,128)S(1)}, f32[256,128]{1,0:T(8,128)S(1)}, u32[]{:S(2)}, u32[]{:S(2)}) collective-permute-start(f32[256,128]{1,0:T(8,128)S(1)} %get-tuple-element.137.refs_0_), channel_id=1, source_target_pairs={{0,16},{4,20},{8,24},{12,28},{16,0},{20,4},{24,8},{28,12},{1,17},{... | collective-permute-start | bytes 393224 | tf_op jit(solution)/shard_map/ppermute | solution.py:355
  133.4 7.4 %collective-permute-start.56 = (f32[8,512]{1,0:T(8,128)S(1)}, f32[8,512]{1,0:T(8,128)S(1)}, u32[]{:S(2)}, u32[]{:S(2)}) collective-permute-start(f32[8,512]{1,0:T(8,128)S(1)} %get-tuple-element.153), channel_id=1, source_target_pairs={{0,28},{4,24},{8,20},{12,16},{16,12},{20,8},{24,4},{28,0},{1,29},{... | collective-permute-start | bytes 49160 | tf_op jit(solution)/shard_map/ppermute | solution.py:355
  136.5 9.9 %collective-permute-start.32 = (f32[256,128]{1,0:T(8,128)S(1)}, f32[256,128]{1,0:T(8,128)S(1)}, u32[]{:S(2)}, u32[]{:S(2)}) collective-permute-start(f32[256,128]{1,0:T(8,128)S(1)} %get-tuple-element.119), channel_id=1, source_target_pairs={{0,12},{4,8},{8,4},{12,0},{16,28},{20,24},{24,20},{28,16},{1,13},{... | collective-permute-start | bytes 393224 | tf_op jit(solution)/shard_map/ppermute | solution.py:355
  140.8 9.8 %collective-permute-start.37 = (f32[256,128]{1,0:T(8,128)S(1)}, f32[256,128]{1,0:T(8,128)S(1)}, u32[]{:S(2)}, u32[]{:S(2)}) collective-permute-start(f32[256,128]{1,0:T(8,128)S(1)} %get-tuple-element.128), channel_id=1, source_target_pairs={{0,4},{4,0},{8,12},{12,8},{16,20},{20,16},{24,28},{28,24},{1,5},{5... | collective-permute-start | bytes 393224 | tf_op jit(solution)/shard_map/ppermute | solution.py:355
  142.6 4.5 %collective-permute-start.57 = (f32[8,512]{1,0:T(8,128)S(1)}, f32[8,512]{1,0:T(8,128)S(1)}, u32[]{:S(2)}, u32[]{:S(2)}) collective-permute-start(f32[8,512]{1,0:T(8,128)S(1)} %newton.5.refs_12_), channel_id=1, source_target_pairs={{0,1},{1,0},{2,3},{3,2},{4,5},{5,4},{6,7},{7,6},{8,9},{9,8},{10,11... | collective-permute-start | bytes 49160 | tf_op jit(solution)/shard_map/ppermute | solution.py:355
  142.7 6.0 %collective-permute-start.58 = (f32[8,512]{1,0:T(8,128)S(1)}, f32[8,512]{1,0:T(8,128)S(1)}, u32[]{:S(2)}, u32[]{:S(2)}) collective-permute-start(f32[8,512]{1,0:T(8,128)S(1)} %newton.5.refs_12_), channel_id=1, source_target_pairs={{0,2},{1,3},{2,0},{3,1},{4,6},{5,7},{6,4},{7,5},{8,10},{9,11},{10,... | collective-permute-start | bytes 49160 | tf_op jit(solution)/shard_map/ppermute | solution.py:355
  143.9 6.1 %collective-permute-start.59 = (f32[8,512]{1,0:T(8,128)S(1)}, f32[8,512]{1,0:T(8,128)S(1)}, u32[]{:S(2)}, u32[]{:S(2)}) collective-permute-start(f32[8,512]{1,0:T(8,128)S(1)} %newton.5.refs_12_), channel_id=1, source_target_pairs={{0,3},{1,2},{2,1},{3,0},{4,7},{5,6},{6,5},{7,4},{8,11},{9,10},{10,... | collective-permute-start | bytes 49160 | tf_op jit(solution)/shard_map/ppermute | solution.py:355
  146.4 6.3 %collective-permute-start.38 = (f32[256,128]{1,0:T(8,128)S(1)}, f32[256,128]{1,0:T(8,128)S(1)}, u32[]{:S(2)}, u32[]{:S(2)}) collective-permute-start(f32[256,128]{1,0:T(8,128)S(1)} %get-tuple-element.129), channel_id=1, source_target_pairs={{0,8},{4,12},{8,0},{12,4},{16,24},{20,28},{24,16},{28,20},{1,9},{5... | collective-permute-start | bytes 393224 | tf_op jit(solution)/shard_map/ppermute | solution.py:355
  147.1 8.7 %collective-permute-start.39 = (f32[256,128]{1,0:T(8,128)S(1)}, f32[256,128]{1,0:T(8,128)S(1)}, u32[]{:S(2)}, u32[]{:S(2)}) collective-permute-start(f32[256,128]{1,0:T(8,128)S(1)} %get-tuple-element.130), channel_id=1, source_target_pairs={{0,12},{4,8},{8,4},{12,0},{16,28},{20,24},{24,20},{28,16},{1,13},{... | collective-permute-start | bytes 393224 | tf_op jit(solution)/shard_map/ppermute | solution.py:355
  148.7 8.0 %collective-permute-start.44 = (f32[256,128]{1,0:T(8,128)S(1)}, f32[256,128]{1,0:T(8,128)S(1)}, u32[]{:S(2)}, u32[]{:S(2)}) collective-permute-start(f32[256,128]{1,0:T(8,128)S(1)} %get-tuple-element.139), channel_id=1, source_target_pairs={{0,4},{4,0},{8,12},{12,8},{16,20},{20,16},{24,28},{28,24},{1,5},{5... | collective-permute-start | bytes 393224 | tf_op jit(solution)/shard_map/ppermute | solution.py:355
  149.9 8.5 %collective-permute-start.45 = (f32[256,128]{1,0:T(8,128)S(1)}, f32[256,128]{1,0:T(8,128)S(1)}, u32[]{:S(2)}, u32[]{:S(2)}) collective-permute-start(f32[256,128]{1,0:T(8,128)S(1)} %get-tuple-element.140), channel_id=1, source_target_pairs={{0,8},{4,12},{8,0},{12,4},{16,24},{20,28},{24,16},{28,20},{1,9},{5... | collective-permute-start | bytes 393224 | tf_op jit(solution)/shard_map/ppermute | solution.py:355
  150.6 10.3 %collective-permute-start.46 = (f32[256,128]{1,0:T(8,128)S(1)}, f32[256,128]{1,0:T(8,128)S(1)}, u32[]{:S(2)}, u32[]{:S(2)}) collective-permute-start(f32[256,128]{1,0:T(8,128)S(1)} %get-tuple-element.141), channel_id=1, source_target_pairs={{0,12},{4,8},{8,4},{12,0},{16,28},{20,24},{24,20},{28,16},{1,13},{... | collective-permute-start | bytes 393224 | tf_op jit(solution)/shard_map/ppermute | solution.py:355

commit v3 on v2

v3 whole, which is shorter than its diff:
```python
import functools
import math

import jax
import jax.numpy as jnp
import numpy as np
from jax import lax
from jax.experimental import pallas as pl
from jax.experimental.pallas import tpu as pltpu
from jax.sharding import PartitionSpec as P

FREQ_GROUPS = 8
DIRS = 32
ITERS = 3
NEWTON = 4
PSEUDO_RATE = 0.03
GROUP = 4
COSINES = (np.float32(0.99995), np.float32(0.9999))

SELF, UPY, UPZ, RATIO, WALL, FULL, FULL_N, FULL_T, FULL_GROUP = range(9)
FORWARD, SHIFT_Y, SHIFT_Z, EDGE_Y, KIND = range(5)
SLAB, MODE = range(2)

SMEM = pl.BlockSpec(memory_space=pltpu.SMEM)
VMEM = pl.BlockSpec(memory_space=pltpu.VMEM)
PARAMS = pltpu.CompilerParams(vmem_limit_bytes=48 * 1024 * 1024)


def diagonal_of(speed, rate, cosine):
    sine = jnp.sqrt(1.0 - cosine * cosine)
    across = np.float32(math.cos(math.pi / 8) + math.sin(math.pi / 8))
    return speed * (cosine + sine * across) + rate + PSEUDO_RATE


def slot_tables(labels, speed, rate, storage, threshold, slab, slabs, depth, width_y, width_z):
    band = labels // DIRS
    direction = labels % DIRS
    of_band = (band[None, :] == jnp.arange(FREQ_GROUPS, dtype=jnp.int32)[:, None]).astype(jnp.float32)
    speed, rate, storage, threshold = (
        jnp.sum(of_band * value[:, None], axis=0) for value in (speed, rate, storage, threshold)
    )
    polar = direction % 4
    outer = (polar == 0) | (polar == 3)
    forward = polar < 2
    cosine = jnp.where(outer, COSINES[0], COSINES[1])
    sine = jnp.sqrt(1.0 - cosine * cosine)
    azimuth = ((direction // 4).astype(jnp.float32) + 0.5) * (2.0 * math.pi / (DIRS // 4))
    vy = speed * sine * jnp.cos(azimuth)
    vz = speed * sine * jnp.sin(azimuth)
    diagonal = diagonal_of(speed, rate, cosine)
    ratio = speed * cosine / diagonal
    full = lax.integer_pow(ratio, depth)
    at_wall = jnp.where(forward, slab == 0, slab == slabs - 1)
    wall = storage * (1.0 + 1.0 / (4.0 * threshold**3))
    floats = jnp.stack(
        [
            PSEUDO_RATE / diagonal,
            jnp.abs(vy) / diagonal,
            jnp.abs(vz) / diagonal,
            ratio,
            jnp.where(at_wall, wall, 0.0),
            full,
            depth * full,
            (depth * (depth + 1) // 2) * full,
            lax.integer_pow(full, GROUP),
        ]
    )
    ints = jnp.stack(
        [
            forward.astype(jnp.int32),
            jnp.where(vy > 0, 1, 7).astype(jnp.int32),
            jnp.where(vz > 0, 1, width_z - 1).astype(jnp.int32),
            jnp.where(vy > 0, 0, 7).astype(jnp.int32),
            2 * band + jnp.where(outer, 0, 1),
        ]
    )
    x = jnp.arange(slabs * depth, dtype=jnp.int32)[:, None]
    past = jnp.where(forward[None, :], x - (slab * depth + depth - 1), slab * depth - x)
    n = past.astype(jnp.float32)
    weight = jnp.where(past > 0, jnp.power(ratio[None, :], jnp.maximum(n, 0.0)), 0.0)
    return floats, ints, jnp.concatenate([weight, n * weight, (0.5 * n * (n + 1.0)) * weight], axis=1)


def kind_table(speed, rate, storage, threshold, generation):
    rows = []
    for cosine in COSINES:
        diagonal = diagonal_of(speed, rate, cosine)
        therm = rate * storage / diagonal
        rows.append(jnp.stack([therm, therm / (4.0 * threshold**3), generation / diagonal]))
    return jnp.stack(rows, axis=2).reshape(3, 2 * FREQ_GROUPS)


def newton(density, kelvin, linear, quart):
    for _ in range(NEWTON):
        cube = kelvin * kelvin * kelvin
        residual = linear * kelvin + quart * (kelvin * cube) - density
        kelvin = kelvin - residual / (linear + 4.0 * quart * cube)
    return kelvin


def stencil(low, high, c_self, c_y, c_z, shift_y, shift_z, at_edge):
    turned_low, turned_high = pltpu.roll(low, shift_y, 0), pltpu.roll(high, shift_y, 0)
    up_low = jnp.where(at_edge, turned_high, turned_low)
    up_high = jnp.where(at_edge, turned_low, turned_high)
    return (
        c_self * low + c_y * up_low + c_z * pltpu.roll(low, shift_z, 1),
        c_self * high + c_y * up_high + c_z * pltpu.roll(high, shift_z, 1),
    )


def sweep_kernel(which, sizes, *refs):
    block, blocks, depth, width_y, slots, modes = sizes
    refs = list(refs)
    take = lambda count: [refs.pop(0) for _ in range(count)]
    meta, floats, ints, kinds, energy, flag, matrix, given = take(8)
    older = take(which - 1)
    swept, shares = take(2)
    if which == 1:
        stencil_one, stencil_two, quarter = take(3)
    elif which == 2:
        (stencil_one,) = take(1)
    else:
        (outgoing,) = take(1)
    if which < ITERS:
        (outgoing,) = take(1)
    density, sources, kelvin = take(3)
    rows = width_y // modes
    step = pl.program_id(0)

    @pl.when(step == 0)
    def _():
        if which == 1:
            kelvin[...] = given[...]
            for yy in range(rows):
                y = meta[MODE] * rows + yy
                quarter[:, yy * 128 : (yy + 1) * 128] = kelvin[pl.ds(y, depth, stride=width_y), :]
        else:
            for y in range(width_y):
                lane = (y % rows) * 128
                kelvin[pl.ds(y, depth, stride=width_y), :] = given[y // rows, :, lane : lane + 128]
        density[...] = jnp.zeros_like(density)

        def one_cell_row(x, carry):
            at = pl.ds(x * width_y, width_y)
            t = kelvin[at, :]
            square = t * t
            fourth = square * square
            heat = flag[at, :].astype(jnp.float32)
            for kind in range(2 * FREQ_GROUPS):
                sources[kind, at, :] = kinds[0, kind] * t + kinds[1, kind] * fourth + kinds[2, kind] * heat
            return carry

        lax.fori_loop(0, depth, one_cell_row, 0)

    row = lax.broadcasted_iota(jnp.int32, (8, 128), 0)

    def one_slot(i, sums):
        s = step * block + i
        forward = ints[FORWARD, s] == 1
        c_self, c_y, c_z, ratio = floats[SELF, s], floats[UPY, s], floats[UPZ, s], floats[RATIO, s]
        kind, shift_y, shift_z = ints[KIND, s], ints[SHIFT_Y, s], ints[SHIFT_Z, s]
        at_edge = row == ints[EDGE_Y, s]
        apply = lambda low, high: stencil(low, high, c_self, c_y, c_z, shift_y, shift_z, at_edge)
        layers = []
        for x in range(depth):
            at = x * 16
            low, high = apply(energy[i, at : at + 8, :], energy[i, at + 8 : at + 16, :])
            layers.append((low + sources[kind, at : at + 8, :], high + sources[kind, at + 8 : at + 16, :]))
        faces, sums = [], list(sums)
        for half in range(2):
            values = [layer[half] for layer in layers]
            values = [jnp.where(forward, a, b) for a, b in zip(values, values[::-1])]
            total = jnp.full((8, 128), floats[WALL, s], jnp.float32)
            for j in range(depth):
                total = ratio * total + values[j]
                values[j] = total
            faces.append(total)
            values = [jnp.where(forward, a, b) for a, b in zip(values, values[::-1])]
            for x in range(depth):
                at = x * 16 + half * 8
                swept[i, at : at + 8, :] = values[x]
                sums[2 * x + half] = sums[2 * x + half] + values[x]
        at_low, at_high = pl.ds(s * 16, 8), pl.ds(s * 16 + 8, 8)
        low, high = faces
        outgoing[at_low, :] = low
        outgoing[at_high, :] = high
        if which < ITERS:
            low, high = apply(low, high)
            stencil_one[at_low, :] = low
            stencil_one[at_high, :] = high
        if which == 1:
            low, high = apply(low, high)
            stencil_two[at_low, :] = low
            stencil_two[at_high, :] = high
        return tuple(sums)

    sums = lax.fori_loop(0, block, one_slot, (jnp.zeros((8, 128), jnp.float32),) * (2 * depth), unroll=4)
    for part in range(2 * depth):
        density[part * 8 : part * 8 + 8, :] += sums[part]

    @pl.when(step == blocks - 1)
    def _():
        planes = [outgoing] + older
        home = pl.ds(meta[SLAB] * depth, depth)
        for at in range(modes):
            ys = [at * rows + yy for yy in range(rows)]
            total = None
            for index, plane in enumerate(planes):
                right = jnp.concatenate([plane[pl.ds(y, slots, stride=width_y), :] for y in ys], axis=1)
                term = jnp.dot(
                    matrix[:, index * slots : (index + 1) * slots],
                    right,
                    precision=lax.Precision.HIGHEST,
                    preferred_element_type=jnp.float32,
                )
                total = term if total is None else total + term
            shares[at] = total
            shares[at, home, :] += jnp.concatenate([density[pl.ds(y, depth, stride=width_y), :] for y in ys], axis=1)


def add_up(ref):
    values = [ref[index] for index in range(ref.shape[0])]
    while len(values) > 1:
        values = [a + b for a, b in zip(values[::2], values[1::2])]
    return values[0]


def partial_kernel(depth, shares, parts):
    total = add_up(shares)
    for slab in range(parts.shape[0]):
        parts[slab] = total[slab * depth : (slab + 1) * depth]


def newton_kernel(sums, before, parts, kelvin, copies):
    now = newton(add_up(parts) * (1.0 / DIRS), before[...], sums[0], sums[1])
    kelvin[...] = now
    for index in range(copies.shape[0]):
        copies[index] = now


def compose_kernel(own, group, earlier, meta, floats, ints, received, *refs):
    entered, composite = refs[:earlier], refs[earlier]
    effective = refs[earlier + 1] if earlier else None
    base = meta[SLAB] % group * own

    def one_slot(i, carry):
        s = base + i
        forward = ints[FORWARD, s] == 1
        at = pl.ds(i * 16, 16)
        values = []
        for k in range(group):
            value = received[k, at, :]
            for back in range(earlier):
                value += floats[FULL_N + back, s] * entered[earlier - 1 - back][k, at, :]
            if earlier:
                effective[k, at, :] = value
            values.append(value)
        values = [jnp.where(forward, a, b) for a, b in zip(values, values[::-1])]
        total = values[0]
        for value in values[1:]:
            total = floats[FULL, s] * total + value
        composite[at, :] = total
        return carry

    lax.fori_loop(0, own, one_slot, 0, unroll=4)


def enter_kernel(own, group, groups, meta, floats, ints, effective, *refs):
    composites, (entered, ordered) = refs[:groups], refs[groups:]
    slab = meta[SLAB]
    place, mine = slab % group, slab // group
    for by in range(groups):
        ordered[mine ^ by] = composites[by][...]

    def one_slot(i, carry):
        s = place * own + i
        forward = ints[FORWARD, s] == 1
        begin = jnp.where(forward, 0, groups - 1)
        stride = jnp.where(forward, 1, -1)
        ahead = jnp.where(forward, mine, groups - 1 - mine)
        at = pl.ds(i * 16, 16)
        total = jnp.zeros((16, 128), jnp.float32)
        for g in range(groups - 1):
            later = floats[FULL_GROUP, s] * total + ordered[begin + stride * g, at, :]
            total = jnp.where(g < ahead, later, total)
        values = [effective[k, at, :] for k in range(group)]
        values = [jnp.where(forward, a, b) for a, b in zip(values, values[::-1])]
        inflow = [total]
        for value in values[:-1]:
            total = floats[FULL, s] * total + value
            inflow.append(total)
        for k in range(group):
            entered[k, at, :] = jnp.where(forward, inflow[k], inflow[group - 1 - k])
        return carry

    lax.fori_loop(0, own, one_slot, 0, unroll=4)


def final_kernel(block, depth, width_y, modes, floats, ints, swept, first, second, third, kelvins, energy, kelvin):
    step = pl.program_id(0)
    rows = width_y // modes

    @pl.when(step == 0)
    def _():
        for y in range(width_y):
            lane = (y % rows) * 128
            kelvin[pl.ds(y, depth, stride=width_y), :] = kelvins[y // rows, :, lane : lane + 128]

    def one_slot(i, carry):
        s = step * block + i
        forward = ints[FORWARD, s] == 1
        ratio = floats[RATIO, s]
        at = pl.ds(s * 16, 16)
        a, b, c = first[at, :], second[at, :], third[at, :]
        values = []
        for j in range(depth):
            a = ratio * a
            b = ratio * b + a
            c = ratio * c + b
            values.append(c)
        for x in range(depth):
            here = slice(x * 16, x * 16 + 16)
            energy[i, here, :] = swept[i, here, :] + jnp.where(forward, values[x], values[depth - 1 - x])
        return carry

    lax.fori_loop(0, block, one_slot, 0, unroll=4)


def local(incoming_occupation, crystal_kelvin_given, generating_region_flag, labels, speed, rate, storage, threshold, generation):
    slots, depth, width_y, width_z = incoming_occupation.shape
    slabs, modes = lax.axis_size("slab"), lax.axis_size("mode")
    group, groups = GROUP, slabs // GROUP
    own = slots // group
    lanes = width_y // modes * width_z
    block = 8
    blocks = slots // block
    slab = lax.axis_index("slab").astype(jnp.int32)
    meta = jnp.stack([slab, lax.axis_index("mode").astype(jnp.int32)])
    floats, ints, matrix = slot_tables(labels, speed, rate, storage, threshold, slab, slabs, depth, width_y, width_z)
    kinds = kind_table(speed, rate, storage, threshold, generation)
    sums = jnp.stack([jnp.sum(storage), jnp.sum(storage / (4.0 * threshold**3))])

    def shape(*dims):
        return jax.ShapeDtypeStruct(dims, jnp.float32)

    def whole(*dims):
        return pl.BlockSpec(dims, lambda i: (0,) * len(dims))

    cells = depth * width_y
    slot_block = pl.BlockSpec((block, cells, width_z), lambda i: (i, 0, 0))
    face_rows = own * width_y
    members = [list(range(g * group, (g + 1) * group)) for g in range(groups)]
    near = functools.partial(lax.all_to_all, axis_name="slab", split_axis=0, concat_axis=0, axis_index_groups=members)
    over = lambda array, axis: lax.all_to_all(array, axis, 0, 0)

    def sweep(which, energy, kelvin, older):
        plane = (whole(slots * width_y, width_z), shape(slots * width_y, width_z))
        outs = [(slot_block, shape(slots, cells, width_z))]
        outs += [(whole(modes, slabs * depth, lanes), shape(modes, slabs * depth, lanes))]
        if which == 1:
            outs += [plane, plane, (whole(depth, lanes), shape(depth, lanes))]
        else:
            outs += [plane]
        face = [pltpu.VMEM((slots * width_y, width_z), jnp.float32)] if which < ITERS else []
        return pl.pallas_call(
            functools.partial(sweep_kernel, which, (block, blocks, depth, width_y, slots, modes)),
            grid=(blocks,),
            in_specs=[SMEM] * 4
            + [slot_block, whole(cells, width_z), whole(slabs * depth, ITERS * slots), whole(*kelvin.shape)]
            + [whole(slots * width_y, width_z)] * len(older),
            out_specs=[spec for spec, _ in outs],
            out_shape=[of for _, of in outs],
            scratch_shapes=face
            + [
                pltpu.VMEM((cells, width_z), jnp.float32),
                pltpu.VMEM((2 * FREQ_GROUPS, cells, width_z), jnp.float32),
                pltpu.VMEM((cells, width_z), jnp.float32),
            ],
            compiler_params=PARAMS,
            name=f"sweep_{which}",
        )(meta, floats, ints, kinds, energy, flag, matrix, kelvin, *older)

    def solve(shares, before):
        parts = pl.pallas_call(
            functools.partial(partial_kernel, depth),
            in_specs=[VMEM],
            out_specs=VMEM,
            out_shape=shape(slabs, depth, lanes),
            compiler_params=PARAMS,
            name="density_parts",
        )(over(shares, "mode"))
        quarter, copies = pl.pallas_call(
            newton_kernel,
            in_specs=[SMEM, VMEM, VMEM],
            out_specs=[VMEM, VMEM],
            out_shape=[shape(depth, lanes), shape(modes, depth, lanes)],
            compiler_params=PARAMS,
            name="newton",
        )(sums, before, over(parts, "slab"))
        return quarter, over(copies, "mode")

    def exchange(face, before):
        received = near(face.reshape(group, face_rows, width_z))
        blocked = shape(group, face_rows, width_z)
        composite, *effective = pl.pallas_call(
            functools.partial(compose_kernel, own, group, len(before)),
            in_specs=[SMEM] * 3 + [VMEM] * (1 + len(before)),
            out_specs=[VMEM] * (2 if before else 1),
            out_shape=[shape(face_rows, width_z)] + ([blocked] if before else []),
            compiler_params=PARAMS,
            name="compose",
        )(meta, floats, ints, received, *before)
        composites = [composite] + [
            lax.ppermute(composite, "slab", [(i, i ^ (by * group)) for i in range(slabs)]) for by in range(1, groups)
        ]
        entered = pl.pallas_call(
            functools.partial(enter_kernel, own, group, groups),
            in_specs=[SMEM] * 3 + [VMEM] * (1 + groups),
            out_specs=VMEM,
            out_shape=blocked,
            scratch_shapes=[pltpu.VMEM((groups, face_rows, width_z), jnp.float32)],
            compiler_params=PARAMS,
            name="enter",
        )(meta, floats, ints, effective[0] if before else received, *composites)
        return entered, near(entered).reshape(slots * width_y, width_z)

    flag = generating_region_flag.reshape(cells, width_z)
    energy = incoming_occupation.reshape(slots, cells, width_z)

    energy, shares, once, twice, quarter = sweep(1, energy, crystal_kelvin_given.reshape(cells, width_z), [])
    quarter, kelvin = solve(shares, quarter)
    entered_one, plane_one = exchange(twice, [])

    energy, shares, once_two = sweep(2, energy, kelvin, [once])
    quarter, kelvin = solve(shares, quarter)
    entered_two, plane_two = exchange(once_two, [entered_one])

    energy, shares, outgoing = sweep(3, energy, kelvin, [once_two, twice])
    quarter, kelvin = solve(shares, quarter)
    _, plane_three = exchange(outgoing, [entered_one, entered_two])

    energy, kelvin = pl.pallas_call(
        functools.partial(final_kernel, block, depth, width_y, modes),
        grid=(blocks,),
        in_specs=[SMEM] * 2
        + [slot_block]
        + [whole(slots * width_y, width_z)] * ITERS
        + [whole(modes, depth, lanes)],
        out_specs=[slot_block, whole(cells, width_z)],
        out_shape=[shape(slots, cells, width_z), shape(cells, width_z)],
        compiler_params=PARAMS,
        name="final_energy",
    )(floats, ints, energy, plane_one, plane_two, plane_three, kelvin)
    return energy.reshape(slots, depth, width_y, width_z), kelvin.reshape(depth, width_y, width_z)


def solution(mesh):
    return jax.shard_map(
        local,
        mesh=mesh,
        in_specs=(
            P("mode", "slab", None, None),
            P("slab", None, None),
            P("slab", None, None),
            P("mode"),
            P(),
            P(),
            P(),
            P(),
            P(),
        ),
        out_specs=(P("mode", "slab", None, None), P("slab", None, None)),
        check_vma=False,
    )
```

time: 167 us -> 210 us (1.26)
  blocking collectives: 0 us -> 75.6 us
  starting transfers between devices: 70 us -> 35.2 us
  local copies, waits for them, and re-layouts: 1.93 us -> 8.14 us
  Pallas kernels: 49.6 us -> 44.9 us
    all_to_all x0 -> x8, blocking collectives: none -> 75.6 us  [the longest x7 64.5 us: local(): over = lambda array, axis: lax.all_to_all(array, axis, 0, 0)]
    ppermute x60 -> x3, starting transfers between devices: 70 us -> 5.6 us  [exchange(): lax.ppermute(composite, 'slab', [(i, i ^ by * group) for i in range(slabs)])]
    all_to_all x0 -> x7, starting transfers between devices: none -> 29.6 us  [the longest x3 11.1 us: exchange(): received = near(face.reshape(group, face_rows, width_z))]
    all_to_all x0 -> x7, waiting for transfers between devices: none -> 19.9 us  [the longest x3 7.42 us: exchange(): received = near(face.reshape(group, face_rows, width_z))]
    ppermute x60 -> x3, waiting for transfers between devices: 38 us -> 19.1 us  [exchange(): lax.ppermute(composite, 'slab', [(i, i ^ by * group) for i in range(slabs)])]
    unnamed x8 -> x12, local copies, waits for them, and re-layouts: 1.69 us -> 7.9 us
    pallas_call x3, Pallas kernels: 33.6 us -> 28.6 us  [sweep(): pl.pallas_call(functools.partial(sweep_kernel, which, (block, blocks, dep...]
  transfers between devices with their start and end apart: 60 -> 10, of which waited for: 21 -> 8; matrix products, arithmetic and copies ran while one was open for 1% -> 1% of each run, Pallas kernels for 19% -> 9%
where the time goes in v3:
time: 210 us; the launch traced here: 209 us
  blocking collectives  75.6 us (36%)
  Pallas kernels  44.9 us (21%)
  waiting for transfers between devices  39 us (19%)
  starting transfers between devices  35.2 us (17%)
  local copies, waits for them, and re-layouts  8.14 us (4%)
  other arithmetic  5.3 us (3%)
    all_to_all x7, blocking collectives, local(): over = lambda array, axis: lax.all_to_all(array, axis, 0, 0)  64.5 us
    pallas_call x3, Pallas kernels, sweep(): pl.pallas_call(functools.partial(sweep_kernel, which, (block, blocks, dep...  28.6 us
    ppermute x3, waiting for transfers between devices, exchange(): lax.ppermute(composite, 'slab', [(i, i ^ by * group) for i in range(slabs)])  19.1 us
    all_to_all x1, blocking collectives, exchange(): return (entered, near(entered).reshape(slots * width_y, width_z))  11.1 us
    all_to_all x3, starting transfers between devices, exchange(): received = near(face.reshape(group, face_rows, width_z))  11.1 us
    all_to_all x2, starting transfers between devices, exchange(): return (entered, near(entered).reshape(slots * width_y, width_z))  9.28 us
    all_to_all x2, starting transfers between devices, local(): over = lambda array, axis: lax.all_to_all(array, axis, 0, 0)  9.22 us
    unnamed x12, local copies, waits for them, and re-layouts  7.9 us
  transfers between devices with their start and end apart: 10, of which 8 were waited for; matrix products, arithmetic and copies ran while one was open for 1% of the time, Pallas kernels for 9%

profile of v3, /device:TPU:0, one launch (start us, length us, event | category | flops | bytes accessed | tf_op | source)
XLA Modules:
  0.0 208.9 jit_solution(8043269987712373430)
XLA Ops:
  0.6 0.0 copy-start.4
  0.6 0.7 add_bitcast_fusion
  1.4 0.7 divide_bitcast_fusion.4
  2.1 0.8 select_reduce_fusion
  2.9 0.1 fusion.14
  3.0 1.4 fusion.23
  4.3 0.1 copy.13
  4.4 0.1 reshape.57.refs_3_
  4.6 0.1 pad_add_fusion.refs_0_.meta
  4.7 0.1 fusion.5
  4.8 0.1 pad_maximum_fusion.refs_6_
  5.0 0.0 copy-start.3
  5.0 0.8 copy-done.3
  5.9 0.0 copy-start.5
  5.9 0.8 copy-done.5
  6.7 9.3 %sweep_1.1 = (f32[64,128,128]{2,1,0:T(8,128)S(1)}, f32[4,64,512]{2,1,0:T(8,128)S(1)}, f32[1024,128]{1,0:T(8,128)S(1)}, f32[1024,128]{1,0:T(8,128)}, f32[8,512]{1,0:T(8,128)S(1)}) custom-call(s32[2]{0:T(128)S(1)} %pad_add_fusion.refs_0_.meta, f32[9,64]{1,0:T(8,128)S(1)} %stack.111.refs_1_.floats, s32[5,64]{1,0:T(8,128)S(1)} %stack.118.refs_2_.ints, ...), custom_call_target="tpu_custom_call" | custom-call | tf_op jit(solution)/shard_map/sweep_1/pallas_call | solution.py:365
  16.0 0.0 copy-start.1
  16.0 2.0 copy-done.1
  18.0 12.8 %all_to_all.75.shares = f32[4,64,512]{2,1,0:T(8,128)S(1)} all-to-all(f32[4,64,512]{2,1,0:T(8,128)S(1)} %get-tuple-element.26), channel_id=1, replica_groups=mesh['slab'=8,'mode'=4] {'mode'}, dimensions={0} | all-to-all | bytes 1048576 | tf_op jit(solution)/shard_map/all_to_all | solution.py:354
  30.9 0.7 density_parts.3
  31.6 5.8 %all-to-all-start.1 = ((f32[8,8,512]{2,1,0:T(8,128)}), f32[8,8,512]{2,1,0:T(8,128)S(1)}, u32[]{:S(2)}, u32[]{:S(2)}) async-start(f32[8,8,512]{2,1,0:T(8,128)} %density_parts.3), calls=%async_computation.1 | async-start | bytes 262144 | tf_op jit(solution)/shard_map/all_to_all | solution.py:354
  37.4 1.2 pad_maximum_fusion.2.sums
  38.6 6.1 %all-to-all-done.1.parts = f32[8,8,512]{2,1,0:T(8,128)S(1)} async-done(((f32[8,8,512]{2,1,0:T(8,128)}), f32[8,8,512]{2,1,0:T(8,128)S(1)}, u32[]{:S(2)}, u32[]{:S(2)}) %all-to-all-start.1) | async-done | bytes 131104 | tf_op jit(solution)/shard_map/all_to_all | solution.py:354
  44.8 0.6 newton.3
  45.4 6.5 %all_to_all.76.refs_7_ = f32[4,8,512]{2,1,0:T(8,128)S(1)} all-to-all(f32[4,8,512]{2,1,0:T(8,128)S(1)} %get-tuple-element.27), channel_id=1, replica_groups=mesh['slab'=8,'mode'=4] {'mode'}, dimensions={0} | all-to-all | bytes 131072 | tf_op jit(solution)/shard_map/all_to_all | solution.py:354
  51.8 0.0 copy-done.4
  51.8 9.2 %sweep_2.1 = (f32[64,128,128]{2,1,0:T(8,128)S(1)}, f32[4,64,512]{2,1,0:T(8,128)S(1)}, f32[1024,128]{1,0:T(8,128)}) custom-call(s32[2]{0:T(128)S(1)} %pad_add_fusion.refs_0_.meta, f32[9,64]{1,0:T(8,128)S(1)} %stack.111.refs_1_.floats, s32[5,64]{1,0:T(8,128)S(1)} %stack.118.refs_2_.ints, f32[3,16]{1,0:T(4,128)S(1)} %reshape.57.refs_3_, ...), custom_call_target="tpu_custom_call" | custom-call | tf_op jit(solution)/shard_map/sweep_2/pallas_call | solution.py:365
  61.0 2.0 copy-done.2
  63.0 11.2 %all_to_all.77.shares = f32[4,64,512]{2,1,0:T(8,128)S(1)} all-to-all(f32[4,64,512]{2,1,0:T(8,128)S(1)} %get-tuple-element.31), channel_id=1, replica_groups=mesh['slab'=8,'mode'=4] {'mode'}, dimensions={0} | all-to-all | bytes 1048576 | tf_op jit(solution)/shard_map/all_to_all | solution.py:354
  74.3 9.7 %all_to_all.78.parts = f32[8,8,512]{2,1,0:T(8,128)S(1)} all-to-all(f32[8,8,512]{2,1,0:T(8,128)S(1)} %density_parts.4), channel_id=1, replica_groups=mesh['slab'=8,'mode'=4] {'slab'}, dimensions={0} | all-to-all | bytes 262144 | tf_op jit(solution)/shard_map/all_to_all | solution.py:354
  84.0 0.6 newton.4
  84.6 6.5 %all_to_all.79.refs_7_ = f32[4,8,512]{2,1,0:T(8,128)S(1)} all-to-all(f32[4,8,512]{2,1,0:T(8,128)S(1)} %get-tuple-element.32), channel_id=1, replica_groups=mesh['slab'=8,'mode'=4] {'mode'}, dimensions={0} | all-to-all | bytes 131072 | tf_op jit(solution)/shard_map/all_to_all | solution.py:354
  91.1 3.5 %all-to-all-start.6 = ((f32[4,256,128]{2,1,0:T(8,128)}), f32[4,256,128]{2,1,0:T(8,128)S(1)}, u32[]{:S(2)}, u32[]{:S(2)}) async-start(f32[4,256,128]{2,1,0:T(8,128)} %bitcast.29), calls=%async_computation.6 | async-start | bytes 1048576 | tf_op jit(solution)/shard_map/all_to_all | solution.py:403
  94.6 10.1 %sweep_3.1 = (f32[64,128,128]{2,1,0:T(8,128)}, f32[4,64,512]{2,1,0:T(8,128)S(1)}, f32[1024,128]{1,0:T(8,128)}) custom-call(s32[2]{0:T(128)S(1)} %pad_add_fusion.refs_0_.meta, f32[9,64]{1,0:T(8,128)S(1)} %stack.111.refs_1_.floats, s32[5,64]{1,0:T(8,128)S(1)} %stack.118.refs_2_.ints, f32[3,16]{1,0:T(4,128)S(1)} %reshape.57.refs_3_, f32[64,128,128]{2,1,0:T(8,128)} %copy-done.2, ...), custom_call_target="tpu_custom_call" | custom-call | tf_op jit(solution)/shard_map/sweep_3/pallas_call | solution.py:365
  104.7 0.0 all-to-all-done.6.received.effective
  104.7 11.2 %all_to_all.80.shares = f32[4,64,512]{2,1,0:T(8,128)S(1)} all-to-all(f32[4,64,512]{2,1,0:T(8,128)S(1)} %get-tuple-element.42), channel_id=1, replica_groups=mesh['slab'=8,'mode'=4] {'mode'}, dimensions={0} | all-to-all | bytes 1048576 | tf_op jit(solution)/shard_map/all_to_all | solution.py:354
  115.9 4.1 %all-to-all-start.8 = ((f32[4,256,128]{2,1,0:T(8,128)}), f32[4,256,128]{2,1,0:T(8,128)S(1)}, u32[]{:S(2)}, u32[]{:S(2)}) async-start(f32[4,256,128]{2,1,0:T(8,128)} %bitcast.31), calls=%async_computation.8 | async-start | bytes 1048576 | tf_op jit(solution)/shard_map/all_to_all | solution.py:403
  120.0 0.7 density_parts.5
  120.7 7.0 %all-to-all-done.8.received = f32[4,256,128]{2,1,0:T(8,128)S(1)} async-done(((f32[4,256,128]{2,1,0:T(8,128)}), f32[4,256,128]{2,1,0:T(8,128)S(1)}, u32[]{:S(2)}, u32[]{:S(2)}) %all-to-all-start.8) | async-done | bytes 524320 | tf_op jit(solution)/shard_map/all_to_all | solution.py:403
  127.7 3.4 %all-to-all-start.13 = ((f32[8,8,512]{2,1,0:T(8,128)}), f32[8,8,512]{2,1,0:T(8,128)S(1)}, u32[]{:S(2)}, u32[]{:S(2)}) async-start(f32[8,8,512]{2,1,0:T(8,128)} %density_parts.5), calls=%async_computation.13 | async-start | bytes 262144 | tf_op jit(solution)/shard_map/all_to_all | solution.py:354
  131.1 0.8 compose.3.refs_0_
  131.9 2.9 %collective-permute-start = (f32[256,128]{1,0:T(8,128)S(1)}, f32[256,128]{1,0:T(8,128)S(1)}, u32[]{:S(2)}, u32[]{:S(2)}) collective-permute-start(f32[256,128]{1,0:T(8,128)S(1)} %compose.3.refs_0_), channel_id=1, source_target_pairs={{0,16},{4,20},{8,24},{12,28},{16,0},{20,4},{24,8},{28,12},{1,17},{... | collective-permute-start | bytes 393224 | tf_op jit(solution)/shard_map/ppermute | solution.py:414
  134.8 7.1 %collective-permute-done.refs_1_ = f32[256,128]{1,0:T(8,128)S(1)} collective-permute-done((f32[256,128]{1,0:T(8,128)S(1)}, f32[256,128]{1,0:T(8,128)S(1)}, u32[]{:S(2)}, u32[]{:S(2)}) %collective-permute-start) | collective-permute-done | bytes 131104 | tf_op jit(solution)/shard_map/ppermute | solution.py:414
  141.9 1.7 enter.3.refs_0_
  143.6 0.0 all-to-all-done.13.parts
  143.6 3.5 %all-to-all-start.7 = ((f32[4,256,128]{2,1,0:T(8,128)}), f32[4,256,128]{2,1,0:T(8,128)S(1)}, u32[]{:S(2)}, u32[]{:S(2)}) async-start(f32[4,256,128]{2,1,0:T(8,128)} %enter.3.refs_0_), calls=%async_computation.7 | async-start | bytes 1048576 | tf_op jit(solution)/shard_map/all_to_all | solution.py:425
  147.1 1.2 newton.5
  148.3 6.1 %all-to-all-done.7 = f32[4,256,128]{2,1,0:T(8,128)S(1)} async-done(((f32[4,256,128]{2,1,0:T(8,128)}), f32[4,256,128]{2,1,0:T(8,128)S(1)}, u32[]{:S(2)}, u32[]{:S(2)}) %all-to-all-start.7) | async-done | bytes 524320 | tf_op jit(solution)/shard_map/all_to_all | solution.py:425
  154.4 6.5 %all_to_all.81.kelvins = f32[4,8,512]{2,1,0:T(8,128)S(1)} all-to-all(f32[4,8,512]{2,1,0:T(8,128)S(1)} %get-tuple-element.43), channel_id=1, replica_groups=mesh['slab'=8,'mode'=4] {'mode'}, dimensions={0} | all-to-all | bytes 131072 | tf_op jit(solution)/shard_map/all_to_all | solution.py:354
  160.9 3.5 %all-to-all-start.10 = ((f32[4,256,128]{2,1,0:T(8,128)}), f32[4,256,128]{2,1,0:T(8,128)S(1)}, u32[]{:S(2)}, u32[]{:S(2)}) async-start(f32[4,256,128]{2,1,0:T(8,128)} %bitcast.33), calls=%async_computation.10 | async-start | bytes 1048576 | tf_op jit(solution)/shard_map/all_to_all | solution.py:403
  164.4 1.2 compose.4
  165.6 2.0 collective-permute-start.1
  167.6 5.5 %collective-permute-done.1.refs_1_ = f32[256,128]{1,0:T(8,128)S(1)} collective-permute-done((f32[256,128]{1,0:T(8,128)S(1)}, f32[256,128]{1,0:T(8,128)S(1)}, u32[]{:S(2)}, u32[]{:S(2)}) %collective-permute-start.1) | collective-permute-done | bytes 131104 | tf_op jit(solution)/shard_map/ppermute | solution.py:414
  173.1 1.7 enter.4.refs_1_
  174.8 0.4 all-to-all-done.10.received
  175.3 5.8 %all-to-all-start.9 = ((f32[4,256,128]{2,1,0:T(8,128)}), f32[4,256,128]{2,1,0:T(8,128)S(1)}, u32[]{:S(2)}, u32[]{:S(2)}) async-start(f32[4,256,128]{2,1,0:T(8,128)} %enter.4.refs_1_), calls=%async_computation.9 | async-start | bytes 1048576 | tf_op jit(solution)/shard_map/all_to_all | solution.py:425
  181.1 1.4 compose.5
  182.5 0.7 collective-permute-start.2
  183.2 6.5 %collective-permute-done.2.refs_1_ = f32[256,128]{1,0:T(8,128)S(1)} collective-permute-done((f32[256,128]{1,0:T(8,128)S(1)}, f32[256,128]{1,0:T(8,128)S(1)}, u32[]{:S(2)}, u32[]{:S(2)}) %collective-permute-start.2) | collective-permute-done | bytes 131104 | tf_op jit(solution)/shard_map/ppermute | solution.py:414
  189.7 0.9 enter.5
  190.6 0.2 all-to-all-done.9
  190.9 11.1 %all_to_all.82 = f32[4,256,128]{2,1,0:T(8,128)S(1)} all-to-all(f32[4,256,128]{2,1,0:T(8,128)S(1)} %enter.5), channel_id=1, replica_groups={{0,4,8,12},{16,20,24,28},{1,5,9,13},{17,21,25,29},{2,6,10,14},{18,22,26..., dimensions={0} | all-to-all | bytes 1048576 | tf_op jit(solution)/shard_map/all_to_all | solution.py:425
  202.0 2.2 %copy-done = f32[64,128,128]{2,1,0:T(8,128)S(1)} copy-done((f32[64,128,128]{2,1,0:T(8,128)S(1)}, f32[64,128,128]{2,1,0:T(8,128)}, u32[]{:S(2)}) %copy-start) | copy-done | bytes 4194328
  204.2 4.8 %final_energy.1 = (f32[64,128,128]{2,1,0:T(8,128)}, f32[128,128]{1,0:T(8,128)}) custom-call(f32[9,64]{1,0:T(8,128)S(1)} %stack.111.refs_1_.floats, s32[5,64]{1,0:T(8,128)S(1)} %stack.118.refs_2_.ints, f32[64,128,128]{2,1,0:T(8,128)S(1)} %copy-done, f32[1024,128]{1,0:T(8,128)S(1)} %bitcast.58, f32[1024,128]{1,0:T(8,128)S(1)} %bitcast.59, ...), custom_call_target="tpu_custom_call" | custom-call | tf_op jit(solution)/shard_map/final_energy/pallas_call | solution.py:442
  (13 shorter events, 0.2 us)
Async XLA Ops:
  0.6 51.2 %copy-start.4 = (s32[8,16,128]{2,1,0:T(8,128)S(1)}, s32[8,16,128]{2,1,0:T(8,128)}, u32[]{:S(2)}) copy-start(s32[8,16,128]{2,1,0:T(8,128)} %param.11) | copy-start | bytes 196612
  5.0 0.8 copy-start.3
  5.9 0.8 copy-start.5
  16.0 2.0 copy-start.1
  31.6 13.2 %all-to-all-start.1 = ((f32[8,8,512]{2,1,0:T(8,128)}), f32[8,8,512]{2,1,0:T(8,128)S(1)}, u32[]{:S(2)}, u32[]{:S(2)}) async-start(f32[8,8,512]{2,1,0:T(8,128)} %density_parts.3), calls=%async_computation.1 | async-start | bytes 262144 | tf_op jit(solution)/shard_map/all_to_all | solution.py:354
  61.0 2.0 copy-start.2
  91.1 13.5 %all-to-all-start.6 = ((f32[4,256,128]{2,1,0:T(8,128)}), f32[4,256,128]{2,1,0:T(8,128)S(1)}, u32[]{:S(2)}, u32[]{:S(2)}) async-start(f32[4,256,128]{2,1,0:T(8,128)} %bitcast.29), calls=%async_computation.6 | async-start | bytes 1048576 | tf_op jit(solution)/shard_map/all_to_all | solution.py:403
  115.9 11.8 %all-to-all-start.8 = ((f32[4,256,128]{2,1,0:T(8,128)}), f32[4,256,128]{2,1,0:T(8,128)S(1)}, u32[]{:S(2)}, u32[]{:S(2)}) async-start(f32[4,256,128]{2,1,0:T(8,128)} %bitcast.31), calls=%async_computation.8 | async-start | bytes 1048576 | tf_op jit(solution)/shard_map/all_to_all | solution.py:403
  127.7 15.9 %all-to-all-start.13 = ((f32[8,8,512]{2,1,0:T(8,128)}), f32[8,8,512]{2,1,0:T(8,128)S(1)}, u32[]{:S(2)}, u32[]{:S(2)}) async-start(f32[8,8,512]{2,1,0:T(8,128)} %density_parts.5), calls=%async_computation.13 | async-start | bytes 262144 | tf_op jit(solution)/shard_map/all_to_all | solution.py:354
  131.9 10.0 %collective-permute-start = (f32[256,128]{1,0:T(8,128)S(1)}, f32[256,128]{1,0:T(8,128)S(1)}, u32[]{:S(2)}, u32[]{:S(2)}) collective-permute-start(f32[256,128]{1,0:T(8,128)S(1)} %compose.3.refs_0_), channel_id=1, source_target_pairs={{0,16},{4,20},{8,24},{12,28},{16,0},{20,4},{24,8},{28,12},{1,17},{... | collective-permute-start | bytes 393224 | tf_op jit(solution)/shard_map/ppermute | solution.py:414
  143.6 10.8 %all-to-all-start.7 = ((f32[4,256,128]{2,1,0:T(8,128)}), f32[4,256,128]{2,1,0:T(8,128)S(1)}, u32[]{:S(2)}, u32[]{:S(2)}) async-start(f32[4,256,128]{2,1,0:T(8,128)} %enter.3.refs_0_), calls=%async_computation.7 | async-start | bytes 1048576 | tf_op jit(solution)/shard_map/all_to_all | solution.py:425
  160.9 14.4 %all-to-all-start.10 = ((f32[4,256,128]{2,1,0:T(8,128)}), f32[4,256,128]{2,1,0:T(8,128)S(1)}, u32[]{:S(2)}, u32[]{:S(2)}) async-start(f32[4,256,128]{2,1,0:T(8,128)} %bitcast.33), calls=%async_computation.10 | async-start | bytes 1048576 | tf_op jit(solution)/shard_map/all_to_all | solution.py:403
  165.6 7.5 %collective-permute-start.1 = (f32[256,128]{1,0:T(8,128)S(1)}, f32[256,128]{1,0:T(8,128)S(1)}, u32[]{:S(2)}, u32[]{:S(2)}) collective-permute-start(f32[256,128]{1,0:T(8,128)S(1)} %get-tuple-element.37.refs_0_), channel_id=1, source_target_pairs={{0,16},{4,20},{8,24},{12,28},{16,0},{20,4},{24,8},{28,12},{1,17},{... | collective-permute-start | bytes 393224 | tf_op jit(solution)/shard_map/ppermute | solution.py:414
  175.3 15.6 %all-to-all-start.9 = ((f32[4,256,128]{2,1,0:T(8,128)}), f32[4,256,128]{2,1,0:T(8,128)S(1)}, u32[]{:S(2)}, u32[]{:S(2)}) async-start(f32[4,256,128]{2,1,0:T(8,128)} %enter.4.refs_1_), calls=%async_computation.9 | async-start | bytes 1048576 | tf_op jit(solution)/shard_map/all_to_all | solution.py:425
  182.5 7.2 %collective-permute-start.2 = (f32[256,128]{1,0:T(8,128)S(1)}, f32[256,128]{1,0:T(8,128)S(1)}, u32[]{:S(2)}, u32[]{:S(2)}) collective-permute-start(f32[256,128]{1,0:T(8,128)S(1)} %get-tuple-element.40.refs_0_), channel_id=1, source_target_pairs={{0,16},{4,20},{8,24},{12,28},{16,0},{20,4},{24,8},{28,12},{1,17},{... | collective-permute-start | bytes 393224 | tf_op jit(solution)/shard_map/ppermute | solution.py:414
  202.0 2.2 %copy-start = (f32[64,128,128]{2,1,0:T(8,128)S(1)}, f32[64,128,128]{2,1,0:T(8,128)}, u32[]{:S(2)}) copy-start(f32[64,128,128]{2,1,0:T(8,128)} %get-tuple-element.35.swept) | copy-start | bytes 12582916

commit v4 on v2

v4 whole, which is shorter than its diff:
```python
import functools
import math

import jax
import jax.numpy as jnp
import numpy as np
from jax import lax
from jax.experimental import pallas as pl
from jax.experimental.pallas import tpu as pltpu
from jax.sharding import PartitionSpec as P

FREQ_GROUPS = 8
DIRS = 32
ITERS = 3
NEWTON = 4
PSEUDO_RATE = 0.03
GROUP = 4
COSINES = (np.float32(0.99995), np.float32(0.9999))

SELF, UPY, UPZ, RATIO, WALL, FULL, FULL_N, FULL_T, FULL_GROUP, WARM = range(10)
FORWARD, SHIFT_Y, SHIFT_Z, EDGE_Y, KIND = range(5)
THERM, QUART, HEAT, DECAY, STAY, AROUND = range(6)
KINDS = 2 * FREQ_GROUPS
SLAB, MODE = range(2)

SMEM = pl.BlockSpec(memory_space=pltpu.SMEM)
VMEM = pl.BlockSpec(memory_space=pltpu.VMEM)
PARAMS = pltpu.CompilerParams(vmem_limit_bytes=48 * 1024 * 1024)
ACROSS = math.cos(math.pi / 8) + math.sin(math.pi / 8)


def diagonal_of(speed, rate, cosine):
    sine = jnp.sqrt(1.0 - cosine * cosine)
    return speed * (cosine + sine * np.float32(ACROSS)) + rate + PSEUDO_RATE


def slot_tables(labels, speed, rate, storage, threshold, generation, slab, slabs, depth, width_z):
    band = labels // DIRS
    direction = labels % DIRS
    of_band = (band[None, :] == jnp.arange(FREQ_GROUPS, dtype=jnp.int32)[:, None]).astype(jnp.float32)
    speed, rate, storage, threshold, generation = (
        jnp.sum(of_band * value[:, None], axis=0) for value in (speed, rate, storage, threshold, generation)
    )
    polar = direction % 4
    outer = (polar == 0) | (polar == 3)
    forward = polar < 2
    cosine = jnp.where(outer, COSINES[0], COSINES[1])
    sine = jnp.sqrt(1.0 - cosine * cosine)
    azimuth = ((direction // 4).astype(jnp.float32) + 0.5) * (2.0 * math.pi / (DIRS // 4))
    vy = speed * sine * jnp.cos(azimuth)
    vz = speed * sine * jnp.sin(azimuth)
    diagonal = diagonal_of(speed, rate, cosine)
    ratio = speed * cosine / diagonal
    full = lax.integer_pow(ratio, depth)
    at_wall = jnp.where(forward, slab == 0, slab == slabs - 1)
    wall = storage * (1.0 + 1.0 / (4.0 * threshold**3))
    floats = jnp.stack(
        [
            PSEUDO_RATE / diagonal,
            jnp.abs(vy) / diagonal,
            jnp.abs(vz) / diagonal,
            ratio,
            jnp.where(at_wall, wall, 0.0),
            full,
            depth * full,
            (depth * (depth + 1) // 2) * full,
            lax.integer_pow(full, GROUP),
            generation / diagonal,
        ]
    )
    ints = jnp.stack(
        [
            forward.astype(jnp.int32),
            jnp.where(vy > 0, 1, 7).astype(jnp.int32),
            jnp.where(vz > 0, 1, width_z - 1).astype(jnp.int32),
            jnp.where(vy > 0, 0, 7).astype(jnp.int32),
            2 * band + jnp.where(outer, 0, 1),
        ]
    )
    x = jnp.arange(slabs * depth, dtype=jnp.int32)[:, None]
    past = jnp.where(forward[None, :], x - (slab * depth + depth - 1), slab * depth - x)
    n = past.astype(jnp.float32)
    weight = jnp.where(past > 0, jnp.power(ratio[None, :], jnp.maximum(n, 0.0)), 0.0)
    return floats, ints, jnp.concatenate([weight, n * weight, (0.5 * n * (n + 1.0)) * weight], axis=1)


def kind_table(speed, rate, storage, threshold, generation):
    rows = []
    for cosine in COSINES:
        diagonal = diagonal_of(speed, rate, cosine)
        therm = rate * storage / diagonal
        quart = therm / (4.0 * threshold**3)
        across = jnp.sqrt(1.0 - cosine * cosine) * np.float32(2.0 * ACROSS)
        rows.append(
            jnp.stack(
                [
                    therm,
                    quart,
                    generation / diagonal,
                    speed * cosine / diagonal,
                    (DIRS // 4) * PSEUDO_RATE / diagonal,
                    across * speed / diagonal,
                ]
            )
        )
    return jnp.stack(rows, axis=2).reshape(6, KINDS)


def heat_matrices(kinds, slab, slabs, depth):
    cells = slabs * depth
    there = jnp.arange(cells, dtype=jnp.int32)
    decay = kinds[DECAY][:, None, None]
    per_cell = (DIRS // 4) / DIRS

    def side_by_side(weight, factor):
        sums = [jnp.sum((factor * kinds[row])[:, None, None] * weight, axis=0) for row in (THERM, QUART)]
        return jnp.concatenate(sums, axis=1)

    def between(here):
        far = jnp.abs(here[:, None] - there[None, :])
        n = far.astype(jnp.float32)
        return n, jnp.power(decay, n[None]) * jnp.where(far == 0, 2.0, 1.0)[None]

    _, everywhere = between(there)
    n, home = between(slab * depth + jnp.arange(depth, dtype=jnp.int32))
    twice = home * (n + 1.0)[None]
    one = jnp.full((KINDS,), per_cell, jnp.float32)
    once = side_by_side(home, one)
    stay = side_by_side(twice, kinds[STAY] / DIRS)
    around = side_by_side(twice, kinds[AROUND] / DIRS)
    before = jnp.stack([slab * depth - 1 - there, there - (slab + 1) * depth])
    n = before.astype(jnp.float32)[:, None, :]
    power = jnp.power(kinds[DECAY][None, :, None], jnp.maximum(n, 0.0))
    inflow = jnp.where(before[:, None, :] >= 0, power, 0.0)
    inflow = jnp.concatenate(
        [inflow * kinds[THERM][None, :, None], inflow * kinds[QUART][None, :, None]], axis=2
    )
    longer = inflow * (jnp.concatenate([n, n], axis=2) + 1.0)
    inflow, longer = (value.reshape(2 * KINDS, 2 * cells) for value in (inflow, longer))
    return (
        side_by_side(everywhere, one),
        jnp.concatenate([inflow, longer, stay, around], axis=0),
        jnp.concatenate([inflow, once], axis=0),
    )


def newton(density, kelvin, linear, quart):
    for _ in range(NEWTON):
        cube = kelvin * kelvin * kelvin
        residual = linear * kelvin + quart * (kelvin * cube) - density
        kelvin = kelvin - residual / (linear + 4.0 * quart * cube)
    return kelvin


def exact_dot(left, right):
    return jnp.dot(left, right, precision=lax.Precision.HIGHEST, preferred_element_type=jnp.float32)


def fourth(value):
    square = value * value
    return square * square


def add_up(values):
    while len(values) > 1:
        values = [a + b for a, b in zip(values[::2], values[1::2])]
    return values[0]


def stencil(low, high, c_self, c_y, c_z, shift_y, shift_z, at_edge):
    turned_low, turned_high = pltpu.roll(low, shift_y, 0), pltpu.roll(high, shift_y, 0)
    up_low = jnp.where(at_edge, turned_high, turned_low)
    up_high = jnp.where(at_edge, turned_low, turned_high)
    return (
        c_self * low + c_y * up_low + c_z * pltpu.roll(low, shift_z, 1),
        c_self * high + c_y * up_high + c_z * pltpu.roll(high, shift_z, 1),
    )


def course(ints, s, depth):
    forward = ints[FORWARD, s] == 1
    return jnp.where(forward, 0, depth - 1), jnp.where(forward, 1, -1)


def slot_stencil(floats, ints, s, row):
    at_edge = row == ints[EDGE_Y, s]
    c_self, c_y, c_z = floats[SELF, s], floats[UPY, s], floats[UPZ, s]
    shift_y, shift_z = ints[SHIFT_Y, s], ints[SHIFT_Z, s]
    return lambda low, high: stencil(low, high, c_self, c_y, c_z, shift_y, shift_z, at_edge)


def rows_of(s):
    at = pl.multiple_of(s * 16, 16)
    return pl.ds(at, 8), pl.ds(at + 8, 8)


def sweeps_kernel(sizes, meta, floats, ints, kinds, energy, flag, given, matrix, swept, quarter, *rest):
    block, blocks, depth, width_y, slots, modes, group = sizes
    faces, rest = rest[:group], rest[group:]
    keep, send, *planes, density, flat, sources, heat = rest
    out_one, turn_one, turn_two, out_two, turn_late, out_three = planes
    rows, own = width_y // modes, slots // group
    step = pl.program_id(0)
    slab, mode = meta[SLAB], meta[MODE]

    @pl.when(step == 0)
    def _():
        for yy in range(rows):
            quarter[:, yy * 128 : (yy + 1) * 128] = given[pl.ds(mode * rows + yy, depth, stride=width_y), :]
        density[...] = jnp.zeros_like(density)

        def one_layer(x, carry):
            at = pl.ds(pl.multiple_of(x * 16, 16), 16)
            t = given[at, :]
            power = fourth(t)
            hot = flag[at, :].astype(jnp.float32)
            heat[x] = hot
            for kind in range(KINDS):
                sources[kind, x] = kinds[THERM, kind] * t + kinds[QUART, kind] * power + kinds[HEAT, kind] * hot
            return carry

        lax.fori_loop(0, depth, one_layer, 0)

    row = lax.broadcasted_iota(jnp.int32, (8, 128), 0)

    def one_slot(i, carry):
        s = step * block + i
        start, stride = course(ints, s, depth)
        side = 1 - ints[FORWARD, s]
        ratio, warm, kind = floats[RATIO, s], floats[WARM, s], ints[KIND, s]
        apply = slot_stencil(floats, ints, s, row)
        xs = [start + stride * j for j in range(depth)]
        layers = [(energy[i, x, :8, :], energy[i, x, 8:, :]) for x in xs]
        last = []
        for turn in range(ITERS):
            total_low = total_high = jnp.full((8, 128), floats[WALL, s], jnp.float32)
            for j, x in enumerate(xs):
                low, high = apply(*layers[j])
                if turn == 0:
                    low, high = low + sources[kind, x, :8, :], high + sources[kind, x, 8:, :]
                else:
                    low, high = low + warm * heat[x, :8, :], high + warm * heat[x, 8:, :]
                total_low = ratio * total_low + low
                total_high = ratio * total_high + high
                layers[j] = (total_low, total_high)
                density[turn, side, j, :8, :] += total_low
                density[turn, side, j, 8:, :] += total_high
                if turn == ITERS - 1:
                    swept[i, x, :8, :] = total_low
                    swept[i, x, 8:, :] = total_high
            last.append((total_low, total_high))
        turned = apply(*last[0])
        at_low, at_high = rows_of(s)
        values = (last[0], turned, apply(*turned), last[1], apply(*last[1]), last[2])
        for plane, (low, high) in zip(planes, values):
            plane[at_low, :] = low
            plane[at_high, :] = high
        return carry

    lax.fori_loop(0, block, one_slot, 0, unroll=2)

    @pl.when(step == blocks - 1)
    def _():
        for by in range(group):
            at = pl.ds(pl.multiple_of(((slab % group) ^ by) * own * 16, 16), own * 16)
            for index, plane in enumerate((turn_two, turn_late, out_three)):
                faces[by][index] = plane[at, :]
        for turn in range(ITERS):
            for x in range(depth):
                flat[turn, x * 16 : x * 16 + 16, :] = density[turn, 0, x] + density[turn, 1, depth - 1 - x]
        home = pl.ds(pl.multiple_of(slab * depth, 8), depth)
        for by in range(modes):
            ys = [(mode ^ by) * rows + yy for yy in range(rows)]
            pick = lambda plane, count: jnp.concatenate([plane[pl.ds(y, count, stride=width_y), :] for y in ys], axis=1)
            one, two = pick(turn_one, slots), pick(turn_late, slots)
            rights = (
                pick(out_one, slots),
                jnp.concatenate([pick(out_two, slots), one], axis=0),
                jnp.concatenate([pick(out_three, slots), two, pick(turn_two, slots)], axis=0),
            )
            target = (send if by % 2 else keep).at[by // 2]
            for turn, right in enumerate(rights):
                target[turn] = exact_dot(matrix[:, : (turn + 1) * slots], right)
                target[turn, home, :] += pick(flat.at[turn], depth)


def split_kernel(mine, other, keep, send):
    for index in range(mine.shape[0]):
        target = send if index % 2 else keep
        target[index // 2] = mine[index] + other[index]


def parts_kernel(depth, mine, other, parts):
    for turn in range(ITERS):
        total = mine[0, turn] + other[0, turn]
        for slab in range(parts.shape[0]):
            parts[slab, turn] = total[slab * depth : (slab + 1) * depth]


def totals_kernel(parts, before, copies, late):
    slabs = parts.shape[0]
    one, two, three = (
        add_up([parts[slab, turn] for slab in range(slabs)]) * (1.0 / DIRS) for turn in range(ITERS)
    )
    late[...] = three
    for slab in range(slabs):
        copies[slab, 0] = one
        copies[slab, 1] = two
        copies[slab, 2] = before[...]


def kelvins_kernel(depth, sums, gathered, late, matrix, packed):
    slabs = gathered.shape[0]
    cells = slabs * depth
    one, two, before = (
        jnp.concatenate([gathered[slab, index] for slab in range(slabs)], axis=0) for index in range(3)
    )
    kelvin = newton(one, before, sums[0], sums[1])
    packed[:cells, :] = kelvin
    two = two + exact_dot(matrix[...], jnp.concatenate([kelvin, fourth(kelvin)], axis=0))
    packed[cells : 2 * cells, :] = newton(two, kelvin, sums[0], sums[1])
    packed[2 * cells :, :] = late[...]


def compose_kernel(own, group, meta, floats, ints, *refs):
    received, (composite, effective, ordered) = refs[:group], refs[group:]
    place = meta[SLAB] % group
    for by in range(group):
        ordered[place ^ by] = received[by][...]

    def one_slot(i, carry):
        s = place * own + i
        start, stride = course(ints, s, group)
        full, full_n, full_t = floats[FULL, s], floats[FULL_N, s], floats[FULL_T, s]
        at = pl.ds(pl.multiple_of(i * 16, 16), 16)
        one = two = three = jnp.zeros((16, 128), jnp.float32)
        for j in range(group):
            k = start + stride * j
            three = full * three + full_n * two + full_t * one + ordered[k, 2, at, :]
            two = full * two + full_n * one + ordered[k, 1, at, :]
            one = full * one + ordered[k, 0, at, :]
        for index, value in enumerate((one, two, three)):
            composite[index, at, :] = value
        return carry

    lax.fori_loop(0, own, one_slot, 0, unroll=4)
    effective[...] = ordered[...]


def enter_kernel(own, group, groups, depth, meta, floats, ints, effective, *refs):
    composites, rest = refs[:groups], refs[groups:]
    outs, (ordered, entered) = rest[:group], rest[group:]
    slab = meta[SLAB]
    place, mine = slab % group, slab // group
    for by in range(groups):
        ordered[mine ^ by] = composites[by][...]
    span = depth * group

    def one_slot(i, carry):
        s = place * own + i
        start, stride = course(ints, s, group)
        begin, leap = course(ints, s, groups)
        ahead = jnp.where(ints[FORWARD, s] == 1, mine, groups - 1 - mine)
        at = pl.ds(pl.multiple_of(i * 16, 16), 16)

        def push(values, full, full_n, full_t, added):
            one, two, three = values
            return (
                full * one + added[0],
                full * two + full_n * one + added[1],
                full * three + full_n * two + full_t * one + added[2],
            )

        values = (jnp.zeros((16, 128), jnp.float32),) * 3
        whole = floats[FULL_GROUP, s]
        for g in range(groups - 1):
            index = begin + leap * g
            added = [ordered[index, plane, at, :] for plane in range(3)]
            later = push(values, whole, span * whole, (span * (span + 1) // 2) * whole, added)
            values = tuple(jnp.where(g < ahead, a, b) for a, b in zip(later, values))
        full, full_n, full_t = floats[FULL, s], floats[FULL_N, s], floats[FULL_T, s]
        for j in range(group):
            k = start + stride * j
            for plane in range(3):
                entered[k, plane, at, :] = values[plane]
            if j < group - 1:
                values = push(values, full, full_n, full_t, [effective[k, plane, at, :] for plane in range(3)])
        return carry

    lax.fori_loop(0, own, one_slot, 0, unroll=2)
    for by in range(group):
        outs[by][...] = entered[place ^ by]


def final_kernel(sizes, order, meta, floats, ints, kinds, sums, swept, *refs):
    block, depth, width_y, width_z, slots, slabs, modes, group = sizes
    received, refs = refs[:group], refs[group:]
    packs, refs = refs[:modes], refs[modes:]
    first_matrix, second_matrix, energy, kelvin, *refs = refs
    warm_one, warm_two, late, enter_one, enter_long, enter_two, second, added, own_one, own_two, *ordered = refs
    step = pl.program_id(0)
    slab, mode = meta[SLAB], meta[MODE]
    own, lanes, cells = slots // group, width_y // modes * width_z, slabs * depth

    @pl.when(step == 0)
    def _():
        for by in range(group):
            at = pl.ds(pl.multiple_of(((slab % group) ^ by) * own * 16, 16), own * 16)
            for index in range(ITERS):
                ordered[index][at, :] = received[by][index]
        for pack, by in zip(packs, order):
            at = pl.ds(pl.multiple_of((mode ^ by) * lanes, 128), lanes)
            warm_one[:, at] = pack[:cells, :]
            warm_two[:, at] = pack[cells : 2 * cells, :]
            late[:, at] = pack[2 * cells :, :]
        home = pl.ds(pl.multiple_of(slab * depth, 8), depth)
        chunk = 4
        plain, around = [], []
        for c in range(width_y // chunk):
            at = slice(c * chunk * 128, (c + 1) * chunk * 128)
            one, two = warm_one[:, at], warm_two[:, at]
            one = exact_dot(first_matrix[...], jnp.concatenate([one, fourth(one)], axis=0))
            two = exact_dot(second_matrix[...], jnp.concatenate([two, fourth(two)], axis=0))
            for yy in range(chunk):
                y, lane = c * chunk + yy, slice(yy * 128, (yy + 1) * 128)
                scattered = pl.ds(y, 2 * KINDS, stride=width_y)
                enter_one[scattered, :] = one[: 2 * KINDS, lane]
                enter_long[scattered, :] = one[2 * KINDS : 4 * KINDS, lane]
                enter_two[scattered, :] = two[: 2 * KINDS, lane]
                plain.append(one[4 * KINDS : 4 * KINDS + depth, lane] + two[2 * KINDS :, lane])
                around.append(one[4 * KINDS + depth :, lane])
        for y in range(width_y):
            lane = slice(y * 128, (y + 1) * 128)
            near = around[y - 1] + around[(y + 1) % width_y]
            near = near + (pltpu.roll(around[y], 1, 1) + pltpu.roll(around[y], width_z - 1, 1))
            density = late[:, lane] + plain[y] + near
            scattered = pl.ds(y, depth, stride=width_y)
            now = warm_two[home, lane]
            kelvin[scattered, :] = newton(density, now, sums[0], sums[1])
            own_one[scattered, :] = warm_one[home, lane]
            own_two[scattered, :] = now

        def one_kind(kind, carry):
            therm, quart, decay = kinds[THERM, kind], kinds[QUART, kind], kinds[DECAY, kind]
            at = pl.ds(pl.multiple_of(kind * 16, 16), 16)
            back_at = pl.ds(pl.multiple_of((kind + KINDS) * 16, 16), 16)
            layers = []
            for x in range(depth):
                here = slice(x * 16, x * 16 + 16)
                t, u = own_one[here, :], own_two[here, :]
                layers.append(therm * t + quart * fourth(t))
                added[kind, x] = therm * u + quart * fourth(u)
            up, down = enter_one[at, :], enter_one[back_at, :]
            for j in range(depth):
                up = decay * up + layers[j]
                down = decay * down + layers[depth - 1 - j]
                second[kind, j] = up
                second[kind + KINDS, j] = down
            return carry

        lax.fori_loop(0, KINDS, one_kind, 0)

    row = lax.broadcasted_iota(jnp.int32, (8, 128), 0)

    def one_slot(i, carry):
        s = step * block + i
        start, stride = course(ints, s, depth)
        ratio, kind = floats[RATIO, s], ints[KIND, s]
        sided = kind + KINDS * (1 - ints[FORWARD, s])
        apply = slot_stencil(floats, ints, s, row)
        at, kind_at = rows_of(s), rows_of(sided)
        one, two, three = ([ref[half, :] for half in at] for ref in ordered)
        longer = apply(*(enter_long[half, :] for half in kind_at))
        three = [a + b + enter_two[half, :] for a, b, half in zip(three, longer, kind_at)]
        for j in range(depth):
            x = start + stride * j
            fresh = apply(second[sided, j, :8, :], second[sided, j, 8:, :])
            for half, here in enumerate((slice(0, 8), slice(8, 16))):
                one[half] = ratio * one[half]
                two[half] = ratio * two[half] + one[half]
                three[half] = ratio * three[half] + (fresh[half] + added[kind, x, here, :] + two[half])
                energy[i, x, here, :] = swept[i, x, here, :] + three[half]
        return carry

    lax.fori_loop(0, block, one_slot, 0, unroll=2)


def local(incoming_occupation, crystal_kelvin_given, generating_region_flag, labels, speed, rate, storage, threshold, generation):
    slots, depth, width_y, width_z = incoming_occupation.shape
    slabs, modes = lax.axis_size("slab"), lax.axis_size("mode")
    group, groups = GROUP, slabs // GROUP
    own = slots // group
    lanes = width_y // modes * width_z
    block = 8
    blocks = slots // block
    cells, all_x = depth * width_y, slabs * depth
    face_rows = own * width_y
    slab = lax.axis_index("slab").astype(jnp.int32)
    meta = jnp.stack([slab, lax.axis_index("mode").astype(jnp.int32)])
    floats, ints, matrix = slot_tables(labels, speed, rate, storage, threshold, generation, slab, slabs, depth, width_z)
    kinds = kind_table(speed, rate, storage, threshold, generation)
    everywhere, first_matrix, second_matrix = heat_matrices(kinds, slab, slabs, depth)
    sums = jnp.stack([jnp.sum(storage), jnp.sum(storage / (4.0 * threshold**3))])

    def shape(*dims):
        return jax.ShapeDtypeStruct(dims, jnp.float32)

    def whole(*dims):
        return pl.BlockSpec(dims, lambda i: (0,) * len(dims))

    def scratch(*dims):
        return pltpu.VMEM(dims, jnp.float32)

    def swap(array, axis, by):
        return lax.ppermute(array, axis, [(i, i ^ by) for i in range(lax.axis_size(axis))])

    def call(kernel, name, in_specs, out_shapes, *args, scratches=()):
        return pl.pallas_call(
            kernel,
            in_specs=in_specs,
            out_specs=[VMEM] * len(out_shapes),
            out_shape=out_shapes,
            scratch_shapes=list(scratches),
            compiler_params=PARAMS,
            name=name,
        )(*args)

    slot_block = pl.BlockSpec((block, depth, width_y, width_z), lambda i: (i, 0, 0, 0))
    slot_shape = shape(slots, depth, width_y, width_z)
    face = (3, face_rows, width_z)
    half = (modes // 2, ITERS, all_x, lanes)
    swept, quarter, *rest = pl.pallas_call(
        functools.partial(sweeps_kernel, (block, blocks, depth, width_y, slots, modes, group)),
        grid=(blocks,),
        in_specs=[SMEM] * 4 + [slot_block, whole(cells, width_z), whole(cells, width_z), whole(all_x, ITERS * slots)],
        out_specs=[slot_block, whole(depth, lanes)] + [whole(*face)] * group + [whole(*half)] * 2,
        out_shape=[slot_shape, shape(depth, lanes)] + [shape(*face)] * group + [shape(*half)] * 2,
        scratch_shapes=[scratch(slots * width_y, width_z)] * 6
        + [
            scratch(ITERS, 2, depth, width_y, width_z),
            scratch(ITERS, cells, width_z),
            scratch(KINDS, depth, width_y, width_z),
            scratch(depth, width_y, width_z),
        ],
        compiler_params=PARAMS,
        name="sweeps",
    )(
        meta,
        floats,
        ints,
        kinds,
        incoming_occupation,
        generating_region_flag.reshape(cells, width_z),
        crystal_kelvin_given.reshape(cells, width_z),
        matrix,
    )
    faces, (keep, send) = rest[:group], rest[group:]

    by = 1
    other = swap(send, "mode", by)
    received = [faces[0]] + [swap(faces[index], "slab", index) for index in range(1, group)]
    while 2 * by < modes:
        by *= 2
        now = (modes // (2 * by), ITERS, all_x, lanes)
        keep, send = call(split_kernel, "density_split", [VMEM] * 2, [shape(*now)] * 2, keep, other)
        other = swap(send, "mode", by)
    piece = (slabs, ITERS, depth, lanes)
    (parts,) = call(functools.partial(parts_kernel, depth), "density_parts", [VMEM] * 2, [shape(*piece)], keep, other)
    parts = lax.all_to_all(parts, "slab", 0, 0)
    copies, late = call(totals_kernel, "density_totals", [VMEM] * 2, [shape(*piece), shape(depth, lanes)], parts, quarter)
    gathered = lax.all_to_all(copies, "slab", 0, 0)
    pack_shape = shape(2 * all_x + depth, lanes)
    (packed,) = call(
        functools.partial(kelvins_kernel, depth), "kelvins", [SMEM] + [VMEM] * 3, [pack_shape], sums, gathered, late, everywhere
    )
    packs, order = [packed], [0]
    while by:
        packs = packs + [swap(pack, "mode", by) for pack in packs]
        order = order + [index ^ by for index in order]
        by //= 2

    composite, effective = call(
        functools.partial(compose_kernel, own, group),
        "compose",
        [SMEM] * 3 + [VMEM] * group,
        [shape(*face), shape(group, *face)],
        meta,
        floats,
        ints,
        *received,
        scratches=[scratch(group, *face)],
    )
    composites = [composite] + [swap(composite, "slab", index * group) for index in range(1, groups)]
    entering = call(
        functools.partial(enter_kernel, own, group, groups, depth),
        "enter",
        [SMEM] * 3 + [VMEM] * (1 + groups),
        [shape(*face)] * group,
        meta,
        floats,
        ints,
        effective,
        *composites,
        scratches=[scratch(groups, *face), scratch(group, *face)],
    )
    entering = [entering[0]] + [swap(entering[index], "slab", index) for index in range(1, group)]

    energy, kelvin = pl.pallas_call(
        functools.partial(final_kernel, (block, depth, width_y, width_z, slots, slabs, modes, group), order),
        grid=(blocks,),
        in_specs=[SMEM] * 5
        + [slot_block]
        + [whole(*face)] * group
        + [whole(*pack_shape.shape)] * modes
        + [whole(*first_matrix.shape), whole(*second_matrix.shape)],
        out_specs=[slot_block, whole(cells, width_z)],
        out_shape=[slot_shape, shape(cells, width_z)],
        scratch_shapes=[scratch(all_x, width_y * width_z)] * 2
        + [scratch(depth, width_y * width_z)]
        + [scratch(2 * KINDS * width_y, width_z)] * 3
        + [scratch(2 * KINDS, depth, width_y, width_z), scratch(KINDS, depth, width_y, width_z)]
        + [scratch(cells, width_z)] * 2
        + [scratch(slots * width_y, width_z)] * 3,
        compiler_params=PARAMS,
        name="final_energy",
    )(meta, floats, ints, kinds, sums, swept, *entering, *packs, first_matrix, second_matrix)
    return energy, kelvin.reshape(depth, width_y, width_z)


def solution(mesh):
    return jax.shard_map(
        local,
        mesh=mesh,
        in_specs=(
            P("mode", "slab", None, None),
            P("slab", None, None),
            P("slab", None, None),
            P("mode"),
            P(),
            P(),
            P(),
            P(),
            P(),
        ),
        out_specs=(P("mode", "slab", None, None), P("slab", None, None)),
        check_vma=False,
    )
```

time: 167 us -> 123 us (0.74)
  starting transfers between devices: 70 us -> 23.9 us
  Pallas kernels: 49.6 us -> 32.9 us
  other arithmetic: 5.41 us -> 13.2 us
  local copies, waits for them, and re-layouts: 1.93 us -> 7.54 us
  waiting for transfers between devices: 38 us -> 43.2 us
    ppermute x60 -> x12, starting transfers between devices: 70 us -> 14.4 us  [swap(): lax.ppermute(array, axis, [(i, i ^ by) for i in range(lax.axis_size(axis))])]
    all_to_all x0 -> x2, waiting for transfers between devices: none -> 21.3 us  [the longest x1 10.9 us: local(): parts = lax.all_to_all(parts, 'slab', 0, 0)]
    pallas_call x16 -> x8, Pallas kernels: 49.6 us -> 32.9 us  [the longest x1 15.1 us: local(): pl.pallas_call(functools.partial(sweeps_kernel, (block, blocks, depth, wi...]
    ppermute x60 -> x12, waiting for transfers between devices: 38 us -> 21.9 us  [swap(): lax.ppermute(array, axis, [(i, i ^ by) for i in range(lax.axis_size(axis))])]
    all_to_all x0 -> x2, starting transfers between devices: none -> 9.54 us  [the longest x1 6.09 us: local(): parts = lax.all_to_all(parts, 'slab', 0, 0)]
    unnamed x8 -> x30, local copies, waits for them, and re-layouts: 1.69 us -> 4.2 us
    reduce_sum x0 -> x2, other arithmetic: none -> 2.14 us  [side_by_side(): jnp.sum((factor * kinds[row])[:, None, None] * weight, axis=0)]
  transfers between devices with their start and end apart: 60 -> 14, of which waited for: 21 -> 8; matrix products, arithmetic and copies ran while one was open for 1% -> 9% of each run, Pallas kernels for 19% -> 6%
where the time goes in v4:
time: 123 us; the launch traced here: 122 us
  waiting for transfers between devices  43.2 us (35%)
  Pallas kernels  32.9 us (27%)
  starting transfers between devices  23.9 us (19%)
  other arithmetic  13.2 us (11%)
  local copies, waits for them, and re-layouts  7.54 us (6%)
    ppermute x12, waiting for transfers between devices, swap(): lax.ppermute(array, axis, [(i, i ^ by) for i in range(lax.axis_size(axis))])  21.9 us
    pallas_call x1, Pallas kernels, local(): pl.pallas_call(functools.partial(sweeps_kernel, (block, blocks, depth, wi...  15.1 us
    ppermute x12, starting transfers between devices, swap(): lax.ppermute(array, axis, [(i, i ^ by) for i in range(lax.axis_size(axis))])  14.4 us
    all_to_all x1, waiting for transfers between devices, local(): parts = lax.all_to_all(parts, 'slab', 0, 0)  10.9 us
    pallas_call x1, Pallas kernels, local(): pl.pallas_call(functools.partial(final_kernel, (block, depth, width_y, wi...  10.5 us
    all_to_all x1, waiting for transfers between devices, local(): gathered = lax.all_to_all(copies, 'slab', 0, 0)  10.5 us
    pallas_call x6, Pallas kernels, call(): pl.pallas_call(kernel, in_specs=in_specs, out_specs=[VMEM] * len(out_shap...  7.23 us
    all_to_all x1, starting transfers between devices, local(): parts = lax.all_to_all(parts, 'slab', 0, 0)  6.09 us
  transfers between devices with their start and end apart: 14, of which 8 were waited for; matrix products, arithmetic and copies ran while one was open for 9% of the time, Pallas kernels for 6%

profile of v4, /device:TPU:0, one launch (start us, length us, event | category | flops | bytes accessed | tf_op | source)
XLA Modules:
  0.0 121.7 jit_solution(12932129767655051986)
XLA Ops:
  0.7 0.7 add_bitcast_fusion
  1.4 0.7 fusion.38
  2.0 0.8 select_reduce_fusion
  3.0 1.4 %fusion.45 = (f32[]{:T(128)}, f32[]{:T(128)}, f32[1,8]{1,0:T(1,128)S(1)}, f32[8]{0:T(128)S(1)}, f32[1,8]{1,0:T(1,128)S(1)}, /*index=5*/f32[1,8]{1,0:T(1,128)S(1)...) fusion(f32[8]{0:T(128)} %param.15, f32[8]{0:T(128)} %param.16, ...), kind=kLoop, calls=%fused_computation.146 | loop fusion | flops 134 | bytes 488 | tf_op jit(solution)/shard_map/reduce_sum | solution.py:503
  4.4 0.7 fusion.40
  5.2 0.1 copy.37
  5.3 0.1 copy.44.kinds
  5.4 0.1 fusion.6
  5.6 0.1 pad_maximum_fusion.matrix
  5.7 0.8 copy-done
  6.6 0.8 copy-done.1
  7.4 15.1 %sweeps.1 = (f32[64,8,16,128]{3,2,1,0:T(8,128)}, f32[8,512]{1,0:T(8,128)S(1)}, f32[3,256,128]{2,1,0:T(8,128)S(1)}, f32[3,256,128]{2,1,0:T(8,128)}, f32[3,256,128...) custom-call(s32[2]{0:T(128)S(1)} %pad_add_fusion.1.meta, ...), custom_call_target="tpu_custom_call" | custom-call | tf_op jit(solution)/shard_map/sweeps/pallas_call | solution.py:532
  22.5 0.5 collective-permute-start.7
  23.0 1.9 %collective-permute-done.7.other = f32[2,3,64,512]{3,2,1,0:T(8,128)S(1)} collective-permute-done((f32[2,3,64,512]{3,2,1,0:T(8,128)S(1)}, f32[2,3,64,512]{3,2,1,0:T(8,128)S(1)}, u32[]{:S(2)}, u32[]{:S(2)}) %collective-permute-start.7) | collective-permute-done | bytes 786464 | tf_op jit(solution)/shard_map/ppermute | solution.py:515
  25.0 2.9 %collective-permute-start.8 = (f32[1,3,64,512]{3,2,1,0:T(8,128)S(1)}, f32[1,3,64,512]{3,2,1,0:T(8,128)S(1)}, u32[]{:S(2)}, u32[]{:S(2)}) collective-permute-start(f32[1,3,64,512]{3,2,1,0:T(8,128)S(1)} %get-tuple-element.36), channel_id=1, source_target_pairs={{0,2},{1,3},{2,0},{3,1},{4,6},{5,7},{6,4},{7,5},{8,10},{9,11},{10,... | collective-permute-start | bytes 1179656 | tf_op jit(solution)/shard_map/ppermute | solution.py:515
  27.9 1.5 %collective-permute-start = (f32[3,256,128]{2,1,0:T(8,128)}, f32[3,256,128]{2,1,0:T(8,128)S(1)}, u32[]{:S(2)}, u32[]{:S(2)}) collective-permute-start(f32[3,256,128]{2,1,0:T(8,128)} %get-tuple-element.24), channel_id=1, source_target_pairs={{0,4},{4,0},{8,12},{12,8},{16,20},{20,16},{24,28},{28,24},{1,5},{5... | collective-permute-start | bytes 1179656 | tf_op jit(solution)/shard_map/ppermute | solution.py:515
  29.5 1.6 %collective-permute-start.1 = (f32[3,256,128]{2,1,0:T(8,128)}, f32[3,256,128]{2,1,0:T(8,128)S(1)}, u32[]{:S(2)}, u32[]{:S(2)}) collective-permute-start(f32[3,256,128]{2,1,0:T(8,128)} %get-tuple-element.25), channel_id=1, source_target_pairs={{0,8},{4,12},{8,0},{12,4},{16,24},{20,28},{24,16},{28,20},{1,9},{5... | collective-permute-start | bytes 1179656 | tf_op jit(solution)/shard_map/ppermute | solution.py:515
  31.0 0.4 collective-permute-start.2
  31.5 5.9 %collective-permute-done.8.other = f32[1,3,64,512]{3,2,1,0:T(8,128)S(1)} collective-permute-done((f32[1,3,64,512]{3,2,1,0:T(8,128)S(1)}, f32[1,3,64,512]{3,2,1,0:T(8,128)S(1)}, u32[]{:S(2)}, u32[]{:S(2)}) %collective-permute-start.8) | collective-permute-done | bytes 393248 | tf_op jit(solution)/shard_map/ppermute | solution.py:515
  37.4 0.8 density_parts.1
  38.2 6.1 %all-to-all-start = ((f32[8,3,8,512]{3,2,1,0:T(8,128)}), f32[8,3,8,512]{3,2,1,0:T(8,128)S(1)}, u32[]{:S(2)}, u32[]{:S(2)}) async-start(f32[8,3,8,512]{3,2,1,0:T(8,128)} %density_parts.1), calls=%async_computation | async-start | bytes 786432 | tf_op jit(solution)/shard_map/all_to_all | solution.py:569
  44.3 0.1 copy.43
  44.3 0.1 div.119
  44.5 0.1 squeeze.4
  44.7 0.1 squeeze.5
  44.8 0.1 div.117
  45.0 0.7 fusion.16
  45.6 0.6 fusion.47
  46.2 10.9 %all-to-all-done.parts = f32[8,3,8,512]{3,2,1,0:T(8,128)S(1)} async-done(((f32[8,3,8,512]{3,2,1,0:T(8,128)}), f32[8,3,8,512]{3,2,1,0:T(8,128)S(1)}, u32[]{:S(2)}, u32[]{:S(2)}) %all-to-all-start) | async-done | bytes 393248 | tf_op jit(solution)/shard_map/all_to_all | solution.py:569
  57.1 0.8 density_totals.1
  57.9 3.5 %all-to-all-start.1 = ((f32[8,3,8,512]{3,2,1,0:T(8,128)}), f32[8,3,8,512]{3,2,1,0:T(8,128)S(1)}, u32[]{:S(2)}, u32[]{:S(2)}) async-start(f32[8,3,8,512]{3,2,1,0:T(8,128)} %get-tuple-element.38), calls=%async_computation.1 | async-start | bytes 786432 | tf_op jit(solution)/shard_map/all_to_all | solution.py:571
  61.3 0.6 broadcast_maximum_fusion
  62.0 0.1 pow.61
  62.1 1.2 %multiply_reduce_fusion.1 = (f32[64,64]{1,0:T(8,128)S(1)}, f32[64,64]{1,0:T(8,128)S(1)}) fusion(f32[64,64]{1,0:T(8,128)S(1)} %fusion.11, f32[64,64]{1,0:T(8,128)S(1)} %fusion.10, f32[16]{0:T(128)S(1)} %pow.61, f32[16]{0:T(128)S(1)} %get-tuple-element.112, f32[16]{0:T(128)S(1)} %get-tuple-element.111), kind=kLoop, calls=%fused_computation.1 | loop fusion | flops 319488 | bytes 65728 | tf_op jit(solution)/shard_map/reduce_sum | solution.py:116
  63.3 0.7 broadcast_add_fusion
  64.1 0.6 copy-done.5
  64.7 1.8 %compose.1 = (f32[3,256,128]{2,1,0:T(8,128)}, f32[4,3,256,128]{3,2,1,0:T(8,128)S(1)}) custom-call(s32[2]{0:T(128)S(1)} %copy-done.5, f32[10,64]{1,0:T(8,128)S(1)} %stack.141.floats, s32[5,64]{1,0:T(8,128)S(1)} %stack.148.ints, f32[3,256,128]{2,1,0:T(8,128)S(1)} %get-tuple-element.23.refs_0_, f32[3,256,128]{2,1,0:T(8,128)S(1)} %collective-permute-done.refs_1_, ...), custom_call_target="tpu_custom_call" | custom-call | tf_op jit(solution)/shard_map/compose/pallas_call | solution.py:518
  66.5 2.8 %collective-permute-start.3 = (f32[3,256,128]{2,1,0:T(8,128)}, f32[3,256,128]{2,1,0:T(8,128)S(1)}, u32[]{:S(2)}, u32[]{:S(2)}) collective-permute-start(f32[3,256,128]{2,1,0:T(8,128)} %get-tuple-element.28.refs_0_), channel_id=1, source_target_pairs={{0,16},{4,20},{8,24},{12,28},{16,0},{20,4},{24,8},{28,12},{1,17},{... | collective-permute-start | bytes 1179656 | tf_op jit(solution)/shard_map/ppermute | solution.py:515
  69.4 1.3 %pad_maximum_fusion.3.sums = f32[2]{0:T(128)S(1)} fusion(f32[1]{0:T(128)} %bitcast.33, f32[1]{0:T(128)} %bitcast.32), kind=kLoop, calls=%fused_computation.91 | loop fusion | flops 2 | bytes 16 | tf_op jit(solution)/shard_map/stack | solution.py:503
  70.7 10.5 %all-to-all-done.1.gathered = f32[8,3,8,512]{3,2,1,0:T(8,128)S(1)} async-done(((f32[8,3,8,512]{3,2,1,0:T(8,128)}), f32[8,3,8,512]{3,2,1,0:T(8,128)S(1)}, u32[]{:S(2)}, u32[]{:S(2)}) %all-to-all-start.1) | async-done | bytes 393248 | tf_op jit(solution)/shard_map/all_to_all | solution.py:571
  81.2 0.7 copy-done.3
  81.9 1.2 kelvins.1.refs_4_
  83.1 0.7 collective-permute-start.9
  83.8 0.7 fusion.42
  84.5 0.9 multiply_reduce_fusion.3
  85.4 2.7 %collective-permute-done.3.refs_1_ = f32[3,256,128]{2,1,0:T(8,128)S(1)} collective-permute-done((f32[3,256,128]{2,1,0:T(8,128)}, f32[3,256,128]{2,1,0:T(8,128)S(1)}, u32[]{:S(2)}, u32[]{:S(2)}) %collective-permute-start.3) | collective-permute-done | bytes 393248 | tf_op jit(solution)/shard_map/ppermute | solution.py:515
  88.1 0.6 copy-done.6
  88.7 2.5 %enter.1 = (f32[3,256,128]{2,1,0:T(8,128)S(1)}, f32[3,256,128]{2,1,0:T(8,128)}, f32[3,256,128]{2,1,0:T(8,128)}, f32[3,256,128]{2,1,0:T(8,128)S(1)}) custom-call(s32[2]{0:T(128)S(1)} %copy-done.6, f32[10,64]{1,0:T(8,128)S(1)} %stack.141.floats, s32[5,64]{1,0:T(8,128)S(1)} %stack.148.ints, f32[4,3,256,128]{3,2,1,0:T(8,128)S(1)} %get-tuple-element.27.effective, ...), custom_call_target="tpu_custom_call" | custom-call | tf_op jit(solution)/shard_map/enter/pallas_call | solution.py:518
  91.2 1.5 %collective-permute-start.4 = (f32[3,256,128]{2,1,0:T(8,128)}, f32[3,256,128]{2,1,0:T(8,128)S(1)}, u32[]{:S(2)}, u32[]{:S(2)}) collective-permute-start(f32[3,256,128]{2,1,0:T(8,128)} %get-tuple-element.30), channel_id=1, source_target_pairs={{0,4},{4,0},{8,12},{12,8},{16,20},{20,16},{24,28},{28,24},{1,5},{5... | collective-permute-start | bytes 1179656 | tf_op jit(solution)/shard_map/ppermute | solution.py:515
  92.6 2.0 %collective-permute-start.6 = (f32[3,256,128]{2,1,0:T(8,128)S(1)}, f32[3,256,128]{2,1,0:T(8,128)S(1)}, u32[]{:S(2)}, u32[]{:S(2)}) collective-permute-start(f32[3,256,128]{2,1,0:T(8,128)S(1)} %get-tuple-element.32), channel_id=1, source_target_pairs={{0,12},{4,8},{8,4},{12,0},{16,28},{20,24},{24,20},{28,16},{1,13},{... | collective-permute-start | bytes 1179656 | tf_op jit(solution)/shard_map/ppermute | solution.py:515
  94.8 0.5 collective-permute-start.11
  95.3 0.7 broadcast_compare_fusion
  95.9 0.7 mul.371
  96.6 0.1 mul.372
  96.7 0.7 pow.65
  97.4 0.1 pow.66
  97.5 0.6 mul.375
  98.1 0.1 mul.376
  98.2 0.8 fusion.14
  99.2 3.4 %collective-permute-done.4.refs_1_ = f32[3,256,128]{2,1,0:T(8,128)S(1)} collective-permute-done((f32[3,256,128]{2,1,0:T(8,128)}, f32[3,256,128]{2,1,0:T(8,128)S(1)}, u32[]{:S(2)}, u32[]{:S(2)}) %collective-permute-start.4) | collective-permute-done | bytes 393248 | tf_op jit(solution)/shard_map/ppermute | solution.py:515
  102.5 2.4 %collective-permute-done.5.refs_2_ = f32[3,256,128]{2,1,0:T(8,128)S(1)} collective-permute-done((f32[3,256,128]{2,1,0:T(8,128)}, f32[3,256,128]{2,1,0:T(8,128)S(1)}, u32[]{:S(2)}, u32[]{:S(2)}) %collective-permute-start.5) | collective-permute-done | bytes 393248 | tf_op jit(solution)/shard_map/ppermute | solution.py:515
  104.9 5.7 %collective-permute-done.6.refs_3_ = f32[3,256,128]{2,1,0:T(8,128)S(1)} collective-permute-done((f32[3,256,128]{2,1,0:T(8,128)S(1)}, f32[3,256,128]{2,1,0:T(8,128)S(1)}, u32[]{:S(2)}, u32[]{:S(2)}) %collective-permute-start.6) | collective-permute-done | bytes 393248 | tf_op jit(solution)/shard_map/ppermute | solution.py:515
  110.6 0.6 copy-done.7
  111.2 10.5 %final_energy.1 = (f32[64,8,16,128]{3,2,1,0:T(8,128)}, f32[128,128]{1,0:T(8,128)}) custom-call(s32[2]{0:T(128)S(1)} %copy-done.7, f32[10,64]{1,0:T(8,128)S(1)} %stack.141.floats, s32[5,64]{1,0:T(8,128)S(1)} %stack.148.ints, f32[6,16]{1,0:T(8,128)S(1)} %copy.44.kinds, f32[2]{0:T(128)S(1)} %pad_maximum_fusion.3.sums, ...), custom_call_target="tpu_custom_call" | custom-call | tf_op jit(solution)/shard_map/final_energy/pallas_call | solution.py:608
  (62 shorter events, 1.3 us)
Async XLA Ops:
  5.4 19.5 %copy-start.4 = (s32[2]{0:T(128)}, s32[2]{0:T(128)S(1)}, u32[]{:S(2)}) copy-start(s32[2]{0:T(128)S(1)} %pad_add_fusion.1.meta) | copy-start | bytes 28
  5.7 0.8 copy-start
  6.6 0.8 copy-start.1
  22.5 2.4 %collective-permute-start.7 = (f32[2,3,64,512]{3,2,1,0:T(8,128)S(1)}, f32[2,3,64,512]{3,2,1,0:T(8,128)S(1)}, u32[]{:S(2)}, u32[]{:S(2)}) collective-permute-start(f32[2,3,64,512]{3,2,1,0:T(8,128)S(1)} %get-tuple-element.34), channel_id=1, source_target_pairs={{0,1},{1,0},{2,3},{3,2},{4,5},{5,4},{6,7},{7,6},{8,9},{9,8},{10,11... | collective-permute-start | bytes 2359304 | tf_op jit(solution)/shard_map/ppermute | solution.py:515
  25.0 12.3 %collective-permute-start.8 = (f32[1,3,64,512]{3,2,1,0:T(8,128)S(1)}, f32[1,3,64,512]{3,2,1,0:T(8,128)S(1)}, u32[]{:S(2)}, u32[]{:S(2)}) collective-permute-start(f32[1,3,64,512]{3,2,1,0:T(8,128)S(1)} %get-tuple-element.36), channel_id=1, source_target_pairs={{0,2},{1,3},{2,0},{3,1},{4,6},{5,7},{6,4},{7,5},{8,10},{9,11},{10,... | collective-permute-start | bytes 1179656 | tf_op jit(solution)/shard_map/ppermute | solution.py:515
  27.9 36.1 %collective-permute-start = (f32[3,256,128]{2,1,0:T(8,128)}, f32[3,256,128]{2,1,0:T(8,128)S(1)}, u32[]{:S(2)}, u32[]{:S(2)}) collective-permute-start(f32[3,256,128]{2,1,0:T(8,128)} %get-tuple-element.24), channel_id=1, source_target_pairs={{0,4},{4,0},{8,12},{12,8},{16,20},{20,16},{24,28},{28,24},{1,5},{5... | collective-permute-start | bytes 1179656 | tf_op jit(solution)/shard_map/ppermute | solution.py:515
  29.5 34.6 %collective-permute-start.1 = (f32[3,256,128]{2,1,0:T(8,128)}, f32[3,256,128]{2,1,0:T(8,128)S(1)}, u32[]{:S(2)}, u32[]{:S(2)}) collective-permute-start(f32[3,256,128]{2,1,0:T(8,128)} %get-tuple-element.25), channel_id=1, source_target_pairs={{0,8},{4,12},{8,0},{12,4},{16,24},{20,28},{24,16},{28,20},{1,9},{5... | collective-permute-start | bytes 1179656 | tf_op jit(solution)/shard_map/ppermute | solution.py:515
  31.0 33.0 %collective-permute-start.2 = (f32[3,256,128]{2,1,0:T(8,128)}, f32[3,256,128]{2,1,0:T(8,128)S(1)}, u32[]{:S(2)}, u32[]{:S(2)}) collective-permute-start(f32[3,256,128]{2,1,0:T(8,128)} %get-tuple-element.26), channel_id=1, source_target_pairs={{0,12},{4,8},{8,4},{12,0},{16,28},{20,24},{24,20},{28,16},{1,13},{... | collective-permute-start | bytes 1179656 | tf_op jit(solution)/shard_map/ppermute | solution.py:515
  31.4 32.6 %copy-start.11 = (s32[1,64]{1,0:T(1,128)}, s32[1,64]{1,0:T(1,128)S(1)}, u32[]{:S(2)}) copy-start(s32[1,64]{1,0:T(1,128)S(1)} %get-tuple-element.125) | copy-start | bytes 772
  31.4 32.6 %copy-start.12 = (s32[1,64]{1,0:T(1,128)}, s32[1,64]{1,0:T(1,128)S(1)}, u32[]{:S(2)}) copy-start(s32[1,64]{1,0:T(1,128)S(1)} %get-tuple-element.126) | copy-start | bytes 772
  38.2 18.9 %all-to-all-start = ((f32[8,3,8,512]{3,2,1,0:T(8,128)}), f32[8,3,8,512]{3,2,1,0:T(8,128)S(1)}, u32[]{:S(2)}, u32[]{:S(2)}) async-start(f32[8,3,8,512]{3,2,1,0:T(8,128)} %density_parts.1), calls=%async_computation | async-start | bytes 786432 | tf_op jit(solution)/shard_map/all_to_all | solution.py:569
  44.6 17.4 %copy-start.14 = (f32[16]{0:T(128)}, f32[16]{0:T(128)S(1)}, u32[]{:S(2)}) copy-start(f32[16]{0:T(128)S(1)} %squeeze.4) | copy-start | bytes 196
  44.7 17.2 %copy-start.13 = (f32[16]{0:T(128)}, f32[16]{0:T(128)S(1)}, u32[]{:S(2)}) copy-start(f32[16]{0:T(128)S(1)} %squeeze.5) | copy-start | bytes 196
  46.2 17.8 %copy-start.9 = (f32[16]{0:T(128)}, f32[16]{0:T(128)S(1)}, u32[]{:S(2)}) copy-start(f32[16]{0:T(128)S(1)} %get-tuple-element.111) | copy-start | bytes 196
  46.2 17.8 %copy-start.10 = (f32[16]{0:T(128)}, f32[16]{0:T(128)S(1)}, u32[]{:S(2)}) copy-start(f32[16]{0:T(128)S(1)} %get-tuple-element.112) | copy-start | bytes 196
  57.9 6.2 %copy-start.2 = (f32[8,512]{1,0:T(8,128)}, f32[8,512]{1,0:T(8,128)S(1)}, u32[]{:S(2)}) copy-start(f32[8,512]{1,0:T(8,128)S(1)} %get-tuple-element.39.late) | copy-start | bytes 49156
  57.9 23.3 %all-to-all-start.1 = ((f32[8,3,8,512]{3,2,1,0:T(8,128)}), f32[8,3,8,512]{3,2,1,0:T(8,128)S(1)}, u32[]{:S(2)}, u32[]{:S(2)}) async-start(f32[8,3,8,512]{3,2,1,0:T(8,128)} %get-tuple-element.38), calls=%async_computation.1 | async-start | bytes 786432 | tf_op jit(solution)/shard_map/all_to_all | solution.py:571
  62.1 2.0 %copy-start.8 = (f32[16]{0:T(128)}, f32[16]{0:T(128)S(1)}, u32[]{:S(2)}) copy-start(f32[16]{0:T(128)S(1)} %pow.61) | copy-start | bytes 196
  64.1 0.6 copy-start.5
  66.5 21.5 %collective-permute-start.3 = (f32[3,256,128]{2,1,0:T(8,128)}, f32[3,256,128]{2,1,0:T(8,128)S(1)}, u32[]{:S(2)}, u32[]{:S(2)}) collective-permute-start(f32[3,256,128]{2,1,0:T(8,128)} %get-tuple-element.28.refs_0_), channel_id=1, source_target_pairs={{0,16},{4,20},{8,24},{12,28},{16,0},{20,4},{24,8},{28,12},{1,17},{... | collective-permute-start | bytes 1179656 | tf_op jit(solution)/shard_map/ppermute | solution.py:515
  81.2 0.7 copy-start.3
  83.1 11.6 %collective-permute-start.9 = (f32[136,512]{1,0:T(8,128)S(1)}, f32[136,512]{1,0:T(8,128)S(1)}, u32[]{:S(2)}, u32[]{:S(2)}) collective-permute-start(f32[136,512]{1,0:T(8,128)S(1)} %kelvins.1.refs_4_), channel_id=1, source_target_pairs={{0,2},{1,3},{2,0},{3,1},{4,6},{5,7},{6,4},{7,5},{8,10},{9,11},{10,... | collective-permute-start | bytes 835592 | tf_op jit(solution)/shard_map/ppermute | solution.py:515
  88.1 0.6 copy-start.6
  91.2 11.4 %collective-permute-start.4 = (f32[3,256,128]{2,1,0:T(8,128)}, f32[3,256,128]{2,1,0:T(8,128)S(1)}, u32[]{:S(2)}, u32[]{:S(2)}) collective-permute-start(f32[3,256,128]{2,1,0:T(8,128)} %get-tuple-element.30), channel_id=1, source_target_pairs={{0,4},{4,0},{8,12},{12,8},{16,20},{20,16},{24,28},{28,24},{1,5},{5... | collective-permute-start | bytes 1179656 | tf_op jit(solution)/shard_map/ppermute | solution.py:515
  92.6 12.3 %collective-permute-start.5 = (f32[3,256,128]{2,1,0:T(8,128)}, f32[3,256,128]{2,1,0:T(8,128)S(1)}, u32[]{:S(2)}, u32[]{:S(2)}) collective-permute-start(f32[3,256,128]{2,1,0:T(8,128)} %get-tuple-element.31), channel_id=1, source_target_pairs={{0,8},{4,12},{8,0},{12,4},{16,24},{20,28},{24,16},{28,20},{1,9},{5... | collective-permute-start | bytes 1179656 | tf_op jit(solution)/shard_map/ppermute | solution.py:515
  92.6 17.9 %collective-permute-start.6 = (f32[3,256,128]{2,1,0:T(8,128)S(1)}, f32[3,256,128]{2,1,0:T(8,128)S(1)}, u32[]{:S(2)}, u32[]{:S(2)}) collective-permute-start(f32[3,256,128]{2,1,0:T(8,128)S(1)} %get-tuple-element.32), channel_id=1, source_target_pairs={{0,12},{4,8},{8,4},{12,0},{16,28},{20,24},{24,20},{28,16},{1,13},{... | collective-permute-start | bytes 1179656 | tf_op jit(solution)/shard_map/ppermute | solution.py:515
  94.7 15.8 %collective-permute-start.10 = (f32[136,512]{1,0:T(8,128)S(1)}, f32[136,512]{1,0:T(8,128)S(1)}, u32[]{:S(2)}, u32[]{:S(2)}) collective-permute-start(f32[136,512]{1,0:T(8,128)S(1)} %kelvins.1.refs_4_), channel_id=1, source_target_pairs={{0,1},{1,0},{2,3},{3,2},{4,5},{5,4},{6,7},{7,6},{8,9},{9,8},{10,11... | collective-permute-start | bytes 835592 | tf_op jit(solution)/shard_map/ppermute | solution.py:515
  94.8 15.8 %collective-permute-start.11 = (f32[136,512]{1,0:T(8,128)S(1)}, f32[136,512]{1,0:T(8,128)S(1)}, u32[]{:S(2)}, u32[]{:S(2)}) collective-permute-start(f32[136,512]{1,0:T(8,128)S(1)} %collective-permute-done.9.refs_5_), channel_id=1, source_target_pairs={{0,1},{1,0},{2,3},{3,2},{4,5},{5,4},{6,7},{7,6},{8,9},{9,8},{10,11... | collective-permute-start | bytes 835592 | tf_op jit(solution)/shard_map/ppermute | solution.py:515
  110.6 0.6 copy-start.7

commit v5 on v4

--- a/solution.py
+++ b/solution.py
@@ -78,9 +78,10 @@
         ]
     )
     x = jnp.arange(slabs * depth, dtype=jnp.int32)[:, None]
-    past = jnp.where(forward[None, :], x - (slab * depth + depth - 1), slab * depth - x)
+    by_half = lambda value: value.reshape(GROUP, 2, -1).transpose(1, 0, 2).reshape(1, -1)
+    past = jnp.where(by_half(forward), x - (slab * depth + depth - 1), slab * depth - x)
     n = past.astype(jnp.float32)
-    weight = jnp.where(past > 0, jnp.power(ratio[None, :], jnp.maximum(n, 0.0)), 0.0)
+    weight = jnp.where(past > 0, jnp.power(by_half(ratio), jnp.maximum(n, 0.0)), 0.0)
     return floats, ints, jnp.concatenate([weight, n * weight, (0.5 * n * (n + 1.0)) * weight], axis=1)
 
 
@@ -194,19 +195,32 @@
     return pl.ds(at, 8), pl.ds(at + 8, 8)
 
 
-def sweeps_kernel(sizes, meta, floats, ints, kinds, energy, flag, given, matrix, swept, quarter, *rest):
-    block, blocks, depth, width_y, slots, modes, group = sizes
-    faces, rest = rest[:group], rest[group:]
-    keep, send, *planes, density, flat, sources, heat = rest
-    out_one, turn_one, turn_two, out_two, turn_late, out_three = planes
-    rows, own = width_y // modes, slots // group
+def sweeps_kernel(half, sizes, *refs):
+    block, depth, width_y, modes, group = sizes
+    refs = list(refs)
+    take = lambda count: [refs.pop(0) for _ in range(count)]
+    meta, floats, ints, kinds, energy, flag, given = take(7)
+    if half:
+        matrix, *older, older_density = take(8)
+    (swept,) = take(1)
+    faces = take(group)
+    if half:
+        keep, send = take(2)
+        planes = take(6)
+        flat, density, sources, heat = take(4)
+    else:
+        (quarter,) = take(1)
+        planes = take(6)
+        flat, density, sources, heat = take(4)
+    rows = width_y // modes
     step = pl.program_id(0)
     slab, mode = meta[SLAB], meta[MODE]
 
     @pl.when(step == 0)
     def _():
-        for yy in range(rows):
-            quarter[:, yy * 128 : (yy + 1) * 128] = given[pl.ds(mode * rows + yy, depth, stride=width_y), :]
+        if not half:
+            for yy in range(rows):
+                quarter[:, yy * 128 : (yy + 1) * 128] = given[pl.ds(mode * rows + yy, depth, stride=width_y), :]
         density[...] = jnp.zeros_like(density)
 
         def one_layer(x, carry):
@@ -224,7 +238,7 @@
     row = lax.broadcasted_iota(jnp.int32, (8, 128), 0)
 
     def one_slot(i, carry):
-        s = step * block + i
+        s = (2 * step + half) * block + i
         start, stride = course(ints, s, depth)
         side = 1 - ints[FORWARD, s]
         ratio, warm, kind = floats[RATIO, s], floats[WARM, s], ints[KIND, s]
@@ -250,7 +264,7 @@
                     swept[i, x, 8:, :] = total_high
             last.append((total_low, total_high))
         turned = apply(*last[0])
-        at_low, at_high = rows_of(s)
+        at_low, at_high = rows_of(step * block + i)
         values = (last[0], turned, apply(*turned), last[1], apply(*last[1]), last[2])
         for plane, (low, high) in zip(planes, values):
             plane[at_low, :] = low
@@ -259,28 +273,32 @@
 
     lax.fori_loop(0, block, one_slot, 0, unroll=2)
 
-    @pl.when(step == blocks - 1)
+    @pl.when(step == group - 1)
     def _():
+        _, turn_one, turn_two, _, turn_late, out_three = planes
         for by in range(group):
-            at = pl.ds(pl.multiple_of(((slab % group) ^ by) * own * 16, 16), own * 16)
+            at = pl.ds(pl.multiple_of(((slab % group) ^ by) * block * 16, 16), block * 16)
             for index, plane in enumerate((turn_two, turn_late, out_three)):
                 faces[by][index] = plane[at, :]
         for turn in range(ITERS):
             for x in range(depth):
-                flat[turn, x * 16 : x * 16 + 16, :] = density[turn, 0, x] + density[turn, 1, depth - 1 - x]
+                at = slice(x * 16, x * 16 + 16)
+                total = density[turn, 0, x] + density[turn, 1, depth - 1 - x]
+                flat[turn, at, :] = total + older_density[turn, at, :] if half else total
+        if not half:
+            return
         home = pl.ds(pl.multiple_of(slab * depth, 8), depth)
+        slots = 2 * group * block
         for by in range(modes):
             ys = [(mode ^ by) * rows + yy for yy in range(rows)]
             pick = lambda plane, count: jnp.concatenate([plane[pl.ds(y, count, stride=width_y), :] for y in ys], axis=1)
-            one, two = pick(turn_one, slots), pick(turn_late, slots)
-            rights = (
-                pick(out_one, slots),
-                jnp.concatenate([pick(out_two, slots), one], axis=0),
-                jnp.concatenate([pick(out_three, slots), two, pick(turn_two, slots)], axis=0),
+            out_one, turn_one, turn_two, out_two, turn_late, out_three = (
+                [pick(before, slots // 2), pick(plane, slots // 2)] for before, plane in zip(older, planes)
             )
+            rights = (out_one, out_two + turn_one, out_three + turn_late + turn_two)
             target = (send if by % 2 else keep).at[by // 2]
             for turn, right in enumerate(rights):
-                target[turn] = exact_dot(matrix[:, : (turn + 1) * slots], right)
+                target[turn] = exact_dot(matrix[:, : (turn + 1) * slots], jnp.concatenate(right, axis=0))
                 target[turn, home, :] += pick(flat.at[turn], depth)
 
 
@@ -297,39 +315,36 @@
             parts[slab, turn] = total[slab * depth : (slab + 1) * depth]
 
 
-def totals_kernel(parts, before, copies, late):
+def totals_kernel(sums, parts, before, copies, late):
     slabs = parts.shape[0]
     one, two, three = (
         add_up([parts[slab, turn] for slab in range(slabs)]) * (1.0 / DIRS) for turn in range(ITERS)
     )
     late[...] = three
+    kelvin = newton(one, before[...], sums[0], sums[1])
     for slab in range(slabs):
-        copies[slab, 0] = one
+        copies[slab, 0] = kelvin
         copies[slab, 1] = two
-        copies[slab, 2] = before[...]
 
 
 def kelvins_kernel(depth, sums, gathered, late, matrix, packed):
     slabs = gathered.shape[0]
     cells = slabs * depth
-    one, two, before = (
-        jnp.concatenate([gathered[slab, index] for slab in range(slabs)], axis=0) for index in range(3)
-    )
-    kelvin = newton(one, before, sums[0], sums[1])
+    kelvin, two = (jnp.concatenate([gathered[slab, index] for slab in range(slabs)], axis=0) for index in range(2))
     packed[:cells, :] = kelvin
     two = two + exact_dot(matrix[...], jnp.concatenate([kelvin, fourth(kelvin)], axis=0))
     packed[cells : 2 * cells, :] = newton(two, kelvin, sums[0], sums[1])
     packed[2 * cells :, :] = late[...]
 
 
-def compose_kernel(own, group, meta, floats, ints, *refs):
+def compose_kernel(half, block, group, meta, floats, ints, *refs):
     received, (composite, effective, ordered) = refs[:group], refs[group:]
     place = meta[SLAB] % group
     for by in range(group):
         ordered[place ^ by] = received[by][...]
 
     def one_slot(i, carry):
-        s = place * own + i
+        s = (2 * place + half) * block + i
         start, stride = course(ints, s, group)
         full, full_n, full_t = floats[FULL, s], floats[FULL_N, s], floats[FULL_T, s]
         at = pl.ds(pl.multiple_of(i * 16, 16), 16)
@@ -343,11 +358,11 @@
             composite[index, at, :] = value
         return carry
 
-    lax.fori_loop(0, own, one_slot, 0, unroll=4)
+    lax.fori_loop(0, block, one_slot, 0, unroll=4)
     effective[...] = ordered[...]
 
 
-def enter_kernel(own, group, groups, depth, meta, floats, ints, effective, *refs):
+def enter_kernel(half, block, group, groups, depth, meta, floats, ints, effective, *refs):
     composites, rest = refs[:groups], refs[groups:]
     outs, (ordered, entered) = rest[:group], rest[group:]
     slab = meta[SLAB]
@@ -357,7 +372,7 @@
     span = depth * group
 
     def one_slot(i, carry):
-        s = place * own + i
+        s = (2 * place + half) * block + i
         start, stride = course(ints, s, group)
         begin, leap = course(ints, s, groups)
         ahead = jnp.where(ints[FORWARD, s] == 1, mine, groups - 1 - mine)
@@ -387,27 +402,49 @@
                 values = push(values, full, full_n, full_t, [effective[k, plane, at, :] for plane in range(3)])
         return carry
 
-    lax.fori_loop(0, own, one_slot, 0, unroll=2)
+    lax.fori_loop(0, block, one_slot, 0, unroll=2)
     for by in range(group):
         outs[by][...] = entered[place ^ by]
 
 
-def final_kernel(sizes, order, meta, floats, ints, kinds, sums, swept, *refs):
-    block, depth, width_y, width_z, slots, slabs, modes, group = sizes
-    received, refs = refs[:group], refs[group:]
-    packs, refs = refs[:modes], refs[modes:]
-    first_matrix, second_matrix, energy, kelvin, *refs = refs
-    warm_one, warm_two, late, enter_one, enter_long, enter_two, second, added, own_one, own_two, *ordered = refs
+def inflow_kernel(half, sizes, meta, floats, ints, swept, *refs):
+    block, depth, group = sizes
+    received, (energy, ordered) = refs[:group], refs[-2:]
     step = pl.program_id(0)
-    slab, mode = meta[SLAB], meta[MODE]
-    own, lanes, cells = slots // group, width_y // modes * width_z, slabs * depth
 
     @pl.when(step == 0)
     def _():
         for by in range(group):
-            at = pl.ds(pl.multiple_of(((slab % group) ^ by) * own * 16, 16), own * 16)
-            for index in range(ITERS):
-                ordered[index][at, :] = received[by][index]
+            ordered[(meta[SLAB] % group) ^ by] = received[by][...]
+
+    def one_slot(i, carry):
+        s = (2 * step + half) * block + i
+        start, stride = course(ints, s, depth)
+        ratio = floats[RATIO, s]
+        at = pl.ds(pl.multiple_of(i * 16, 16), 16)
+        one, two, three = (ordered[step, plane, at, :] for plane in range(ITERS))
+        for j in range(depth):
+            x = start + stride * j
+            one = ratio * one
+            two = ratio * two + one
+            three = ratio * three + two
+            energy[i, x] = swept[i, x] + three
+        return carry
+
+    lax.fori_loop(0, block, one_slot, 0, unroll=4)
+
+
+def final_kernel(sizes, order, meta, floats, ints, kinds, sums, inflown, *refs):
+    block, depth, width_y, width_z, slabs, modes = sizes
+    packs, refs = refs[:modes], refs[modes:]
+    first_matrix, second_matrix, energy, kelvin, *refs = refs
+    warm_one, warm_two, late, enter_one, enter_long, enter_two, second, added, own_one, own_two = refs
+    step = pl.program_id(0)
+    slab, mode = meta[SLAB], meta[MODE]
+    lanes, cells = width_y // modes * width_z, slabs * depth
+
+    @pl.when(step == 0)
+    def _():
         for pack, by in zip(packs, order):
             at = pl.ds(pl.multiple_of((mode ^ by) * lanes, 128), lanes)
             warm_one[:, at] = pack[:cells, :]
@@ -442,20 +479,18 @@
 
         def one_kind(kind, carry):
             therm, quart, decay = kinds[THERM, kind], kinds[QUART, kind], kinds[DECAY, kind]
-            at = pl.ds(pl.multiple_of(kind * 16, 16), 16)
-            back_at = pl.ds(pl.multiple_of((kind + KINDS) * 16, 16), 16)
-            layers = []
-            for x in range(depth):
-                here = slice(x * 16, x * 16 + 16)
-                t, u = own_one[here, :], own_two[here, :]
-                layers.append(therm * t + quart * fourth(t))
-                added[kind, x] = therm * u + quart * fourth(u)
-            up, down = enter_one[at, :], enter_one[back_at, :]
-            for j in range(depth):
-                up = decay * up + layers[j]
-                down = decay * down + layers[depth - 1 - j]
-                second[kind, j] = up
-                second[kind + KINDS, j] = down
+            for sided in (kind, kind + KINDS):
+                at = pl.ds(pl.multiple_of(sided * 16, 16), 16)
+                once, twice, new = enter_one[at, :], enter_long[at, :], enter_two[at, :]
+                for j in range(depth):
+                    x = j if sided is kind else depth - 1 - j
+                    here = slice(x * 16, x * 16 + 16)
+                    t, u = own_one[here, :], own_two[here, :]
+                    once = decay * once + (therm * t + quart * fourth(t))
+                    twice = decay * twice + once
+                    new = decay * new + (therm * u + quart * fourth(u))
+                    second[sided, x] = twice
+                    added[sided, x] = new
             return carry
 
         lax.fori_loop(0, KINDS, one_kind, 0)
@@ -464,22 +499,12 @@
 
     def one_slot(i, carry):
         s = step * block + i
-        start, stride = course(ints, s, depth)
-        ratio, kind = floats[RATIO, s], ints[KIND, s]
-        sided = kind + KINDS * (1 - ints[FORWARD, s])
+        sided = ints[KIND, s] + KINDS * (1 - ints[FORWARD, s])
         apply = slot_stencil(floats, ints, s, row)
-        at, kind_at = rows_of(s), rows_of(sided)
-        one, two, three = ([ref[half, :] for half in at] for ref in ordered)
-        longer = apply(*(enter_long[half, :] for half in kind_at))
-        three = [a + b + enter_two[half, :] for a, b, half in zip(three, longer, kind_at)]
-        for j in range(depth):
-            x = start + stride * j
-            fresh = apply(second[sided, j, :8, :], second[sided, j, 8:, :])
-            for half, here in enumerate((slice(0, 8), slice(8, 16))):
-                one[half] = ratio * one[half]
-                two[half] = ratio * two[half] + one[half]
-                three[half] = ratio * three[half] + (fresh[half] + added[kind, x, here, :] + two[half])
-                energy[i, x, here, :] = swept[i, x, here, :] + three[half]
+        for x in range(depth):
+            low, high = apply(second[sided, x, :8, :], second[sided, x, 8:, :])
+            energy[i, x, :8, :] = inflown[i, x, :8, :] + (low + added[sided, x, :8, :])
+            energy[i, x, 8:, :] = inflown[i, x, 8:, :] + (high + added[sided, x, 8:, :])
         return carry
 
     lax.fori_loop(0, block, one_slot, 0, unroll=2)
@@ -489,12 +514,10 @@
     slots, depth, width_y, width_z = incoming_occupation.shape
     slabs, modes = lax.axis_size("slab"), lax.axis_size("mode")
     group, groups = GROUP, slabs // GROUP
-    own = slots // group
     lanes = width_y // modes * width_z
-    block = 8
-    blocks = slots // block
+    block = slots // group // 2
     cells, all_x = depth * width_y, slabs * depth
-    face_rows = own * width_y
+    face_rows = block * width_y
     slab = lax.axis_index("slab").astype(jnp.int32)
     meta = jnp.stack([slab, lax.axis_index("mode").astype(jnp.int32)])
     floats, ints, matrix = slot_tables(labels, speed, rate, storage, threshold, generation, slab, slabs, depth, width_z)
@@ -525,51 +548,136 @@
             name=name,
         )(*args)
 
+    tied = lax.optimization_barrier
     slot_block = pl.BlockSpec((block, depth, width_y, width_z), lambda i: (i, 0, 0, 0))
+    half_blocks = [pl.BlockSpec((block, depth, width_y, width_z), lambda i, h=h: (2 * i + h, 0, 0, 0)) for h in range(2)]
     slot_shape = shape(slots, depth, width_y, width_z)
+    half_shape = shape(slots // 2, depth, width_y, width_z)
     face = (3, face_rows, width_z)
-    half = (modes // 2, ITERS, all_x, lanes)
-    swept, quarter, *rest = pl.pallas_call(
-        functools.partial(sweeps_kernel, (block, blocks, depth, width_y, slots, modes, group)),
-        grid=(blocks,),
-        in_specs=[SMEM] * 4 + [slot_block, whole(cells, width_z), whole(cells, width_z), whole(all_x, ITERS * slots)],
-        out_specs=[slot_block, whole(depth, lanes)] + [whole(*face)] * group + [whole(*half)] * 2,
-        out_shape=[slot_shape, shape(depth, lanes)] + [shape(*face)] * group + [shape(*half)] * 2,
-        scratch_shapes=[scratch(slots * width_y, width_z)] * 6
-        + [
-            scratch(ITERS, 2, depth, width_y, width_z),
-            scratch(ITERS, cells, width_z),
-            scratch(KINDS, depth, width_y, width_z),
-            scratch(depth, width_y, width_z),
-        ],
-        compiler_params=PARAMS,
-        name="sweeps",
-    )(
-        meta,
-        floats,
-        ints,
-        kinds,
-        incoming_occupation,
-        generating_region_flag.reshape(cells, width_z),
-        crystal_kelvin_given.reshape(cells, width_z),
-        matrix,
-    )
-    faces, (keep, send) = rest[:group], rest[group:]
+    share = (modes // 2, ITERS, all_x, lanes)
+    plane = (slots // 2 * width_y, width_z)
+    flat = (ITERS, cells, width_z)
+    flag = generating_region_flag.reshape(cells, width_z)
+    given = crystal_kelvin_given.reshape(cells, width_z)
+
+    def sweeps(half, extra):
+        outs = [(slot_block, half_shape)] + [(whole(*face), shape(*face))] * group
+        scratches = []
+        if half:
+            outs += [(whole(*share), shape(*share))] * 2
+            scratches = [scratch(*plane)] * 6 + [scratch(*flat)]
+        else:
+            outs += [(whole(*dims), shape(*dims)) for dims in [(depth, lanes)] + [plane] * 6 + [flat]]
+        return pl.pallas_call(
+            functools.partial(sweeps_kernel, half, (block, depth, width_y, modes, group)),
+            grid=(group,),
+            in_specs=[SMEM] * 4
+            + [half_blocks[half], whole(cells, width_z), whole(cells, width_z)]
+            + [whole(*array.shape) for array in extra],
+            out_specs=[spec for spec, _ in outs],
+            out_shape=[of for _, of in outs],
+            scratch_shapes=scratches
+            + [
+                scratch(ITERS, 2, depth, width_y, width_z),
+                scratch(KINDS, depth, width_y, width_z),
+                scratch(depth, width_y, width_z),
+            ],
+            compiler_params=PARAMS,
+            name=f"sweeps_{half}",
+        )(meta, floats, ints, kinds, incoming_occupation, flag, given, *extra)
+
+    def around_group(faces):
+        return [faces[0]] + [swap(faces[index], "slab", index) for index in range(1, group)]
+
+    def compose(half, received):
+        return call(
+            functools.partial(compose_kernel, half, block, group),
+            f"compose_{half}",
+            [SMEM] * 3 + [VMEM] * group,
+            [shape(*face), shape(group, *face)],
+            meta,
+            floats,
+            ints,
+            *received,
+            scratches=[scratch(group, *face)],
+        )
+
+    def across_groups(composite):
+        return [composite] + [swap(composite, "slab", index * group) for index in range(1, groups)]
+
+    def enter(half, effective, composites):
+        return call(
+            functools.partial(enter_kernel, half, block, group, groups, depth),
+            f"enter_{half}",
+            [SMEM] * 3 + [VMEM] * (1 + groups),
+            [shape(*face)] * group,
+            meta,
+            floats,
+            ints,
+            effective,
+            *composites,
+            scratches=[scratch(groups, *face), scratch(group, *face)],
+        )
+
+    def add_inflow(half, swept, received, energy):
+        return pl.pallas_call(
+            functools.partial(inflow_kernel, half, (block, depth, group)),
+            grid=(group,),
+            in_specs=[SMEM] * 3
+            + [slot_block]
+            + [whole(*face)] * group
+            + [pl.BlockSpec(memory_space=pl.ANY)] * len(energy),
+            out_specs=half_blocks[half],
+            out_shape=slot_shape,
+            scratch_shapes=[scratch(group, *face)],
+            input_output_aliases={4 + group: 0} if energy else {},
+            compiler_params=PARAMS,
+            name=f"inflow_{half}",
+        )(meta, floats, ints, swept, *received, *energy)
+
+    swept_0, *rest = sweeps(0, [])
+    received_0 = around_group(rest[:group])
+    quarter, *older = rest[group:]
+    swept_1, *rest = sweeps(1, [matrix] + older)
+    keep, send = rest[group:]
 
     by = 1
     other = swap(send, "mode", by)
-    received = [faces[0]] + [swap(faces[index], "slab", index) for index in range(1, group)]
+    received_1 = around_group(rest[:group])
     while 2 * by < modes:
         by *= 2
         now = (modes // (2 * by), ITERS, all_x, lanes)
         keep, send = call(split_kernel, "density_split", [VMEM] * 2, [shape(*now)] * 2, keep, other)
         other = swap(send, "mode", by)
-    piece = (slabs, ITERS, depth, lanes)
-    (parts,) = call(functools.partial(parts_kernel, depth), "density_parts", [VMEM] * 2, [shape(*piece)], keep, other)
+    composite_0, effective_0 = compose(0, received_0)
+    other, composite_0 = tied((other, composite_0))
+    composites_0 = across_groups(composite_0)
+    (parts,) = call(
+        functools.partial(parts_kernel, depth), "density_parts", [VMEM] * 2, [shape(slabs, ITERS, depth, lanes)], keep, other
+    )
+    composite_1, effective_1 = compose(1, received_1)
+    parts, composite_1 = tied((parts, composite_1))
     parts = lax.all_to_all(parts, "slab", 0, 0)
-    copies, late = call(totals_kernel, "density_totals", [VMEM] * 2, [shape(*piece), shape(depth, lanes)], parts, quarter)
+    composites_1 = across_groups(composite_1)
+    entering_0 = enter(0, effective_0, composites_0)
+    parts, entering_0 = tied((parts, entering_0))
+    copies, late = call(
+        totals_kernel,
+        "density_totals",
+        [SMEM] + [VMEM] * 2,
+        [shape(slabs, 2, depth, lanes), shape(depth, lanes)],
+        sums,
+        parts,
+        quarter,
+    )
+    entering_0 = around_group(entering_0)
+    entering_1 = enter(1, effective_1, composites_1)
+    copies, entering_1 = tied((copies, entering_1))
     gathered = lax.all_to_all(copies, "slab", 0, 0)
+    entering_1 = around_group(entering_1)
     pack_shape = shape(2 * all_x + depth, lanes)
+    energy = add_inflow(0, swept_0, entering_0, [])
+    gathered, energy = tied((gathered, energy))
     (packed,) = call(
         functools.partial(kelvins_kernel, depth), "kelvins", [SMEM] + [VMEM] * 3, [pack_shape], sums, gathered, late, everywhere
     )
@@ -578,39 +686,13 @@
         packs = packs + [swap(pack, "mode", by) for pack in packs]
         order = order + [index ^ by for index in order]
         by //= 2
-
-    composite, effective = call(
-        functools.partial(compose_kernel, own, group),
-        "compose",
-        [SMEM] * 3 + [VMEM] * group,
-        [shape(*face), shape(group, *face)],
-        meta,
-        floats,
-        ints,
-        *received,
-        scratches=[scratch(group, *face)],
-    )
-    composites = [composite] + [swap(composite, "slab", index * group) for index in range(1, groups)]
-    entering = call(
-        functools.partial(enter_kernel, own, group, groups, depth),
-        "enter",
-        [SMEM] * 3 + [VMEM] * (1 + groups),
-        [shape(*face)] * group,
-        meta,
-        floats,
-        ints,
-        effective,
-        *composites,
-        scratches=[scratch(groups, *face), scratch(group, *face)],
-    )
-    entering = [entering[0]] + [swap(entering[index], "slab", index) for index in range(1, group)]
+    energy = add_inflow(1, swept_1, entering_1, [energy])
 
     energy, kelvin = pl.pallas_call(
-        functools.partial(final_kernel, (block, depth, width_y, width_z, slots, slabs, modes, group), order),
-        grid=(blocks,),
+        functools.partial(final_kernel, (block, depth, width_y, width_z, slabs, modes), order),
+        grid=(slots // block,),
         in_specs=[SMEM] * 5
         + [slot_block]
-        + [whole(*face)] * group
         + [whole(*pack_shape.shape)] * modes
         + [whole(*first_matrix.shape), whole(*second_matrix.shape)],
         out_specs=[slot_block, whole(cells, width_z)],
@@ -618,12 +700,11 @@
         scratch_shapes=[scratch(all_x, width_y * width_z)] * 2
         + [scratch(depth, width_y * width_z)]
         + [scratch(2 * KINDS * width_y, width_z)] * 3
-        + [scratch(2 * KINDS, depth, width_y, width_z), scratch(KINDS, depth, width_y, width_z)]
-        + [scratch(cells, width_z)] * 2
-        + [scratch(slots * width_y, width_z)] * 3,
+        + [scratch(2 * KINDS, depth, width_y, width_z)] * 2
+        + [scratch(cells, width_z)] * 2,
         compiler_params=PARAMS,
         name="final_energy",
-    )(meta, floats, ints, kinds, sums, swept, *entering, *packs, first_matrix, second_matrix)
+    )(meta, floats, ints, kinds, sums, energy, *packs, first_matrix, second_matrix)
     return energy, kelvin.reshape(depth, width_y, width_z)
 
 

time: 123 us -> 148 us (1.20)
  waiting for transfers between devices: 43.2 us -> 56.2 us
  starting transfers between devices: 23.9 us -> 32.4 us
  Pallas kernels: 32.9 us -> 39.4 us
  other arithmetic: 13.2 us -> 8.53 us
  local copies, waits for them, and re-layouts: 7.54 us -> 10.2 us
    ppermute x12 -> x19, waiting for transfers between devices: 21.9 us -> 56.2 us  [swap(): lax.ppermute(array, axis, [(i, i ^ by) for i in range(lax.axis_size(axis))])]
    all_to_all x1, waiting for transfers between devices: 10.9 us -> 0.01 us  [local(): parts = lax.all_to_all(parts, 'slab', 0, 0)]
    all_to_all x1, waiting for transfers between devices: 10.5 us -> 0.01 us  [local(): gathered = lax.all_to_all(copies, 'slab', 0, 0)]
    ppermute x12 -> x19, starting transfers between devices: 14.4 us -> 22.6 us  [swap(): lax.ppermute(array, axis, [(i, i ^ by) for i in range(lax.axis_size(axis))])]
    pallas_call x1 -> x4, Pallas kernels: 15.1 us -> 22.7 us  [the longest x2 16.8 us: sweeps(): pl.pallas_call(functools.partial(sweeps_kernel, half, (block, depth, widt...]
    unnamed x30 -> x40, local copies, waits for them, and re-layouts: 4.2 us -> 8.42 us
    pallas_call x1, Pallas kernels: 10.5 us -> 8.77 us  [local(): pl.pallas_call(functools.partial(final_kernel, (block, depth, width_y, wi...]
    pallas_call x6 -> x8, Pallas kernels: 7.23 us -> 7.91 us  [call(): pl.pallas_call(kernel, in_specs=in_specs, out_specs=[VMEM] * len(out_shap...]
  transfers between devices with their start and end apart: 14 -> 21, of which waited for: 8 -> 13; matrix products, arithmetic and copies ran while one was open for 9% -> 3% of each run, Pallas kernels for 6% -> 7%
where the time goes in v5:
time: 148 us
  waiting for transfers between devices  56.2 us (38%)
  Pallas kernels  39.4 us (27%)
  starting transfers between devices  32.4 us (22%)
  local copies, waits for them, and re-layouts  10.2 us (7%)
  other arithmetic  8.53 us (6%)
    ppermute x19, waiting for transfers between devices, swap(): lax.ppermute(array, axis, [(i, i ^ by) for i in range(lax.axis_size(axis))])  56.2 us
    ppermute x19, starting transfers between devices, swap(): lax.ppermute(array, axis, [(i, i ^ by) for i in range(lax.axis_size(axis))])  22.6 us
    pallas_call x2, Pallas kernels, sweeps(): pl.pallas_call(functools.partial(sweeps_kernel, half, (block, depth, widt...  16.8 us
    pallas_call x1, Pallas kernels, local(): pl.pallas_call(functools.partial(final_kernel, (block, depth, width_y, wi...  8.77 us
    unnamed x40, local copies, waits for them, and re-layouts  8.42 us
    pallas_call x8, Pallas kernels, call(): pl.pallas_call(kernel, in_specs=in_specs, out_specs=[VMEM] * len(out_shap...  7.91 us
    all_to_all x1, starting transfers between devices, local(): parts = lax.all_to_all(parts, 'slab', 0, 0)  6.02 us
    pallas_call x2, Pallas kernels, add_inflow(): pl.pallas_call(functools.partial(inflow_kernel, half, (block, depth, grou...  5.87 us
  transfers between devices with their start and end apart: 21, of which 13 were waited for; matrix products, arithmetic and copies ran while one was open for 3% of the time, Pallas kernels for 7%

profile of v5, /device:TPU:0, one launch (start us, length us, event | category | flops | bytes accessed | tf_op | source)
XLA Modules:
  0.0 147.7 jit_solution(1111332026352489838)
XLA Ops:
  0.6 0.7 add_bitcast_fusion
  1.3 0.7 fusion.38
  2.0 0.8 select_reduce_fusion
  3.0 1.3 fusion.45
  4.3 0.7 fusion.40
  5.1 0.1 copy.47
  5.3 0.1 reshape.298
  5.4 0.1 pow.61
  5.5 0.1 reshape.297
  5.6 0.1 broadcast_in_dim.124
  5.7 0.1 fusion.6
  6.1 0.8 copy-done.4
  6.9 0.8 copy-done.5
  7.7 7.1 %sweeps_0.1 = (f32[32,8,16,128]{3,2,1,0:T(8,128)S(1)}, f32[3,128,128]{2,1,0:T(8,128)S(1)}, f32[3,128,128]{2,1,0:T(8,128)}, f32[3,128,128]{2,1,0:T(8,128)}, f32[3...) custom-call(s32[2]{0:T(128)S(1)} %pad_add_fusion.1.refs_0_.meta, ...), custom_call_target="tpu_custom_call" | custom-call | tf_op jit(solution)/shard_map/sweeps_0/pallas_call | solution.py:571
  14.8 1.3 copy-done.2
  16.1 9.7 %sweeps_1.1 = (f32[32,8,16,128]{3,2,1,0:T(8,128)}, f32[3,128,128]{2,1,0:T(8,128)S(1)}, f32[3,128,128]{2,1,0:T(8,128)}, f32[3,128,128]{2,1,0:T(8,128)S(1)}, f32[3...) custom-call(s32[2]{0:T(128)S(1)} %pad_add_fusion.1.refs_0_.meta, ...), custom_call_target="tpu_custom_call" | custom-call | tf_op jit(solution)/shard_map/sweeps_1/pallas_call | solution.py:571
  25.9 0.5 collective-permute-start
  26.3 2.6 %collective-permute-start.2 = (f32[3,128,128]{2,1,0:T(8,128)}, f32[3,128,128]{2,1,0:T(8,128)S(1)}, u32[]{:S(2)}, u32[]{:S(2)}) collective-permute-start(f32[3,128,128]{2,1,0:T(8,128)} %get-tuple-element.69), channel_id=1, source_target_pairs={{0,4},{4,0},{8,12},{12,8},{16,20},{20,16},{24,28},{28,24},{1,5},{5... | collective-permute-start | bytes 589832 | tf_op jit(solution)/shard_map/ppermute | solution.py:538
  28.9 1.6 %collective-permute-start.3 = (f32[3,128,128]{2,1,0:T(8,128)}, f32[3,128,128]{2,1,0:T(8,128)S(1)}, u32[]{:S(2)}, u32[]{:S(2)}) collective-permute-start(f32[3,128,128]{2,1,0:T(8,128)} %get-tuple-element.70), channel_id=1, source_target_pairs={{0,8},{4,12},{8,0},{12,4},{16,24},{20,28},{24,16},{28,20},{1,9},{5... | collective-permute-start | bytes 589832 | tf_op jit(solution)/shard_map/ppermute | solution.py:538
  30.5 1.9 %collective-permute-start.5 = (f32[3,128,128]{2,1,0:T(8,128)}, f32[3,128,128]{2,1,0:T(8,128)S(1)}, u32[]{:S(2)}, u32[]{:S(2)}) collective-permute-start(f32[3,128,128]{2,1,0:T(8,128)} %get-tuple-element.75), channel_id=1, source_target_pairs={{0,4},{4,0},{8,12},{12,8},{16,20},{20,16},{24,28},{28,24},{1,5},{5... | collective-permute-start | bytes 589832 | tf_op jit(solution)/shard_map/ppermute | solution.py:538
  32.4 0.8 density_split.1
  33.2 1.5 %collective-permute-start.1 = (f32[1,3,64,512]{3,2,1,0:T(8,128)}, f32[1,3,64,512]{3,2,1,0:T(8,128)S(1)}, u32[]{:S(2)}, u32[]{:S(2)}) collective-permute-start(f32[1,3,64,512]{3,2,1,0:T(8,128)} %get-tuple-element.67), channel_id=1, source_target_pairs={{0,2},{1,3},{2,0},{3,1},{4,6},{5,7},{6,4},{7,5},{8,10},{9,11},{10,... | collective-permute-start | bytes 1179656 | tf_op jit(solution)/shard_map/ppermute | solution.py:538
  35.6 1.6 %collective-permute-start.6 = (f32[3,128,128]{2,1,0:T(8,128)S(1)}, f32[3,128,128]{2,1,0:T(8,128)S(1)}, u32[]{:S(2)}, u32[]{:S(2)}) collective-permute-start(f32[3,128,128]{2,1,0:T(8,128)S(1)} %get-tuple-element.76), channel_id=1, source_target_pairs={{0,8},{4,12},{8,0},{12,4},{16,24},{20,28},{24,16},{28,20},{1,9},{5... | collective-permute-start | bytes 589832 | tf_op jit(solution)/shard_map/ppermute | solution.py:538
  37.2 1.1 collective-permute-start.7
  38.4 2.2 %collective-permute-done.4.refs_3_ = f32[3,128,128]{2,1,0:T(8,128)S(1)} collective-permute-done((f32[3,128,128]{2,1,0:T(8,128)S(1)}, f32[3,128,128]{2,1,0:T(8,128)S(1)}, u32[]{:S(2)}, u32[]{:S(2)}) %collective-permute-start.4) | collective-permute-done | bytes 196640 | tf_op jit(solution)/shard_map/ppermute | solution.py:538
  40.6 1.0 compose_0.1
  41.6 1.5 collective-permute-done.5.refs_1_
  43.0 2.3 %collective-permute-done.6.refs_2_ = f32[3,128,128]{2,1,0:T(8,128)S(1)} collective-permute-done((f32[3,128,128]{2,1,0:T(8,128)S(1)}, f32[3,128,128]{2,1,0:T(8,128)S(1)}, u32[]{:S(2)}, u32[]{:S(2)}) %collective-permute-start.6) | collective-permute-done | bytes 196640 | tf_op jit(solution)/shard_map/ppermute | solution.py:538
  45.3 3.2 %collective-permute-done.7.refs_3_ = f32[3,128,128]{2,1,0:T(8,128)S(1)} collective-permute-done((f32[3,128,128]{2,1,0:T(8,128)S(1)}, f32[3,128,128]{2,1,0:T(8,128)S(1)}, u32[]{:S(2)}, u32[]{:S(2)}) %collective-permute-start.7) | collective-permute-done | bytes 196640 | tf_op jit(solution)/shard_map/ppermute | solution.py:538
  48.5 1.0 compose_1.1
  49.5 0.8 density_parts.1
  50.3 6.0 %all-to-all-start = ((f32[8,3,8,512]{3,2,1,0:T(8,128)}), f32[8,3,8,512]{3,2,1,0:T(8,128)S(1)}, u32[]{:S(2)}, u32[]{:S(2)}) async-start(f32[8,3,8,512]{3,2,1,0:T(8,128)} %density_parts.1), calls=%async_computation | async-start | bytes 786432 | tf_op jit(solution)/shard_map/all_to_all | solution.py:660
  56.3 0.5 fusion.47
  56.9 1.2 multiply_reduce_fusion.1
  58.1 3.0 %collective-permute-start.8 = (f32[3,128,128]{2,1,0:T(8,128)S(1)}, f32[3,128,128]{2,1,0:T(8,128)S(1)}, u32[]{:S(2)}, u32[]{:S(2)}) collective-permute-start(f32[3,128,128]{2,1,0:T(8,128)S(1)} %get-tuple-element.81.refs_0_), channel_id=1, source_target_pairs={{0,16},{4,20},{8,24},{12,28},{16,0},{20,4},{24,8},{28,12},{1,17},{... | collective-permute-start | bytes 589832 | tf_op jit(solution)/shard_map/ppermute | solution.py:538
  61.2 1.2 pad_maximum_fusion.3.sums
  62.4 19.3 %collective-permute-done.8.refs_1_ = f32[3,128,128]{2,1,0:T(8,128)S(1)} collective-permute-done((f32[3,128,128]{2,1,0:T(8,128)S(1)}, f32[3,128,128]{2,1,0:T(8,128)S(1)}, u32[]{:S(2)}, u32[]{:S(2)}) %collective-permute-start.8) | collective-permute-done | bytes 196640 | tf_op jit(solution)/shard_map/ppermute | solution.py:538
  81.8 1.1 enter_0.1
  82.9 0.7 copy-done.13
  83.5 0.9 collective-permute-done.9.refs_1_
  84.4 1.0 enter_1.1
  85.5 1.3 density_totals.1
  86.8 3.8 %all-to-all-start.1 = ((f32[8,2,8,512]{3,2,1,0:T(8,128)}), f32[8,2,8,512]{3,2,1,0:T(8,128)S(1)}, u32[]{:S(2)}, u32[]{:S(2)}) async-start(f32[8,2,8,512]{3,2,1,0:T(8,128)} %get-tuple-element.99), calls=%async_computation.1 | async-start | bytes 524288 | tf_op jit(solution)/shard_map/all_to_all | solution.py:676
  90.7 2.0 %collective-permute-start.13 = (f32[3,128,128]{2,1,0:T(8,128)}, f32[3,128,128]{2,1,0:T(8,128)S(1)}, u32[]{:S(2)}, u32[]{:S(2)}) collective-permute-start(f32[3,128,128]{2,1,0:T(8,128)} %copy-done.13), channel_id=1, source_target_pairs={{0,4},{4,0},{8,12},{12,8},{16,20},{20,16},{24,28},{28,24},{1,5},{5... | collective-permute-start | bytes 589832 | tf_op jit(solution)/shard_map/ppermute | solution.py:538
  92.7 1.5 collective-permute-start.14
  94.3 5.0 %collective-permute-done.13.refs_1_ = f32[3,128,128]{2,1,0:T(8,128)S(1)} collective-permute-done((f32[3,128,128]{2,1,0:T(8,128)}, f32[3,128,128]{2,1,0:T(8,128)S(1)}, u32[]{:S(2)}, u32[]{:S(2)}) %collective-permute-start.13) | collective-permute-done | bytes 196640 | tf_op jit(solution)/shard_map/ppermute | solution.py:538
  99.3 3.4 %collective-permute-done.14.refs_2_ = f32[3,128,128]{2,1,0:T(8,128)S(1)} collective-permute-done((f32[3,128,128]{2,1,0:T(8,128)}, f32[3,128,128]{2,1,0:T(8,128)S(1)}, u32[]{:S(2)}, u32[]{:S(2)}) %collective-permute-start.14) | collective-permute-done | bytes 196640 | tf_op jit(solution)/shard_map/ppermute | solution.py:538
  102.8 3.4 %collective-permute-done.15.refs_3_ = f32[3,128,128]{2,1,0:T(8,128)S(1)} collective-permute-done((f32[3,128,128]{2,1,0:T(8,128)}, f32[3,128,128]{2,1,0:T(8,128)S(1)}, u32[]{:S(2)}, u32[]{:S(2)}) %collective-permute-start.15) | collective-permute-done | bytes 196640 | tf_op jit(solution)/shard_map/ppermute | solution.py:538
  106.2 1.6 %copy-done.3 = f32[32,8,16,128]{3,2,1,0:T(8,128)S(1)} copy-done((f32[32,8,16,128]{3,2,1,0:T(8,128)S(1)}, f32[32,8,16,128]{3,2,1,0:T(8,128)}, u32[]{:S(2)}) %copy-start.3) | copy-done | bytes 2097176
  107.8 2.9 %inflow_0.1.refs_4_ = f32[64,8,16,128]{3,2,1,0:T(8,128)} custom-call(s32[2]{0:T(128)S(1)} %pad_add_fusion.1.refs_0_.meta, f32[10,64]{1,0:T(8,128)S(1)} %stack.141.refs_1_.floats, s32[5,64]{1,0:T(8,128)S(1)} %stack.148.refs_2_.ints, f32[32,8,16,128]{3,2,1,0:T(8,128)S(1)} %copy-done.3, f32[3,128,128]{2,1,0:T(8,128)S(1)} %get-tuple-element.101.refs_0_, ...), custom_call_target="tpu_custom_call" | custom-call | tf_op jit(solution)/shard_map/inflow_0/pallas_call | solution.py:623
  110.7 1.0 kelvins.1.refs_0_
  111.8 1.6 %collective-permute-start.16 = (f32[136,512]{1,0:T(8,128)S(1)}, f32[136,512]{1,0:T(8,128)S(1)}, u32[]{:S(2)}, u32[]{:S(2)}) collective-permute-start(f32[136,512]{1,0:T(8,128)S(1)} %kelvins.1.refs_0_), channel_id=1, source_target_pairs={{0,2},{1,3},{2,0},{3,1},{4,6},{5,7},{6,4},{7,5},{8,10},{9,11},{10,... | collective-permute-start | bytes 835592 | tf_op jit(solution)/shard_map/ppermute | solution.py:538
  113.4 0.2 multiply_reduce_fusion.3
  113.7 5.4 %collective-permute-done.16.refs_1_ = f32[136,512]{1,0:T(8,128)S(1)} collective-permute-done((f32[136,512]{1,0:T(8,128)S(1)}, f32[136,512]{1,0:T(8,128)S(1)}, u32[]{:S(2)}, u32[]{:S(2)}) %collective-permute-start.16) | collective-permute-done | bytes 278560 | tf_op jit(solution)/shard_map/ppermute | solution.py:538
  119.4 0.1 fusion.14
  119.6 2.0 %collective-permute-start.10 = (f32[3,128,128]{2,1,0:T(8,128)}, f32[3,128,128]{2,1,0:T(8,128)S(1)}, u32[]{:S(2)}, u32[]{:S(2)}) collective-permute-start(f32[3,128,128]{2,1,0:T(8,128)} %copy-done.10), channel_id=1, source_target_pairs={{0,4},{4,0},{8,12},{12,8},{16,20},{20,16},{24,28},{28,24},{1,5},{5... | collective-permute-start | bytes 589832 | tf_op jit(solution)/shard_map/ppermute | solution.py:538
  121.6 1.5 %collective-permute-start.12 = (f32[3,128,128]{2,1,0:T(8,128)}, f32[3,128,128]{2,1,0:T(8,128)S(1)}, u32[]{:S(2)}, u32[]{:S(2)}) collective-permute-start(f32[3,128,128]{2,1,0:T(8,128)} %copy-done.8), channel_id=1, source_target_pairs={{0,12},{4,8},{8,4},{12,0},{16,28},{20,24},{24,20},{28,16},{1,13},{... | collective-permute-start | bytes 589832 | tf_op jit(solution)/shard_map/ppermute | solution.py:538
  123.3 4.1 %collective-permute-done.10.refs_1_ = f32[3,128,128]{2,1,0:T(8,128)S(1)} collective-permute-done((f32[3,128,128]{2,1,0:T(8,128)}, f32[3,128,128]{2,1,0:T(8,128)S(1)}, u32[]{:S(2)}, u32[]{:S(2)}) %collective-permute-start.10) | collective-permute-done | bytes 196640 | tf_op jit(solution)/shard_map/ppermute | solution.py:538
  127.4 2.2 %collective-permute-done.11.refs_2_ = f32[3,128,128]{2,1,0:T(8,128)S(1)} collective-permute-done((f32[3,128,128]{2,1,0:T(8,128)}, f32[3,128,128]{2,1,0:T(8,128)S(1)}, u32[]{:S(2)}, u32[]{:S(2)}) %collective-permute-start.11) | collective-permute-done | bytes 196640 | tf_op jit(solution)/shard_map/ppermute | solution.py:538
  129.5 3.3 %collective-permute-done.12.refs_3_ = f32[3,128,128]{2,1,0:T(8,128)S(1)} collective-permute-done((f32[3,128,128]{2,1,0:T(8,128)}, f32[3,128,128]{2,1,0:T(8,128)S(1)}, u32[]{:S(2)}, u32[]{:S(2)}) %collective-permute-start.12) | collective-permute-done | bytes 196640 | tf_op jit(solution)/shard_map/ppermute | solution.py:538
  132.9 0.9 copy-done.7
  133.8 2.9 %inflow_1.1.inflown = f32[64,8,16,128]{3,2,1,0:T(8,128)} custom-call(s32[2]{0:T(128)S(1)} %pad_add_fusion.1.refs_0_.meta, f32[10,64]{1,0:T(8,128)S(1)} %stack.141.refs_1_.floats, s32[5,64]{1,0:T(8,128)S(1)} %stack.148.refs_2_.ints, f32[32,8,16,128]{3,2,1,0:T(8,128)S(1)} %copy-done.1, f32[3,128,128]{2,1,0:T(8,128)S(1)} %copy-done.7, ...), custom_call_target="tpu_custom_call", output_to_operand_aliasing={{}: (8, {})} | custom-call | tf_op jit(solution)/shard_map/inflow_1/pallas_call | solution.py:623
  136.7 2.2 %copy-done = f32[64,8,16,128]{3,2,1,0:T(8,128)S(1)} copy-done((f32[64,8,16,128]{3,2,1,0:T(8,128)S(1)}, f32[64,8,16,128]{3,2,1,0:T(8,128)}, u32[]{:S(2)}) %copy-start) | copy-done | bytes 4194328
  138.9 8.8 %final_energy.1 = (f32[64,8,16,128]{3,2,1,0:T(8,128)}, f32[128,128]{1,0:T(8,128)}) custom-call(s32[2]{0:T(128)S(1)} %pad_add_fusion.1.refs_0_.meta, f32[10,64]{1,0:T(8,128)S(1)} %stack.141.refs_1_.floats, s32[5,64]{1,0:T(8,128)S(1)} %stack.148.refs_2_.ints, f32[6,16]{1,0:T(8,128)S(1)} %copy.57.refs_3_.kinds, f32[2]{0:T(128)S(1)} %pad_maximum_fusion.3.sums, ...), custom_call_target="tpu_custom_call" | custom-call | tf_op jit(solution)/shard_map/final_energy/pallas_call | solution.py:691
  (97 shorter events, 2.6 us)
Async XLA Ops:
  6.1 0.8 copy-start.4
  6.9 0.8 copy-start.5
  14.8 1.3 copy-start.2
  25.9 6.5 %collective-permute-start = (f32[2,3,64,512]{3,2,1,0:T(8,128)S(1)}, f32[2,3,64,512]{3,2,1,0:T(8,128)S(1)}, u32[]{:S(2)}, u32[]{:S(2)}) collective-permute-start(f32[2,3,64,512]{3,2,1,0:T(8,128)S(1)} %get-tuple-element.65), channel_id=1, source_target_pairs={{0,1},{1,0},{2,3},{3,2},{4,5},{5,4},{6,7},{7,6},{8,9},{9,8},{10,11... | collective-permute-start | bytes 2359304 | tf_op jit(solution)/shard_map/ppermute | solution.py:538
  26.3 9.3 %collective-permute-start.2 = (f32[3,128,128]{2,1,0:T(8,128)}, f32[3,128,128]{2,1,0:T(8,128)S(1)}, u32[]{:S(2)}, u32[]{:S(2)}) collective-permute-start(f32[3,128,128]{2,1,0:T(8,128)} %get-tuple-element.69), channel_id=1, source_target_pairs={{0,4},{4,0},{8,12},{12,8},{16,20},{20,16},{24,28},{28,24},{1,5},{5... | collective-permute-start | bytes 589832 | tf_op jit(solution)/shard_map/ppermute | solution.py:538
  28.9 8.3 %collective-permute-start.3 = (f32[3,128,128]{2,1,0:T(8,128)}, f32[3,128,128]{2,1,0:T(8,128)S(1)}, u32[]{:S(2)}, u32[]{:S(2)}) collective-permute-start(f32[3,128,128]{2,1,0:T(8,128)} %get-tuple-element.70), channel_id=1, source_target_pairs={{0,8},{4,12},{8,0},{12,4},{16,24},{20,28},{24,16},{28,20},{1,9},{5... | collective-permute-start | bytes 589832 | tf_op jit(solution)/shard_map/ppermute | solution.py:538
  30.5 10.1 %collective-permute-start.4 = (f32[3,128,128]{2,1,0:T(8,128)S(1)}, f32[3,128,128]{2,1,0:T(8,128)S(1)}, u32[]{:S(2)}, u32[]{:S(2)}) collective-permute-start(f32[3,128,128]{2,1,0:T(8,128)S(1)} %get-tuple-element.71), channel_id=1, source_target_pairs={{0,12},{4,8},{8,4},{12,0},{16,28},{20,24},{24,20},{28,16},{1,13},{... | collective-permute-start | bytes 589832 | tf_op jit(solution)/shard_map/ppermute | solution.py:538
  30.5 12.6 %collective-permute-start.5 = (f32[3,128,128]{2,1,0:T(8,128)}, f32[3,128,128]{2,1,0:T(8,128)S(1)}, u32[]{:S(2)}, u32[]{:S(2)}) collective-permute-start(f32[3,128,128]{2,1,0:T(8,128)} %get-tuple-element.75), channel_id=1, source_target_pairs={{0,4},{4,0},{8,12},{12,8},{16,20},{20,16},{24,28},{28,24},{1,5},{5... | collective-permute-start | bytes 589832 | tf_op jit(solution)/shard_map/ppermute | solution.py:538
  33.2 16.3 %collective-permute-start.1 = (f32[1,3,64,512]{3,2,1,0:T(8,128)}, f32[1,3,64,512]{3,2,1,0:T(8,128)S(1)}, u32[]{:S(2)}, u32[]{:S(2)}) collective-permute-start(f32[1,3,64,512]{3,2,1,0:T(8,128)} %get-tuple-element.67), channel_id=1, source_target_pairs={{0,2},{1,3},{2,0},{3,1},{4,6},{5,7},{6,4},{7,5},{8,10},{9,11},{10,... | collective-permute-start | bytes 1179656 | tf_op jit(solution)/shard_map/ppermute | solution.py:538
  35.2 55.4 %copy-start.16 = (f32[16]{0:T(128)}, f32[16]{0:T(128)S(1)}, u32[]{:S(2)}) copy-start(f32[16]{0:T(128)S(1)} %squeeze.4) | copy-start | bytes 196
  35.6 55.1 %copy-start.18 = (f32[16]{0:T(128)}, f32[16]{0:T(128)S(1)}, u32[]{:S(2)}) copy-start(f32[16]{0:T(128)S(1)} %squeeze.5) | copy-start | bytes 196
  35.6 9.7 %collective-permute-start.6 = (f32[3,128,128]{2,1,0:T(8,128)S(1)}, f32[3,128,128]{2,1,0:T(8,128)S(1)}, u32[]{:S(2)}, u32[]{:S(2)}) collective-permute-start(f32[3,128,128]{2,1,0:T(8,128)S(1)} %get-tuple-element.76), channel_id=1, source_target_pairs={{0,8},{4,12},{8,0},{12,4},{16,24},{20,28},{24,16},{28,20},{1,9},{5... | collective-permute-start | bytes 589832 | tf_op jit(solution)/shard_map/ppermute | solution.py:538
  37.2 11.3 %collective-permute-start.7 = (f32[3,128,128]{2,1,0:T(8,128)S(1)}, f32[3,128,128]{2,1,0:T(8,128)S(1)}, u32[]{:S(2)}, u32[]{:S(2)}) collective-permute-start(f32[3,128,128]{2,1,0:T(8,128)S(1)} %get-tuple-element.77), channel_id=1, source_target_pairs={{0,12},{4,8},{8,4},{12,0},{16,28},{20,24},{24,20},{28,16},{1,13},{... | collective-permute-start | bytes 589832 | tf_op jit(solution)/shard_map/ppermute | solution.py:538
  50.3 35.2 %all-to-all-start = ((f32[8,3,8,512]{3,2,1,0:T(8,128)}), f32[8,3,8,512]{3,2,1,0:T(8,128)S(1)}, u32[]{:S(2)}, u32[]{:S(2)}) async-start(f32[8,3,8,512]{3,2,1,0:T(8,128)} %density_parts.1), calls=%async_computation | async-start | bytes 786432 | tf_op jit(solution)/shard_map/all_to_all | solution.py:660
  58.1 23.7 %collective-permute-start.8 = (f32[3,128,128]{2,1,0:T(8,128)S(1)}, f32[3,128,128]{2,1,0:T(8,128)S(1)}, u32[]{:S(2)}, u32[]{:S(2)}) collective-permute-start(f32[3,128,128]{2,1,0:T(8,128)S(1)} %get-tuple-element.81.refs_0_), channel_id=1, source_target_pairs={{0,16},{4,20},{8,24},{12,28},{16,0},{20,4},{24,8},{28,12},{1,17},{... | collective-permute-start | bytes 589832 | tf_op jit(solution)/shard_map/ppermute | solution.py:538
  61.1 23.3 %collective-permute-start.9 = (f32[3,128,128]{2,1,0:T(8,128)S(1)}, f32[3,128,128]{2,1,0:T(8,128)S(1)}, u32[]{:S(2)}, u32[]{:S(2)}) collective-permute-start(f32[3,128,128]{2,1,0:T(8,128)S(1)} %get-tuple-element.90.refs_0_), channel_id=1, source_target_pairs={{0,16},{4,20},{8,24},{12,28},{16,0},{20,4},{24,8},{28,12},{1,17},{... | collective-permute-start | bytes 589832 | tf_op jit(solution)/shard_map/ppermute | solution.py:538
  82.8 0.7 copy-start.13
  83.5 0.9 copy-start.11
  83.5 0.9 copy-start.12
  85.5 1.4 copy-start.8
  85.5 1.3 copy-start.9
  85.5 25.3 %copy-start.6 = (f32[3,128,128]{2,1,0:T(8,128)}, f32[3,128,128]{2,1,0:T(8,128)S(1)}, u32[]{:S(2)}) copy-start(f32[3,128,128]{2,1,0:T(8,128)S(1)} %get-tuple-element.95.refs_0_) | copy-start | bytes 589828
  85.5 26.3 %copy-start.10 = (f32[3,128,128]{2,1,0:T(8,128)}, f32[3,128,128]{2,1,0:T(8,128)S(1)}, u32[]{:S(2)}) copy-start(f32[3,128,128]{2,1,0:T(8,128)S(1)} %get-tuple-element.96) | copy-start | bytes 589828
  86.8 26.6 %copy-start.14 = (f32[16]{0:T(128)S(1)}, f32[16]{0:T(128)}, u32[]{:S(2)}) copy-start(f32[16]{0:T(128)} %get-tuple-element.177) | copy-start | bytes 196
  86.8 26.6 %copy-start.15 = (f32[16]{0:T(128)S(1)}, f32[16]{0:T(128)}, u32[]{:S(2)}) copy-start(f32[16]{0:T(128)} %get-tuple-element.178) | copy-start | bytes 196
  86.8 46.0 %copy-start.1 = (f32[32,8,16,128]{3,2,1,0:T(8,128)S(1)}, f32[32,8,16,128]{3,2,1,0:T(8,128)}, u32[]{:S(2)}) copy-start(f32[32,8,16,128]{3,2,1,0:T(8,128)} %get-tuple-element.63.swept) | copy-start | bytes 6291460
  86.8 23.9 %all-to-all-start.1 = ((f32[8,2,8,512]{3,2,1,0:T(8,128)}), f32[8,2,8,512]{3,2,1,0:T(8,128)S(1)}, u32[]{:S(2)}, u32[]{:S(2)}) async-start(f32[8,2,8,512]{3,2,1,0:T(8,128)} %get-tuple-element.99), calls=%async_computation.1 | async-start | bytes 524288 | tf_op jit(solution)/shard_map/all_to_all | solution.py:676
  90.7 8.6 %collective-permute-start.13 = (f32[3,128,128]{2,1,0:T(8,128)}, f32[3,128,128]{2,1,0:T(8,128)S(1)}, u32[]{:S(2)}, u32[]{:S(2)}) collective-permute-start(f32[3,128,128]{2,1,0:T(8,128)} %copy-done.13), channel_id=1, source_target_pairs={{0,4},{4,0},{8,12},{12,8},{16,20},{20,16},{24,28},{28,24},{1,5},{5... | collective-permute-start | bytes 589832 | tf_op jit(solution)/shard_map/ppermute | solution.py:538
  92.7 10.1 %collective-permute-start.14 = (f32[3,128,128]{2,1,0:T(8,128)}, f32[3,128,128]{2,1,0:T(8,128)S(1)}, u32[]{:S(2)}, u32[]{:S(2)}) collective-permute-start(f32[3,128,128]{2,1,0:T(8,128)} %copy-done.12), channel_id=1, source_target_pairs={{0,8},{4,12},{8,0},{12,4},{16,24},{20,28},{24,16},{28,20},{1,9},{5... | collective-permute-start | bytes 589832 | tf_op jit(solution)/shard_map/ppermute | solution.py:538
  94.2 12.0 %collective-permute-start.15 = (f32[3,128,128]{2,1,0:T(8,128)}, f32[3,128,128]{2,1,0:T(8,128)S(1)}, u32[]{:S(2)}, u32[]{:S(2)}) collective-permute-start(f32[3,128,128]{2,1,0:T(8,128)} %copy-done.11), channel_id=1, source_target_pairs={{0,12},{4,8},{8,4},{12,0},{16,28},{20,24},{24,20},{28,16},{1,13},{... | collective-permute-start | bytes 589832 | tf_op jit(solution)/shard_map/ppermute | solution.py:538
  106.2 1.6 %copy-start.3 = (f32[32,8,16,128]{3,2,1,0:T(8,128)S(1)}, f32[32,8,16,128]{3,2,1,0:T(8,128)}, u32[]{:S(2)}) copy-start(f32[32,8,16,128]{3,2,1,0:T(8,128)} %copy-done.2) | copy-start | bytes 6291460
  107.8 11.3 %copy-start.17 = (f32[16]{0:T(128)S(1)}, f32[16]{0:T(128)}, u32[]{:S(2)}) copy-start(f32[16]{0:T(128)} %copy-done.16) | copy-start | bytes 196
  107.8 11.5 %copy-start.19 = (f32[16]{0:T(128)S(1)}, f32[16]{0:T(128)}, u32[]{:S(2)}) copy-start(f32[16]{0:T(128)} %copy-done.18) | copy-start | bytes 196
  111.8 7.3 %collective-permute-start.16 = (f32[136,512]{1,0:T(8,128)S(1)}, f32[136,512]{1,0:T(8,128)S(1)}, u32[]{:S(2)}, u32[]{:S(2)}) collective-permute-start(f32[136,512]{1,0:T(8,128)S(1)} %kelvins.1.refs_0_), channel_id=1, source_target_pairs={{0,2},{1,3},{2,0},{3,1},{4,6},{5,7},{6,4},{7,5},{8,10},{9,11},{10,... | collective-permute-start | bytes 835592 | tf_op jit(solution)/shard_map/ppermute | solution.py:538
  113.6 23.1 %collective-permute-start.17 = (f32[136,512]{1,0:T(8,128)S(1)}, f32[136,512]{1,0:T(8,128)S(1)}, u32[]{:S(2)}, u32[]{:S(2)}) collective-permute-start(f32[136,512]{1,0:T(8,128)S(1)} %kelvins.1.refs_0_), channel_id=1, source_target_pairs={{0,1},{1,0},{2,3},{3,2},{4,5},{5,4},{6,7},{7,6},{8,9},{9,8},{10,11... | collective-permute-start | bytes 835592 | tf_op jit(solution)/shard_map/ppermute | solution.py:538
  119.1 17.6 %collective-permute-start.18 = (f32[136,512]{1,0:T(8,128)S(1)}, f32[136,512]{1,0:T(8,128)S(1)}, u32[]{:S(2)}, u32[]{:S(2)}) collective-permute-start(f32[136,512]{1,0:T(8,128)S(1)} %collective-permute-done.16.refs_1_), channel_id=1, source_target_pairs={{0,1},{1,0},{2,3},{3,2},{4,5},{5,4},{6,7},{7,6},{8,9},{9,8},{10,11... | collective-permute-start | bytes 835592 | tf_op jit(solution)/shard_map/ppermute | solution.py:538
  119.6 7.8 %collective-permute-start.10 = (f32[3,128,128]{2,1,0:T(8,128)}, f32[3,128,128]{2,1,0:T(8,128)S(1)}, u32[]{:S(2)}, u32[]{:S(2)}) collective-permute-start(f32[3,128,128]{2,1,0:T(8,128)} %copy-done.10), channel_id=1, source_target_pairs={{0,4},{4,0},{8,12},{12,8},{16,20},{20,16},{24,28},{28,24},{1,5},{5... | collective-permute-start | bytes 589832 | tf_op jit(solution)/shard_map/ppermute | solution.py:538
  121.6 7.9 %collective-permute-start.11 = (f32[3,128,128]{2,1,0:T(8,128)}, f32[3,128,128]{2,1,0:T(8,128)S(1)}, u32[]{:S(2)}, u32[]{:S(2)}) collective-permute-start(f32[3,128,128]{2,1,0:T(8,128)} %copy-done.9), channel_id=1, source_target_pairs={{0,8},{4,12},{8,0},{12,4},{16,24},{20,28},{24,16},{28,20},{1,9},{5... | collective-permute-start | bytes 589832 | tf_op jit(solution)/shard_map/ppermute | solution.py:538
  121.6 11.2 %collective-permute-start.12 = (f32[3,128,128]{2,1,0:T(8,128)}, f32[3,128,128]{2,1,0:T(8,128)S(1)}, u32[]{:S(2)}, u32[]{:S(2)}) collective-permute-start(f32[3,128,128]{2,1,0:T(8,128)} %copy-done.8), channel_id=1, source_target_pairs={{0,12},{4,8},{8,4},{12,0},{16,28},{20,24},{24,20},{28,16},{1,13},{... | collective-permute-start | bytes 589832 | tf_op jit(solution)/shard_map/ppermute | solution.py:538
  132.9 0.9 copy-start.7
  136.7 2.2 %copy-start = (f32[64,8,16,128]{3,2,1,0:T(8,128)S(1)}, f32[64,8,16,128]{3,2,1,0:T(8,128)}, u32[]{:S(2)}) copy-start(f32[64,8,16,128]{3,2,1,0:T(8,128)} %inflow_1.1.inflown) | copy-start | bytes 12582916

commit v6 on v5

--- a/solution.py
+++ b/solution.py
@@ -25,7 +25,8 @@
 
 SMEM = pl.BlockSpec(memory_space=pltpu.SMEM)
 VMEM = pl.BlockSpec(memory_space=pltpu.VMEM)
-PARAMS = pltpu.CompilerParams(vmem_limit_bytes=48 * 1024 * 1024)
+PARAMS = pltpu.CompilerParams(vmem_limit_bytes=32 * 1024 * 1024)
+LARGE = pltpu.CompilerParams(vmem_limit_bytes=60 * 1024 * 1024)
 ACROSS = math.cos(math.pi / 8) + math.sin(math.pi / 8)
 
 
@@ -582,7 +583,7 @@
                 scratch(KINDS, depth, width_y, width_z),
                 scratch(depth, width_y, width_z),
             ],
-            compiler_params=PARAMS,
+            compiler_params=LARGE,
             name=f"sweeps_{half}",
         )(meta, floats, ints, kinds, incoming_occupation, flag, given, *extra)
 
@@ -631,36 +632,36 @@
             out_shape=slot_shape,
             scratch_shapes=[scratch(group, *face)],
             input_output_aliases={4 + group: 0} if energy else {},
-            compiler_params=PARAMS,
+            compiler_params=LARGE,
             name=f"inflow_{half}",
         )(meta, floats, ints, swept, *received, *energy)
 
     swept_0, *rest = sweeps(0, [])
-    received_0 = around_group(rest[:group])
-    quarter, *older = rest[group:]
+    received_0, (quarter, *older) = around_group(rest[:group]), rest[group:]
     swept_1, *rest = sweeps(1, [matrix] + older)
-    keep, send = rest[group:]
-
+    faces_1, (keep, send), received_0 = tied((rest[:group], rest[group:], received_0))
+
+    composite_0, effective_0 = compose(0, received_0)
+    composites_0 = across_groups(composite_0)
     by = 1
     other = swap(send, "mode", by)
-    received_1 = around_group(rest[:group])
+    received_1 = around_group(faces_1)
     while 2 * by < modes:
         by *= 2
         now = (modes // (2 * by), ITERS, all_x, lanes)
         keep, send = call(split_kernel, "density_split", [VMEM] * 2, [shape(*now)] * 2, keep, other)
         other = swap(send, "mode", by)
-    composite_0, effective_0 = compose(0, received_0)
-    other, composite_0 = tied((other, composite_0))
-    composites_0 = across_groups(composite_0)
+    other, received_1, composites_0 = tied((other, received_1, composites_0))
+
     (parts,) = call(
         functools.partial(parts_kernel, depth), "density_parts", [VMEM] * 2, [shape(slabs, ITERS, depth, lanes)], keep, other
     )
+    entering_0 = around_group(enter(0, effective_0, composites_0))
     composite_1, effective_1 = compose(1, received_1)
-    parts, composite_1 = tied((parts, composite_1))
+    composites_1 = across_groups(composite_1)
     parts = lax.all_to_all(parts, "slab", 0, 0)
-    composites_1 = across_groups(composite_1)
-    entering_0 = enter(0, effective_0, composites_0)
-    parts, entering_0 = tied((parts, entering_0))
+    parts, entering_0, composites_1 = tied((parts, entering_0, composites_1))
+
     copies, late = call(
         totals_kernel,
         "density_totals",
@@ -670,14 +671,12 @@
         parts,
         quarter,
     )
-    entering_0 = around_group(entering_0)
-    entering_1 = enter(1, effective_1, composites_1)
-    copies, entering_1 = tied((copies, entering_1))
+    entering_1 = around_group(enter(1, effective_1, composites_1))
     gathered = lax.all_to_all(copies, "slab", 0, 0)
-    entering_1 = around_group(entering_1)
+    energy = add_inflow(0, swept_0, entering_0, [])
+    gathered, entering_1, energy = tied((gathered, entering_1, energy))
+
     pack_shape = shape(2 * all_x + depth, lanes)
-    energy = add_inflow(0, swept_0, entering_0, [])
-    gathered, energy = tied((gathered, energy))
     (packed,) = call(
         functools.partial(kelvins_kernel, depth), "kelvins", [SMEM] + [VMEM] * 3, [pack_shape], sums, gathered, late, everywhere
     )
@@ -702,7 +701,7 @@
         + [scratch(2 * KINDS * width_y, width_z)] * 3
         + [scratch(2 * KINDS, depth, width_y, width_z)] * 2
         + [scratch(cells, width_z)] * 2,
-        compiler_params=PARAMS,
+        compiler_params=LARGE,
         name="final_energy",
     )(meta, floats, ints, kinds, sums, energy, *packs, first_matrix, second_matrix)
     return energy, kelvin.reshape(depth, width_y, width_z)

time: 148 us -> 136 us (0.919)
  waiting for transfers between devices: 56.2 us -> 35.7 us
  Pallas kernels: 39.4 us -> 46.9 us
  other arithmetic: 8.53 us -> 10.6 us
  local copies, waits for them, and re-layouts: 10.2 us -> 8.69 us
    ppermute x19, waiting for transfers between devices: 56.2 us -> 35.7 us  [swap(): lax.ppermute(array, axis, [(i, i ^ by) for i in range(lax.axis_size(axis))])]
    unnamed x40, local copies, waits for them, and re-layouts: 8.42 us -> 4.61 us
    pallas_call x2, Pallas kernels: 5.87 us -> 8.78 us  [add_inflow(): pl.pallas_call(functools.partial(inflow_kernel, half, (block, depth, grou...]
    pallas_call x2, Pallas kernels: 16.8 us -> 19.4 us  [sweeps(): pl.pallas_call(functools.partial(sweeps_kernel, half, (block, depth, widt...]
    pallas_call x1, Pallas kernels: 8.77 us -> 10.8 us  [local(): pl.pallas_call(functools.partial(final_kernel, (block, depth, width_y, wi...]
  transfers between devices with their start and end apart: 21 -> 21, of which waited for: 13 -> 9; matrix products, arithmetic and copies ran while one was open for 3% -> 5% of each run, Pallas kernels for 7% -> 18%
where the time goes in v6:
time: 136 us
  Pallas kernels  46.9 us (34%)
  waiting for transfers between devices  35.7 us (26%)
  starting transfers between devices  32.7 us (24%)
  other arithmetic  10.6 us (8%)
  local copies, waits for them, and re-layouts  8.69 us (6%)
    ppermute x19, waiting for transfers between devices, swap(): lax.ppermute(array, axis, [(i, i ^ by) for i in range(lax.axis_size(axis))])  35.7 us
    ppermute x19, starting transfers between devices, swap(): lax.ppermute(array, axis, [(i, i ^ by) for i in range(lax.axis_size(axis))])  23.4 us
    pallas_call x2, Pallas kernels, sweeps(): pl.pallas_call(functools.partial(sweeps_kernel, half, (block, depth, widt...  19.4 us
    pallas_call x1, Pallas kernels, local(): pl.pallas_call(functools.partial(final_kernel, (block, depth, width_y, wi...  10.8 us
    pallas_call x2, Pallas kernels, add_inflow(): pl.pallas_call(functools.partial(inflow_kernel, half, (block, depth, grou...  8.78 us
    pallas_call x8, Pallas kernels, call(): pl.pallas_call(kernel, in_specs=in_specs, out_specs=[VMEM] * len(out_shap...  7.94 us
    all_to_all x1, starting transfers between devices, local(): parts = lax.all_to_all(parts, 'slab', 0, 0)  5.85 us
    unnamed x40, local copies, waits for them, and re-layouts  4.61 us
  transfers between devices with their start and end apart: 21, of which 9 were waited for; matrix products, arithmetic and copies ran while one was open for 5% of the time, Pallas kernels for 18%

profile of v6, /device:TPU:0, one launch (start us, length us, event | category | flops | bytes accessed | tf_op | source)
XLA Modules:
  0.0 135.6 jit_solution(10809900940178420778)
XLA Ops:
  0.6 0.7 add_bitcast_fusion
  1.3 0.7 fusion.38
  2.0 0.8 select_reduce_fusion
  3.0 1.4 %fusion.45 = (f32[]{:T(128)}, f32[]{:T(128)}, f32[1,8]{1,0:T(1,128)S(1)}, f32[8]{0:T(128)S(1)}, f32[1,8]{1,0:T(1,128)S(1)}, /*index=5*/f32[1,8]{1,0:T(1,128)S(1)...) fusion(f32[8]{0:T(128)} %param.15, f32[8]{0:T(128)} %param.16, ...), kind=kLoop, calls=%fused_computation.146 | loop fusion | flops 134 | bytes 488 | tf_op jit(solution)/shard_map/reduce_sum | solution.py:527
  4.4 0.7 fusion.40
  5.2 0.1 copy.47
  5.3 0.7 copy.57.refs_3_.kinds
  5.9 0.6 pad_add_fusion.1.refs_0_.meta
  6.5 0.6 stack.148.refs_2_.ints
  7.1 1.2 stack.141.refs_1_.floats
  8.4 8.2 %sweeps_0.1 = (f32[32,8,16,128]{3,2,1,0:T(8,128)}, f32[3,128,128]{2,1,0:T(8,128)}, f32[3,128,128]{2,1,0:T(8,128)}, f32[3,128,128]{2,1,0:T(8,128)}, f32[3,128,128...) custom-call(s32[2]{0:T(128)} %pad_add_fusion.1.refs_0_.meta, ...), custom_call_target="tpu_custom_call" | custom-call | tf_op jit(solution)/shard_map/sweeps_0/pallas_call | solution.py:572
  16.5 3.0 %collective-permute-start = (f32[3,128,128]{2,1,0:T(8,128)}, f32[3,128,128]{2,1,0:T(8,128)S(1)}, u32[]{:S(2)}, u32[]{:S(2)}) collective-permute-start(f32[3,128,128]{2,1,0:T(8,128)} %get-tuple-element.85), channel_id=1, source_target_pairs={{0,4},{4,0},{8,12},{12,8},{16,20},{20,16},{24,28},{28,24},{1,5},{5... | collective-permute-start | bytes 589832 | tf_op jit(solution)/shard_map/ppermute | solution.py:539
  19.6 1.6 %collective-permute-start.1 = (f32[3,128,128]{2,1,0:T(8,128)}, f32[3,128,128]{2,1,0:T(8,128)S(1)}, u32[]{:S(2)}, u32[]{:S(2)}) collective-permute-start(f32[3,128,128]{2,1,0:T(8,128)} %get-tuple-element.86), channel_id=1, source_target_pairs={{0,8},{4,12},{8,0},{12,4},{16,24},{20,28},{24,16},{28,20},{1,9},{5... | collective-permute-start | bytes 589832 | tf_op jit(solution)/shard_map/ppermute | solution.py:539
  21.2 0.1 reshape.297
  21.4 0.1 broadcast_in_dim.124
  21.5 0.1 fusion.6
  21.7 0.7 pad_maximum_fusion.refs_7_
  22.4 11.2 %sweeps_1.1 = (f32[32,8,16,128]{3,2,1,0:T(8,128)}, f32[3,128,128]{2,1,0:T(8,128)}, f32[3,128,128]{2,1,0:T(8,128)}, f32[3,128,128]{2,1,0:T(8,128)}, f32[3,128,128...) custom-call(s32[2]{0:T(128)} %pad_add_fusion.1.refs_0_.meta, f32[10,64]{1,0:T(8,128)} %stack.141.refs_1_.floats, ...), custom_call_target="tpu_custom_call" | custom-call | tf_op jit(solution)/shard_map/sweeps_1/pallas_call | solution.py:572
  33.7 2.5 %collective-permute-done.3.other = f32[2,3,64,512]{3,2,1,0:T(8,128)S(1)} collective-permute-done((f32[2,3,64,512]{3,2,1,0:T(8,128)}, f32[2,3,64,512]{3,2,1,0:T(8,128)S(1)}, u32[]{:S(2)}, u32[]{:S(2)}) %collective-permute-start.3) | collective-permute-done | bytes 786464 | tf_op jit(solution)/shard_map/ppermute | solution.py:539
  36.2 1.1 copy-done.2
  37.4 0.8 density_split.1
  38.2 1.9 %collective-permute-start.4 = (f32[1,3,64,512]{3,2,1,0:T(8,128)}, f32[1,3,64,512]{3,2,1,0:T(8,128)S(1)}, u32[]{:S(2)}, u32[]{:S(2)}) collective-permute-start(f32[1,3,64,512]{3,2,1,0:T(8,128)} %get-tuple-element.91), channel_id=1, source_target_pairs={{0,2},{1,3},{2,0},{3,1},{4,6},{5,7},{6,4},{7,5},{8,10},{9,11},{10,... | collective-permute-start | bytes 1179656 | tf_op jit(solution)/shard_map/ppermute | solution.py:539
  40.9 1.6 %collective-permute-start.5 = (f32[3,128,128]{2,1,0:T(8,128)}, f32[3,128,128]{2,1,0:T(8,128)S(1)}, u32[]{:S(2)}, u32[]{:S(2)}) collective-permute-start(f32[3,128,128]{2,1,0:T(8,128)} %get-tuple-element.93), channel_id=1, source_target_pairs={{0,4},{4,0},{8,12},{12,8},{16,20},{20,16},{24,28},{28,24},{1,5},{5... | collective-permute-start | bytes 589832 | tf_op jit(solution)/shard_map/ppermute | solution.py:539
  42.5 1.6 %collective-permute-start.6 = (f32[3,128,128]{2,1,0:T(8,128)}, f32[3,128,128]{2,1,0:T(8,128)S(1)}, u32[]{:S(2)}, u32[]{:S(2)}) collective-permute-start(f32[3,128,128]{2,1,0:T(8,128)} %get-tuple-element.94), channel_id=1, source_target_pairs={{0,8},{4,12},{8,0},{12,4},{16,24},{20,28},{24,16},{28,20},{1,9},{5... | collective-permute-start | bytes 589832 | tf_op jit(solution)/shard_map/ppermute | solution.py:539
  44.1 0.4 collective-permute-start.7
  44.5 1.0 compose_0.1
  45.5 2.7 %collective-permute-start.8 = (f32[3,128,128]{2,1,0:T(8,128)S(1)}, f32[3,128,128]{2,1,0:T(8,128)S(1)}, u32[]{:S(2)}, u32[]{:S(2)}) collective-permute-start(f32[3,128,128]{2,1,0:T(8,128)S(1)} %get-tuple-element.103.refs_0_), channel_id=1, source_target_pairs={{0,16},{4,20},{8,24},{12,28},{16,0},{20,4},{24,8},{28,12},{1,17},{... | collective-permute-start | bytes 589832 | tf_op jit(solution)/shard_map/ppermute | solution.py:539
  48.2 6.6 %collective-permute-done.6.refs_2_ = f32[3,128,128]{2,1,0:T(8,128)S(1)} collective-permute-done((f32[3,128,128]{2,1,0:T(8,128)}, f32[3,128,128]{2,1,0:T(8,128)S(1)}, u32[]{:S(2)}, u32[]{:S(2)}) %collective-permute-start.6) | collective-permute-done | bytes 196640 | tf_op jit(solution)/shard_map/ppermute | solution.py:539
  54.8 2.7 %collective-permute-done.7.refs_3_ = f32[3,128,128]{2,1,0:T(8,128)S(1)} collective-permute-done((f32[3,128,128]{2,1,0:T(8,128)}, f32[3,128,128]{2,1,0:T(8,128)S(1)}, u32[]{:S(2)}, u32[]{:S(2)}) %collective-permute-start.7) | collective-permute-done | bytes 196640 | tf_op jit(solution)/shard_map/ppermute | solution.py:539
  57.5 0.8 density_parts.1
  58.3 5.9 %all-to-all-start = ((f32[8,3,8,512]{3,2,1,0:T(8,128)}), f32[8,3,8,512]{3,2,1,0:T(8,128)S(1)}, u32[]{:S(2)}, u32[]{:S(2)}) async-start(f32[8,3,8,512]{3,2,1,0:T(8,128)} %density_parts.1), calls=%async_computation | async-start | bytes 786432 | tf_op jit(solution)/shard_map/all_to_all | solution.py:662
  64.2 1.2 multiply_reduce_fusion.1
  65.4 1.1 enter_0.1
  66.5 0.7 copy-done.7
  67.1 2.0 %collective-permute-start.9 = (f32[3,128,128]{2,1,0:T(8,128)S(1)}, f32[3,128,128]{2,1,0:T(8,128)S(1)}, u32[]{:S(2)}, u32[]{:S(2)}) collective-permute-start(f32[3,128,128]{2,1,0:T(8,128)S(1)} %get-tuple-element.106), channel_id=1, source_target_pairs={{0,4},{4,0},{8,12},{12,8},{16,20},{20,16},{24,28},{28,24},{1,5},{5... | collective-permute-start | bytes 589832 | tf_op jit(solution)/shard_map/ppermute | solution.py:539
  69.1 1.5 %collective-permute-start.10 = (f32[3,128,128]{2,1,0:T(8,128)S(1)}, f32[3,128,128]{2,1,0:T(8,128)S(1)}, u32[]{:S(2)}, u32[]{:S(2)}) collective-permute-start(f32[3,128,128]{2,1,0:T(8,128)S(1)} %get-tuple-element.107), channel_id=1, source_target_pairs={{0,8},{4,12},{8,0},{12,4},{16,24},{20,28},{24,16},{28,20},{1,9},{5... | collective-permute-start | bytes 589832 | tf_op jit(solution)/shard_map/ppermute | solution.py:539
  70.6 1.0 compose_1.1
  71.6 3.0 %collective-permute-start.12 = (f32[3,128,128]{2,1,0:T(8,128)S(1)}, f32[3,128,128]{2,1,0:T(8,128)S(1)}, u32[]{:S(2)}, u32[]{:S(2)}) collective-permute-start(f32[3,128,128]{2,1,0:T(8,128)S(1)} %get-tuple-element.118.refs_0_), channel_id=1, source_target_pairs={{0,16},{4,20},{8,24},{12,28},{16,0},{20,4},{24,8},{28,12},{1,17},{... | collective-permute-start | bytes 589832 | tf_op jit(solution)/shard_map/ppermute | solution.py:539
  74.6 1.4 %pad_maximum_fusion.3.sums = f32[2]{0:T(128)S(1)} fusion(f32[1]{0:T(128)} %bitcast.33, f32[1]{0:T(128)} %bitcast.32), kind=kLoop, calls=%fused_computation.91 | loop fusion | flops 2 | bytes 16 | tf_op jit(solution)/shard_map/stack | solution.py:527
  76.0 6.1 %collective-permute-done.10.refs_2_ = f32[3,128,128]{2,1,0:T(8,128)S(1)} collective-permute-done((f32[3,128,128]{2,1,0:T(8,128)S(1)}, f32[3,128,128]{2,1,0:T(8,128)S(1)}, u32[]{:S(2)}, u32[]{:S(2)}) %collective-permute-start.10) | collective-permute-done | bytes 196640 | tf_op jit(solution)/shard_map/ppermute | solution.py:539
  82.2 4.0 %collective-permute-done.11.refs_3_ = f32[3,128,128]{2,1,0:T(8,128)S(1)} collective-permute-done((f32[3,128,128]{2,1,0:T(8,128)S(1)}, f32[3,128,128]{2,1,0:T(8,128)S(1)}, u32[]{:S(2)}, u32[]{:S(2)}) %collective-permute-start.11) | collective-permute-done | bytes 196640 | tf_op jit(solution)/shard_map/ppermute | solution.py:539
  86.2 0.7 copy-done.19
  86.9 1.3 density_totals.1
  88.2 3.4 %all-to-all-start.1 = ((f32[8,2,8,512]{3,2,1,0:T(8,128)}), f32[8,2,8,512]{3,2,1,0:T(8,128)S(1)}, u32[]{:S(2)}, u32[]{:S(2)}) async-start(f32[8,2,8,512]{3,2,1,0:T(8,128)} %get-tuple-element.116), calls=%async_computation.1 | async-start | bytes 524288 | tf_op jit(solution)/shard_map/all_to_all | solution.py:675
  91.7 1.0 enter_1.1
  92.7 0.7 copy-done.6
  93.4 1.9 %collective-permute-start.13 = (f32[3,128,128]{2,1,0:T(8,128)S(1)}, f32[3,128,128]{2,1,0:T(8,128)S(1)}, u32[]{:S(2)}, u32[]{:S(2)}) collective-permute-start(f32[3,128,128]{2,1,0:T(8,128)S(1)} %get-tuple-element.121), channel_id=1, source_target_pairs={{0,4},{4,0},{8,12},{12,8},{16,20},{20,16},{24,28},{28,24},{1,5},{5... | collective-permute-start | bytes 589832 | tf_op jit(solution)/shard_map/ppermute | solution.py:539
  95.3 1.5 %collective-permute-start.14 = (f32[3,128,128]{2,1,0:T(8,128)S(1)}, f32[3,128,128]{2,1,0:T(8,128)S(1)}, u32[]{:S(2)}, u32[]{:S(2)}) collective-permute-start(f32[3,128,128]{2,1,0:T(8,128)S(1)} %get-tuple-element.122), channel_id=1, source_target_pairs={{0,8},{4,12},{8,0},{12,4},{16,24},{20,28},{24,16},{28,20},{1,9},{5... | collective-permute-start | bytes 589832 | tf_op jit(solution)/shard_map/ppermute | solution.py:539
  96.8 0.1 collective-permute-start.15
  97.0 4.4 %inflow_0.1.refs_4_ = f32[64,8,16,128]{3,2,1,0:T(8,128)} custom-call(s32[2]{0:T(128)} %pad_add_fusion.1.refs_0_.meta, f32[10,64]{1,0:T(8,128)} %stack.141.refs_1_.floats, s32[5,64]{1,0:T(8,128)} %stack.148.refs_2_.ints, f32[32,8,16,128]{3,2,1,0:T(8,128)} %get-tuple-element.124.swept, f32[3,128,128]{2,1,0:T(8,128)} %copy-done.7, f32[3,128,128]{2,1,0:T(8,128)} %copy-done.17, ...), custom_call_target="tpu_custom_call" | custom-call | tf_op jit(solution)/shard_map/inflow_0/pallas_call | solution.py:624
  101.4 0.2 collective-permute-done.13.refs_1_
  101.6 2.2 %collective-permute-done.14.refs_2_ = f32[3,128,128]{2,1,0:T(8,128)S(1)} collective-permute-done((f32[3,128,128]{2,1,0:T(8,128)S(1)}, f32[3,128,128]{2,1,0:T(8,128)S(1)}, u32[]{:S(2)}, u32[]{:S(2)}) %collective-permute-start.14) | collective-permute-done | bytes 196640 | tf_op jit(solution)/shard_map/ppermute | solution.py:539
  103.8 4.0 %collective-permute-done.15.refs_3_ = f32[3,128,128]{2,1,0:T(8,128)S(1)} collective-permute-done((f32[3,128,128]{2,1,0:T(8,128)S(1)}, f32[3,128,128]{2,1,0:T(8,128)S(1)}, u32[]{:S(2)}, u32[]{:S(2)}) %collective-permute-start.15) | collective-permute-done | bytes 196640 | tf_op jit(solution)/shard_map/ppermute | solution.py:539
  107.8 1.0 kelvins.1.refs_0_
  108.8 0.6 collective-permute-start.16
  109.5 0.2 multiply_reduce_fusion.3
  109.8 7.3 %collective-permute-done.16.refs_1_ = f32[136,512]{1,0:T(8,128)S(1)} collective-permute-done((f32[136,512]{1,0:T(8,128)S(1)}, f32[136,512]{1,0:T(8,128)S(1)}, u32[]{:S(2)}, u32[]{:S(2)}) %collective-permute-start.16) | collective-permute-done | bytes 278560 | tf_op jit(solution)/shard_map/ppermute | solution.py:539
  117.4 0.1 fusion.14
  117.6 0.7 maximum_maximum_fusion.1.refs_5_
  118.2 0.7 maximum_maximum_fusion.refs_4_
  118.9 4.4 %inflow_1.1.inflown = f32[64,8,16,128]{3,2,1,0:T(8,128)} custom-call(s32[2]{0:T(128)} %pad_add_fusion.1.refs_0_.meta, f32[10,64]{1,0:T(8,128)} %stack.141.refs_1_.floats, s32[5,64]{1,0:T(8,128)} %stack.148.refs_2_.ints, f32[32,8,16,128]{3,2,1,0:T(8,128)} %get-tuple-element.77.swept, f32[3,128,128]{2,1,0:T(8,128)} %copy-done.6, ...), custom_call_target="tpu_custom_call", output_to_operand_aliasing={{}: (8, {})} | custom-call | tf_op jit(solution)/shard_map/inflow_1/pallas_call | solution.py:624
  123.4 0.7 copy-done.12
  124.1 0.7 copy-done.13
  124.8 10.8 %final_energy.1 = (f32[64,8,16,128]{3,2,1,0:T(8,128)}, f32[128,128]{1,0:T(8,128)}) custom-call(s32[2]{0:T(128)} %pad_add_fusion.1.refs_0_.meta, f32[10,64]{1,0:T(8,128)} %stack.141.refs_1_.floats, s32[5,64]{1,0:T(8,128)} %stack.148.refs_2_.ints, f32[6,16]{1,0:T(8,128)} %copy.57.refs_3_.kinds, f32[2]{0:T(128)} %copy-done.10, ...), custom_call_target="tpu_custom_call" | custom-call | tf_op jit(solution)/shard_map/final_energy/pallas_call | solution.py:690
  (97 shorter events, 2.2 us)
Async XLA Ops:
  16.5 28.0 %copy-start.1 = (f32[10,64]{1,0:T(8,128)S(1)}, f32[10,64]{1,0:T(8,128)}, u32[]{:S(2)}) copy-start(f32[10,64]{1,0:T(8,128)} %stack.141.refs_1_.floats) | copy-start | bytes 7684
  16.5 28.0 %copy-start.3 = (s32[5,64]{1,0:T(8,128)S(1)}, s32[5,64]{1,0:T(8,128)}, u32[]{:S(2)}) copy-start(s32[5,64]{1,0:T(8,128)} %stack.148.refs_2_.ints) | copy-start | bytes 3844
  16.5 28.0 %copy-start.5 = (f32[3,128,128]{2,1,0:T(8,128)S(1)}, f32[3,128,128]{2,1,0:T(8,128)}, u32[]{:S(2)}) copy-start(f32[3,128,128]{2,1,0:T(8,128)} %get-tuple-element.96.refs_0_) | copy-start | bytes 589828
  16.5 28.0 %copy-start.8 = (s32[2]{0:T(128)S(1)}, s32[2]{0:T(128)}, u32[]{:S(2)}) copy-start(s32[2]{0:T(128)} %pad_add_fusion.1.refs_0_.meta) | copy-start | bytes 28
  16.5 17.1 %collective-permute-start = (f32[3,128,128]{2,1,0:T(8,128)}, f32[3,128,128]{2,1,0:T(8,128)S(1)}, u32[]{:S(2)}, u32[]{:S(2)}) collective-permute-start(f32[3,128,128]{2,1,0:T(8,128)} %get-tuple-element.85), channel_id=1, source_target_pairs={{0,4},{4,0},{8,12},{12,8},{16,20},{20,16},{24,28},{28,24},{1,5},{5... | collective-permute-start | bytes 589832 | tf_op jit(solution)/shard_map/ppermute | solution.py:539
  19.6 14.1 %collective-permute-start.1 = (f32[3,128,128]{2,1,0:T(8,128)}, f32[3,128,128]{2,1,0:T(8,128)S(1)}, u32[]{:S(2)}, u32[]{:S(2)}) collective-permute-start(f32[3,128,128]{2,1,0:T(8,128)} %get-tuple-element.86), channel_id=1, source_target_pairs={{0,8},{4,12},{8,0},{12,4},{16,24},{20,28},{24,16},{28,20},{1,9},{5... | collective-permute-start | bytes 589832 | tf_op jit(solution)/shard_map/ppermute | solution.py:539
  21.2 12.5 %collective-permute-start.2 = (f32[3,128,128]{2,1,0:T(8,128)}, f32[3,128,128]{2,1,0:T(8,128)S(1)}, u32[]{:S(2)}, u32[]{:S(2)}) collective-permute-start(f32[3,128,128]{2,1,0:T(8,128)} %get-tuple-element.87), channel_id=1, source_target_pairs={{0,12},{4,8},{8,4},{12,0},{16,28},{20,24},{24,20},{28,16},{1,13},{... | collective-permute-start | bytes 589832 | tf_op jit(solution)/shard_map/ppermute | solution.py:539
  22.4 64.5 %copy-start.9 = (f32[8,512]{1,0:T(8,128)S(1)}, f32[8,512]{1,0:T(8,128)}, u32[]{:S(2)}) copy-start(f32[8,512]{1,0:T(8,128)} %get-tuple-element.115.before) | copy-start | bytes 49156
  33.7 2.6 %collective-permute-start.3 = (f32[2,3,64,512]{3,2,1,0:T(8,128)}, f32[2,3,64,512]{3,2,1,0:T(8,128)S(1)}, u32[]{:S(2)}, u32[]{:S(2)}) collective-permute-start(f32[2,3,64,512]{3,2,1,0:T(8,128)} %get-tuple-element.89), channel_id=1, source_target_pairs={{0,1},{1,0},{2,3},{3,2},{4,5},{5,4},{6,7},{7,6},{8,9},{9,8},{10,11... | collective-permute-start | bytes 2359304 | tf_op jit(solution)/shard_map/ppermute | solution.py:539
  36.2 1.1 copy-start.2
  37.4 33.2 %copy-start.4 = (f32[3,128,128]{2,1,0:T(8,128)S(1)}, f32[3,128,128]{2,1,0:T(8,128)}, u32[]{:S(2)}) copy-start(f32[3,128,128]{2,1,0:T(8,128)} %get-tuple-element.109.refs_0_) | copy-start | bytes 589828
  38.2 19.3 %collective-permute-start.4 = (f32[1,3,64,512]{3,2,1,0:T(8,128)}, f32[1,3,64,512]{3,2,1,0:T(8,128)S(1)}, u32[]{:S(2)}, u32[]{:S(2)}) collective-permute-start(f32[1,3,64,512]{3,2,1,0:T(8,128)} %get-tuple-element.91), channel_id=1, source_target_pairs={{0,2},{1,3},{2,0},{3,1},{4,6},{5,7},{6,4},{7,5},{8,10},{9,11},{10,... | collective-permute-start | bytes 1179656 | tf_op jit(solution)/shard_map/ppermute | solution.py:539
  40.9 7.2 %collective-permute-start.5 = (f32[3,128,128]{2,1,0:T(8,128)}, f32[3,128,128]{2,1,0:T(8,128)S(1)}, u32[]{:S(2)}, u32[]{:S(2)}) collective-permute-start(f32[3,128,128]{2,1,0:T(8,128)} %get-tuple-element.93), channel_id=1, source_target_pairs={{0,4},{4,0},{8,12},{12,8},{16,20},{20,16},{24,28},{28,24},{1,5},{5... | collective-permute-start | bytes 589832 | tf_op jit(solution)/shard_map/ppermute | solution.py:539
  42.5 12.3 %collective-permute-start.6 = (f32[3,128,128]{2,1,0:T(8,128)}, f32[3,128,128]{2,1,0:T(8,128)S(1)}, u32[]{:S(2)}, u32[]{:S(2)}) collective-permute-start(f32[3,128,128]{2,1,0:T(8,128)} %get-tuple-element.94), channel_id=1, source_target_pairs={{0,8},{4,12},{8,0},{12,4},{16,24},{20,28},{24,16},{28,20},{1,9},{5... | collective-permute-start | bytes 589832 | tf_op jit(solution)/shard_map/ppermute | solution.py:539
  44.1 13.4 %collective-permute-start.7 = (f32[3,128,128]{2,1,0:T(8,128)}, f32[3,128,128]{2,1,0:T(8,128)S(1)}, u32[]{:S(2)}, u32[]{:S(2)}) collective-permute-start(f32[3,128,128]{2,1,0:T(8,128)} %get-tuple-element.95), channel_id=1, source_target_pairs={{0,12},{4,8},{8,4},{12,0},{16,28},{20,24},{24,20},{28,16},{1,13},{... | collective-permute-start | bytes 589832 | tf_op jit(solution)/shard_map/ppermute | solution.py:539
  45.5 12.0 %collective-permute-start.8 = (f32[3,128,128]{2,1,0:T(8,128)S(1)}, f32[3,128,128]{2,1,0:T(8,128)S(1)}, u32[]{:S(2)}, u32[]{:S(2)}) collective-permute-start(f32[3,128,128]{2,1,0:T(8,128)S(1)} %get-tuple-element.103.refs_0_), channel_id=1, source_target_pairs={{0,16},{4,20},{8,24},{12,28},{16,0},{20,4},{24,8},{28,12},{1,17},{... | collective-permute-start | bytes 589832 | tf_op jit(solution)/shard_map/ppermute | solution.py:539
  58.3 28.6 %all-to-all-start = ((f32[8,3,8,512]{3,2,1,0:T(8,128)}), f32[8,3,8,512]{3,2,1,0:T(8,128)S(1)}, u32[]{:S(2)}, u32[]{:S(2)}) async-start(f32[8,3,8,512]{3,2,1,0:T(8,128)} %density_parts.1), calls=%async_computation | async-start | bytes 786432 | tf_op jit(solution)/shard_map/all_to_all | solution.py:662
  66.4 0.7 copy-start.7
  67.1 8.9 %collective-permute-start.9 = (f32[3,128,128]{2,1,0:T(8,128)S(1)}, f32[3,128,128]{2,1,0:T(8,128)S(1)}, u32[]{:S(2)}, u32[]{:S(2)}) collective-permute-start(f32[3,128,128]{2,1,0:T(8,128)S(1)} %get-tuple-element.106), channel_id=1, source_target_pairs={{0,4},{4,0},{8,12},{12,8},{16,20},{20,16},{24,28},{28,24},{1,5},{5... | collective-permute-start | bytes 589832 | tf_op jit(solution)/shard_map/ppermute | solution.py:539
  69.1 13.0 %collective-permute-start.10 = (f32[3,128,128]{2,1,0:T(8,128)S(1)}, f32[3,128,128]{2,1,0:T(8,128)S(1)}, u32[]{:S(2)}, u32[]{:S(2)}) collective-permute-start(f32[3,128,128]{2,1,0:T(8,128)S(1)} %get-tuple-element.107), channel_id=1, source_target_pairs={{0,8},{4,12},{8,0},{12,4},{16,24},{20,28},{24,16},{28,20},{1,9},{5... | collective-permute-start | bytes 589832 | tf_op jit(solution)/shard_map/ppermute | solution.py:539
  70.6 15.6 %collective-permute-start.11 = (f32[3,128,128]{2,1,0:T(8,128)S(1)}, f32[3,128,128]{2,1,0:T(8,128)S(1)}, u32[]{:S(2)}, u32[]{:S(2)}) collective-permute-start(f32[3,128,128]{2,1,0:T(8,128)S(1)} %get-tuple-element.108), channel_id=1, source_target_pairs={{0,12},{4,8},{8,4},{12,0},{16,28},{20,24},{24,20},{28,16},{1,13},{... | collective-permute-start | bytes 589832 | tf_op jit(solution)/shard_map/ppermute | solution.py:539
  71.6 15.3 %collective-permute-start.12 = (f32[3,128,128]{2,1,0:T(8,128)S(1)}, f32[3,128,128]{2,1,0:T(8,128)S(1)}, u32[]{:S(2)}, u32[]{:S(2)}) collective-permute-start(f32[3,128,128]{2,1,0:T(8,128)S(1)} %get-tuple-element.118.refs_0_), channel_id=1, source_target_pairs={{0,16},{4,20},{8,24},{12,28},{16,0},{20,4},{24,8},{28,12},{1,17},{... | collective-permute-start | bytes 589832 | tf_op jit(solution)/shard_map/ppermute | solution.py:539
  75.9 31.8 %copy-start.10 = (f32[2]{0:T(128)}, f32[2]{0:T(128)S(1)}, u32[]{:S(2)}) copy-start(f32[2]{0:T(128)S(1)} %pad_maximum_fusion.3.sums) | copy-start | bytes 28
  76.0 21.0 %copy-start.17 = (f32[3,128,128]{2,1,0:T(8,128)}, f32[3,128,128]{2,1,0:T(8,128)S(1)}, u32[]{:S(2)}) copy-start(f32[3,128,128]{2,1,0:T(8,128)S(1)} %collective-permute-done.9.refs_1_) | copy-start | bytes 589828
  82.2 14.8 %copy-start.18 = (f32[3,128,128]{2,1,0:T(8,128)}, f32[3,128,128]{2,1,0:T(8,128)S(1)}, u32[]{:S(2)}) copy-start(f32[3,128,128]{2,1,0:T(8,128)S(1)} %collective-permute-done.10.refs_2_) | copy-start | bytes 589828
  86.2 0.7 copy-start.19
  88.2 19.6 %all-to-all-start.1 = ((f32[8,2,8,512]{3,2,1,0:T(8,128)}), f32[8,2,8,512]{3,2,1,0:T(8,128)S(1)}, u32[]{:S(2)}, u32[]{:S(2)}) async-start(f32[8,2,8,512]{3,2,1,0:T(8,128)} %get-tuple-element.116), calls=%async_computation.1 | async-start | bytes 524288 | tf_op jit(solution)/shard_map/all_to_all | solution.py:675
  92.7 0.7 copy-start.6
  93.4 8.2 %collective-permute-start.13 = (f32[3,128,128]{2,1,0:T(8,128)S(1)}, f32[3,128,128]{2,1,0:T(8,128)S(1)}, u32[]{:S(2)}, u32[]{:S(2)}) collective-permute-start(f32[3,128,128]{2,1,0:T(8,128)S(1)} %get-tuple-element.121), channel_id=1, source_target_pairs={{0,4},{4,0},{8,12},{12,8},{16,20},{20,16},{24,28},{28,24},{1,5},{5... | collective-permute-start | bytes 589832 | tf_op jit(solution)/shard_map/ppermute | solution.py:539
  95.3 8.5 %collective-permute-start.14 = (f32[3,128,128]{2,1,0:T(8,128)S(1)}, f32[3,128,128]{2,1,0:T(8,128)S(1)}, u32[]{:S(2)}, u32[]{:S(2)}) collective-permute-start(f32[3,128,128]{2,1,0:T(8,128)S(1)} %get-tuple-element.122), channel_id=1, source_target_pairs={{0,8},{4,12},{8,0},{12,4},{16,24},{20,28},{24,16},{28,20},{1,9},{5... | collective-permute-start | bytes 589832 | tf_op jit(solution)/shard_map/ppermute | solution.py:539
  96.8 11.0 %collective-permute-start.15 = (f32[3,128,128]{2,1,0:T(8,128)S(1)}, f32[3,128,128]{2,1,0:T(8,128)S(1)}, u32[]{:S(2)}, u32[]{:S(2)}) collective-permute-start(f32[3,128,128]{2,1,0:T(8,128)S(1)} %get-tuple-element.123), channel_id=1, source_target_pairs={{0,12},{4,8},{8,4},{12,0},{16,28},{20,24},{24,20},{28,16},{1,13},{... | collective-permute-start | bytes 589832 | tf_op jit(solution)/shard_map/ppermute | solution.py:539
  101.6 17.4 %copy-start.14 = (f32[3,128,128]{2,1,0:T(8,128)}, f32[3,128,128]{2,1,0:T(8,128)S(1)}, u32[]{:S(2)}) copy-start(f32[3,128,128]{2,1,0:T(8,128)S(1)} %collective-permute-done.13.refs_1_) | copy-start | bytes 589828
  103.8 15.1 %copy-start.15 = (f32[3,128,128]{2,1,0:T(8,128)}, f32[3,128,128]{2,1,0:T(8,128)S(1)}, u32[]{:S(2)}) copy-start(f32[3,128,128]{2,1,0:T(8,128)S(1)} %collective-permute-done.14.refs_2_) | copy-start | bytes 589828
  107.8 11.2 %copy-start.16 = (f32[3,128,128]{2,1,0:T(8,128)}, f32[3,128,128]{2,1,0:T(8,128)S(1)}, u32[]{:S(2)}) copy-start(f32[3,128,128]{2,1,0:T(8,128)S(1)} %collective-permute-done.15.refs_3_) | copy-start | bytes 589828
  108.8 14.6 %copy-start = (f32[136,512]{1,0:T(8,128)}, f32[136,512]{1,0:T(8,128)S(1)}, u32[]{:S(2)}) copy-start(f32[136,512]{1,0:T(8,128)S(1)} %kelvins.1.refs_0_) | copy-start | bytes 835588
  108.8 8.3 %collective-permute-start.16 = (f32[136,512]{1,0:T(8,128)S(1)}, f32[136,512]{1,0:T(8,128)S(1)}, u32[]{:S(2)}, u32[]{:S(2)}) collective-permute-start(f32[136,512]{1,0:T(8,128)S(1)} %kelvins.1.refs_0_), channel_id=1, source_target_pairs={{0,2},{1,3},{2,0},{3,1},{4,6},{5,7},{6,4},{7,5},{8,10},{9,11},{10,... | collective-permute-start | bytes 835592 | tf_op jit(solution)/shard_map/ppermute | solution.py:539
  109.7 13.6 %collective-permute-start.17 = (f32[136,512]{1,0:T(8,128)S(1)}, f32[136,512]{1,0:T(8,128)S(1)}, u32[]{:S(2)}, u32[]{:S(2)}) collective-permute-start(f32[136,512]{1,0:T(8,128)S(1)} %kelvins.1.refs_0_), channel_id=1, source_target_pairs={{0,1},{1,0},{2,3},{3,2},{4,5},{5,4},{6,7},{7,6},{8,9},{9,8},{10,11... | collective-permute-start | bytes 835592 | tf_op jit(solution)/shard_map/ppermute | solution.py:539
  117.1 6.2 %copy-start.11 = (f32[136,512]{1,0:T(8,128)}, f32[136,512]{1,0:T(8,128)S(1)}, u32[]{:S(2)}) copy-start(f32[136,512]{1,0:T(8,128)S(1)} %collective-permute-done.16.refs_1_) | copy-start | bytes 835588
  117.1 6.3 %collective-permute-start.18 = (f32[136,512]{1,0:T(8,128)S(1)}, f32[136,512]{1,0:T(8,128)S(1)}, u32[]{:S(2)}, u32[]{:S(2)}) collective-permute-start(f32[136,512]{1,0:T(8,128)S(1)} %collective-permute-done.16.refs_1_), channel_id=1, source_target_pairs={{0,1},{1,0},{2,3},{3,2},{4,5},{5,4},{6,7},{7,6},{8,9},{9,8},{10,11... | collective-permute-start | bytes 835592 | tf_op jit(solution)/shard_map/ppermute | solution.py:539
  123.3 0.7 copy-start.12
  124.1 0.7 copy-start.13

commit v7 on v4

--- a/solution.py
+++ b/solution.py
@@ -77,11 +77,7 @@
             2 * band + jnp.where(outer, 0, 1),
         ]
     )
-    x = jnp.arange(slabs * depth, dtype=jnp.int32)[:, None]
-    past = jnp.where(forward[None, :], x - (slab * depth + depth - 1), slab * depth - x)
-    n = past.astype(jnp.float32)
-    weight = jnp.where(past > 0, jnp.power(ratio[None, :], jnp.maximum(n, 0.0)), 0.0)
-    return floats, ints, jnp.concatenate([weight, n * weight, (0.5 * n * (n + 1.0)) * weight], axis=1)
+    return floats, ints
 
 
 def kind_table(speed, rate, storage, threshold, generation):
@@ -194,29 +190,64 @@
     return pl.ds(at, 8), pl.ds(at + 8, 8)
 
 
-def sweeps_kernel(sizes, meta, floats, ints, kinds, energy, flag, given, matrix, swept, quarter, *rest):
+K_SELF, K_LARGE, K_SMALL, K_RATIO, K_THERM, K_QUART, K_HEAT, K_WALL = range(8)
+
+
+def fill_kinds(table, bands):
+    speeds, rates, storages, thresholds, generations = bands
+    for kind in range(KINDS):
+        band, cosine = kind // 2, COSINES[kind % 2]
+        sine = np.sqrt(np.float32(1.0) - cosine * cosine)
+        speed, rate, storage, threshold, generation = (
+            jnp.full((8, 128), ref[band], jnp.float32) for ref in (speeds, rates, storages, thresholds, generations)
+        )
+        inverse = 1.0 / (speed * float(cosine + sine * np.float32(ACROSS)) + rate + PSEUDO_RATE)
+        quart = 1.0 / (4.0 * (threshold * threshold * threshold))
+        across = speed * float(sine) * inverse
+        therm = rate * storage * inverse
+        rows = (
+            PSEUDO_RATE * inverse,
+            across * math.cos(math.pi / 8),
+            across * math.sin(math.pi / 8),
+            speed * float(cosine) * inverse,
+            therm,
+            therm * quart,
+            generation * inverse,
+            storage * (1.0 + quart),
+        )
+        for row, value in enumerate(rows):
+            table[row, kind] = value
+
+
+def sweeps_kernel(sizes, meta, labels, *refs):
     block, blocks, depth, width_y, slots, modes, group = sizes
+    bands, refs = refs[:5], refs[5:]
+    energy, flag, given, label_row, swept, quarter, *rest = refs
     faces, rest = rest[:group], rest[group:]
-    keep, send, *planes, density, flat, sources, heat = rest
+    keep, send, *planes, density, flat, sources, heat, table = rest
     out_one, turn_one, turn_two, out_two, turn_late, out_three = planes
     rows, own = width_y // modes, slots // group
     step = pl.program_id(0)
     slab, mode = meta[SLAB], meta[MODE]
+    slabs = keep.shape[2] // depth
 
     @pl.when(step == 0)
     def _():
+        fill_kinds(table, bands)
         for yy in range(rows):
             quarter[:, yy * 128 : (yy + 1) * 128] = given[pl.ds(mode * rows + yy, depth, stride=width_y), :]
         density[...] = jnp.zeros_like(density)
 
         def one_layer(x, carry):
-            at = pl.ds(pl.multiple_of(x * 16, 16), 16)
-            t = given[at, :]
-            power = fourth(t)
-            hot = flag[at, :].astype(jnp.float32)
-            heat[x] = hot
-            for kind in range(KINDS):
-                sources[kind, x] = kinds[THERM, kind] * t + kinds[QUART, kind] * power + kinds[HEAT, kind] * hot
+            at = pl.multiple_of(x * 16, 16)
+            for low in (0, 8):
+                t = given[pl.ds(at + low, 8), :]
+                power = fourth(t)
+                hot = flag[pl.ds(at + low, 8), :].astype(jnp.float32)
+                heat[x, low : low + 8, :] = hot
+                for kind in range(KINDS):
+                    value = table[K_THERM, kind] * t + table[K_QUART, kind] * power + table[K_HEAT, kind] * hot
+                    sources[kind, x, low : low + 8, :] = value
             return carry
 
         lax.fori_loop(0, depth, one_layer, 0)
@@ -225,15 +256,27 @@
 
     def one_slot(i, carry):
         s = step * block + i
-        start, stride = course(ints, s, depth)
-        side = 1 - ints[FORWARD, s]
-        ratio, warm, kind = floats[RATIO, s], floats[WARM, s], ints[KIND, s]
-        apply = slot_stencil(floats, ints, s, row)
+        label = labels[s]
+        polar, turn_of = label % 4, (label // 4) % 8
+        forward = polar < 2
+        kind = 2 * (label // DIRS) + jnp.where((polar == 0) | (polar == 3), 0, 1)
+        right, up = (turn_of < 2) | (turn_of > 5), turn_of < 4
+        wide = (turn_of % 4 == 0) | (turn_of % 4 == 3)
+        start, stride = jnp.where(forward, 0, depth - 1), jnp.where(forward, 1, -1)
+        side = jnp.where(forward, 0, 1)
+        at_wall = jnp.where(forward, slab == 0, slab == slabs - 1)
+        c_self, ratio, warm = table[K_SELF, kind], table[K_RATIO, kind], table[K_HEAT, kind]
+        c_y = table[jnp.where(wide, K_LARGE, K_SMALL), kind]
+        c_z = table[jnp.where(wide, K_SMALL, K_LARGE), kind]
+        wall = jnp.where(at_wall, 1.0, 0.0) * table[K_WALL, kind]
+        shift_y, shift_z = jnp.where(right, 1, 7), jnp.where(up, 1, 127)
+        at_edge = row == jnp.where(right, 0, 7)
+        apply = lambda low, high: stencil(low, high, c_self, c_y, c_z, shift_y, shift_z, at_edge)
         xs = [start + stride * j for j in range(depth)]
         layers = [(energy[i, x, :8, :], energy[i, x, 8:, :]) for x in xs]
         last = []
         for turn in range(ITERS):
-            total_low = total_high = jnp.full((8, 128), floats[WALL, s], jnp.float32)
+            total_low = total_high = wall
             for j, x in enumerate(xs):
                 low, high = apply(*layers[j])
                 if turn == 0:
@@ -268,19 +311,30 @@
         for turn in range(ITERS):
             for x in range(depth):
                 flat[turn, x * 16 : x * 16 + 16, :] = density[turn, 0, x] + density[turn, 1, depth - 1 - x]
+        label = label_row[...]
+        polar = label % 4
+        kinds = 2 * (label // DIRS) + jnp.where((polar == 0) | (polar == 3), 0, 1)
+        decay = jnp.ones((1, slots), jnp.float32)
+        for kind in range(KINDS):
+            decay = jnp.where(kinds == kind, table[K_RATIO, kind][:1, :slots], decay)
+        x = lax.broadcasted_iota(jnp.int32, (slabs * depth, slots), 0)
+        past = jnp.where(polar < 2, x - (slab * depth + depth - 1), slab * depth - x)
+        n = past.astype(jnp.float32)
+        weight = jnp.where(past > 0, jnp.exp(jnp.maximum(n, 0.0) * jnp.log(decay)), 0.0)
+        weights = (weight, n * weight, (0.5 * n * (n + 1.0)) * weight)
         home = pl.ds(pl.multiple_of(slab * depth, 8), depth)
         for by in range(modes):
             ys = [(mode ^ by) * rows + yy for yy in range(rows)]
             pick = lambda plane, count: jnp.concatenate([plane[pl.ds(y, count, stride=width_y), :] for y in ys], axis=1)
-            one, two = pick(turn_one, slots), pick(turn_late, slots)
-            rights = (
-                pick(out_one, slots),
-                jnp.concatenate([pick(out_two, slots), one], axis=0),
-                jnp.concatenate([pick(out_three, slots), two, pick(turn_two, slots)], axis=0),
-            )
+            plain = exact_dot(weights[0], jnp.concatenate([pick(p, slots) for p in (out_one, out_two, out_three)], axis=1))
+            once = exact_dot(weights[1], jnp.concatenate([pick(p, slots) for p in (turn_one, turn_late)], axis=1))
+            twice = exact_dot(weights[2], pick(turn_two, slots))
+            lanes = rows * 128
             target = (send if by % 2 else keep).at[by // 2]
-            for turn, right in enumerate(rights):
-                target[turn] = exact_dot(matrix[:, : (turn + 1) * slots], right)
+            target[0] = plain[:, :lanes]
+            target[1] = plain[:, lanes : 2 * lanes] + once[:, :lanes]
+            target[2] = plain[:, 2 * lanes :] + once[:, lanes:] + twice
+            for turn in range(ITERS):
                 target[turn, home, :] += pick(flat.at[turn], depth)
 
 
@@ -297,33 +351,42 @@
             parts[slab, turn] = total[slab * depth : (slab + 1) * depth]
 
 
-def totals_kernel(parts, before, copies, late):
+def totals_kernel(sums, parts, before, copies, late):
     slabs = parts.shape[0]
     one, two, three = (
         add_up([parts[slab, turn] for slab in range(slabs)]) * (1.0 / DIRS) for turn in range(ITERS)
     )
     late[...] = three
+    kelvin = newton(one, before[...], sums[0], sums[1])
     for slab in range(slabs):
-        copies[slab, 0] = one
+        copies[slab, 0] = kelvin
         copies[slab, 1] = two
-        copies[slab, 2] = before[...]
-
-
-def kelvins_kernel(depth, sums, gathered, late, matrix, packed):
+
+
+def kelvins_kernel(depth, meta, sums, gathered, late, matrix_one, matrix_two, packed):
     slabs = gathered.shape[0]
     cells = slabs * depth
-    one, two, before = (
-        jnp.concatenate([gathered[slab, index] for slab in range(slabs)], axis=0) for index in range(3)
-    )
-    kelvin = newton(one, before, sums[0], sums[1])
-    packed[:cells, :] = kelvin
-    two = two + exact_dot(matrix[...], jnp.concatenate([kelvin, fourth(kelvin)], axis=0))
-    packed[cells : 2 * cells, :] = newton(two, kelvin, sums[0], sums[1])
-    packed[2 * cells :, :] = late[...]
+    one, two = (jnp.concatenate([gathered[slab, index] for slab in range(slabs)], axis=0) for index in range(2))
+    first = exact_dot(matrix_one[...], jnp.concatenate([one, fourth(one)], axis=0))
+    two = newton(two + first[:cells], one, sums[0], sums[1])
+    second = exact_dot(matrix_two[...], jnp.concatenate([two, fourth(two)], axis=0))
+    sided = 2 * KINDS
+    packed[: 2 * sided, :] = first[cells : cells + 2 * sided]
+    packed[2 * sided : 3 * sided, :] = second[:sided]
+    base = 3 * sided
+    packed[base : base + depth, :] = gathered[meta[SLAB], 0]
+    stay = first[cells + 2 * sided : cells + 2 * sided + depth]
+    around = first[cells + 2 * sided + depth :]
+    own = jnp.zeros_like(around)
+    for slab in range(slabs):
+        own = jnp.where(meta[SLAB] == slab, two[slab * depth : (slab + 1) * depth], own)
+    packed[base + depth : base + 2 * depth, :] = own
+    packed[base + 2 * depth : base + 3 * depth, :] = late[...] + stay + second[sided:]
+    packed[base + 3 * depth :, :] = around
 
 
 def compose_kernel(own, group, meta, floats, ints, *refs):
-    received, (composite, effective, ordered) = refs[:group], refs[group:]
+    received, (_, composite, effective, ordered) = refs[:group], refs[group:]
     place = meta[SLAB] % group
     for by in range(group):
         ordered[place ^ by] = received[by][...]
@@ -392,97 +455,95 @@
         outs[by][...] = entered[place ^ by]
 
 
-def final_kernel(sizes, order, meta, floats, ints, kinds, sums, swept, *refs):
-    block, depth, width_y, width_z, slots, slabs, modes, group = sizes
-    received, refs = refs[:group], refs[group:]
+def warm_kernel(sizes, order, meta, floats, ints, kinds, sums, swept, *refs):
+    block, depth, width_y, width_z, modes = sizes
     packs, refs = refs[:modes], refs[modes:]
-    first_matrix, second_matrix, energy, kelvin, *refs = refs
-    warm_one, warm_two, late, enter_one, enter_long, enter_two, second, added, own_one, own_two, *ordered = refs
+    energy, kelvin, enter_one, enter_long, enter_two, second, added, own_one, own_two, plain, around = refs
     step = pl.program_id(0)
-    slab, mode = meta[SLAB], meta[MODE]
-    own, lanes, cells = slots // group, width_y // modes * width_z, slabs * depth
+    rows = width_y // modes
+
+    @pl.when(step == 0)
+    def _():
+        sided, base = 2 * KINDS, 6 * KINDS
+        for pack, by in zip(packs, order):
+            for yy in range(rows):
+                y, lane = (meta[MODE] ^ by) * rows + yy, slice(yy * 128, (yy + 1) * 128)
+                for index, target in enumerate((enter_one, enter_long, enter_two)):
+                    target[pl.ds(y, sided, stride=width_y), :] = pack[index * sided : (index + 1) * sided, lane]
+                scattered = pl.ds(y, depth, stride=width_y)
+                own_one[scattered, :] = pack[base : base + depth, lane]
+                own_two[scattered, :] = pack[base + depth : base + 2 * depth, lane]
+                plain[y] = pack[base + 2 * depth : base + 3 * depth, lane]
+                around[y] = pack[base + 3 * depth :, lane]
+        for y in range(width_y):
+            here = around[y]
+            near = around[(y - 1) % width_y] + around[(y + 1) % width_y]
+            near = near + (pltpu.roll(here, 1, 1) + pltpu.roll(here, width_z - 1, 1))
+            scattered = pl.ds(y, depth, stride=width_y)
+            kelvin[scattered, :] = newton(plain[y] + near, own_two[scattered, :], sums[0], sums[1])
+
+        def one_kind(kind, carry):
+            therm, quart, decay = kinds[THERM, kind], kinds[QUART, kind], kinds[DECAY, kind]
+            ones, twos = [], []
+            for x in range(depth):
+                here = slice(x * 16, x * 16 + 16)
+                t, u = own_one[here, :], own_two[here, :]
+                ones.append(therm * t + quart * fourth(t))
+                twos.append(therm * u + quart * fourth(u))
+            for back in (0, KINDS):
+                at = pl.ds(pl.multiple_of((kind + back) * 16, 16), 16)
+                once, twice, new = enter_one[at, :], enter_long[at, :], enter_two[at, :]
+                for j in range(depth):
+                    x = depth - 1 - j if back else j
+                    once = decay * once + ones[x]
+                    twice = decay * twice + once
+                    new = decay * new + twos[x]
+                    second[kind + back, x] = twice
+                    added[kind + back, x] = new
+            return carry
+
+        lax.fori_loop(0, KINDS, one_kind, 0)
+
+    row = lax.broadcasted_iota(jnp.int32, (8, 128), 0)
+
+    def one_slot(i, carry):
+        s = step * block + i
+        sided = ints[KIND, s] + KINDS * (1 - ints[FORWARD, s])
+        apply = slot_stencil(floats, ints, s, row)
+        for x in range(depth):
+            low, high = apply(second[sided, x, :8, :], second[sided, x, 8:, :])
+            energy[i, x, :8, :] = swept[i, x, :8, :] + (low + added[sided, x, :8, :])
+            energy[i, x, 8:, :] = swept[i, x, 8:, :] + (high + added[sided, x, 8:, :])
+        return carry
+
+    lax.fori_loop(0, block, one_slot, 0, unroll=2)
+
+
+def inflow_kernel(sizes, meta, floats, ints, warm, *refs):
+    block, depth, own, group = sizes
+    received, (energy, ordered) = refs[:group], refs[group:]
+    step = pl.program_id(0)
 
     @pl.when(step == 0)
     def _():
         for by in range(group):
-            at = pl.ds(pl.multiple_of(((slab % group) ^ by) * own * 16, 16), own * 16)
-            for index in range(ITERS):
-                ordered[index][at, :] = received[by][index]
-        for pack, by in zip(packs, order):
-            at = pl.ds(pl.multiple_of((mode ^ by) * lanes, 128), lanes)
-            warm_one[:, at] = pack[:cells, :]
-            warm_two[:, at] = pack[cells : 2 * cells, :]
-            late[:, at] = pack[2 * cells :, :]
-        home = pl.ds(pl.multiple_of(slab * depth, 8), depth)
-        chunk = 4
-        plain, around = [], []
-        for c in range(width_y // chunk):
-            at = slice(c * chunk * 128, (c + 1) * chunk * 128)
-            one, two = warm_one[:, at], warm_two[:, at]
-            one = exact_dot(first_matrix[...], jnp.concatenate([one, fourth(one)], axis=0))
-            two = exact_dot(second_matrix[...], jnp.concatenate([two, fourth(two)], axis=0))
-            for yy in range(chunk):
-                y, lane = c * chunk + yy, slice(yy * 128, (yy + 1) * 128)
-                scattered = pl.ds(y, 2 * KINDS, stride=width_y)
-                enter_one[scattered, :] = one[: 2 * KINDS, lane]
-                enter_long[scattered, :] = one[2 * KINDS : 4 * KINDS, lane]
-                enter_two[scattered, :] = two[: 2 * KINDS, lane]
-                plain.append(one[4 * KINDS : 4 * KINDS + depth, lane] + two[2 * KINDS :, lane])
-                around.append(one[4 * KINDS + depth :, lane])
-        for y in range(width_y):
-            lane = slice(y * 128, (y + 1) * 128)
-            near = around[y - 1] + around[(y + 1) % width_y]
-            near = near + (pltpu.roll(around[y], 1, 1) + pltpu.roll(around[y], width_z - 1, 1))
-            density = late[:, lane] + plain[y] + near
-            scattered = pl.ds(y, depth, stride=width_y)
-            now = warm_two[home, lane]
-            kelvin[scattered, :] = newton(density, now, sums[0], sums[1])
-            own_one[scattered, :] = warm_one[home, lane]
-            own_two[scattered, :] = now
-
-        def one_kind(kind, carry):
-            therm, quart, decay = kinds[THERM, kind], kinds[QUART, kind], kinds[DECAY, kind]
-            at = pl.ds(pl.multiple_of(kind * 16, 16), 16)
-            back_at = pl.ds(pl.multiple_of((kind + KINDS) * 16, 16), 16)
-            layers = []
-            for x in range(depth):
-                here = slice(x * 16, x * 16 + 16)
-                t, u = own_one[here, :], own_two[here, :]
-                layers.append(therm * t + quart * fourth(t))
-                added[kind, x] = therm * u + quart * fourth(u)
-            up, down = enter_one[at, :], enter_one[back_at, :]
-            for j in range(depth):
-                up = decay * up + layers[j]
-                down = decay * down + layers[depth - 1 - j]
-                second[kind, j] = up
-                second[kind + KINDS, j] = down
-            return carry
-
-        lax.fori_loop(0, KINDS, one_kind, 0)
-
-    row = lax.broadcasted_iota(jnp.int32, (8, 128), 0)
+            ordered[(meta[SLAB] % group) ^ by] = received[by][...]
 
     def one_slot(i, carry):
         s = step * block + i
         start, stride = course(ints, s, depth)
-        ratio, kind = floats[RATIO, s], ints[KIND, s]
-        sided = kind + KINDS * (1 - ints[FORWARD, s])
-        apply = slot_stencil(floats, ints, s, row)
-        at, kind_at = rows_of(s), rows_of(sided)
-        one, two, three = ([ref[half, :] for half in at] for ref in ordered)
-        longer = apply(*(enter_long[half, :] for half in kind_at))
-        three = [a + b + enter_two[half, :] for a, b, half in zip(three, longer, kind_at)]
+        ratio = floats[RATIO, s]
+        at = pl.ds(pl.multiple_of((s % own) * 16, 16), 16)
+        one, two, three = (ordered[s // own, plane, at, :] for plane in range(ITERS))
         for j in range(depth):
             x = start + stride * j
-            fresh = apply(second[sided, j, :8, :], second[sided, j, 8:, :])
-            for half, here in enumerate((slice(0, 8), slice(8, 16))):
-                one[half] = ratio * one[half]
-                two[half] = ratio * two[half] + one[half]
-                three[half] = ratio * three[half] + (fresh[half] + added[kind, x, here, :] + two[half])
-                energy[i, x, here, :] = swept[i, x, here, :] + three[half]
+            one = ratio * one
+            two = ratio * two + one
+            three = ratio * three + two
+            energy[i, x] = warm[i, x] + three
         return carry
 
-    lax.fori_loop(0, block, one_slot, 0, unroll=2)
+    lax.fori_loop(0, block, one_slot, 0, unroll=4)
 
 
 def local(incoming_occupation, crystal_kelvin_given, generating_region_flag, labels, speed, rate, storage, threshold, generation):
@@ -497,7 +558,7 @@
     face_rows = own * width_y
     slab = lax.axis_index("slab").astype(jnp.int32)
     meta = jnp.stack([slab, lax.axis_index("mode").astype(jnp.int32)])
-    floats, ints, matrix = slot_tables(labels, speed, rate, storage, threshold, generation, slab, slabs, depth, width_z)
+    floats, ints = slot_tables(labels, speed, rate, storage, threshold, generation, slab, slabs, depth, width_z)
     kinds = kind_table(speed, rate, storage, threshold, generation)
     everywhere, first_matrix, second_matrix = heat_matrices(kinds, slab, slabs, depth)
     sums = jnp.stack([jnp.sum(storage), jnp.sum(storage / (4.0 * threshold**3))])
@@ -532,7 +593,7 @@
     swept, quarter, *rest = pl.pallas_call(
         functools.partial(sweeps_kernel, (block, blocks, depth, width_y, slots, modes, group)),
         grid=(blocks,),
-        in_specs=[SMEM] * 4 + [slot_block, whole(cells, width_z), whole(cells, width_z), whole(all_x, ITERS * slots)],
+        in_specs=[SMEM] * 7 + [slot_block, whole(cells, width_z), whole(cells, width_z), whole(1, slots)],
         out_specs=[slot_block, whole(depth, lanes)] + [whole(*face)] * group + [whole(*half)] * 2,
         out_shape=[slot_shape, shape(depth, lanes)] + [shape(*face)] * group + [shape(*half)] * 2,
         scratch_shapes=[scratch(slots * width_y, width_z)] * 6
@@ -541,18 +602,22 @@
             scratch(ITERS, cells, width_z),
             scratch(KINDS, depth, width_y, width_z),
             scratch(depth, width_y, width_z),
+            scratch(8, KINDS, 8, width_z),
         ],
         compiler_params=PARAMS,
         name="sweeps",
     )(
         meta,
-        floats,
-        ints,
-        kinds,
+        labels,
+        speed,
+        rate,
+        storage,
+        threshold,
+        generation,
         incoming_occupation,
         generating_region_flag.reshape(cells, width_z),
         crystal_kelvin_given.reshape(cells, width_z),
-        matrix,
+        labels.reshape(1, slots),
     )
     faces, (keep, send) = rest[:group], rest[group:]
 
@@ -566,31 +631,32 @@
         other = swap(send, "mode", by)
     piece = (slabs, ITERS, depth, lanes)
     (parts,) = call(functools.partial(parts_kernel, depth), "density_parts", [VMEM] * 2, [shape(*piece)], keep, other)
-    parts = lax.all_to_all(parts, "slab", 0, 0)
-    copies, late = call(totals_kernel, "density_totals", [VMEM] * 2, [shape(*piece), shape(depth, lanes)], parts, quarter)
-    gathered = lax.all_to_all(copies, "slab", 0, 0)
-    pack_shape = shape(2 * all_x + depth, lanes)
-    (packed,) = call(
-        functools.partial(kelvins_kernel, depth), "kelvins", [SMEM] + [VMEM] * 3, [pack_shape], sums, gathered, late, everywhere
-    )
-    packs, order = [packed], [0]
-    while by:
-        packs = packs + [swap(pack, "mode", by) for pack in packs]
-        order = order + [index ^ by for index in order]
-        by //= 2
+    summed = lax.all_to_all(parts, "slab", 0, 0)
 
     composite, effective = call(
         functools.partial(compose_kernel, own, group),
         "compose",
-        [SMEM] * 3 + [VMEM] * group,
+        [SMEM] * 3 + [VMEM] * group + [pl.BlockSpec(memory_space=pl.ANY)],
         [shape(*face), shape(group, *face)],
         meta,
         floats,
         ints,
         *received,
+        parts,
         scratches=[scratch(group, *face)],
     )
+    summed, composite = lax.optimization_barrier((summed, composite))
     composites = [composite] + [swap(composite, "slab", index * group) for index in range(1, groups)]
+    copies, late = call(
+        totals_kernel,
+        "density_totals",
+        [SMEM] + [VMEM] * 2,
+        [shape(slabs, 2, depth, lanes), shape(depth, lanes)],
+        sums,
+        summed,
+        quarter,
+    )
+    gathered = lax.all_to_all(copies, "slab", 0, 0)
     entering = call(
         functools.partial(enter_kernel, own, group, groups, depth),
         "enter",
@@ -603,27 +669,51 @@
         *composites,
         scratches=[scratch(groups, *face), scratch(group, *face)],
     )
+    gathered, entering = lax.optimization_barrier((gathered, entering))
     entering = [entering[0]] + [swap(entering[index], "slab", index) for index in range(1, group)]
 
-    energy, kelvin = pl.pallas_call(
-        functools.partial(final_kernel, (block, depth, width_y, width_z, slots, slabs, modes, group), order),
+    pack_shape = shape(6 * KINDS + 4 * depth, lanes)
+    (packed,) = call(
+        functools.partial(kelvins_kernel, depth),
+        "kelvins",
+        [SMEM] * 2 + [VMEM] * 4,
+        [pack_shape],
+        meta,
+        sums,
+        gathered,
+        late,
+        jnp.concatenate([everywhere, first_matrix], axis=0),
+        second_matrix,
+    )
+    packs, order = [packed], [0]
+    while by:
+        packs = packs + [swap(pack, "mode", by) for pack in packs]
+        order = order + [index ^ by for index in order]
+        by //= 2
+
+    warm, kelvin = pl.pallas_call(
+        functools.partial(warm_kernel, (block, depth, width_y, width_z, modes), order),
         grid=(blocks,),
-        in_specs=[SMEM] * 5
-        + [slot_block]
-        + [whole(*face)] * group
-        + [whole(*pack_shape.shape)] * modes
-        + [whole(*first_matrix.shape), whole(*second_matrix.shape)],
+        in_specs=[SMEM] * 5 + [slot_block] + [whole(*pack_shape.shape)] * modes,
         out_specs=[slot_block, whole(cells, width_z)],
         out_shape=[slot_shape, shape(cells, width_z)],
-        scratch_shapes=[scratch(all_x, width_y * width_z)] * 2
-        + [scratch(depth, width_y * width_z)]
-        + [scratch(2 * KINDS * width_y, width_z)] * 3
-        + [scratch(2 * KINDS, depth, width_y, width_z), scratch(KINDS, depth, width_y, width_z)]
+        scratch_shapes=[scratch(2 * KINDS * width_y, width_z)] * 3
+        + [scratch(2 * KINDS, depth, width_y, width_z)] * 2
         + [scratch(cells, width_z)] * 2
-        + [scratch(slots * width_y, width_z)] * 3,
+        + [scratch(width_y, depth, width_z)] * 2,
         compiler_params=PARAMS,
-        name="final_energy",
-    )(meta, floats, ints, kinds, sums, swept, *entering, *packs, first_matrix, second_matrix)
+        name="warm",
+    )(meta, floats, ints, kinds, sums, swept, *packs)
+    energy = pl.pallas_call(
+        functools.partial(inflow_kernel, (block, depth, own, group)),
+        grid=(blocks,),
+        in_specs=[SMEM] * 3 + [slot_block] + [whole(*face)] * group,
+        out_specs=slot_block,
+        out_shape=slot_shape,
+        scratch_shapes=[scratch(group, *face)],
+        compiler_params=PARAMS,
+        name="inflow",
+    )(meta, floats, ints, warm, *entering)
     return energy, kelvin.reshape(depth, width_y, width_z)
 
 

time: 123 us -> 133 us (1.081)
  local copies, waits for them, and re-layouts: 7.54 us -> 18.4 us
  waiting for transfers between devices: 43.2 us -> 35.5 us
  Pallas kernels: 32.9 us -> 37.9 us
  other arithmetic: 13.2 us -> 14.6 us
    unnamed x30 -> x63, local copies, waits for them, and re-layouts: 4.2 us -> 15.2 us
    all_to_all x1, waiting for transfers between devices: 10.5 us -> 0.01 us  [local(): gathered = lax.all_to_all(copies, 'slab', 0, 0)]
    ppermute x12, waiting for transfers between devices: 21.9 us -> 28.9 us  [swap(): lax.ppermute(array, axis, [(i, i ^ by) for i in range(lax.axis_size(axis))])]
    all_to_all x1, waiting for transfers between devices: 10.9 us -> 6.62 us  [local(): summed = lax.all_to_all(parts, 'slab', 0, 0)]
    pallas_call x1 -> x2, Pallas kernels: 10.5 us -> 13.9 us  [the longest x1 8.74 us: local(): pl.pallas_call(functools.partial(warm_kernel, (block, depth, width_y, wid...]
    unnamed x0 -> x2, other arithmetic: none -> 2.03 us
    pallas_call x1, Pallas kernels: 15.1 us -> 16.9 us  [local(): pl.pallas_call(functools.partial(sweeps_kernel, (block, blocks, depth, wi...]
  transfers between devices with their start and end apart: 14 -> 14, of which waited for: 8 -> 6; matrix products, arithmetic and copies ran while one was open for 9% -> 14% of each run, Pallas kernels for 6% -> 10%
where the time goes in v7:
time: 133 us; the launch traced here: 132 us
  Pallas kernels  37.9 us (28%)
  waiting for transfers between devices  35.5 us (27%)
  starting transfers between devices  24.2 us (18%)
  local copies, waits for them, and re-layouts  18.4 us (14%)
  other arithmetic  14.6 us (11%)
    ppermute x12, waiting for transfers between devices, swap(): lax.ppermute(array, axis, [(i, i ^ by) for i in range(lax.axis_size(axis))])  28.9 us
    pallas_call x1, Pallas kernels, local(): pl.pallas_call(functools.partial(sweeps_kernel, (block, blocks, depth, wi...  16.9 us
    unnamed x63, local copies, waits for them, and re-layouts  15.2 us
    ppermute x12, starting transfers between devices, swap(): lax.ppermute(array, axis, [(i, i ^ by) for i in range(lax.axis_size(axis))])  14.4 us
    pallas_call x1, Pallas kernels, local(): pl.pallas_call(functools.partial(warm_kernel, (block, depth, width_y, wid...  8.74 us
    pallas_call x6, Pallas kernels, call(): pl.pallas_call(kernel, in_specs=in_specs, out_specs=[VMEM] * len(out_shap...  7.04 us
    all_to_all x1, waiting for transfers between devices, local(): summed = lax.all_to_all(parts, 'slab', 0, 0)  6.62 us
    all_to_all x1, starting transfers between devices, local(): summed = lax.all_to_all(parts, 'slab', 0, 0)  6.12 us
  transfers between devices with their start and end apart: 14, of which 6 were waited for; matrix products, arithmetic and copies ran while one was open for 14% of the time, Pallas kernels for 10%

profile of v7, /device:TPU:0, one launch (start us, length us, event | category | flops | bytes accessed | tf_op | source)
XLA Modules:
  0.0 131.7 jit_solution(17198749237643846015)
XLA Ops:
  0.8 0.8 copy-done.4
  1.6 0.8 copy-done.5
  2.4 0.7 copy-done.10
  3.1 0.7 copy-done.12
  3.8 0.7 copy-done.14
  4.4 0.7 copy-done.19
  5.1 0.7 copy-done.21
  5.7 0.7 copy-done.22
  6.4 16.9 %sweeps.1 = (f32[64,8,16,128]{3,2,1,0:T(8,128)}, f32[8,512]{1,0:T(8,128)S(1)}, f32[3,256,128]{2,1,0:T(8,128)S(1)}, f32[3,256,128]{2,1,0:T(8,128)}, f32[3,256,128...) custom-call(s32[2]{0:T(128)S(1)} %pad_add_fusion.1.meta, ...), custom_call_target="tpu_custom_call" | custom-call | tf_op jit(solution)/shard_map/sweeps/pallas_call | solution.py:593
  23.3 0.6 copy-done.6
  23.9 3.0 %collective-permute-start.2 = (f32[3,256,128]{2,1,0:T(8,128)}, f32[3,256,128]{2,1,0:T(8,128)S(1)}, u32[]{:S(2)}, u32[]{:S(2)}) collective-permute-start(f32[3,256,128]{2,1,0:T(8,128)} %get-tuple-element.35), channel_id=1, source_target_pairs={{0,4},{4,0},{8,12},{12,8},{16,20},{20,16},{24,28},{28,24},{1,5},{5... | collective-permute-start | bytes 1179656 | tf_op jit(solution)/shard_map/ppermute | solution.py:576
  26.9 1.6 %collective-permute-start.3 = (f32[3,256,128]{2,1,0:T(8,128)}, f32[3,256,128]{2,1,0:T(8,128)S(1)}, u32[]{:S(2)}, u32[]{:S(2)}) collective-permute-start(f32[3,256,128]{2,1,0:T(8,128)} %get-tuple-element.36), channel_id=1, source_target_pairs={{0,8},{4,12},{8,0},{12,4},{16,24},{20,28},{24,16},{28,20},{1,9},{5... | collective-permute-start | bytes 1179656 | tf_op jit(solution)/shard_map/ppermute | solution.py:576
  28.5 0.6 broadcast_maximum_fusion
  29.2 0.1 select_reduce_fusion
  29.3 0.7 fusion.38
  30.1 0.6 copy-done.25
  31.6 0.2 copy-done.30
  31.9 1.2 multiply_reduce_fusion.1
  33.1 0.6 maximum_add_fusion
  33.7 0.7 maximum_dynamic-update-slice_fusion
  34.6 1.9 %collective-permute-start.1 = (f32[1,3,64,512]{3,2,1,0:T(8,128)S(1)}, f32[1,3,64,512]{3,2,1,0:T(8,128)S(1)}, u32[]{:S(2)}, u32[]{:S(2)}) collective-permute-start(f32[1,3,64,512]{3,2,1,0:T(8,128)S(1)} %get-tuple-element.33), channel_id=1, source_target_pairs={{0,2},{1,3},{2,0},{3,1},{4,6},{5,7},{6,4},{7,5},{8,10},{9,11},{10,... | collective-permute-start | bytes 1179656 | tf_op jit(solution)/shard_map/ppermute | solution.py:576
  36.5 9.8 %collective-permute-done.1.other = f32[1,3,64,512]{3,2,1,0:T(8,128)S(1)} collective-permute-done((f32[1,3,64,512]{3,2,1,0:T(8,128)S(1)}, f32[1,3,64,512]{3,2,1,0:T(8,128)S(1)}, u32[]{:S(2)}, u32[]{:S(2)}) %collective-permute-start.1) | collective-permute-done | bytes 393248 | tf_op jit(solution)/shard_map/ppermute | solution.py:576
  46.3 0.8 density_parts.1.refs_4_
  47.1 6.1 %all-to-all-start = ((f32[8,3,8,512]{3,2,1,0:T(8,128)}), f32[8,3,8,512]{3,2,1,0:T(8,128)S(1)}, u32[]{:S(2)}, u32[]{:S(2)}) async-start(f32[8,3,8,512]{3,2,1,0:T(8,128)} %density_parts.1.refs_4_), calls=%async_computation | async-start | bytes 786432 | tf_op jit(solution)/shard_map/all_to_all | solution.py:634
  53.3 2.0 %pad_maximum_fusion.2.sums = f32[2]{0:T(128)} fusion(f32[1]{0:T(128)} %bitcast.33, f32[1]{0:T(128)} %bitcast.32), kind=kLoop, calls=%fused_computation.86 | loop fusion | flops 2 | bytes 16 | tf_op jit(solution)/shard_map/stack | solution.py:564
  55.4 0.8 multiply_reduce_fusion.3
  56.2 1.2 compose.1
  57.4 0.8 copy-done
  58.2 6.6 %all-to-all-done.parts = f32[8,3,8,512]{3,2,1,0:T(8,128)S(1)} async-done(((f32[8,3,8,512]{3,2,1,0:T(8,128)}), f32[8,3,8,512]{3,2,1,0:T(8,128)S(1)}, u32[]{:S(2)}, u32[]{:S(2)}) %all-to-all-start) | async-done | bytes 393248 | tf_op jit(solution)/shard_map/all_to_all | solution.py:634
  64.8 0.7 copy-done.7
  65.5 0.7 copy-done.16
  66.2 1.3 density_totals.1
  67.5 3.6 %all-to-all-start.1 = ((f32[8,2,8,512]{3,2,1,0:T(8,128)}), f32[8,2,8,512]{3,2,1,0:T(8,128)S(1)}, u32[]{:S(2)}, u32[]{:S(2)}) async-start(f32[8,2,8,512]{3,2,1,0:T(8,128)} %get-tuple-element.41), calls=%async_computation.1 | async-start | bytes 524288 | tf_op jit(solution)/shard_map/all_to_all | solution.py:659
  71.2 0.7 broadcast_compare_fusion
  71.8 0.7 mul.349
  72.6 0.6 pow.55
  73.3 0.6 mul.353
  73.9 0.7 fusion.6
  74.7 1.3 %bitcast_multiply_fusion = (f32[32,128]{1,0:T(8,128)S(1)}, f32[144,128]{1,0:T(8,128)}) fusion(f32[2,128]{1,0:T(2,128)} %maximum_add_fusion, f32[32,64]{1,0:T(8,128)S(1)} %get-tuple-element.101, f32[32,64]{1,0:T(8,128)S(1)} %get-tuple-element.100, f32[144,128]{1,0:T(8,128)} %maximum_dynamic-update-slice_fusion), kind=kLoop, calls=%fused_computation.18 | loop fusion | flops 8192 | bytes 50176 | tf_op jit(solution)/shard_map/mul | solution.py:134
  76.0 2.9 %collective-permute-start.5 = (f32[3,256,128]{2,1,0:T(8,128)}, f32[3,256,128]{2,1,0:T(8,128)S(1)}, u32[]{:S(2)}, u32[]{:S(2)}) collective-permute-start(f32[3,256,128]{2,1,0:T(8,128)} %copy-done), channel_id=1, source_target_pairs={{0,16},{4,20},{8,24},{12,28},{16,0},{20,4},{24,8},{28,12},{1,17},{... | collective-permute-start | bytes 1179656 | tf_op jit(solution)/shard_map/ppermute | solution.py:576
  78.9 0.6 constant_dynamic-update-slice_fusion.2
  79.5 1.4 %constant_dynamic-update-slice_fusion.1 = f32[144,128]{1,0:T(8,128)} fusion(f32[144,128]{1,0:T(8,128)} %constant_dynamic-update-slice_fusion.2, f32[8,64]{1,0:T(8,128)} %get-tuple-element.65, f32[8,64]{1,0:T(8,128)} %get-tuple-element.64), kind=kLoop, calls=%fused_computation.24 | loop fusion | flops 1024 | bytes 12288
  80.9 1.3 %constant_dynamic-update-slice_fusion.matrix_one = f32[144,128]{1,0:T(8,128)} fusion(f32[144,128]{1,0:T(8,128)} %constant_dynamic-update-slice_fusion.1, f32[8,64]{1,0:T(8,128)} %get-tuple-element.66, f32[8,64]{1,0:T(8,128)} %get-tuple-element.67), kind=kLoop, calls=%fused_computation.23 | loop fusion | flops 1024 | bytes 12288 | tf_op jit(solution)/shard_map/concatenate | solution.py:685
  82.2 1.4 %maximum_maximum_fusion.matrix_two = f32[40,128]{1,0:T(8,128)} fusion(f32[8,64]{1,0:T(8,128)} %get-tuple-element.63, f32[8,64]{1,0:T(8,128)} %get-tuple-element.62, f32[32,64]{1,0:T(8,128)S(1)} %get-tuple-element.101, f32[32,64]{1,0:T(8,128)S(1)} %get-tuple-element.100), kind=kLoop, calls=%fused_computation.16 | loop fusion | flops 15360 | bytes 40960 | tf_op jit(solution)/shard_map/concatenate | solution.py:139
  83.6 12.9 %collective-permute-done.5.refs_1_ = f32[3,256,128]{2,1,0:T(8,128)S(1)} collective-permute-done((f32[3,256,128]{2,1,0:T(8,128)}, f32[3,256,128]{2,1,0:T(8,128)S(1)}, u32[]{:S(2)}, u32[]{:S(2)}) %collective-permute-start.5) | collective-permute-done | bytes 393248 | tf_op jit(solution)/shard_map/ppermute | solution.py:576
  96.5 1.0 copy-done.1
  97.5 2.3 %enter.1 = (f32[3,256,128]{2,1,0:T(8,128)S(1)}, f32[3,256,128]{2,1,0:T(8,128)}, f32[3,256,128]{2,1,0:T(8,128)}, f32[3,256,128]{2,1,0:T(8,128)S(1)}) custom-call(s32[2]{0:T(128)S(1)} %pad_add_fusion.1.meta, f32[10,64]{1,0:T(8,128)S(1)} %stack.141.floats, s32[5,64]{1,0:T(8,128)S(1)} %stack.148.ints, f32[4,3,256,128]{3,2,1,0:T(8,128)S(1)} %get-tuple-element.42.effective, ...), custom_call_target="tpu_custom_call" | custom-call | tf_op jit(solution)/shard_map/enter/pallas_call | solution.py:579
  99.8 0.7 copy-done.23
  100.5 0.9 copy-done.2
  101.4 0.7 copy-done.3
  102.1 0.7 copy-done.9
  102.9 0.7 copy-done.17
  103.5 1.4 %kelvins.1.refs_0_ = f32[128,512]{1,0:T(8,128)S(1)} custom-call(s32[2]{0:T(128)S(1)} %pad_add_fusion.1.meta, f32[2]{0:T(128)S(1)} %copy-done.17, f32[8,2,8,512]{3,2,1,0:T(8,128)S(1)} %all-to-all-done.1.gathered, f32[8,512]{1,0:T(8,128)S(1)} %copy-done.9, f32[144,128]{1,0:T(8,128)S(1)} %copy-done.2, f32[40,128]{1,0:T(8,128)S(1)} %copy-done.3), custom_call_target="tpu_custom_call" | custom-call | tf_op jit(solution)/shard_map/kelvins/pallas_call | solution.py:579
  104.9 1.5 %collective-permute-start.6 = (f32[128,512]{1,0:T(8,128)S(1)}, f32[128,512]{1,0:T(8,128)S(1)}, u32[]{:S(2)}, u32[]{:S(2)}) collective-permute-start(f32[128,512]{1,0:T(8,128)S(1)} %kelvins.1.refs_0_), channel_id=1, source_target_pairs={{0,2},{1,3},{2,0},{3,1},{4,6},{5,7},{6,4},{7,5},{8,10},{9,11},{10,... | collective-permute-start | bytes 786440 | tf_op jit(solution)/shard_map/ppermute | solution.py:576
  106.5 1.3 collective-permute-start.9
  107.8 2.2 %collective-permute-start.11 = (f32[3,256,128]{2,1,0:T(8,128)}, f32[3,256,128]{2,1,0:T(8,128)S(1)}, u32[]{:S(2)}, u32[]{:S(2)}) collective-permute-start(f32[3,256,128]{2,1,0:T(8,128)} %copy-done.23), channel_id=1, source_target_pairs={{0,12},{4,8},{8,4},{12,0},{16,28},{20,24},{24,20},{28,16},{1,13},{... | collective-permute-start | bytes 1179656 | tf_op jit(solution)/shard_map/ppermute | solution.py:576
  109.9 2.7 %collective-permute-done.6.refs_1_ = f32[128,512]{1,0:T(8,128)S(1)} collective-permute-done((f32[128,512]{1,0:T(8,128)S(1)}, f32[128,512]{1,0:T(8,128)S(1)}, u32[]{:S(2)}, u32[]{:S(2)}) %collective-permute-start.6) | collective-permute-done | bytes 262176 | tf_op jit(solution)/shard_map/ppermute | solution.py:576
  112.7 0.7 pad_maximum_fusion.1
  113.4 0.1 copy.34
  113.6 0.7 collective-permute-done.8.refs_3_
  114.2 0.7 copy-done.18
  114.9 8.7 %warm.1 = (f32[64,8,16,128]{3,2,1,0:T(8,128)S(1)}, f32[128,128]{1,0:T(8,128)}) custom-call(s32[2]{0:T(128)S(1)} %pad_add_fusion.1.meta, f32[10,64]{1,0:T(8,128)S(1)} %stack.141.floats, s32[5,64]{1,0:T(8,128)S(1)} %stack.148.ints, f32[6,16]{1,0:T(8,128)S(1)} %copy.40.kinds, f32[2]{0:T(128)S(1)} %copy-done.18, f32[64,8,16,128]{3,2,1,0:T(8,128)} %get-tuple-element.29.swept, ...), custom_call_target="tpu_custom_call" | custom-call | tf_op jit(solution)/shard_map/warm/pallas_call | solution.py:694
  123.6 2.8 %collective-permute-done.11.refs_3_ = f32[3,256,128]{2,1,0:T(8,128)S(1)} collective-permute-done((f32[3,256,128]{2,1,0:T(8,128)}, f32[3,256,128]{2,1,0:T(8,128)S(1)}, u32[]{:S(2)}, u32[]{:S(2)}) %collective-permute-start.11) | collective-permute-done | bytes 393248 | tf_op jit(solution)/shard_map/ppermute | solution.py:576
  126.5 5.2 %inflow.1 = f32[64,8,16,128]{3,2,1,0:T(8,128)} custom-call(s32[2]{0:T(128)S(1)} %pad_add_fusion.1.meta, f32[10,64]{1,0:T(8,128)S(1)} %stack.141.floats, s32[5,64]{1,0:T(8,128)S(1)} %stack.148.ints, f32[64,8,16,128]{3,2,1,0:T(8,128)S(1)} %get-tuple-element.50.warm, f32[3,256,128]{2,1,0:T(8,128)S(1)} %get-tuple-element.51.refs_0_, ...), custom_call_target="tpu_custom_call" | custom-call | tf_op jit(solution)/shard_map/inflow/pallas_call | solution.py:707
  (95 shorter events, 2.0 us)
Async XLA Ops:
  0.6 28.6 %copy-start.11 = (f32[8]{0:T(128)S(1)}, f32[8]{0:T(128)}, u32[]{:S(2)}) copy-start(f32[8]{0:T(128)} %refs_3_.1) | copy-start | bytes 100
  0.6 28.4 %copy-start.13 = (f32[8]{0:T(128)S(1)}, f32[8]{0:T(128)}, u32[]{:S(2)}) copy-start(f32[8]{0:T(128)} %refs_1_.1) | copy-start | bytes 100
  0.7 28.4 %copy-start.15 = (f32[8]{0:T(128)S(1)}, f32[8]{0:T(128)}, u32[]{:S(2)}) copy-start(f32[8]{0:T(128)} %refs_0_.1) | copy-start | bytes 100
  0.7 28.5 %copy-start.20 = (s32[64]{0:T(128)S(1)}, s32[64]{0:T(128)}, u32[]{:S(2)}) copy-start(s32[64]{0:T(128)} %labels.1) | copy-start | bytes 772
  0.8 0.8 copy-start.4
  1.6 0.8 copy-start.5
  2.4 0.7 copy-start.10
  3.1 0.7 copy-start.12
  3.8 0.7 copy-start.14
  4.4 0.7 copy-start.19
  5.1 0.7 copy-start.21
  5.7 0.7 copy-start.22
  23.3 0.6 copy-start.6
  23.9 32.3 %collective-permute-start.2 = (f32[3,256,128]{2,1,0:T(8,128)}, f32[3,256,128]{2,1,0:T(8,128)S(1)}, u32[]{:S(2)}, u32[]{:S(2)}) collective-permute-start(f32[3,256,128]{2,1,0:T(8,128)} %get-tuple-element.35), channel_id=1, source_target_pairs={{0,4},{4,0},{8,12},{12,8},{16,20},{20,16},{24,28},{28,24},{1,5},{5... | collective-permute-start | bytes 1179656 | tf_op jit(solution)/shard_map/ppermute | solution.py:576
  26.9 29.3 %collective-permute-start.3 = (f32[3,256,128]{2,1,0:T(8,128)}, f32[3,256,128]{2,1,0:T(8,128)S(1)}, u32[]{:S(2)}, u32[]{:S(2)}) collective-permute-start(f32[3,256,128]{2,1,0:T(8,128)} %get-tuple-element.36), channel_id=1, source_target_pairs={{0,8},{4,12},{8,0},{12,4},{16,24},{20,28},{24,16},{28,20},{1,9},{5... | collective-permute-start | bytes 1179656 | tf_op jit(solution)/shard_map/ppermute | solution.py:576
  28.5 27.8 %collective-permute-start.4 = (f32[3,256,128]{2,1,0:T(8,128)}, f32[3,256,128]{2,1,0:T(8,128)S(1)}, u32[]{:S(2)}, u32[]{:S(2)}) collective-permute-start(f32[3,256,128]{2,1,0:T(8,128)} %get-tuple-element.37), channel_id=1, source_target_pairs={{0,12},{4,8},{8,4},{12,0},{16,28},{20,24},{24,20},{28,16},{1,13},{... | collective-permute-start | bytes 1179656 | tf_op jit(solution)/shard_map/ppermute | solution.py:576
  28.5 6.0 %collective-permute-start = (f32[2,3,64,512]{3,2,1,0:T(8,128)}, f32[2,3,64,512]{3,2,1,0:T(8,128)S(1)}, u32[]{:S(2)}, u32[]{:S(2)}) collective-permute-start(f32[2,3,64,512]{3,2,1,0:T(8,128)} %get-tuple-element.31), channel_id=1, source_target_pairs={{0,1},{1,0},{2,3},{3,2},{4,5},{5,4},{6,7},{7,6},{8,9},{9,8},{10,11... | collective-permute-start | bytes 2359304 | tf_op jit(solution)/shard_map/ppermute | solution.py:576
  28.5 0.6 copy-start.27
  28.5 0.6 copy-start.28
  30.0 1.6 %copy-start.24 = (f32[6,8,1]{1,2,0:T(1,128)}, f32[6,8,1]{1,2,0:T(1,128)S(1)}, u32[]{:S(2)}) copy-start(f32[6,8,1]{1,2,0:T(1,128)S(1)} %copy.33) | copy-start | bytes 580
  30.1 0.6 copy-start.25
  31.0 0.6 copy-start.29
  31.2 25.1 %copy-start.26 = (f32[16]{0:T(128)}, f32[16]{0:T(128)S(1)}, u32[]{:S(2)}) copy-start(f32[16]{0:T(128)S(1)} %pow.51) | copy-start | bytes 196
  31.3 0.5 copy-start.30
  34.6 11.7 %collective-permute-start.1 = (f32[1,3,64,512]{3,2,1,0:T(8,128)S(1)}, f32[1,3,64,512]{3,2,1,0:T(8,128)S(1)}, u32[]{:S(2)}, u32[]{:S(2)}) collective-permute-start(f32[1,3,64,512]{3,2,1,0:T(8,128)S(1)} %get-tuple-element.33), channel_id=1, source_target_pairs={{0,2},{1,3},{2,0},{3,1},{4,6},{5,7},{6,4},{7,5},{8,10},{9,11},{10,... | collective-permute-start | bytes 1179656 | tf_op jit(solution)/shard_map/ppermute | solution.py:576
  47.1 17.7 %all-to-all-start = ((f32[8,3,8,512]{3,2,1,0:T(8,128)}), f32[8,3,8,512]{3,2,1,0:T(8,128)S(1)}, u32[]{:S(2)}, u32[]{:S(2)}) async-start(f32[8,3,8,512]{3,2,1,0:T(8,128)} %density_parts.1.refs_4_), calls=%async_computation | async-start | bytes 786432 | tf_op jit(solution)/shard_map/all_to_all | solution.py:634
  57.4 0.8 copy-start
  64.8 0.7 copy-start.7
  65.5 0.7 copy-start.16
  67.5 29.0 %copy-start.8 = (f32[8,512]{1,0:T(8,128)}, f32[8,512]{1,0:T(8,128)S(1)}, u32[]{:S(2)}) copy-start(f32[8,512]{1,0:T(8,128)S(1)} %get-tuple-element.49.late) | copy-start | bytes 49156
  67.5 33.0 %all-to-all-start.1 = ((f32[8,2,8,512]{3,2,1,0:T(8,128)}), f32[8,2,8,512]{3,2,1,0:T(8,128)S(1)}, u32[]{:S(2)}, u32[]{:S(2)}) async-start(f32[8,2,8,512]{3,2,1,0:T(8,128)} %get-tuple-element.41), calls=%async_computation.1 | async-start | bytes 524288 | tf_op jit(solution)/shard_map/all_to_all | solution.py:659
  76.0 20.5 %collective-permute-start.5 = (f32[3,256,128]{2,1,0:T(8,128)}, f32[3,256,128]{2,1,0:T(8,128)S(1)}, u32[]{:S(2)}, u32[]{:S(2)}) collective-permute-start(f32[3,256,128]{2,1,0:T(8,128)} %copy-done), channel_id=1, source_target_pairs={{0,16},{4,20},{8,24},{12,28},{16,0},{20,4},{24,8},{28,12},{1,17},{... | collective-permute-start | bytes 1179656 | tf_op jit(solution)/shard_map/ppermute | solution.py:576
  96.5 1.0 copy-start.1
  99.8 0.7 copy-start.23
  100.5 0.9 copy-start.2
  101.4 0.7 copy-start.3
  102.1 0.7 copy-start.9
  102.9 0.7 copy-start.17
  104.9 7.7 %collective-permute-start.6 = (f32[128,512]{1,0:T(8,128)S(1)}, f32[128,512]{1,0:T(8,128)S(1)}, u32[]{:S(2)}, u32[]{:S(2)}) collective-permute-start(f32[128,512]{1,0:T(8,128)S(1)} %kelvins.1.refs_0_), channel_id=1, source_target_pairs={{0,2},{1,3},{2,0},{3,1},{4,6},{5,7},{6,4},{7,5},{8,10},{9,11},{10,... | collective-permute-start | bytes 786440 | tf_op jit(solution)/shard_map/ppermute | solution.py:576
  106.5 17.2 %collective-permute-start.9 = (f32[3,256,128]{2,1,0:T(8,128)}, f32[3,256,128]{2,1,0:T(8,128)S(1)}, u32[]{:S(2)}, u32[]{:S(2)}) collective-permute-start(f32[3,256,128]{2,1,0:T(8,128)} %get-tuple-element.52), channel_id=1, source_target_pairs={{0,4},{4,0},{8,12},{12,8},{16,20},{20,16},{24,28},{28,24},{1,5},{5... | collective-permute-start | bytes 1179656 | tf_op jit(solution)/shard_map/ppermute | solution.py:576
  107.8 15.9 %collective-permute-start.10 = (f32[3,256,128]{2,1,0:T(8,128)}, f32[3,256,128]{2,1,0:T(8,128)S(1)}, u32[]{:S(2)}, u32[]{:S(2)}) collective-permute-start(f32[3,256,128]{2,1,0:T(8,128)} %get-tuple-element.53), channel_id=1, source_target_pairs={{0,8},{4,12},{8,0},{12,4},{16,24},{20,28},{24,16},{28,20},{1,9},{5... | collective-permute-start | bytes 1179656 | tf_op jit(solution)/shard_map/ppermute | solution.py:576
  107.8 18.7 %collective-permute-start.11 = (f32[3,256,128]{2,1,0:T(8,128)}, f32[3,256,128]{2,1,0:T(8,128)S(1)}, u32[]{:S(2)}, u32[]{:S(2)}) collective-permute-start(f32[3,256,128]{2,1,0:T(8,128)} %copy-done.23), channel_id=1, source_target_pairs={{0,12},{4,8},{8,4},{12,0},{16,28},{20,24},{24,20},{28,16},{1,13},{... | collective-permute-start | bytes 1179656 | tf_op jit(solution)/shard_map/ppermute | solution.py:576
  109.9 3.6 %collective-permute-start.7 = (f32[128,512]{1,0:T(8,128)S(1)}, f32[128,512]{1,0:T(8,128)S(1)}, u32[]{:S(2)}, u32[]{:S(2)}) collective-permute-start(f32[128,512]{1,0:T(8,128)S(1)} %kelvins.1.refs_0_), channel_id=1, source_target_pairs={{0,1},{1,0},{2,3},{3,2},{4,5},{5,4},{6,7},{7,6},{8,9},{9,8},{10,11... | collective-permute-start | bytes 786440 | tf_op jit(solution)/shard_map/ppermute | solution.py:576
  112.7 1.5 %collective-permute-start.8 = (f32[128,512]{1,0:T(8,128)S(1)}, f32[128,512]{1,0:T(8,128)S(1)}, u32[]{:S(2)}, u32[]{:S(2)}) collective-permute-start(f32[128,512]{1,0:T(8,128)S(1)} %collective-permute-done.6.refs_1_), channel_id=1, source_target_pairs={{0,1},{1,0},{2,3},{3,2},{4,5},{5,4},{6,7},{7,6},{8,9},{9,8},{10,11... | collective-permute-start | bytes 786440 | tf_op jit(solution)/shard_map/ppermute | solution.py:576
  114.2 0.7 copy-start.18

commit v8 on v7

--- a/solution.py
+++ b/solution.py
@@ -26,6 +26,7 @@
 SMEM = pl.BlockSpec(memory_space=pltpu.SMEM)
 VMEM = pl.BlockSpec(memory_space=pltpu.VMEM)
 PARAMS = pltpu.CompilerParams(vmem_limit_bytes=48 * 1024 * 1024)
+LARGE = pltpu.CompilerParams(vmem_limit_bytes=62 * 1024 * 1024)
 ACROSS = math.cos(math.pi / 8) + math.sin(math.pi / 8)
 
 
@@ -102,42 +103,49 @@
     return jnp.stack(rows, axis=2).reshape(6, KINDS)
 
 
-def heat_matrices(kinds, slab, slabs, depth):
-    cells = slabs * depth
-    there = jnp.arange(cells, dtype=jnp.int32)
-    decay = kinds[DECAY][:, None, None]
+def matrices_kernel(depth, meta, kinds, first, second):
+    cells = first.shape[1] // 2
+    slab = meta[SLAB]
+    sided = 2 * KINDS
     per_cell = (DIRS // 4) / DIRS
 
-    def side_by_side(weight, factor):
-        sums = [jnp.sum((factor * kinds[row])[:, None, None] * weight, axis=0) for row in (THERM, QUART)]
-        return jnp.concatenate(sums, axis=1)
-
-    def between(here):
-        far = jnp.abs(here[:, None] - there[None, :])
-        n = far.astype(jnp.float32)
-        return n, jnp.power(decay, n[None]) * jnp.where(far == 0, 2.0, 1.0)[None]
-
-    _, everywhere = between(there)
-    n, home = between(slab * depth + jnp.arange(depth, dtype=jnp.int32))
-    twice = home * (n + 1.0)[None]
-    one = jnp.full((KINDS,), per_cell, jnp.float32)
-    once = side_by_side(home, one)
-    stay = side_by_side(twice, kinds[STAY] / DIRS)
-    around = side_by_side(twice, kinds[AROUND] / DIRS)
-    before = jnp.stack([slab * depth - 1 - there, there - (slab + 1) * depth])
-    n = before.astype(jnp.float32)[:, None, :]
-    power = jnp.power(kinds[DECAY][None, :, None], jnp.maximum(n, 0.0))
-    inflow = jnp.where(before[:, None, :] >= 0, power, 0.0)
-    inflow = jnp.concatenate(
-        [inflow * kinds[THERM][None, :, None], inflow * kinds[QUART][None, :, None]], axis=2
-    )
-    longer = inflow * (jnp.concatenate([n, n], axis=2) + 1.0)
-    inflow, longer = (value.reshape(2 * KINDS, 2 * cells) for value in (inflow, longer))
-    return (
-        side_by_side(everywhere, one),
-        jnp.concatenate([inflow, longer, stay, around], axis=0),
-        jnp.concatenate([inflow, once], axis=0),
-    )
+    def places(rows):
+        column = lax.broadcasted_iota(jnp.int32, (rows, 2 * cells), 1)
+        quart = column >= cells
+        return jnp.where(quart, column - cells, column), quart
+
+    def distance(rows, base):
+        there, quart = places(rows)
+        far = jnp.abs(lax.broadcasted_iota(jnp.int32, (rows, 2 * cells), 0) + base - there)
+        return far.astype(jnp.float32), jnp.where(far == 0, 2.0, 1.0), quart
+
+    full, twice_full, quart_full = distance(cells, 0)
+    home, twice_home, quart_home = distance(depth, slab * depth)
+    there, quart_row = places(1)
+    gaps = [value.astype(jnp.float32) for value in (slab * depth - 1 - there, there - (slab + 1) * depth)]
+    everywhere = jnp.zeros((cells, 2 * cells), jnp.float32)
+    once = stay = around = jnp.zeros((depth, 2 * cells), jnp.float32)
+    for kind in range(KINDS):
+        therm, quart = kinds[THERM, kind], kinds[QUART, kind]
+        slope = jnp.log(jnp.full((1, 2 * cells), kinds[DECAY, kind], jnp.float32))
+        everywhere += jnp.where(quart_full, quart, therm) * (jnp.exp(full * slope) * twice_full)
+        weight = jnp.where(quart_home, quart, therm) * (jnp.exp(home * slope) * twice_home)
+        once += weight
+        weight = weight * (home + 1.0)
+        stay += kinds[STAY, kind] * weight
+        around += kinds[AROUND, kind] * weight
+        for side, gap in enumerate(gaps):
+            weight = jnp.where(quart_row, quart, therm) * jnp.exp(jnp.maximum(gap, 0.0) * slope)
+            weight = jnp.where(gap >= 0, weight, 0.0)
+            at = kind + side * KINDS
+            first[cells + at : cells + at + 1, :] = weight
+            first[cells + sided + at : cells + sided + at + 1, :] = weight * (gap + 1.0)
+            second[at : at + 1, :] = weight
+    first[:cells, :] = everywhere * per_cell
+    base = cells + 2 * sided
+    first[base : base + depth, :] = stay * (1.0 / DIRS)
+    first[base + depth :, :] = around * (1.0 / DIRS)
+    second[sided:, :] = once * per_cell
 
 
 def newton(density, kelvin, linear, quart):
@@ -560,7 +568,6 @@
     meta = jnp.stack([slab, lax.axis_index("mode").astype(jnp.int32)])
     floats, ints = slot_tables(labels, speed, rate, storage, threshold, generation, slab, slabs, depth, width_z)
     kinds = kind_table(speed, rate, storage, threshold, generation)
-    everywhere, first_matrix, second_matrix = heat_matrices(kinds, slab, slabs, depth)
     sums = jnp.stack([jnp.sum(storage), jnp.sum(storage / (4.0 * threshold**3))])
 
     def shape(*dims):
@@ -604,7 +611,7 @@
             scratch(depth, width_y, width_z),
             scratch(8, KINDS, 8, width_z),
         ],
-        compiler_params=PARAMS,
+        compiler_params=LARGE,
         name="sweeps",
     )(
         meta,
@@ -630,6 +637,17 @@
         keep, send = call(split_kernel, "density_split", [VMEM] * 2, [shape(*now)] * 2, keep, other)
         other = swap(send, "mode", by)
     piece = (slabs, ITERS, depth, lanes)
+    first_matrix, second_matrix = call(
+        functools.partial(matrices_kernel, depth),
+        "heat_matrices",
+        [SMEM] * 2,
+        [shape(all_x + 4 * KINDS + 2 * depth, 2 * all_x), shape(2 * KINDS + depth, 2 * all_x)],
+        meta,
+        kinds,
+    )
+    other, floats, ints, kinds, sums, first_matrix, second_matrix = lax.optimization_barrier(
+        (other, floats, ints, kinds, sums, first_matrix, second_matrix)
+    )
     (parts,) = call(functools.partial(parts_kernel, depth), "density_parts", [VMEM] * 2, [shape(*piece)], keep, other)
     summed = lax.all_to_all(parts, "slab", 0, 0)
 
@@ -682,7 +700,7 @@
         sums,
         gathered,
         late,
-        jnp.concatenate([everywhere, first_matrix], axis=0),
+        first_matrix,
         second_matrix,
     )
     packs, order = [packed], [0]

time: 133 us -> 131 us (0.985)
  waiting for transfers between devices: 35.5 us -> 59.7 us
  local copies, waits for them, and re-layouts: 18.4 us -> 4.04 us
  other arithmetic: 14.6 us -> 2.83 us
    ppermute x12, waiting for transfers between devices: 28.9 us -> 59.7 us  [swap(): lax.ppermute(array, axis, [(i, i ^ by) for i in range(lax.axis_size(axis))])]
    unnamed x63 -> x24, local copies, waits for them, and re-layouts: 15.2 us -> 3.66 us
    all_to_all x1, waiting for transfers between devices: 6.62 us -> 0.01 us  [local(): summed = lax.all_to_all(parts, 'slab', 0, 0)]
    concatenate x2 -> x0, other arithmetic: 2.7 us -> none  [the longest x1 1.36 us: heat_matrices(): jnp.concatenate([inflow, once], axis=0)]
    mul x3 -> x0, other arithmetic: 2.07 us -> none  [the longest x1 1.33 us: heat_matrices(): longer = inflow * (jnp.concatenate([n, n], axis=2) + 1.0)]
    reduce_sum x2 -> x0, other arithmetic: 2.03 us -> none  [side_by_side(): jnp.sum((factor * kinds[row])[:, None, None] * weight, axis=0)]
    unnamed x2 -> x0, other arithmetic: 2.03 us -> none
    mul x4 -> x0, local copies, waits for them, and re-layouts: 1.44 us -> none  [the longest x2 0.75 us: heat_matrices(): inflow * kinds[THERM][None, :, None]]
  transfers between devices with their start and end apart: 14 -> 14, of which waited for: 6 -> 9; matrix products, arithmetic and copies ran while one was open for 14% -> 2% of each run, Pallas kernels for 10% -> 9%
where the time goes in v8:
time: 131 us; the launch traced here: 130 us
  waiting for transfers between devices  59.7 us (46%)
  Pallas kernels  38.4 us (29%)
  starting transfers between devices  24.6 us (19%)
  local copies, waits for them, and re-layouts  4.04 us (3%)
  other arithmetic  2.83 us (2%)
    ppermute x12, waiting for transfers between devices, swap(): lax.ppermute(array, axis, [(i, i ^ by) for i in range(lax.axis_size(axis))])  59.7 us
    pallas_call x1, Pallas kernels, local(): pl.pallas_call(functools.partial(sweeps_kernel, (block, blocks, depth, wi...  17.5 us
    ppermute x12, starting transfers between devices, swap(): lax.ppermute(array, axis, [(i, i ^ by) for i in range(lax.axis_size(axis))])  15 us
    pallas_call x1, Pallas kernels, local(): pl.pallas_call(functools.partial(warm_kernel, (block, depth, width_y, wid...  8.74 us
    pallas_call x7, Pallas kernels, call(): pl.pallas_call(kernel, in_specs=in_specs, out_specs=[VMEM] * len(out_shap...  6.92 us
    all_to_all x1, starting transfers between devices, local(): summed = lax.all_to_all(parts, 'slab', 0, 0)  6.07 us
    pallas_call x1, Pallas kernels, local(): pl.pallas_call(functools.partial(inflow_kernel, (block, depth, own, group...  5.19 us
    unnamed x24, local copies, waits for them, and re-layouts  3.66 us
  transfers between devices with their start and end apart: 14, of which 9 were waited for; matrix products, arithmetic and copies ran while one was open for 2% of the time, Pallas kernels for 9%

profile of v8, /device:TPU:0, one launch (start us, length us, event | category | flops | bytes accessed | tf_op | source)
XLA Modules:
  0.0 130.4 jit_solution(3925423097385645866)
XLA Ops:
  0.6 0.0 copy-start.6
  0.6 0.0 copy-start.7
  0.7 0.0 copy-start.8
  0.7 0.0 copy-start.10
  0.7 0.0 copy-start.11
  0.7 0.0 copy-start.9
  0.7 0.6 pad_add_fusion.meta
  1.3 17.5 %sweeps.1 = (f32[64,8,16,128]{3,2,1,0:T(8,128)}, f32[8,512]{1,0:T(8,128)}, f32[3,256,128]{2,1,0:T(8,128)}, f32[3,256,128]{2,1,0:T(8,128)}, f32[3,256,128]{2,1,0:...) custom-call(s32[2]{0:T(128)} %pad_add_fusion.meta, s32[64]{0:T(128)} %labels.1, ...), custom_call_target="tpu_custom_call" | custom-call | tf_op jit(solution)/shard_map/sweeps/pallas_call | solution.py:600
  18.8 0.0 copy-start.3
  18.8 0.5 collective-permute-start
  19.3 0.0 copy-done.7
  19.3 0.0 copy-done.8
  19.3 0.0 copy-done.9
  19.3 0.0 copy-done.6
  19.3 0.0 copy-done.10
  19.4 0.0 copy-done.11
  19.4 0.1 select_reduce_fusion
  19.5 0.6 fusion.20
  20.1 0.1 fusion.7
  20.4 1.1 collective-permute-done.other
  21.4 1.1 copy-done
  22.5 0.1 density_split.1
  22.6 3.0 %collective-permute-start.1 = (f32[1,3,64,512]{3,2,1,0:T(8,128)S(1)}, f32[1,3,64,512]{3,2,1,0:T(8,128)S(1)}, u32[]{:S(2)}, u32[]{:S(2)}) collective-permute-start(f32[1,3,64,512]{3,2,1,0:T(8,128)S(1)} %get-tuple-element.40), channel_id=1, source_target_pairs={{0,2},{1,3},{2,0},{3,1},{4,6},{5,7},{6,4},{7,5},{8,10},{9,11},{10,... | collective-permute-start | bytes 1179656 | tf_op jit(solution)/shard_map/ppermute | solution.py:583
  25.6 0.1 copy.14
  25.7 0.1 copy.15.kinds
  25.8 0.0 copy-done.2
  25.8 0.8 heat_matrices.1
  26.7 1.3 %pad_maximum_fusion.1.sums = f32[2]{0:T(128)S(1)} fusion(f32[1]{0:T(128)} %bitcast.36, f32[1]{0:T(128)} %bitcast.35), kind=kLoop, calls=%fused_computation.35 | loop fusion | flops 2 | bytes 16 | tf_op jit(solution)/shard_map/stack | solution.py:571
  28.0 7.0 %collective-permute-done.1.other = f32[1,3,64,512]{3,2,1,0:T(8,128)S(1)} collective-permute-done((f32[1,3,64,512]{3,2,1,0:T(8,128)S(1)}, f32[1,3,64,512]{3,2,1,0:T(8,128)S(1)}, u32[]{:S(2)}, u32[]{:S(2)}) %collective-permute-start.1) | collective-permute-done | bytes 393248 | tf_op jit(solution)/shard_map/ppermute | solution.py:583
  35.0 0.8 density_parts.1.refs_4_
  35.8 6.1 %all-to-all-start = ((f32[8,3,8,512]{3,2,1,0:T(8,128)}), f32[8,3,8,512]{3,2,1,0:T(8,128)S(1)}, u32[]{:S(2)}, u32[]{:S(2)}) async-start(f32[8,3,8,512]{3,2,1,0:T(8,128)} %density_parts.1.refs_4_), calls=%async_computation | async-start | bytes 786432 | tf_op jit(solution)/shard_map/all_to_all | solution.py:652
  41.9 2.0 %collective-permute-start.2 = (f32[3,256,128]{2,1,0:T(8,128)}, f32[3,256,128]{2,1,0:T(8,128)S(1)}, u32[]{:S(2)}, u32[]{:S(2)}) collective-permute-start(f32[3,256,128]{2,1,0:T(8,128)} %get-tuple-element.51), channel_id=1, source_target_pairs={{0,4},{4,0},{8,12},{12,8},{16,20},{20,16},{24,28},{28,24},{1,5},{5... | collective-permute-start | bytes 1179656 | tf_op jit(solution)/shard_map/ppermute | solution.py:583
  43.9 1.5 %collective-permute-start.3 = (f32[3,256,128]{2,1,0:T(8,128)}, f32[3,256,128]{2,1,0:T(8,128)S(1)}, u32[]{:S(2)}, u32[]{:S(2)}) collective-permute-start(f32[3,256,128]{2,1,0:T(8,128)} %get-tuple-element.52), channel_id=1, source_target_pairs={{0,8},{4,12},{8,0},{12,4},{16,24},{20,28},{24,16},{28,20},{1,9},{5... | collective-permute-start | bytes 1179656 | tf_op jit(solution)/shard_map/ppermute | solution.py:583
  45.3 0.0 collective-permute-start.4
  45.4 10.9 %collective-permute-done.2.refs_1_ = f32[3,256,128]{2,1,0:T(8,128)S(1)} collective-permute-done((f32[3,256,128]{2,1,0:T(8,128)}, f32[3,256,128]{2,1,0:T(8,128)S(1)}, u32[]{:S(2)}, u32[]{:S(2)}) %collective-permute-start.2) | collective-permute-done | bytes 393248 | tf_op jit(solution)/shard_map/ppermute | solution.py:583
  56.3 4.0 %collective-permute-done.3.refs_2_ = f32[3,256,128]{2,1,0:T(8,128)S(1)} collective-permute-done((f32[3,256,128]{2,1,0:T(8,128)}, f32[3,256,128]{2,1,0:T(8,128)S(1)}, u32[]{:S(2)}, u32[]{:S(2)}) %collective-permute-start.3) | collective-permute-done | bytes 393248 | tf_op jit(solution)/shard_map/ppermute | solution.py:583
  60.3 7.5 %collective-permute-done.4.refs_3_ = f32[3,256,128]{2,1,0:T(8,128)S(1)} collective-permute-done((f32[3,256,128]{2,1,0:T(8,128)}, f32[3,256,128]{2,1,0:T(8,128)S(1)}, u32[]{:S(2)}, u32[]{:S(2)}) %collective-permute-start.4) | collective-permute-done | bytes 393248 | tf_op jit(solution)/shard_map/ppermute | solution.py:583
  67.8 1.0 copy-done.1
  68.8 1.2 compose.1
  70.0 0.0 all-to-all-done.parts
  70.0 1.3 %density_totals.1 = (f32[8,2,8,512]{3,2,1,0:T(8,128)}, f32[8,512]{1,0:T(8,128)S(1)}) custom-call(f32[2]{0:T(128)S(1)} %pad_maximum_fusion.1.sums, f32[8,3,8,512]{3,2,1,0:T(8,128)S(1)} %all-to-all-done.parts, f32[8,512]{1,0:T(8,128)S(1)} %copy-done.3), custom_call_target="tpu_custom_call" | custom-call | tf_op jit(solution)/shard_map/density_totals/pallas_call | solution.py:586
  71.3 3.6 %all-to-all-start.1 = ((f32[8,2,8,512]{3,2,1,0:T(8,128)}), f32[8,2,8,512]{3,2,1,0:T(8,128)S(1)}, u32[]{:S(2)}, u32[]{:S(2)}) async-start(f32[8,2,8,512]{3,2,1,0:T(8,128)} %get-tuple-element.57), calls=%async_computation.1 | async-start | bytes 524288 | tf_op jit(solution)/shard_map/all_to_all | solution.py:677
  74.9 2.9 %collective-permute-start.5 = (f32[3,256,128]{2,1,0:T(8,128)S(1)}, f32[3,256,128]{2,1,0:T(8,128)S(1)}, u32[]{:S(2)}, u32[]{:S(2)}) collective-permute-start(f32[3,256,128]{2,1,0:T(8,128)S(1)} %get-tuple-element.59.refs_0_), channel_id=1, source_target_pairs={{0,16},{4,20},{8,24},{12,28},{16,0},{20,4},{24,8},{28,12},{1,17},{... | collective-permute-start | bytes 1179656 | tf_op jit(solution)/shard_map/ppermute | solution.py:583
  77.9 22.4 %collective-permute-done.5.refs_1_ = f32[3,256,128]{2,1,0:T(8,128)S(1)} collective-permute-done((f32[3,256,128]{2,1,0:T(8,128)S(1)}, f32[3,256,128]{2,1,0:T(8,128)S(1)}, u32[]{:S(2)}, u32[]{:S(2)}) %collective-permute-start.5) | collective-permute-done | bytes 393248 | tf_op jit(solution)/shard_map/ppermute | solution.py:583
  100.2 1.4 %enter.1 = (f32[3,256,128]{2,1,0:T(8,128)S(1)}, f32[3,256,128]{2,1,0:T(8,128)S(1)}, f32[3,256,128]{2,1,0:T(8,128)S(1)}, f32[3,256,128]{2,1,0:T(8,128)S(1)}) custom-call(s32[2]{0:T(128)S(1)} %copy-done.2, f32[10,64]{1,0:T(8,128)S(1)} %stack.136.floats, s32[5,64]{1,0:T(8,128)S(1)} %stack.143.ints, f32[4,3,256,128]{3,2,1,0:T(8,128)S(1)} %get-tuple-element.58.effective, ...), custom_call_target="tpu_custom_call" | custom-call | tf_op jit(solution)/shard_map/enter/pallas_call | solution.py:586
  101.6 0.7 copy-done.4
  102.4 0.7 copy-done.5
  103.1 0.0 all-to-all-done.1.gathered
  103.1 1.4 %kelvins.1.refs_0_ = f32[128,512]{1,0:T(8,128)S(1)} custom-call(s32[2]{0:T(128)S(1)} %copy-done.2, f32[2]{0:T(128)S(1)} %pad_maximum_fusion.1.sums, f32[8,2,8,512]{3,2,1,0:T(8,128)S(1)} %all-to-all-done.1.gathered, f32[8,512]{1,0:T(8,128)S(1)} %get-tuple-element.65.late, f32[144,128]{1,0:T(8,128)S(1)} %get-tuple-element.66.matrix_one, ...), custom_call_target="tpu_custom_call" | custom-call | tf_op jit(solution)/shard_map/kelvins/pallas_call | solution.py:586
  104.5 1.6 %collective-permute-start.6 = (f32[128,512]{1,0:T(8,128)S(1)}, f32[128,512]{1,0:T(8,128)S(1)}, u32[]{:S(2)}, u32[]{:S(2)}) collective-permute-start(f32[128,512]{1,0:T(8,128)S(1)} %kelvins.1.refs_0_), channel_id=1, source_target_pairs={{0,2},{1,3},{2,0},{3,1},{4,6},{5,7},{6,4},{7,5},{8,10},{9,11},{10,... | collective-permute-start | bytes 786440 | tf_op jit(solution)/shard_map/ppermute | solution.py:583
  106.0 1.5 %collective-permute-start.9 = (f32[3,256,128]{2,1,0:T(8,128)}, f32[3,256,128]{2,1,0:T(8,128)S(1)}, u32[]{:S(2)}, u32[]{:S(2)}) collective-permute-start(f32[3,256,128]{2,1,0:T(8,128)} %copy-done.5), channel_id=1, source_target_pairs={{0,4},{4,0},{8,12},{12,8},{16,20},{20,16},{24,28},{28,24},{1,5},{5... | collective-permute-start | bytes 1179656 | tf_op jit(solution)/shard_map/ppermute | solution.py:583
  107.6 0.0 collective-permute-start.10
  107.6 2.0 %collective-permute-start.11 = (f32[3,256,128]{2,1,0:T(8,128)S(1)}, f32[3,256,128]{2,1,0:T(8,128)S(1)}, u32[]{:S(2)}, u32[]{:S(2)}) collective-permute-start(f32[3,256,128]{2,1,0:T(8,128)S(1)} %get-tuple-element.72), channel_id=1, source_target_pairs={{0,12},{4,8},{8,4},{12,0},{16,28},{20,24},{24,20},{28,16},{1,13},{... | collective-permute-start | bytes 1179656 | tf_op jit(solution)/shard_map/ppermute | solution.py:583
  109.5 0.0 collective-permute-start.7
  109.5 1.8 %collective-permute-done.6.refs_1_ = f32[128,512]{1,0:T(8,128)S(1)} collective-permute-done((f32[128,512]{1,0:T(8,128)S(1)}, f32[128,512]{1,0:T(8,128)S(1)}, u32[]{:S(2)}, u32[]{:S(2)}) %collective-permute-start.6) | collective-permute-done | bytes 262176 | tf_op jit(solution)/shard_map/ppermute | solution.py:583
  111.3 0.0 collective-permute-start.8
  111.3 0.1 copy.16.kinds
  111.4 0.0 collective-permute-done.7.refs_2_
  111.4 1.4 %collective-permute-done.8.refs_3_ = f32[128,512]{1,0:T(8,128)S(1)} collective-permute-done((f32[128,512]{1,0:T(8,128)S(1)}, f32[128,512]{1,0:T(8,128)S(1)}, u32[]{:S(2)}, u32[]{:S(2)}) %collective-permute-start.8) | collective-permute-done | bytes 262176 | tf_op jit(solution)/shard_map/ppermute | solution.py:583
  112.9 8.7 %warm.1 = (f32[64,8,16,128]{3,2,1,0:T(8,128)S(1)}, f32[128,128]{1,0:T(8,128)}) custom-call(s32[2]{0:T(128)S(1)} %copy-done.2, f32[10,64]{1,0:T(8,128)S(1)} %stack.136.floats, s32[5,64]{1,0:T(8,128)S(1)} %stack.143.ints, f32[6,16]{1,0:T(8,128)S(1)} %copy.16.kinds, f32[2]{0:T(128)S(1)} %pad_maximum_fusion.1.sums, f32[64,8,16,128]{3,2,1,0:T(8,128)} %get-tuple-element.47.swept, ...), custom_call_target="tpu_custom_call" | custom-call | tf_op jit(solution)/shard_map/warm/pallas_call | solution.py:712
  121.6 0.0 collective-permute-done.9.refs_1_
  121.6 0.0 collective-permute-done.10.refs_2_
  121.6 3.6 %collective-permute-done.11.refs_3_ = f32[3,256,128]{2,1,0:T(8,128)S(1)} collective-permute-done((f32[3,256,128]{2,1,0:T(8,128)S(1)}, f32[3,256,128]{2,1,0:T(8,128)S(1)}, u32[]{:S(2)}, u32[]{:S(2)}) %collective-permute-start.11) | collective-permute-done | bytes 393248 | tf_op jit(solution)/shard_map/ppermute | solution.py:583
  125.2 5.2 %inflow.1 = f32[64,8,16,128]{3,2,1,0:T(8,128)} custom-call(s32[2]{0:T(128)S(1)} %copy-done.2, f32[10,64]{1,0:T(8,128)S(1)} %stack.136.floats, s32[5,64]{1,0:T(8,128)S(1)} %stack.143.ints, f32[64,8,16,128]{3,2,1,0:T(8,128)S(1)} %get-tuple-element.68.warm, f32[3,256,128]{2,1,0:T(8,128)S(1)} %get-tuple-element.69.refs_0_, ...), custom_call_target="tpu_custom_call" | custom-call | tf_op jit(solution)/shard_map/inflow/pallas_call | solution.py:725
  (20 shorter events, 0.3 us)
Async XLA Ops:
  0.6 18.7 %copy-start.6 = (f32[8]{0:T(128)S(1)}, f32[8]{0:T(128)}, u32[]{:S(2)}) copy-start(f32[8]{0:T(128)} %refs_3_.1) | copy-start | bytes 100
  0.6 18.6 %copy-start.7 = (f32[8]{0:T(128)S(1)}, f32[8]{0:T(128)}, u32[]{:S(2)}) copy-start(f32[8]{0:T(128)} %refs_1_.1) | copy-start | bytes 100
  0.7 18.6 %copy-start.8 = (f32[8]{0:T(128)S(1)}, f32[8]{0:T(128)}, u32[]{:S(2)}) copy-start(f32[8]{0:T(128)} %refs_0_.1) | copy-start | bytes 100
  0.7 18.7 %copy-start.10 = (f32[8]{0:T(128)S(1)}, f32[8]{0:T(128)}, u32[]{:S(2)}) copy-start(f32[8]{0:T(128)} %refs_4_.1) | copy-start | bytes 100
  0.7 18.7 %copy-start.11 = (f32[8]{0:T(128)S(1)}, f32[8]{0:T(128)}, u32[]{:S(2)}) copy-start(f32[8]{0:T(128)} %refs_2_.1) | copy-start | bytes 100
  0.7 18.6 %copy-start.9 = (s32[64]{0:T(128)S(1)}, s32[64]{0:T(128)}, u32[]{:S(2)}) copy-start(s32[64]{0:T(128)} %labels.1) | copy-start | bytes 772
  1.3 24.5 %copy-start.2 = (s32[2]{0:T(128)S(1)}, s32[2]{0:T(128)}, u32[]{:S(2)}) copy-start(s32[2]{0:T(128)} %pad_add_fusion.meta) | copy-start | bytes 28
  18.8 51.2 %copy-start.3 = (f32[8,512]{1,0:T(8,128)S(1)}, f32[8,512]{1,0:T(8,128)}, u32[]{:S(2)}) copy-start(f32[8,512]{1,0:T(8,128)} %get-tuple-element.56.before) | copy-start | bytes 49156
  18.8 2.6 %collective-permute-start = (f32[2,3,64,512]{3,2,1,0:T(8,128)}, f32[2,3,64,512]{3,2,1,0:T(8,128)S(1)}, u32[]{:S(2)}, u32[]{:S(2)}) collective-permute-start(f32[2,3,64,512]{3,2,1,0:T(8,128)} %get-tuple-element.39), channel_id=1, source_target_pairs={{0,1},{1,0},{2,3},{3,2},{4,5},{5,4},{6,7},{7,6},{8,9},{9,8},{10,11... | collective-permute-start | bytes 2359304 | tf_op jit(solution)/shard_map/ppermute | solution.py:583
  21.4 1.1 copy-start
  22.6 12.4 %collective-permute-start.1 = (f32[1,3,64,512]{3,2,1,0:T(8,128)S(1)}, f32[1,3,64,512]{3,2,1,0:T(8,128)S(1)}, u32[]{:S(2)}, u32[]{:S(2)}) collective-permute-start(f32[1,3,64,512]{3,2,1,0:T(8,128)S(1)} %get-tuple-element.40), channel_id=1, source_target_pairs={{0,2},{1,3},{2,0},{3,1},{4,6},{5,7},{6,4},{7,5},{8,10},{9,11},{10,... | collective-permute-start | bytes 1179656 | tf_op jit(solution)/shard_map/ppermute | solution.py:583
  35.8 34.2 %all-to-all-start = ((f32[8,3,8,512]{3,2,1,0:T(8,128)}), f32[8,3,8,512]{3,2,1,0:T(8,128)S(1)}, u32[]{:S(2)}, u32[]{:S(2)}) async-start(f32[8,3,8,512]{3,2,1,0:T(8,128)} %density_parts.1.refs_4_), calls=%async_computation | async-start | bytes 786432 | tf_op jit(solution)/shard_map/all_to_all | solution.py:652
  41.9 14.5 %collective-permute-start.2 = (f32[3,256,128]{2,1,0:T(8,128)}, f32[3,256,128]{2,1,0:T(8,128)S(1)}, u32[]{:S(2)}, u32[]{:S(2)}) collective-permute-start(f32[3,256,128]{2,1,0:T(8,128)} %get-tuple-element.51), channel_id=1, source_target_pairs={{0,4},{4,0},{8,12},{12,8},{16,20},{20,16},{24,28},{28,24},{1,5},{5... | collective-permute-start | bytes 1179656 | tf_op jit(solution)/shard_map/ppermute | solution.py:583
  43.9 16.4 %collective-permute-start.3 = (f32[3,256,128]{2,1,0:T(8,128)}, f32[3,256,128]{2,1,0:T(8,128)S(1)}, u32[]{:S(2)}, u32[]{:S(2)}) collective-permute-start(f32[3,256,128]{2,1,0:T(8,128)} %get-tuple-element.52), channel_id=1, source_target_pairs={{0,8},{4,12},{8,0},{12,4},{16,24},{20,28},{24,16},{28,20},{1,9},{5... | collective-permute-start | bytes 1179656 | tf_op jit(solution)/shard_map/ppermute | solution.py:583
  45.3 22.5 %collective-permute-start.4 = (f32[3,256,128]{2,1,0:T(8,128)}, f32[3,256,128]{2,1,0:T(8,128)S(1)}, u32[]{:S(2)}, u32[]{:S(2)}) collective-permute-start(f32[3,256,128]{2,1,0:T(8,128)} %get-tuple-element.53), channel_id=1, source_target_pairs={{0,12},{4,8},{8,4},{12,0},{16,28},{20,24},{24,20},{28,16},{1,13},{... | collective-permute-start | bytes 1179656 | tf_op jit(solution)/shard_map/ppermute | solution.py:583
  67.8 1.0 copy-start.1
  71.3 31.8 %all-to-all-start.1 = ((f32[8,2,8,512]{3,2,1,0:T(8,128)}), f32[8,2,8,512]{3,2,1,0:T(8,128)S(1)}, u32[]{:S(2)}, u32[]{:S(2)}) async-start(f32[8,2,8,512]{3,2,1,0:T(8,128)} %get-tuple-element.57), calls=%async_computation.1 | async-start | bytes 524288 | tf_op jit(solution)/shard_map/all_to_all | solution.py:677
  74.9 25.3 %collective-permute-start.5 = (f32[3,256,128]{2,1,0:T(8,128)S(1)}, f32[3,256,128]{2,1,0:T(8,128)S(1)}, u32[]{:S(2)}, u32[]{:S(2)}) collective-permute-start(f32[3,256,128]{2,1,0:T(8,128)S(1)} %get-tuple-element.59.refs_0_), channel_id=1, source_target_pairs={{0,16},{4,20},{8,24},{12,28},{16,0},{20,4},{24,8},{28,12},{1,17},{... | collective-permute-start | bytes 1179656 | tf_op jit(solution)/shard_map/ppermute | solution.py:583
  101.6 0.8 copy-start.4
  102.4 0.7 copy-start.5
  104.5 6.8 %collective-permute-start.6 = (f32[128,512]{1,0:T(8,128)S(1)}, f32[128,512]{1,0:T(8,128)S(1)}, u32[]{:S(2)}, u32[]{:S(2)}) collective-permute-start(f32[128,512]{1,0:T(8,128)S(1)} %kelvins.1.refs_0_), channel_id=1, source_target_pairs={{0,2},{1,3},{2,0},{3,1},{4,6},{5,7},{6,4},{7,5},{8,10},{9,11},{10,... | collective-permute-start | bytes 786440 | tf_op jit(solution)/shard_map/ppermute | solution.py:583
  106.0 15.6 %collective-permute-start.9 = (f32[3,256,128]{2,1,0:T(8,128)}, f32[3,256,128]{2,1,0:T(8,128)S(1)}, u32[]{:S(2)}, u32[]{:S(2)}) collective-permute-start(f32[3,256,128]{2,1,0:T(8,128)} %copy-done.5), channel_id=1, source_target_pairs={{0,4},{4,0},{8,12},{12,8},{16,20},{20,16},{24,28},{28,24},{1,5},{5... | collective-permute-start | bytes 1179656 | tf_op jit(solution)/shard_map/ppermute | solution.py:583
  107.6 14.1 %collective-permute-start.10 = (f32[3,256,128]{2,1,0:T(8,128)}, f32[3,256,128]{2,1,0:T(8,128)S(1)}, u32[]{:S(2)}, u32[]{:S(2)}) collective-permute-start(f32[3,256,128]{2,1,0:T(8,128)} %copy-done.4), channel_id=1, source_target_pairs={{0,8},{4,12},{8,0},{12,4},{16,24},{20,28},{24,16},{28,20},{1,9},{5... | collective-permute-start | bytes 1179656 | tf_op jit(solution)/shard_map/ppermute | solution.py:583
  107.6 17.6 %collective-permute-start.11 = (f32[3,256,128]{2,1,0:T(8,128)S(1)}, f32[3,256,128]{2,1,0:T(8,128)S(1)}, u32[]{:S(2)}, u32[]{:S(2)}) collective-permute-start(f32[3,256,128]{2,1,0:T(8,128)S(1)} %get-tuple-element.72), channel_id=1, source_target_pairs={{0,12},{4,8},{8,4},{12,0},{16,28},{20,24},{24,20},{28,16},{1,13},{... | collective-permute-start | bytes 1179656 | tf_op jit(solution)/shard_map/ppermute | solution.py:583
  109.5 1.9 %collective-permute-start.7 = (f32[128,512]{1,0:T(8,128)S(1)}, f32[128,512]{1,0:T(8,128)S(1)}, u32[]{:S(2)}, u32[]{:S(2)}) collective-permute-start(f32[128,512]{1,0:T(8,128)S(1)} %kelvins.1.refs_0_), channel_id=1, source_target_pairs={{0,1},{1,0},{2,3},{3,2},{4,5},{5,4},{6,7},{7,6},{8,9},{9,8},{10,11... | collective-permute-start | bytes 786440 | tf_op jit(solution)/shard_map/ppermute | solution.py:583
  111.3 1.5 %collective-permute-start.8 = (f32[128,512]{1,0:T(8,128)S(1)}, f32[128,512]{1,0:T(8,128)S(1)}, u32[]{:S(2)}, u32[]{:S(2)}) collective-permute-start(f32[128,512]{1,0:T(8,128)S(1)} %collective-permute-done.6.refs_1_), channel_id=1, source_target_pairs={{0,1},{1,0},{2,3},{3,2},{4,5},{5,4},{6,7},{7,6},{8,9},{9,8},{10,11... | collective-permute-start | bytes 786440 | tf_op jit(solution)/shard_map/ppermute | solution.py:583

commit v9 on v8

--- a/solution.py
+++ b/solution.py
@@ -645,8 +645,8 @@
         meta,
         kinds,
     )
-    other, floats, ints, kinds, sums, first_matrix, second_matrix = lax.optimization_barrier(
-        (other, floats, ints, kinds, sums, first_matrix, second_matrix)
+    other, received[1:3], floats, ints, kinds, sums, first_matrix, second_matrix = lax.optimization_barrier(
+        (other, received[1:3], floats, ints, kinds, sums, first_matrix, second_matrix)
     )
     (parts,) = call(functools.partial(parts_kernel, depth), "density_parts", [VMEM] * 2, [shape(*piece)], keep, other)
     summed = lax.all_to_all(parts, "slab", 0, 0)

time: 131 us -> 124 us (0.947)
  waiting for transfers between devices: 59.7 us -> 52.4 us
    ppermute x12, waiting for transfers between devices: 59.7 us -> 52.4 us  [swap(): lax.ppermute(array, axis, [(i, i ^ by) for i in range(lax.axis_size(axis))])]
    all_to_all x1, starting transfers between devices: 6.07 us -> 3.87 us  [local(): summed = lax.all_to_all(parts, 'slab', 0, 0)]
    ppermute x12, starting transfers between devices: 15 us -> 17 us  [swap(): lax.ppermute(array, axis, [(i, i ^ by) for i in range(lax.axis_size(axis))])]
    unnamed x24 -> x26, local copies, waits for them, and re-layouts: 3.66 us -> 4.4 us
  transfers between devices with their start and end apart: 14 -> 14, of which waited for: 9 -> 8; matrix products, arithmetic and copies ran while one was open for 2% -> 2% of each run, Pallas kernels for 9% -> 10%
where the time goes in v9:
time: 124 us
  waiting for transfers between devices  52.4 us (42%)
  Pallas kernels  38.4 us (31%)
  starting transfers between devices  24.5 us (20%)
  local copies, waits for them, and re-layouts  4.78 us (4%)
  other arithmetic  2.92 us (2%)
    ppermute x12, waiting for transfers between devices, swap(): lax.ppermute(array, axis, [(i, i ^ by) for i in range(lax.axis_size(axis))])  52.4 us
    pallas_call x1, Pallas kernels, local(): pl.pallas_call(functools.partial(sweeps_kernel, (block, blocks, depth, wi...  17.6 us
    ppermute x12, starting transfers between devices, swap(): lax.ppermute(array, axis, [(i, i ^ by) for i in range(lax.axis_size(axis))])  17 us
    pallas_call x1, Pallas kernels, local(): pl.pallas_call(functools.partial(warm_kernel, (block, depth, width_y, wid...  8.74 us
    pallas_call x7, Pallas kernels, call(): pl.pallas_call(kernel, in_specs=in_specs, out_specs=[VMEM] * len(out_shap...  6.9 us
    pallas_call x1, Pallas kernels, local(): pl.pallas_call(functools.partial(inflow_kernel, (block, depth, own, group...  5.19 us
    unnamed x26, local copies, waits for them, and re-layouts  4.4 us
    all_to_all x1, starting transfers between devices, local(): summed = lax.all_to_all(parts, 'slab', 0, 0)  3.87 us
  transfers between devices with their start and end apart: 14, of which 8 were waited for; matrix products, arithmetic and copies ran while one was open for 2% of the time, Pallas kernels for 10%

profile of v9, /device:TPU:0, one launch (start us, length us, event | category | flops | bytes accessed | tf_op | source)
XLA Modules:
  0.0 123.9 jit_solution(12739271977154819393)
XLA Ops:
  0.6 0.0 copy-start.7
  0.6 0.0 copy-start.8
  0.7 0.0 copy-start.9
  0.7 0.0 copy-start.11
  0.7 0.0 copy-start.12
  0.7 0.0 copy-start.10
  0.7 0.6 pad_add_fusion.meta
  1.3 17.6 %sweeps.1 = (f32[64,8,16,128]{3,2,1,0:T(8,128)}, f32[8,512]{1,0:T(8,128)}, f32[3,256,128]{2,1,0:T(8,128)}, f32[3,256,128]{2,1,0:T(8,128)}, f32[3,256,128]{2,1,0:...) custom-call(s32[2]{0:T(128)} %pad_add_fusion.meta, s32[64]{0:T(128)} %labels.1, ...), custom_call_target="tpu_custom_call" | custom-call | tf_op jit(solution)/shard_map/sweeps/pallas_call | solution.py:600
  18.9 0.0 copy-start.3
  18.9 3.0 %collective-permute-start.2 = (f32[3,256,128]{2,1,0:T(8,128)}, f32[3,256,128]{2,1,0:T(8,128)S(1)}, u32[]{:S(2)}, u32[]{:S(2)}) collective-permute-start(f32[3,256,128]{2,1,0:T(8,128)} %get-tuple-element.43), channel_id=1, source_target_pairs={{0,4},{4,0},{8,12},{12,8},{16,20},{20,16},{24,28},{28,24},{1,5},{5... | collective-permute-start | bytes 1179656 | tf_op jit(solution)/shard_map/ppermute | solution.py:583
  21.9 1.6 %collective-permute-start.3 = (f32[3,256,128]{2,1,0:T(8,128)}, f32[3,256,128]{2,1,0:T(8,128)S(1)}, u32[]{:S(2)}, u32[]{:S(2)}) collective-permute-start(f32[3,256,128]{2,1,0:T(8,128)} %get-tuple-element.44), channel_id=1, source_target_pairs={{0,8},{4,12},{8,0},{12,4},{16,24},{20,28},{24,16},{28,20},{1,9},{5... | collective-permute-start | bytes 1179656 | tf_op jit(solution)/shard_map/ppermute | solution.py:583
  23.5 0.0 collective-permute-start
  23.5 0.0 copy-done.8
  23.5 0.0 copy-done.9
  23.5 0.0 copy-done.10
  23.5 0.0 copy-done.7
  23.6 0.0 copy-done.11
  23.6 0.1 select_reduce_fusion
  23.7 0.7 fusion.20
  24.4 0.1 fusion.7
  24.6 1.4 %collective-permute-done.other = f32[2,3,64,512]{3,2,1,0:T(8,128)S(1)} collective-permute-done((f32[2,3,64,512]{3,2,1,0:T(8,128)}, f32[2,3,64,512]{3,2,1,0:T(8,128)S(1)}, u32[]{:S(2)}, u32[]{:S(2)}) %collective-permute-start) | collective-permute-done | bytes 786464 | tf_op jit(solution)/shard_map/ppermute | solution.py:583
  26.0 1.1 copy-done
  27.1 0.1 density_split.1
  27.2 1.5 %collective-permute-start.1 = (f32[1,3,64,512]{3,2,1,0:T(8,128)S(1)}, f32[1,3,64,512]{3,2,1,0:T(8,128)S(1)}, u32[]{:S(2)}, u32[]{:S(2)}) collective-permute-start(f32[1,3,64,512]{3,2,1,0:T(8,128)S(1)} %get-tuple-element.42), channel_id=1, source_target_pairs={{0,2},{1,3},{2,0},{3,1},{4,6},{5,7},{6,4},{7,5},{8,10},{9,11},{10,... | collective-permute-start | bytes 1179656 | tf_op jit(solution)/shard_map/ppermute | solution.py:583
  28.7 0.1 copy.14
  28.8 0.1 copy.15.kinds
  28.9 0.8 heat_matrices.1
  29.8 1.3 %pad_maximum_fusion.1.sums = f32[2]{0:T(128)S(1)} fusion(f32[1]{0:T(128)} %bitcast.36, f32[1]{0:T(128)} %bitcast.35), kind=kLoop, calls=%fused_computation.35 | loop fusion | flops 2 | bytes 16 | tf_op jit(solution)/shard_map/stack | solution.py:571
  31.1 0.0 collective-permute-done.2.refs_1_
  31.2 1.5 %collective-permute-done.3.refs_2_ = f32[3,256,128]{2,1,0:T(8,128)S(1)} collective-permute-done((f32[3,256,128]{2,1,0:T(8,128)}, f32[3,256,128]{2,1,0:T(8,128)S(1)}, u32[]{:S(2)}, u32[]{:S(2)}) %collective-permute-start.3) | collective-permute-done | bytes 393248 | tf_op jit(solution)/shard_map/ppermute | solution.py:583
  32.7 5.8 %collective-permute-done.1.other = f32[1,3,64,512]{3,2,1,0:T(8,128)S(1)} collective-permute-done((f32[1,3,64,512]{3,2,1,0:T(8,128)S(1)}, f32[1,3,64,512]{3,2,1,0:T(8,128)S(1)}, u32[]{:S(2)}, u32[]{:S(2)}) %collective-permute-start.1) | collective-permute-done | bytes 393248 | tf_op jit(solution)/shard_map/ppermute | solution.py:583
  38.4 0.8 density_parts.1.refs_4_
  39.2 3.9 %all-to-all-start = ((f32[8,3,8,512]{3,2,1,0:T(8,128)}), f32[8,3,8,512]{3,2,1,0:T(8,128)S(1)}, u32[]{:S(2)}, u32[]{:S(2)}) async-start(f32[8,3,8,512]{3,2,1,0:T(8,128)} %density_parts.1.refs_4_), calls=%async_computation | async-start | bytes 786432 | tf_op jit(solution)/shard_map/all_to_all | solution.py:652
  43.1 2.9 %collective-permute-start.4 = (f32[3,256,128]{2,1,0:T(8,128)}, f32[3,256,128]{2,1,0:T(8,128)S(1)}, u32[]{:S(2)}, u32[]{:S(2)}) collective-permute-start(f32[3,256,128]{2,1,0:T(8,128)} %get-tuple-element.57), channel_id=1, source_target_pairs={{0,12},{4,8},{8,4},{12,0},{16,28},{20,24},{24,20},{28,16},{1,13},{... | collective-permute-start | bytes 1179656 | tf_op jit(solution)/shard_map/ppermute | solution.py:583
  46.0 14.6 %collective-permute-done.4.refs_3_ = f32[3,256,128]{2,1,0:T(8,128)S(1)} collective-permute-done((f32[3,256,128]{2,1,0:T(8,128)}, f32[3,256,128]{2,1,0:T(8,128)S(1)}, u32[]{:S(2)}, u32[]{:S(2)}) %collective-permute-start.4) | collective-permute-done | bytes 393248 | tf_op jit(solution)/shard_map/ppermute | solution.py:583
  60.5 1.0 copy-done.1
  61.5 1.2 compose.1
  62.7 0.0 all-to-all-done.parts
  62.8 1.3 %density_totals.1 = (f32[8,2,8,512]{3,2,1,0:T(8,128)}, f32[8,512]{1,0:T(8,128)S(1)}) custom-call(f32[2]{0:T(128)S(1)} %pad_maximum_fusion.1.sums, f32[8,3,8,512]{3,2,1,0:T(8,128)S(1)} %all-to-all-done.parts, f32[8,512]{1,0:T(8,128)S(1)} %copy-done.3), custom_call_target="tpu_custom_call" | custom-call | tf_op jit(solution)/shard_map/density_totals/pallas_call | solution.py:586
  64.1 3.6 %all-to-all-start.1 = ((f32[8,2,8,512]{3,2,1,0:T(8,128)}), f32[8,2,8,512]{3,2,1,0:T(8,128)S(1)}, u32[]{:S(2)}, u32[]{:S(2)}) async-start(f32[8,2,8,512]{3,2,1,0:T(8,128)} %get-tuple-element.61), calls=%async_computation.1 | async-start | bytes 524288 | tf_op jit(solution)/shard_map/all_to_all | solution.py:677
  67.7 2.9 %collective-permute-start.5 = (f32[3,256,128]{2,1,0:T(8,128)S(1)}, f32[3,256,128]{2,1,0:T(8,128)S(1)}, u32[]{:S(2)}, u32[]{:S(2)}) collective-permute-start(f32[3,256,128]{2,1,0:T(8,128)S(1)} %get-tuple-element.63.refs_0_), channel_id=1, source_target_pairs={{0,16},{4,20},{8,24},{12,28},{16,0},{20,4},{24,8},{28,12},{1,17},{... | collective-permute-start | bytes 1179656 | tf_op jit(solution)/shard_map/ppermute | solution.py:583
  70.6 22.4 %collective-permute-done.5.refs_1_ = f32[3,256,128]{2,1,0:T(8,128)S(1)} collective-permute-done((f32[3,256,128]{2,1,0:T(8,128)S(1)}, f32[3,256,128]{2,1,0:T(8,128)S(1)}, u32[]{:S(2)}, u32[]{:S(2)}) %collective-permute-start.5) | collective-permute-done | bytes 393248 | tf_op jit(solution)/shard_map/ppermute | solution.py:583
  93.0 1.4 %enter.1 = (f32[3,256,128]{2,1,0:T(8,128)S(1)}, f32[3,256,128]{2,1,0:T(8,128)S(1)}, f32[3,256,128]{2,1,0:T(8,128)S(1)}, f32[3,256,128]{2,1,0:T(8,128)S(1)}) custom-call(s32[2]{0:T(128)S(1)} %copy-done.2, f32[10,64]{1,0:T(8,128)S(1)} %stack.136.floats, s32[5,64]{1,0:T(8,128)S(1)} %stack.143.ints, f32[4,3,256,128]{3,2,1,0:T(8,128)S(1)} %get-tuple-element.62.effective, ...), custom_call_target="tpu_custom_call" | custom-call | tf_op jit(solution)/shard_map/enter/pallas_call | solution.py:586
  94.4 0.0 copy-start.4
  94.4 0.7 copy-done.4
  95.1 0.7 copy-done.5
  95.8 0.8 copy-done.6
  96.6 0.0 all-to-all-done.1.gathered
  96.6 1.4 %kelvins.1.refs_0_ = f32[128,512]{1,0:T(8,128)S(1)} custom-call(s32[2]{0:T(128)S(1)} %copy-done.2, f32[2]{0:T(128)S(1)} %pad_maximum_fusion.1.sums, f32[8,2,8,512]{3,2,1,0:T(8,128)S(1)} %all-to-all-done.1.gathered, f32[8,512]{1,0:T(8,128)S(1)} %get-tuple-element.69.late, f32[144,128]{1,0:T(8,128)S(1)} %get-tuple-element.70.matrix_one, ...), custom_call_target="tpu_custom_call" | custom-call | tf_op jit(solution)/shard_map/kelvins/pallas_call | solution.py:586
  98.0 1.5 %collective-permute-start.6 = (f32[128,512]{1,0:T(8,128)S(1)}, f32[128,512]{1,0:T(8,128)S(1)}, u32[]{:S(2)}, u32[]{:S(2)}) collective-permute-start(f32[128,512]{1,0:T(8,128)S(1)} %kelvins.1.refs_0_), channel_id=1, source_target_pairs={{0,2},{1,3},{2,0},{3,1},{4,6},{5,7},{6,4},{7,5},{8,10},{9,11},{10,... | collective-permute-start | bytes 786440 | tf_op jit(solution)/shard_map/ppermute | solution.py:583
  99.5 1.5 %collective-permute-start.9 = (f32[3,256,128]{2,1,0:T(8,128)}, f32[3,256,128]{2,1,0:T(8,128)S(1)}, u32[]{:S(2)}, u32[]{:S(2)}) collective-permute-start(f32[3,256,128]{2,1,0:T(8,128)} %copy-done.6), channel_id=1, source_target_pairs={{0,4},{4,0},{8,12},{12,8},{16,20},{20,16},{24,28},{28,24},{1,5},{5... | collective-permute-start | bytes 1179656 | tf_op jit(solution)/shard_map/ppermute | solution.py:583
  101.0 0.0 collective-permute-start.10
  101.0 2.0 %collective-permute-start.11 = (f32[3,256,128]{2,1,0:T(8,128)}, f32[3,256,128]{2,1,0:T(8,128)S(1)}, u32[]{:S(2)}, u32[]{:S(2)}) collective-permute-start(f32[3,256,128]{2,1,0:T(8,128)} %copy-done.4), channel_id=1, source_target_pairs={{0,12},{4,8},{8,4},{12,0},{16,28},{20,24},{24,20},{28,16},{1,13},{... | collective-permute-start | bytes 1179656 | tf_op jit(solution)/shard_map/ppermute | solution.py:583
  103.0 0.0 collective-permute-start.7
  103.0 1.8 %collective-permute-done.6.refs_1_ = f32[128,512]{1,0:T(8,128)S(1)} collective-permute-done((f32[128,512]{1,0:T(8,128)S(1)}, f32[128,512]{1,0:T(8,128)S(1)}, u32[]{:S(2)}, u32[]{:S(2)}) %collective-permute-start.6) | collective-permute-done | bytes 262176 | tf_op jit(solution)/shard_map/ppermute | solution.py:583
  104.8 0.0 collective-permute-start.8
  104.9 0.1 copy.16.kinds
  104.9 0.0 collective-permute-done.7.refs_2_
  104.9 1.4 %collective-permute-done.8.refs_3_ = f32[128,512]{1,0:T(8,128)S(1)} collective-permute-done((f32[128,512]{1,0:T(8,128)S(1)}, f32[128,512]{1,0:T(8,128)S(1)}, u32[]{:S(2)}, u32[]{:S(2)}) %collective-permute-start.8) | collective-permute-done | bytes 262176 | tf_op jit(solution)/shard_map/ppermute | solution.py:583
  106.4 8.7 %warm.1 = (f32[64,8,16,128]{3,2,1,0:T(8,128)S(1)}, f32[128,128]{1,0:T(8,128)}) custom-call(s32[2]{0:T(128)S(1)} %copy-done.2, f32[10,64]{1,0:T(8,128)S(1)} %stack.136.floats, s32[5,64]{1,0:T(8,128)S(1)} %stack.143.ints, f32[6,16]{1,0:T(8,128)S(1)} %copy.16.kinds, f32[2]{0:T(128)S(1)} %pad_maximum_fusion.1.sums, f32[64,8,16,128]{3,2,1,0:T(8,128)} %get-tuple-element.51.swept, ...), custom_call_target="tpu_custom_call" | custom-call | tf_op jit(solution)/shard_map/warm/pallas_call | solution.py:712
  115.1 0.0 collective-permute-done.9.refs_1_
  115.1 0.0 collective-permute-done.10.refs_2_
  115.1 3.5 %collective-permute-done.11.refs_3_ = f32[3,256,128]{2,1,0:T(8,128)S(1)} collective-permute-done((f32[3,256,128]{2,1,0:T(8,128)}, f32[3,256,128]{2,1,0:T(8,128)S(1)}, u32[]{:S(2)}, u32[]{:S(2)}) %collective-permute-start.11) | collective-permute-done | bytes 393248 | tf_op jit(solution)/shard_map/ppermute | solution.py:583
  118.7 5.2 %inflow.1 = f32[64,8,16,128]{3,2,1,0:T(8,128)} custom-call(s32[2]{0:T(128)S(1)} %copy-done.2, f32[10,64]{1,0:T(8,128)S(1)} %stack.136.floats, s32[5,64]{1,0:T(8,128)S(1)} %stack.143.ints, f32[64,8,16,128]{3,2,1,0:T(8,128)S(1)} %get-tuple-element.72.warm, f32[3,256,128]{2,1,0:T(8,128)S(1)} %get-tuple-element.73.refs_0_, ...), custom_call_target="tpu_custom_call" | custom-call | tf_op jit(solution)/shard_map/inflow/pallas_call | solution.py:725
  (22 shorter events, 0.3 us)
Async XLA Ops:
  0.6 22.9 %copy-start.7 = (f32[8]{0:T(128)S(1)}, f32[8]{0:T(128)}, u32[]{:S(2)}) copy-start(f32[8]{0:T(128)} %refs_3_.1) | copy-start | bytes 100
  0.6 22.8 %copy-start.8 = (f32[8]{0:T(128)S(1)}, f32[8]{0:T(128)}, u32[]{:S(2)}) copy-start(f32[8]{0:T(128)} %refs_1_.1) | copy-start | bytes 100
  0.7 22.8 %copy-start.9 = (f32[8]{0:T(128)S(1)}, f32[8]{0:T(128)}, u32[]{:S(2)}) copy-start(f32[8]{0:T(128)} %refs_0_.1) | copy-start | bytes 100
  0.7 22.9 %copy-start.11 = (f32[8]{0:T(128)S(1)}, f32[8]{0:T(128)}, u32[]{:S(2)}) copy-start(f32[8]{0:T(128)} %refs_4_.1) | copy-start | bytes 100
  0.7 22.9 %copy-start.12 = (f32[8]{0:T(128)S(1)}, f32[8]{0:T(128)}, u32[]{:S(2)}) copy-start(f32[8]{0:T(128)} %refs_2_.1) | copy-start | bytes 100
  0.7 22.8 %copy-start.10 = (s32[64]{0:T(128)S(1)}, s32[64]{0:T(128)}, u32[]{:S(2)}) copy-start(s32[64]{0:T(128)} %labels.1) | copy-start | bytes 772
  1.3 27.6 %copy-start.2 = (s32[2]{0:T(128)S(1)}, s32[2]{0:T(128)}, u32[]{:S(2)}) copy-start(s32[2]{0:T(128)} %pad_add_fusion.meta) | copy-start | bytes 28
  18.9 43.9 %copy-start.3 = (f32[8,512]{1,0:T(8,128)S(1)}, f32[8,512]{1,0:T(8,128)}, u32[]{:S(2)}) copy-start(f32[8,512]{1,0:T(8,128)} %get-tuple-element.60.before) | copy-start | bytes 49156
  18.9 12.3 %collective-permute-start.2 = (f32[3,256,128]{2,1,0:T(8,128)}, f32[3,256,128]{2,1,0:T(8,128)S(1)}, u32[]{:S(2)}, u32[]{:S(2)}) collective-permute-start(f32[3,256,128]{2,1,0:T(8,128)} %get-tuple-element.43), channel_id=1, source_target_pairs={{0,4},{4,0},{8,12},{12,8},{16,20},{20,16},{24,28},{28,24},{1,5},{5... | collective-permute-start | bytes 1179656 | tf_op jit(solution)/shard_map/ppermute | solution.py:583
  21.9 10.7 %collective-permute-start.3 = (f32[3,256,128]{2,1,0:T(8,128)}, f32[3,256,128]{2,1,0:T(8,128)S(1)}, u32[]{:S(2)}, u32[]{:S(2)}) collective-permute-start(f32[3,256,128]{2,1,0:T(8,128)} %get-tuple-element.44), channel_id=1, source_target_pairs={{0,8},{4,12},{8,0},{12,4},{16,24},{20,28},{24,16},{28,20},{1,9},{5... | collective-permute-start | bytes 1179656 | tf_op jit(solution)/shard_map/ppermute | solution.py:583
  23.5 2.5 %collective-permute-start = (f32[2,3,64,512]{3,2,1,0:T(8,128)}, f32[2,3,64,512]{3,2,1,0:T(8,128)S(1)}, u32[]{:S(2)}, u32[]{:S(2)}) collective-permute-start(f32[2,3,64,512]{3,2,1,0:T(8,128)} %get-tuple-element.41), channel_id=1, source_target_pairs={{0,1},{1,0},{2,3},{3,2},{4,5},{5,4},{6,7},{7,6},{8,9},{9,8},{10,11... | collective-permute-start | bytes 2359304 | tf_op jit(solution)/shard_map/ppermute | solution.py:583
  26.0 1.1 copy-start
  27.2 11.2 %collective-permute-start.1 = (f32[1,3,64,512]{3,2,1,0:T(8,128)S(1)}, f32[1,3,64,512]{3,2,1,0:T(8,128)S(1)}, u32[]{:S(2)}, u32[]{:S(2)}) collective-permute-start(f32[1,3,64,512]{3,2,1,0:T(8,128)S(1)} %get-tuple-element.42), channel_id=1, source_target_pairs={{0,2},{1,3},{2,0},{3,1},{4,6},{5,7},{6,4},{7,5},{8,10},{9,11},{10,... | collective-permute-start | bytes 1179656 | tf_op jit(solution)/shard_map/ppermute | solution.py:583
  39.2 23.5 %all-to-all-start = ((f32[8,3,8,512]{3,2,1,0:T(8,128)}), f32[8,3,8,512]{3,2,1,0:T(8,128)S(1)}, u32[]{:S(2)}, u32[]{:S(2)}) async-start(f32[8,3,8,512]{3,2,1,0:T(8,128)} %density_parts.1.refs_4_), calls=%async_computation | async-start | bytes 786432 | tf_op jit(solution)/shard_map/all_to_all | solution.py:652
  43.1 17.5 %collective-permute-start.4 = (f32[3,256,128]{2,1,0:T(8,128)}, f32[3,256,128]{2,1,0:T(8,128)S(1)}, u32[]{:S(2)}, u32[]{:S(2)}) collective-permute-start(f32[3,256,128]{2,1,0:T(8,128)} %get-tuple-element.57), channel_id=1, source_target_pairs={{0,12},{4,8},{8,4},{12,0},{16,28},{20,24},{24,20},{28,16},{1,13},{... | collective-permute-start | bytes 1179656 | tf_op jit(solution)/shard_map/ppermute | solution.py:583
  60.5 1.0 copy-start.1
  64.1 32.6 %all-to-all-start.1 = ((f32[8,2,8,512]{3,2,1,0:T(8,128)}), f32[8,2,8,512]{3,2,1,0:T(8,128)S(1)}, u32[]{:S(2)}, u32[]{:S(2)}) async-start(f32[8,2,8,512]{3,2,1,0:T(8,128)} %get-tuple-element.61), calls=%async_computation.1 | async-start | bytes 524288 | tf_op jit(solution)/shard_map/all_to_all | solution.py:677
  67.7 25.3 %collective-permute-start.5 = (f32[3,256,128]{2,1,0:T(8,128)S(1)}, f32[3,256,128]{2,1,0:T(8,128)S(1)}, u32[]{:S(2)}, u32[]{:S(2)}) collective-permute-start(f32[3,256,128]{2,1,0:T(8,128)S(1)} %get-tuple-element.63.refs_0_), channel_id=1, source_target_pairs={{0,16},{4,20},{8,24},{12,28},{16,0},{20,4},{24,8},{28,12},{1,17},{... | collective-permute-start | bytes 1179656 | tf_op jit(solution)/shard_map/ppermute | solution.py:583
  94.4 0.7 copy-start.4
  95.1 0.7 copy-start.5
  95.8 0.8 copy-start.6
  98.0 6.8 %collective-permute-start.6 = (f32[128,512]{1,0:T(8,128)S(1)}, f32[128,512]{1,0:T(8,128)S(1)}, u32[]{:S(2)}, u32[]{:S(2)}) collective-permute-start(f32[128,512]{1,0:T(8,128)S(1)} %kelvins.1.refs_0_), channel_id=1, source_target_pairs={{0,2},{1,3},{2,0},{3,1},{4,6},{5,7},{6,4},{7,5},{8,10},{9,11},{10,... | collective-permute-start | bytes 786440 | tf_op jit(solution)/shard_map/ppermute | solution.py:583
  99.5 15.6 %collective-permute-start.9 = (f32[3,256,128]{2,1,0:T(8,128)}, f32[3,256,128]{2,1,0:T(8,128)S(1)}, u32[]{:S(2)}, u32[]{:S(2)}) collective-permute-start(f32[3,256,128]{2,1,0:T(8,128)} %copy-done.6), channel_id=1, source_target_pairs={{0,4},{4,0},{8,12},{12,8},{16,20},{20,16},{24,28},{28,24},{1,5},{5... | collective-permute-start | bytes 1179656 | tf_op jit(solution)/shard_map/ppermute | solution.py:583
  101.0 14.1 %collective-permute-start.10 = (f32[3,256,128]{2,1,0:T(8,128)}, f32[3,256,128]{2,1,0:T(8,128)S(1)}, u32[]{:S(2)}, u32[]{:S(2)}) collective-permute-start(f32[3,256,128]{2,1,0:T(8,128)} %copy-done.5), channel_id=1, source_target_pairs={{0,8},{4,12},{8,0},{12,4},{16,24},{20,28},{24,16},{28,20},{1,9},{5... | collective-permute-start | bytes 1179656 | tf_op jit(solution)/shard_map/ppermute | solution.py:583
  101.0 17.6 %collective-permute-start.11 = (f32[3,256,128]{2,1,0:T(8,128)}, f32[3,256,128]{2,1,0:T(8,128)S(1)}, u32[]{:S(2)}, u32[]{:S(2)}) collective-permute-start(f32[3,256,128]{2,1,0:T(8,128)} %copy-done.4), channel_id=1, source_target_pairs={{0,12},{4,8},{8,4},{12,0},{16,28},{20,24},{24,20},{28,16},{1,13},{... | collective-permute-start | bytes 1179656 | tf_op jit(solution)/shard_map/ppermute | solution.py:583
  103.0 1.9 %collective-permute-start.7 = (f32[128,512]{1,0:T(8,128)S(1)}, f32[128,512]{1,0:T(8,128)S(1)}, u32[]{:S(2)}, u32[]{:S(2)}) collective-permute-start(f32[128,512]{1,0:T(8,128)S(1)} %kelvins.1.refs_0_), channel_id=1, source_target_pairs={{0,1},{1,0},{2,3},{3,2},{4,5},{5,4},{6,7},{7,6},{8,9},{9,8},{10,11... | collective-permute-start | bytes 786440 | tf_op jit(solution)/shard_map/ppermute | solution.py:583
  104.8 1.5 %collective-permute-start.8 = (f32[128,512]{1,0:T(8,128)S(1)}, f32[128,512]{1,0:T(8,128)S(1)}, u32[]{:S(2)}, u32[]{:S(2)}) collective-permute-start(f32[128,512]{1,0:T(8,128)S(1)} %collective-permute-done.6.refs_1_), channel_id=1, source_target_pairs={{0,1},{1,0},{2,3},{3,2},{4,5},{5,4},{6,7},{7,6},{8,9},{9,8},{10,11... | collective-permute-start | bytes 786440 | tf_op jit(solution)/shard_map/ppermute | solution.py:583

commit v10 on v9

--- a/solution.py
+++ b/solution.py
@@ -394,7 +394,7 @@
 
 
 def compose_kernel(own, group, meta, floats, ints, *refs):
-    received, (_, composite, effective, ordered) = refs[:group], refs[group:]
+    received, (composite, effective, ordered) = refs[:group], refs[group:]
     place = meta[SLAB] % group
     for by in range(group):
         ordered[place ^ by] = received[by][...]
@@ -645,26 +645,24 @@
         meta,
         kinds,
     )
-    other, received[1:3], floats, ints, kinds, sums, first_matrix, second_matrix = lax.optimization_barrier(
-        (other, received[1:3], floats, ints, kinds, sums, first_matrix, second_matrix)
-    )
-    (parts,) = call(functools.partial(parts_kernel, depth), "density_parts", [VMEM] * 2, [shape(*piece)], keep, other)
-    summed = lax.all_to_all(parts, "slab", 0, 0)
-
     composite, effective = call(
         functools.partial(compose_kernel, own, group),
         "compose",
-        [SMEM] * 3 + [VMEM] * group + [pl.BlockSpec(memory_space=pl.ANY)],
+        [SMEM] * 3 + [VMEM] * group,
         [shape(*face), shape(group, *face)],
         meta,
         floats,
         ints,
         *received,
-        parts,
         scratches=[scratch(group, *face)],
     )
-    summed, composite = lax.optimization_barrier((summed, composite))
+    other, composite, floats, ints, kinds, sums, first_matrix, second_matrix = lax.optimization_barrier(
+        (other, composite, floats, ints, kinds, sums, first_matrix, second_matrix)
+    )
     composites = [composite] + [swap(composite, "slab", index * group) for index in range(1, groups)]
+    (parts,) = call(functools.partial(parts_kernel, depth), "density_parts", [VMEM] * 2, [shape(*piece)], keep, other)
+    summed = lax.all_to_all(parts, "slab", 0, 0)
+
     copies, late = call(
         totals_kernel,
         "density_totals",

time: 124 us -> 122 us (0.984)
  blocking collectives: 0 us -> 16.7 us
  waiting for transfers between devices: 52.4 us -> 36 us
  starting transfers between devices: 24.5 us -> 17.8 us
  local copies, waits for them, and re-layouts: 4.78 us -> 8.3 us
    all_to_all x0 -> x1, blocking collectives: none -> 16.7 us  [local(): summed = lax.all_to_all(parts, 'slab', 0, 0)]
    ppermute x12, waiting for transfers between devices: 52.4 us -> 36 us  [swap(): lax.ppermute(array, axis, [(i, i ^ by) for i in range(lax.axis_size(axis))])]
    all_to_all x1 -> x0, starting transfers between devices: 3.87 us -> none  [local(): summed = lax.all_to_all(parts, 'slab', 0, 0)]
    unnamed x26 -> x40, local copies, waits for them, and re-layouts: 4.4 us -> 7.23 us
    ppermute x12, starting transfers between devices: 17 us -> 14.4 us  [swap(): lax.ppermute(array, axis, [(i, i ^ by) for i in range(lax.axis_size(axis))])]
  transfers between devices with their start and end apart: 14 -> 13, of which waited for: 8 -> 7; matrix products, arithmetic and copies ran while one was open for 2% -> 3% of each run, Pallas kernels for 10% -> 11%
where the time goes in v10:
time: 122 us
  Pallas kernels  39.1 us (32%)
  waiting for transfers between devices  36 us (30%)
  starting transfers between devices  17.8 us (15%)
  blocking collectives  16.7 us (14%)
  local copies, waits for them, and re-layouts  8.3 us (7%)
  other arithmetic  2.91 us (2%)
    ppermute x12, waiting for transfers between devices, swap(): lax.ppermute(array, axis, [(i, i ^ by) for i in range(lax.axis_size(axis))])  36 us
    pallas_call x1, Pallas kernels, local(): pl.pallas_call(functools.partial(sweeps_kernel, (block, blocks, depth, wi...  17.5 us
    all_to_all x1, blocking collectives, local(): summed = lax.all_to_all(parts, 'slab', 0, 0)  16.7 us
    ppermute x12, starting transfers between devices, swap(): lax.ppermute(array, axis, [(i, i ^ by) for i in range(lax.axis_size(axis))])  14.4 us
    pallas_call x1, Pallas kernels, local(): pl.pallas_call(functools.partial(warm_kernel, (block, depth, width_y, wid...  8.74 us
    pallas_call x7, Pallas kernels, call(): pl.pallas_call(kernel, in_specs=in_specs, out_specs=[VMEM] * len(out_shap...  7.69 us
    unnamed x40, local copies, waits for them, and re-layouts  7.23 us
    pallas_call x1, Pallas kernels, local(): pl.pallas_call(functools.partial(inflow_kernel, (block, depth, own, group...  5.19 us
  transfers between devices with their start and end apart: 13, of which 7 were waited for; matrix products, arithmetic and copies ran while one was open for 3% of the time, Pallas kernels for 11%

profile of v10, /device:TPU:0, one launch (start us, length us, event | category | flops | bytes accessed | tf_op | source)
XLA Modules:
  0.0 121.7 jit_solution(1786011600567507373)
XLA Ops:
  0.6 0.0 copy-start.14
  0.6 0.0 copy-start.15
  0.7 0.0 copy-start.16
  0.7 0.0 copy-start.18
  0.7 0.0 copy-start.19
  0.7 0.0 copy-start.17
  0.7 0.6 pad_add_fusion.meta
  1.3 17.5 %sweeps.1 = (f32[64,8,16,128]{3,2,1,0:T(8,128)}, f32[8,512]{1,0:T(8,128)}, f32[3,256,128]{2,1,0:T(8,128)}, f32[3,256,128]{2,1,0:T(8,128)}, f32[3,256,128]{2,1,0:...) custom-call(s32[2]{0:T(128)} %pad_add_fusion.meta, s32[64]{0:T(128)} %labels.1, ...), custom_call_target="tpu_custom_call" | custom-call | tf_op jit(solution)/shard_map/sweeps/pallas_call | solution.py:600
  18.8 3.0 %collective-permute-start.2 = (f32[3,256,128]{2,1,0:T(8,128)}, f32[3,256,128]{2,1,0:T(8,128)S(1)}, u32[]{:S(2)}, u32[]{:S(2)}) collective-permute-start(f32[3,256,128]{2,1,0:T(8,128)} %get-tuple-element.41), channel_id=1, source_target_pairs={{0,4},{4,0},{8,12},{12,8},{16,20},{20,16},{24,28},{28,24},{1,5},{5... | collective-permute-start | bytes 1179656 | tf_op jit(solution)/shard_map/ppermute | solution.py:583
  21.8 1.6 %collective-permute-start.3 = (f32[3,256,128]{2,1,0:T(8,128)}, f32[3,256,128]{2,1,0:T(8,128)S(1)}, u32[]{:S(2)}, u32[]{:S(2)}) collective-permute-start(f32[3,256,128]{2,1,0:T(8,128)} %get-tuple-element.42), channel_id=1, source_target_pairs={{0,8},{4,12},{8,0},{12,4},{16,24},{20,28},{24,16},{28,20},{1,9},{5... | collective-permute-start | bytes 1179656 | tf_op jit(solution)/shard_map/ppermute | solution.py:583
  23.4 0.0 collective-permute-start.4
  23.4 0.0 collective-permute-start
  23.4 0.0 copy-done.15
  23.4 0.0 copy-done.16
  23.5 0.0 copy-done.14
  23.5 0.0 copy-done.18
  23.5 0.0 copy-done.19
  23.5 0.1 select_reduce_fusion
  23.6 0.7 fusion.20
  24.3 0.1 fusion.7
  24.6 1.4 %collective-permute-done.other = f32[2,3,64,512]{3,2,1,0:T(8,128)S(1)} collective-permute-done((f32[2,3,64,512]{3,2,1,0:T(8,128)}, f32[2,3,64,512]{3,2,1,0:T(8,128)S(1)}, u32[]{:S(2)}, u32[]{:S(2)}) %collective-permute-start) | collective-permute-done | bytes 786464 | tf_op jit(solution)/shard_map/ppermute | solution.py:583
  25.9 1.1 copy-done
  27.1 0.8 density_split.1
  27.9 1.9 %collective-permute-start.1 = (f32[1,3,64,512]{3,2,1,0:T(8,128)}, f32[1,3,64,512]{3,2,1,0:T(8,128)S(1)}, u32[]{:S(2)}, u32[]{:S(2)}) collective-permute-start(f32[1,3,64,512]{3,2,1,0:T(8,128)} %get-tuple-element.39), channel_id=1, source_target_pairs={{0,2},{1,3},{2,0},{3,1},{4,6},{5,7},{6,4},{7,5},{8,10},{9,11},{10,... | collective-permute-start | bytes 1179656 | tf_op jit(solution)/shard_map/ppermute | solution.py:583
  29.8 0.1 copy.14
  29.9 0.1 copy.15.kinds
  30.0 0.8 heat_matrices.1
  30.8 0.6 copy-done.4
  31.4 0.6 copy-done.7
  32.1 1.3 %pad_maximum_fusion.1.sums = f32[2]{0:T(128)S(1)} fusion(f32[1]{0:T(128)} %bitcast.36, f32[1]{0:T(128)} %bitcast.35), kind=kLoop, calls=%fused_computation.35 | loop fusion | flops 2 | bytes 16 | tf_op jit(solution)/shard_map/stack | solution.py:571
  33.4 0.0 collective-permute-done.2.refs_1_
  33.4 0.7 collective-permute-done.3.refs_2_
  34.1 6.8 %collective-permute-done.4.refs_3_ = f32[3,256,128]{2,1,0:T(8,128)S(1)} collective-permute-done((f32[3,256,128]{2,1,0:T(8,128)}, f32[3,256,128]{2,1,0:T(8,128)S(1)}, u32[]{:S(2)}, u32[]{:S(2)}) %collective-permute-start.4) | collective-permute-done | bytes 393248 | tf_op jit(solution)/shard_map/ppermute | solution.py:583
  40.9 1.0 copy-done.1
  41.9 1.2 compose.1
  43.1 0.8 copy-done.2
  43.8 0.0 collective-permute-done.1.other
  43.9 16.7 %all_to_all.10.parts = f32[8,3,8,512]{3,2,1,0:T(8,128)S(1)} all-to-all(f32[8,3,8,512]{3,2,1,0:T(8,128)S(1)} %density_parts.1), channel_id=1, replica_groups=mesh['slab'=8,'mode'=4] {'slab'}, dimensions={0} | all-to-all | bytes 786432 | tf_op jit(solution)/shard_map/all_to_all | solution.py:664
  60.6 0.7 copy-done.9
  61.3 1.3 %density_totals.1 = (f32[8,2,8,512]{3,2,1,0:T(8,128)}, f32[8,512]{1,0:T(8,128)S(1)}) custom-call(f32[2]{0:T(128)S(1)} %pad_maximum_fusion.1.sums, f32[8,3,8,512]{3,2,1,0:T(8,128)S(1)} %all_to_all.10.parts, f32[8,512]{1,0:T(8,128)S(1)} %copy-done.9), custom_call_target="tpu_custom_call" | custom-call | tf_op jit(solution)/shard_map/density_totals/pallas_call | solution.py:586
  62.6 3.4 %all-to-all-start.1 = ((f32[8,2,8,512]{3,2,1,0:T(8,128)}), f32[8,2,8,512]{3,2,1,0:T(8,128)S(1)}, u32[]{:S(2)}, u32[]{:S(2)}) async-start(f32[8,2,8,512]{3,2,1,0:T(8,128)} %get-tuple-element.55), calls=%async_computation.1 | async-start | bytes 524288 | tf_op jit(solution)/shard_map/all_to_all | solution.py:675
  66.0 2.8 %collective-permute-start.5 = (f32[3,256,128]{2,1,0:T(8,128)}, f32[3,256,128]{2,1,0:T(8,128)S(1)}, u32[]{:S(2)}, u32[]{:S(2)}) collective-permute-start(f32[3,256,128]{2,1,0:T(8,128)} %copy-done.2), channel_id=1, source_target_pairs={{0,16},{4,20},{8,24},{12,28},{16,0},{20,4},{24,8},{28,12},{1,17},{... | collective-permute-start | bytes 1179656 | tf_op jit(solution)/shard_map/ppermute | solution.py:583
  68.9 22.1 %collective-permute-done.5.refs_1_ = f32[3,256,128]{2,1,0:T(8,128)S(1)} collective-permute-done((f32[3,256,128]{2,1,0:T(8,128)}, f32[3,256,128]{2,1,0:T(8,128)S(1)}, u32[]{:S(2)}, u32[]{:S(2)}) %collective-permute-start.5) | collective-permute-done | bytes 393248 | tf_op jit(solution)/shard_map/ppermute | solution.py:583
  91.0 1.0 copy-done.3
  92.0 2.1 %enter.1 = (f32[3,256,128]{2,1,0:T(8,128)S(1)}, f32[3,256,128]{2,1,0:T(8,128)}, f32[3,256,128]{2,1,0:T(8,128)S(1)}, f32[3,256,128]{2,1,0:T(8,128)S(1)}) custom-call(s32[2]{0:T(128)S(1)} %copy-done.6, f32[10,64]{1,0:T(8,128)S(1)} %stack.136.floats, s32[5,64]{1,0:T(8,128)S(1)} %stack.143.ints, f32[4,3,256,128]{3,2,1,0:T(8,128)S(1)} %get-tuple-element.56.effective, ...), custom_call_target="tpu_custom_call" | custom-call | tf_op jit(solution)/shard_map/enter/pallas_call | solution.py:586
  94.1 0.0 all-to-all-done.1.gathered
  94.1 0.7 copy-done.11
  94.8 1.4 %kelvins.1.refs_0_ = f32[128,512]{1,0:T(8,128)S(1)} custom-call(s32[2]{0:T(128)S(1)} %copy-done.6, f32[2]{0:T(128)S(1)} %copy-done.11, f32[8,2,8,512]{3,2,1,0:T(8,128)S(1)} %all-to-all-done.1.gathered, f32[8,512]{1,0:T(8,128)S(1)} %get-tuple-element.63.late, f32[144,128]{1,0:T(8,128)S(1)} %copy-done.5, f32[40,128]{1,0:T(8,128)S(1)} %copy-done.8), custom_call_target="tpu_custom_call" | custom-call | tf_op jit(solution)/shard_map/kelvins/pallas_call | solution.py:586
  96.2 1.5 %collective-permute-start.6 = (f32[128,512]{1,0:T(8,128)S(1)}, f32[128,512]{1,0:T(8,128)S(1)}, u32[]{:S(2)}, u32[]{:S(2)}) collective-permute-start(f32[128,512]{1,0:T(8,128)S(1)} %kelvins.1.refs_0_), channel_id=1, source_target_pairs={{0,2},{1,3},{2,0},{3,1},{4,6},{5,7},{6,4},{7,5},{8,10},{9,11},{10,... | collective-permute-start | bytes 786440 | tf_op jit(solution)/shard_map/ppermute | solution.py:583
  97.7 1.5 %collective-permute-start.9 = (f32[3,256,128]{2,1,0:T(8,128)}, f32[3,256,128]{2,1,0:T(8,128)S(1)}, u32[]{:S(2)}, u32[]{:S(2)}) collective-permute-start(f32[3,256,128]{2,1,0:T(8,128)} %get-tuple-element.68), channel_id=1, source_target_pairs={{0,4},{4,0},{8,12},{12,8},{16,20},{20,16},{24,28},{28,24},{1,5},{5... | collective-permute-start | bytes 1179656 | tf_op jit(solution)/shard_map/ppermute | solution.py:583
  99.2 0.0 collective-permute-start.10
  99.3 2.0 %collective-permute-start.11 = (f32[3,256,128]{2,1,0:T(8,128)S(1)}, f32[3,256,128]{2,1,0:T(8,128)S(1)}, u32[]{:S(2)}, u32[]{:S(2)}) collective-permute-start(f32[3,256,128]{2,1,0:T(8,128)S(1)} %get-tuple-element.70), channel_id=1, source_target_pairs={{0,12},{4,8},{8,4},{12,0},{16,28},{20,24},{24,20},{28,16},{1,13},{... | collective-permute-start | bytes 1179656 | tf_op jit(solution)/shard_map/ppermute | solution.py:583
  101.2 0.0 collective-permute-start.7
  101.2 1.7 %collective-permute-done.6.refs_1_ = f32[128,512]{1,0:T(8,128)S(1)} collective-permute-done((f32[128,512]{1,0:T(8,128)S(1)}, f32[128,512]{1,0:T(8,128)S(1)}, u32[]{:S(2)}, u32[]{:S(2)}) %collective-permute-start.6) | collective-permute-done | bytes 262176 | tf_op jit(solution)/shard_map/ppermute | solution.py:583
  102.9 0.0 collective-permute-start.8
  102.9 0.8 copy.16.kinds
  103.7 0.0 collective-permute-done.7.refs_2_
  103.7 0.8 collective-permute-done.8.refs_3_
  104.4 0.7 copy-done.12
  105.1 8.7 %warm.1 = (f32[64,8,16,128]{3,2,1,0:T(8,128)S(1)}, f32[128,128]{1,0:T(8,128)}) custom-call(s32[2]{0:T(128)S(1)} %copy-done.6, f32[10,64]{1,0:T(8,128)S(1)} %stack.136.floats, s32[5,64]{1,0:T(8,128)S(1)} %stack.143.ints, f32[6,16]{1,0:T(8,128)S(1)} %copy.16.kinds, f32[2]{0:T(128)S(1)} %copy-done.12, f32[64,8,16,128]{3,2,1,0:T(8,128)} %get-tuple-element.51.swept, ...), custom_call_target="tpu_custom_call" | custom-call | tf_op jit(solution)/shard_map/warm/pallas_call | solution.py:710
  113.9 0.0 collective-permute-done.9.refs_1_
  113.9 0.0 collective-permute-done.10.refs_2_
  113.9 2.6 %collective-permute-done.11.refs_3_ = f32[3,256,128]{2,1,0:T(8,128)S(1)} collective-permute-done((f32[3,256,128]{2,1,0:T(8,128)S(1)}, f32[3,256,128]{2,1,0:T(8,128)S(1)}, u32[]{:S(2)}, u32[]{:S(2)}) %collective-permute-start.11) | collective-permute-done | bytes 393248 | tf_op jit(solution)/shard_map/ppermute | solution.py:583
  116.5 5.2 %inflow.1 = f32[64,8,16,128]{3,2,1,0:T(8,128)} custom-call(s32[2]{0:T(128)S(1)} %copy-done.6, f32[10,64]{1,0:T(8,128)S(1)} %stack.136.floats, s32[5,64]{1,0:T(8,128)S(1)} %stack.143.ints, f32[64,8,16,128]{3,2,1,0:T(8,128)S(1)} %get-tuple-element.66.warm, f32[3,256,128]{2,1,0:T(8,128)S(1)} %get-tuple-element.67.refs_0_, ...), custom_call_target="tpu_custom_call" | custom-call | tf_op jit(solution)/shard_map/inflow/pallas_call | solution.py:723
  (35 shorter events, 0.4 us)
Async XLA Ops:
  0.6 22.9 %copy-start.14 = (f32[8]{0:T(128)S(1)}, f32[8]{0:T(128)}, u32[]{:S(2)}) copy-start(f32[8]{0:T(128)} %refs_3_.1) | copy-start | bytes 100
  0.6 22.8 %copy-start.15 = (f32[8]{0:T(128)S(1)}, f32[8]{0:T(128)}, u32[]{:S(2)}) copy-start(f32[8]{0:T(128)} %refs_1_.1) | copy-start | bytes 100
  0.7 22.8 %copy-start.16 = (f32[8]{0:T(128)S(1)}, f32[8]{0:T(128)}, u32[]{:S(2)}) copy-start(f32[8]{0:T(128)} %refs_0_.1) | copy-start | bytes 100
  0.7 22.8 %copy-start.18 = (f32[8]{0:T(128)S(1)}, f32[8]{0:T(128)}, u32[]{:S(2)}) copy-start(f32[8]{0:T(128)} %refs_4_.1) | copy-start | bytes 100
  0.7 22.8 %copy-start.19 = (f32[8]{0:T(128)S(1)}, f32[8]{0:T(128)}, u32[]{:S(2)}) copy-start(f32[8]{0:T(128)} %refs_2_.1) | copy-start | bytes 100
  0.7 22.8 %copy-start.17 = (s32[64]{0:T(128)S(1)}, s32[64]{0:T(128)}, u32[]{:S(2)}) copy-start(s32[64]{0:T(128)} %labels.1) | copy-start | bytes 772
  1.3 28.7 %copy-start.6 = (s32[2]{0:T(128)S(1)}, s32[2]{0:T(128)}, u32[]{:S(2)}) copy-start(s32[2]{0:T(128)} %pad_add_fusion.meta) | copy-start | bytes 28
  18.8 14.6 %collective-permute-start.2 = (f32[3,256,128]{2,1,0:T(8,128)}, f32[3,256,128]{2,1,0:T(8,128)S(1)}, u32[]{:S(2)}, u32[]{:S(2)}) collective-permute-start(f32[3,256,128]{2,1,0:T(8,128)} %get-tuple-element.41), channel_id=1, source_target_pairs={{0,4},{4,0},{8,12},{12,8},{16,20},{20,16},{24,28},{28,24},{1,5},{5... | collective-permute-start | bytes 1179656 | tf_op jit(solution)/shard_map/ppermute | solution.py:583
  21.8 12.3 %collective-permute-start.3 = (f32[3,256,128]{2,1,0:T(8,128)}, f32[3,256,128]{2,1,0:T(8,128)S(1)}, u32[]{:S(2)}, u32[]{:S(2)}) collective-permute-start(f32[3,256,128]{2,1,0:T(8,128)} %get-tuple-element.42), channel_id=1, source_target_pairs={{0,8},{4,12},{8,0},{12,4},{16,24},{20,28},{24,16},{28,20},{1,9},{5... | collective-permute-start | bytes 1179656 | tf_op jit(solution)/shard_map/ppermute | solution.py:583
  23.4 17.5 %collective-permute-start.4 = (f32[3,256,128]{2,1,0:T(8,128)}, f32[3,256,128]{2,1,0:T(8,128)S(1)}, u32[]{:S(2)}, u32[]{:S(2)}) collective-permute-start(f32[3,256,128]{2,1,0:T(8,128)} %get-tuple-element.43), channel_id=1, source_target_pairs={{0,12},{4,8},{8,4},{12,0},{16,28},{20,24},{24,20},{28,16},{1,13},{... | collective-permute-start | bytes 1179656 | tf_op jit(solution)/shard_map/ppermute | solution.py:583
  23.4 2.5 %collective-permute-start = (f32[2,3,64,512]{3,2,1,0:T(8,128)}, f32[2,3,64,512]{3,2,1,0:T(8,128)S(1)}, u32[]{:S(2)}, u32[]{:S(2)}) collective-permute-start(f32[2,3,64,512]{3,2,1,0:T(8,128)} %get-tuple-element.38), channel_id=1, source_target_pairs={{0,1},{1,0},{2,3},{3,2},{4,5},{5,4},{6,7},{7,6},{8,9},{9,8},{10,11... | collective-permute-start | bytes 2359304 | tf_op jit(solution)/shard_map/ppermute | solution.py:583
  25.9 1.1 copy-start
  27.9 15.9 %collective-permute-start.1 = (f32[1,3,64,512]{3,2,1,0:T(8,128)}, f32[1,3,64,512]{3,2,1,0:T(8,128)S(1)}, u32[]{:S(2)}, u32[]{:S(2)}) collective-permute-start(f32[1,3,64,512]{3,2,1,0:T(8,128)} %get-tuple-element.39), channel_id=1, source_target_pairs={{0,2},{1,3},{2,0},{3,1},{4,6},{5,7},{6,4},{7,5},{8,10},{9,11},{10,... | collective-permute-start | bytes 1179656 | tf_op jit(solution)/shard_map/ppermute | solution.py:583
  29.9 2.1 %copy-start.13 = (f32[6,8,2]{0,2,1:T(2,128)}, f32[6,8,2]{0,2,1:T(2,128)S(1)}, u32[]{:S(2)}) copy-start(f32[6,8,2]{0,2,1:T(2,128)S(1)} %copy.14) | copy-start | bytes 1156
  30.8 0.6 copy-start.4
  31.4 0.6 copy-start.7
  33.4 29.2 %copy-start.10 = (f32[2]{0:T(128)}, f32[2]{0:T(128)S(1)}, u32[]{:S(2)}) copy-start(f32[2]{0:T(128)S(1)} %pad_maximum_fusion.1.sums) | copy-start | bytes 28
  40.9 1.0 copy-start.1
  43.1 0.8 copy-start.2
  43.8 50.3 %copy-start.5 = (f32[144,128]{1,0:T(8,128)S(1)}, f32[144,128]{1,0:T(8,128)}, u32[]{:S(2)}) copy-start(f32[144,128]{1,0:T(8,128)} %copy-done.4) | copy-start | bytes 221188
  43.8 50.3 %copy-start.8 = (f32[40,128]{1,0:T(8,128)S(1)}, f32[40,128]{1,0:T(8,128)}, u32[]{:S(2)}) copy-start(f32[40,128]{1,0:T(8,128)} %copy-done.7) | copy-start | bytes 61444
  60.6 0.7 copy-start.9
  62.6 31.5 %all-to-all-start.1 = ((f32[8,2,8,512]{3,2,1,0:T(8,128)}), f32[8,2,8,512]{3,2,1,0:T(8,128)S(1)}, u32[]{:S(2)}, u32[]{:S(2)}) async-start(f32[8,2,8,512]{3,2,1,0:T(8,128)} %get-tuple-element.55), calls=%async_computation.1 | async-start | bytes 524288 | tf_op jit(solution)/shard_map/all_to_all | solution.py:675
  66.0 25.0 %collective-permute-start.5 = (f32[3,256,128]{2,1,0:T(8,128)}, f32[3,256,128]{2,1,0:T(8,128)S(1)}, u32[]{:S(2)}, u32[]{:S(2)}) collective-permute-start(f32[3,256,128]{2,1,0:T(8,128)} %copy-done.2), channel_id=1, source_target_pairs={{0,16},{4,20},{8,24},{12,28},{16,0},{20,4},{24,8},{28,12},{1,17},{... | collective-permute-start | bytes 1179656 | tf_op jit(solution)/shard_map/ppermute | solution.py:583
  91.0 1.0 copy-start.3
  94.1 0.7 copy-start.11
  96.2 6.7 %collective-permute-start.6 = (f32[128,512]{1,0:T(8,128)S(1)}, f32[128,512]{1,0:T(8,128)S(1)}, u32[]{:S(2)}, u32[]{:S(2)}) collective-permute-start(f32[128,512]{1,0:T(8,128)S(1)} %kelvins.1.refs_0_), channel_id=1, source_target_pairs={{0,2},{1,3},{2,0},{3,1},{4,6},{5,7},{6,4},{7,5},{8,10},{9,11},{10,... | collective-permute-start | bytes 786440 | tf_op jit(solution)/shard_map/ppermute | solution.py:583
  97.7 16.1 %collective-permute-start.9 = (f32[3,256,128]{2,1,0:T(8,128)}, f32[3,256,128]{2,1,0:T(8,128)S(1)}, u32[]{:S(2)}, u32[]{:S(2)}) collective-permute-start(f32[3,256,128]{2,1,0:T(8,128)} %get-tuple-element.68), channel_id=1, source_target_pairs={{0,4},{4,0},{8,12},{12,8},{16,20},{20,16},{24,28},{28,24},{1,5},{5... | collective-permute-start | bytes 1179656 | tf_op jit(solution)/shard_map/ppermute | solution.py:583
  99.2 14.6 %collective-permute-start.10 = (f32[3,256,128]{2,1,0:T(8,128)S(1)}, f32[3,256,128]{2,1,0:T(8,128)S(1)}, u32[]{:S(2)}, u32[]{:S(2)}) collective-permute-start(f32[3,256,128]{2,1,0:T(8,128)S(1)} %get-tuple-element.69), channel_id=1, source_target_pairs={{0,8},{4,12},{8,0},{12,4},{16,24},{20,28},{24,16},{28,20},{1,9},{5... | collective-permute-start | bytes 1179656 | tf_op jit(solution)/shard_map/ppermute | solution.py:583
  99.3 17.3 %collective-permute-start.11 = (f32[3,256,128]{2,1,0:T(8,128)S(1)}, f32[3,256,128]{2,1,0:T(8,128)S(1)}, u32[]{:S(2)}, u32[]{:S(2)}) collective-permute-start(f32[3,256,128]{2,1,0:T(8,128)S(1)} %get-tuple-element.70), channel_id=1, source_target_pairs={{0,12},{4,8},{8,4},{12,0},{16,28},{20,24},{24,20},{28,16},{1,13},{... | collective-permute-start | bytes 1179656 | tf_op jit(solution)/shard_map/ppermute | solution.py:583
  101.2 2.5 %collective-permute-start.7 = (f32[128,512]{1,0:T(8,128)S(1)}, f32[128,512]{1,0:T(8,128)S(1)}, u32[]{:S(2)}, u32[]{:S(2)}) collective-permute-start(f32[128,512]{1,0:T(8,128)S(1)} %kelvins.1.refs_0_), channel_id=1, source_target_pairs={{0,1},{1,0},{2,3},{3,2},{4,5},{5,4},{6,7},{7,6},{8,9},{9,8},{10,11... | collective-permute-start | bytes 786440 | tf_op jit(solution)/shard_map/ppermute | solution.py:583
  102.9 1.5 %collective-permute-start.8 = (f32[128,512]{1,0:T(8,128)S(1)}, f32[128,512]{1,0:T(8,128)S(1)}, u32[]{:S(2)}, u32[]{:S(2)}) collective-permute-start(f32[128,512]{1,0:T(8,128)S(1)} %collective-permute-done.6.refs_1_), channel_id=1, source_target_pairs={{0,1},{1,0},{2,3},{3,2},{4,5},{5,4},{6,7},{7,6},{8,9},{9,8},{10,11... | collective-permute-start | bytes 786440 | tf_op jit(solution)/shard_map/ppermute | solution.py:583
  104.4 0.7 copy-start.12

commit v11 on v10

--- a/solution.py
+++ b/solution.py
@@ -662,17 +662,8 @@
     composites = [composite] + [swap(composite, "slab", index * group) for index in range(1, groups)]
     (parts,) = call(functools.partial(parts_kernel, depth), "density_parts", [VMEM] * 2, [shape(*piece)], keep, other)
     summed = lax.all_to_all(parts, "slab", 0, 0)
-
-    copies, late = call(
-        totals_kernel,
-        "density_totals",
-        [SMEM] + [VMEM] * 2,
-        [shape(slabs, 2, depth, lanes), shape(depth, lanes)],
-        sums,
-        summed,
-        quarter,
-    )
-    gathered = lax.all_to_all(copies, "slab", 0, 0)
+    summed, composites = lax.optimization_barrier((summed, composites))
+
     entering = call(
         functools.partial(enter_kernel, own, group, groups, depth),
         "enter",
@@ -685,7 +676,16 @@
         *composites,
         scratches=[scratch(groups, *face), scratch(group, *face)],
     )
-    gathered, entering = lax.optimization_barrier((gathered, entering))
+    copies, late = call(
+        totals_kernel,
+        "density_totals",
+        [SMEM] + [VMEM] * 2,
+        [shape(slabs, 2, depth, lanes), shape(depth, lanes)],
+        sums,
+        summed,
+        quarter,
+    )
+    gathered = lax.all_to_all(copies, "slab", 0, 0)
     entering = [entering[0]] + [swap(entering[index], "slab", index) for index in range(1, group)]
 
     pack_shape = shape(6 * KINDS + 4 * depth, lanes)

time: 122 us -> 124 us (1.016)
  blocking collectives: 16.7 us -> 11.8 us
  starting transfers between devices: 17.8 us -> 21.2 us
  waiting for transfers between devices: 36 us -> 38.8 us
    all_to_all x1, blocking collectives: 16.7 us -> 11.8 us  [local(): gathered = lax.all_to_all(copies, 'slab', 0, 0)]
    ppermute x12, waiting for transfers between devices: 36 us -> 38.8 us  [swap(): lax.ppermute(array, axis, [(i, i ^ by) for i in range(lax.axis_size(axis))])]
    all_to_all x1, starting transfers between devices: 3.41 us -> 6.12 us  [local(): summed = lax.all_to_all(parts, 'slab', 0, 0)]
where the time goes in v11:
time: 124 us; the launch traced here: 123 us
  Pallas kernels  39.3 us (32%)
  waiting for transfers between devices  38.8 us (31%)
  starting transfers between devices  21.2 us (17%)
  blocking collectives  11.8 us (10%)
  local copies, waits for them, and re-layouts  7.92 us (6%)
  other arithmetic  3.49 us (3%)
    ppermute x12, waiting for transfers between devices, swap(): lax.ppermute(array, axis, [(i, i ^ by) for i in range(lax.axis_size(axis))])  38.8 us
    pallas_call x1, Pallas kernels, local(): pl.pallas_call(functools.partial(sweeps_kernel, (block, blocks, depth, wi...  17.5 us
    ppermute x12, starting transfers between devices, swap(): lax.ppermute(array, axis, [(i, i ^ by) for i in range(lax.axis_size(axis))])  15.1 us
    all_to_all x1, blocking collectives, local(): gathered = lax.all_to_all(copies, 'slab', 0, 0)  11.8 us
    pallas_call x1, Pallas kernels, local(): pl.pallas_call(functools.partial(warm_kernel, (block, depth, width_y, wid...  8.74 us
    pallas_call x7, Pallas kernels, call(): pl.pallas_call(kernel, in_specs=in_specs, out_specs=[VMEM] * len(out_shap...  7.88 us
    unnamed x40, local copies, waits for them, and re-layouts  7.54 us
    all_to_all x1, starting transfers between devices, local(): summed = lax.all_to_all(parts, 'slab', 0, 0)  6.12 us
  transfers between devices with their start and end apart: 13, of which 7 were waited for; matrix products, arithmetic and copies ran while one was open for 3% of the time, Pallas kernels for 11%

profile of v11, /device:TPU:0, one launch (start us, length us, event | category | flops | bytes accessed | tf_op | source)
XLA Modules:
  0.0 123.3 jit_solution(14706690355174991506)
XLA Ops:
  0.6 0.0 copy-start.14
  0.6 0.0 copy-start.15
  0.7 0.0 copy-start.16
  0.7 0.0 copy-start.18
  0.7 0.0 copy-start.19
  0.7 0.0 copy-start.17
  0.7 0.6 pad_add_fusion.meta
  1.3 17.5 %sweeps.1 = (f32[64,8,16,128]{3,2,1,0:T(8,128)}, f32[8,512]{1,0:T(8,128)}, f32[3,256,128]{2,1,0:T(8,128)}, f32[3,256,128]{2,1,0:T(8,128)}, f32[3,256,128]{2,1,0:...) custom-call(s32[2]{0:T(128)} %pad_add_fusion.meta, s32[64]{0:T(128)} %labels.1, ...), custom_call_target="tpu_custom_call" | custom-call | tf_op jit(solution)/shard_map/sweeps/pallas_call | solution.py:600
  18.8 3.0 %collective-permute-start.2 = (f32[3,256,128]{2,1,0:T(8,128)}, f32[3,256,128]{2,1,0:T(8,128)S(1)}, u32[]{:S(2)}, u32[]{:S(2)}) collective-permute-start(f32[3,256,128]{2,1,0:T(8,128)} %get-tuple-element.39), channel_id=1, source_target_pairs={{0,4},{4,0},{8,12},{12,8},{16,20},{20,16},{24,28},{28,24},{1,5},{5... | collective-permute-start | bytes 1179656 | tf_op jit(solution)/shard_map/ppermute | solution.py:583
  21.8 1.6 %collective-permute-start.3 = (f32[3,256,128]{2,1,0:T(8,128)}, f32[3,256,128]{2,1,0:T(8,128)S(1)}, u32[]{:S(2)}, u32[]{:S(2)}) collective-permute-start(f32[3,256,128]{2,1,0:T(8,128)} %get-tuple-element.40), channel_id=1, source_target_pairs={{0,8},{4,12},{8,0},{12,4},{16,24},{20,28},{24,16},{28,20},{1,9},{5... | collective-permute-start | bytes 1179656 | tf_op jit(solution)/shard_map/ppermute | solution.py:583
  23.4 0.0 collective-permute-start.4
  23.4 0.0 collective-permute-start
  23.4 0.0 copy-done.15
  23.4 0.0 copy-done.16
  23.5 0.1 select_reduce_fusion
  23.6 0.7 fusion.20
  24.3 0.1 fusion.7
  24.5 1.4 %collective-permute-done.other = f32[2,3,64,512]{3,2,1,0:T(8,128)S(1)} collective-permute-done((f32[2,3,64,512]{3,2,1,0:T(8,128)}, f32[2,3,64,512]{3,2,1,0:T(8,128)S(1)}, u32[]{:S(2)}, u32[]{:S(2)}) %collective-permute-start) | collective-permute-done | bytes 786464 | tf_op jit(solution)/shard_map/ppermute | solution.py:583
  25.9 1.1 copy-done
  27.0 0.8 density_split.1
  27.9 1.9 %collective-permute-start.1 = (f32[1,3,64,512]{3,2,1,0:T(8,128)}, f32[1,3,64,512]{3,2,1,0:T(8,128)S(1)}, u32[]{:S(2)}, u32[]{:S(2)}) collective-permute-start(f32[1,3,64,512]{3,2,1,0:T(8,128)} %get-tuple-element.37), channel_id=1, source_target_pairs={{0,2},{1,3},{2,0},{3,1},{4,6},{5,7},{6,4},{7,5},{8,10},{9,11},{10,... | collective-permute-start | bytes 1179656 | tf_op jit(solution)/shard_map/ppermute | solution.py:583
  29.8 0.1 copy.14
  29.9 0.1 copy.15.kinds
  29.9 0.0 copy-done.6
  29.9 0.8 heat_matrices.1
  30.8 0.6 copy-done.4
  31.5 1.9 %pad_maximum_fusion.1.sums = f32[2]{0:T(128)} fusion(f32[1]{0:T(128)} %bitcast.36, f32[1]{0:T(128)} %bitcast.35), kind=kLoop, calls=%fused_computation.35 | loop fusion | flops 2 | bytes 16 | tf_op jit(solution)/shard_map/stack | solution.py:571
  33.4 0.0 collective-permute-done.2.refs_1_
  33.4 0.7 collective-permute-done.3.refs_2_
  34.1 6.8 %collective-permute-done.4.refs_3_ = f32[3,256,128]{2,1,0:T(8,128)S(1)} collective-permute-done((f32[3,256,128]{2,1,0:T(8,128)}, f32[3,256,128]{2,1,0:T(8,128)S(1)}, u32[]{:S(2)}, u32[]{:S(2)}) %collective-permute-start.4) | collective-permute-done | bytes 393248 | tf_op jit(solution)/shard_map/ppermute | solution.py:583
  40.9 1.0 copy-done.1
  41.9 1.2 compose.1
  43.1 0.0 copy-start.2
  43.1 0.8 copy-done.2
  43.8 0.0 collective-permute-done.1.other
  43.8 0.8 density_parts.1
  44.6 6.1 %all-to-all-start = ((f32[8,3,8,512]{3,2,1,0:T(8,128)}), f32[8,3,8,512]{3,2,1,0:T(8,128)S(1)}, u32[]{:S(2)}, u32[]{:S(2)}) async-start(f32[8,3,8,512]{3,2,1,0:T(8,128)} %density_parts.1), calls=%async_computation | async-start | bytes 786432 | tf_op jit(solution)/shard_map/all_to_all | solution.py:664
  50.8 2.9 %collective-permute-start.5 = (f32[3,256,128]{2,1,0:T(8,128)}, f32[3,256,128]{2,1,0:T(8,128)S(1)}, u32[]{:S(2)}, u32[]{:S(2)}) collective-permute-start(f32[3,256,128]{2,1,0:T(8,128)} %copy-done.2), channel_id=1, source_target_pairs={{0,16},{4,20},{8,24},{12,28},{16,0},{20,4},{24,8},{28,12},{1,17},{... | collective-permute-start | bytes 1179656 | tf_op jit(solution)/shard_map/ppermute | solution.py:583
  53.7 24.5 %collective-permute-done.5.refs_1_ = f32[3,256,128]{2,1,0:T(8,128)S(1)} collective-permute-done((f32[3,256,128]{2,1,0:T(8,128)}, f32[3,256,128]{2,1,0:T(8,128)S(1)}, u32[]{:S(2)}, u32[]{:S(2)}) %collective-permute-start.5) | collective-permute-done | bytes 393248 | tf_op jit(solution)/shard_map/ppermute | solution.py:583
  78.2 0.0 all-to-all-done.parts
  78.2 0.7 copy-done.9
  78.9 0.7 copy-done.10
  79.5 0.6 density_totals.1
  80.2 11.8 %all_to_all.10.gathered = f32[8,2,8,512]{3,2,1,0:T(8,128)S(1)} all-to-all(f32[8,2,8,512]{3,2,1,0:T(8,128)S(1)} %get-tuple-element.55), channel_id=1, replica_groups=mesh['slab'=8,'mode'=4] {'slab'}, dimensions={0} | all-to-all | bytes 524288 | tf_op jit(solution)/shard_map/all_to_all | solution.py:688
  92.0 0.9 copy-done.5
  92.9 0.7 copy-done.8
  93.6 1.4 %kelvins.1.refs_0_ = f32[128,512]{1,0:T(8,128)S(1)} custom-call(s32[2]{0:T(128)S(1)} %copy-done.6, f32[2]{0:T(128)S(1)} %copy-done.10, f32[8,2,8,512]{3,2,1,0:T(8,128)S(1)} %all_to_all.10.gathered, f32[8,512]{1,0:T(8,128)S(1)} %get-tuple-element.56.late, f32[144,128]{1,0:T(8,128)S(1)} %copy-done.5, f32[40,128]{1,0:T(8,128)S(1)} %copy-done.8), custom_call_target="tpu_custom_call" | custom-call | tf_op jit(solution)/shard_map/kelvins/pallas_call | solution.py:586
  95.0 1.7 %collective-permute-start.6 = (f32[128,512]{1,0:T(8,128)S(1)}, f32[128,512]{1,0:T(8,128)S(1)}, u32[]{:S(2)}, u32[]{:S(2)}) collective-permute-start(f32[128,512]{1,0:T(8,128)S(1)} %kelvins.1.refs_0_), channel_id=1, source_target_pairs={{0,2},{1,3},{2,0},{3,1},{4,6},{5,7},{6,4},{7,5},{8,10},{9,11},{10,... | collective-permute-start | bytes 786440 | tf_op jit(solution)/shard_map/ppermute | solution.py:583
  96.7 1.0 copy-done.3
  97.7 2.3 %enter.1 = (f32[3,256,128]{2,1,0:T(8,128)S(1)}, f32[3,256,128]{2,1,0:T(8,128)}, f32[3,256,128]{2,1,0:T(8,128)}, f32[3,256,128]{2,1,0:T(8,128)S(1)}) custom-call(s32[2]{0:T(128)S(1)} %copy-done.6, f32[10,64]{1,0:T(8,128)S(1)} %stack.136.floats, s32[5,64]{1,0:T(8,128)S(1)} %stack.143.ints, f32[4,3,256,128]{3,2,1,0:T(8,128)S(1)} %get-tuple-element.60.effective, ...), custom_call_target="tpu_custom_call" | custom-call | tf_op jit(solution)/shard_map/enter/pallas_call | solution.py:586
  99.9 1.3 %collective-permute-start.9 = (f32[3,256,128]{2,1,0:T(8,128)}, f32[3,256,128]{2,1,0:T(8,128)S(1)}, u32[]{:S(2)}, u32[]{:S(2)}) collective-permute-start(f32[3,256,128]{2,1,0:T(8,128)} %get-tuple-element.64), channel_id=1, source_target_pairs={{0,4},{4,0},{8,12},{12,8},{16,20},{20,16},{24,28},{28,24},{1,5},{5... | collective-permute-start | bytes 1179656 | tf_op jit(solution)/shard_map/ppermute | solution.py:583
  101.2 0.0 collective-permute-start.10
  101.3 2.1 %collective-permute-start.11 = (f32[3,256,128]{2,1,0:T(8,128)S(1)}, f32[3,256,128]{2,1,0:T(8,128)S(1)}, u32[]{:S(2)}, u32[]{:S(2)}) collective-permute-start(f32[3,256,128]{2,1,0:T(8,128)S(1)} %get-tuple-element.66), channel_id=1, source_target_pairs={{0,12},{4,8},{8,4},{12,0},{16,28},{20,24},{24,20},{28,16},{1,13},{... | collective-permute-start | bytes 1179656 | tf_op jit(solution)/shard_map/ppermute | solution.py:583
  103.4 0.0 collective-permute-start.7
  103.4 0.0 collective-permute-done.6.refs_1_
  103.4 0.5 collective-permute-start.8
  103.9 0.1 copy.16.kinds
  104.0 0.9 collective-permute-done.7.refs_2_
  104.9 0.4 collective-permute-done.8.refs_3_
  105.3 8.7 %warm.1 = (f32[64,8,16,128]{3,2,1,0:T(8,128)S(1)}, f32[128,128]{1,0:T(8,128)}) custom-call(s32[2]{0:T(128)S(1)} %copy-done.6, f32[10,64]{1,0:T(8,128)S(1)} %stack.136.floats, s32[5,64]{1,0:T(8,128)S(1)} %stack.143.ints, f32[6,16]{1,0:T(8,128)S(1)} %copy.16.kinds, f32[2]{0:T(128)S(1)} %copy-done.11, f32[64,8,16,128]{3,2,1,0:T(8,128)} %get-tuple-element.49.swept, ...), custom_call_target="tpu_custom_call" | custom-call | tf_op jit(solution)/shard_map/warm/pallas_call | solution.py:710
  114.1 0.0 collective-permute-done.9.refs_1_
  114.1 0.0 collective-permute-done.10.refs_2_
  114.1 4.1 %collective-permute-done.11.refs_3_ = f32[3,256,128]{2,1,0:T(8,128)S(1)} collective-permute-done((f32[3,256,128]{2,1,0:T(8,128)S(1)}, f32[3,256,128]{2,1,0:T(8,128)S(1)}, u32[]{:S(2)}, u32[]{:S(2)}) %collective-permute-start.11) | collective-permute-done | bytes 393248 | tf_op jit(solution)/shard_map/ppermute | solution.py:583
  118.2 5.2 %inflow.1 = f32[64,8,16,128]{3,2,1,0:T(8,128)} custom-call(s32[2]{0:T(128)S(1)} %copy-done.6, f32[10,64]{1,0:T(8,128)S(1)} %stack.136.floats, s32[5,64]{1,0:T(8,128)S(1)} %stack.143.ints, f32[64,8,16,128]{3,2,1,0:T(8,128)S(1)} %get-tuple-element.59.warm, f32[3,256,128]{2,1,0:T(8,128)S(1)} %get-tuple-element.63.refs_0_, ...), custom_call_target="tpu_custom_call" | custom-call | tf_op jit(solution)/shard_map/inflow/pallas_call | solution.py:723
  (35 shorter events, 0.3 us)
Async XLA Ops:
  0.6 22.8 %copy-start.14 = (f32[8]{0:T(128)S(1)}, f32[8]{0:T(128)}, u32[]{:S(2)}) copy-start(f32[8]{0:T(128)} %refs_3_.1) | copy-start | bytes 100
  0.6 22.8 %copy-start.15 = (f32[8]{0:T(128)S(1)}, f32[8]{0:T(128)}, u32[]{:S(2)}) copy-start(f32[8]{0:T(128)} %refs_1_.1) | copy-start | bytes 100
  0.7 22.8 %copy-start.16 = (f32[8]{0:T(128)S(1)}, f32[8]{0:T(128)}, u32[]{:S(2)}) copy-start(f32[8]{0:T(128)} %refs_0_.1) | copy-start | bytes 100
  0.7 22.8 %copy-start.18 = (f32[8]{0:T(128)S(1)}, f32[8]{0:T(128)}, u32[]{:S(2)}) copy-start(f32[8]{0:T(128)} %refs_4_.1) | copy-start | bytes 100
  0.7 22.8 %copy-start.19 = (f32[8]{0:T(128)S(1)}, f32[8]{0:T(128)}, u32[]{:S(2)}) copy-start(f32[8]{0:T(128)} %refs_2_.1) | copy-start | bytes 100
  0.7 22.8 %copy-start.17 = (s32[64]{0:T(128)S(1)}, s32[64]{0:T(128)}, u32[]{:S(2)}) copy-start(s32[64]{0:T(128)} %labels.1) | copy-start | bytes 772
  1.3 28.6 %copy-start.6 = (s32[2]{0:T(128)S(1)}, s32[2]{0:T(128)}, u32[]{:S(2)}) copy-start(s32[2]{0:T(128)} %pad_add_fusion.meta) | copy-start | bytes 28
  18.8 14.6 %collective-permute-start.2 = (f32[3,256,128]{2,1,0:T(8,128)}, f32[3,256,128]{2,1,0:T(8,128)S(1)}, u32[]{:S(2)}, u32[]{:S(2)}) collective-permute-start(f32[3,256,128]{2,1,0:T(8,128)} %get-tuple-element.39), channel_id=1, source_target_pairs={{0,4},{4,0},{8,12},{12,8},{16,20},{20,16},{24,28},{28,24},{1,5},{5... | collective-permute-start | bytes 1179656 | tf_op jit(solution)/shard_map/ppermute | solution.py:583
  21.8 12.2 %collective-permute-start.3 = (f32[3,256,128]{2,1,0:T(8,128)}, f32[3,256,128]{2,1,0:T(8,128)S(1)}, u32[]{:S(2)}, u32[]{:S(2)}) collective-permute-start(f32[3,256,128]{2,1,0:T(8,128)} %get-tuple-element.40), channel_id=1, source_target_pairs={{0,8},{4,12},{8,0},{12,4},{16,24},{20,28},{24,16},{28,20},{1,9},{5... | collective-permute-start | bytes 1179656 | tf_op jit(solution)/shard_map/ppermute | solution.py:583
  23.4 17.5 %collective-permute-start.4 = (f32[3,256,128]{2,1,0:T(8,128)}, f32[3,256,128]{2,1,0:T(8,128)S(1)}, u32[]{:S(2)}, u32[]{:S(2)}) collective-permute-start(f32[3,256,128]{2,1,0:T(8,128)} %get-tuple-element.41), channel_id=1, source_target_pairs={{0,12},{4,8},{8,4},{12,0},{16,28},{20,24},{24,20},{28,16},{1,13},{... | collective-permute-start | bytes 1179656 | tf_op jit(solution)/shard_map/ppermute | solution.py:583
  23.4 2.5 %collective-permute-start = (f32[2,3,64,512]{3,2,1,0:T(8,128)}, f32[2,3,64,512]{3,2,1,0:T(8,128)S(1)}, u32[]{:S(2)}, u32[]{:S(2)}) collective-permute-start(f32[2,3,64,512]{3,2,1,0:T(8,128)} %get-tuple-element.36), channel_id=1, source_target_pairs={{0,1},{1,0},{2,3},{3,2},{4,5},{5,4},{6,7},{7,6},{8,9},{9,8},{10,11... | collective-permute-start | bytes 2359304 | tf_op jit(solution)/shard_map/ppermute | solution.py:583
  25.9 1.1 copy-start
  27.9 16.0 %collective-permute-start.1 = (f32[1,3,64,512]{3,2,1,0:T(8,128)}, f32[1,3,64,512]{3,2,1,0:T(8,128)S(1)}, u32[]{:S(2)}, u32[]{:S(2)}) collective-permute-start(f32[1,3,64,512]{3,2,1,0:T(8,128)} %get-tuple-element.37), channel_id=1, source_target_pairs={{0,2},{1,3},{2,0},{3,1},{4,6},{5,7},{6,4},{7,5},{8,10},{9,11},{10,... | collective-permute-start | bytes 1179656 | tf_op jit(solution)/shard_map/ppermute | solution.py:583
  29.9 1.5 %copy-start.12 = (f32[6,8,2]{0,2,1:T(2,128)}, f32[6,8,2]{0,2,1:T(2,128)S(1)}, u32[]{:S(2)}) copy-start(f32[6,8,2]{0,2,1:T(2,128)S(1)} %copy.14) | copy-start | bytes 1156
  30.8 0.6 copy-start.4
  31.4 9.5 %copy-start.7 = (f32[40,128]{1,0:T(8,128)}, f32[40,128]{1,0:T(8,128)S(1)}, u32[]{:S(2)}) copy-start(f32[40,128]{1,0:T(8,128)S(1)} %get-tuple-element.58.matrix_two) | copy-start | bytes 61444
  40.9 1.0 copy-start.1
  43.1 0.8 copy-start.2
  43.8 61.5 %copy-start.11 = (f32[2]{0:T(128)S(1)}, f32[2]{0:T(128)}, u32[]{:S(2)}) copy-start(f32[2]{0:T(128)} %pad_maximum_fusion.1.sums) | copy-start | bytes 28
  44.6 59.3 %copy-start.13 = (f32[6,8,2]{0,2,1:T(2,128)S(1)}, f32[6,8,2]{0,2,1:T(2,128)}, u32[]{:S(2)}) copy-start(f32[6,8,2]{0,2,1:T(2,128)} %copy-done.12) | copy-start | bytes 1156
  44.6 33.5 %all-to-all-start = ((f32[8,3,8,512]{3,2,1,0:T(8,128)}), f32[8,3,8,512]{3,2,1,0:T(8,128)S(1)}, u32[]{:S(2)}, u32[]{:S(2)}) async-start(f32[8,3,8,512]{3,2,1,0:T(8,128)} %density_parts.1), calls=%async_computation | async-start | bytes 786432 | tf_op jit(solution)/shard_map/all_to_all | solution.py:664
  50.8 27.4 %collective-permute-start.5 = (f32[3,256,128]{2,1,0:T(8,128)}, f32[3,256,128]{2,1,0:T(8,128)S(1)}, u32[]{:S(2)}, u32[]{:S(2)}) collective-permute-start(f32[3,256,128]{2,1,0:T(8,128)} %copy-done.2), channel_id=1, source_target_pairs={{0,16},{4,20},{8,24},{12,28},{16,0},{20,4},{24,8},{28,12},{1,17},{... | collective-permute-start | bytes 1179656 | tf_op jit(solution)/shard_map/ppermute | solution.py:583
  78.2 0.7 copy-start.9
  78.9 0.7 copy-start.10
  92.0 0.9 copy-start.5
  92.9 0.7 copy-start.8
  95.0 8.4 %collective-permute-start.6 = (f32[128,512]{1,0:T(8,128)S(1)}, f32[128,512]{1,0:T(8,128)S(1)}, u32[]{:S(2)}, u32[]{:S(2)}) collective-permute-start(f32[128,512]{1,0:T(8,128)S(1)} %kelvins.1.refs_0_), channel_id=1, source_target_pairs={{0,2},{1,3},{2,0},{3,1},{4,6},{5,7},{6,4},{7,5},{8,10},{9,11},{10,... | collective-permute-start | bytes 786440 | tf_op jit(solution)/shard_map/ppermute | solution.py:583
  96.7 1.0 copy-start.3
  99.9 14.1 %collective-permute-start.9 = (f32[3,256,128]{2,1,0:T(8,128)}, f32[3,256,128]{2,1,0:T(8,128)S(1)}, u32[]{:S(2)}, u32[]{:S(2)}) collective-permute-start(f32[3,256,128]{2,1,0:T(8,128)} %get-tuple-element.64), channel_id=1, source_target_pairs={{0,4},{4,0},{8,12},{12,8},{16,20},{20,16},{24,28},{28,24},{1,5},{5... | collective-permute-start | bytes 1179656 | tf_op jit(solution)/shard_map/ppermute | solution.py:583
  101.2 12.8 %collective-permute-start.10 = (f32[3,256,128]{2,1,0:T(8,128)}, f32[3,256,128]{2,1,0:T(8,128)S(1)}, u32[]{:S(2)}, u32[]{:S(2)}) collective-permute-start(f32[3,256,128]{2,1,0:T(8,128)} %get-tuple-element.65), channel_id=1, source_target_pairs={{0,8},{4,12},{8,0},{12,4},{16,24},{20,28},{24,16},{28,20},{1,9},{5... | collective-permute-start | bytes 1179656 | tf_op jit(solution)/shard_map/ppermute | solution.py:583
  101.3 16.9 %collective-permute-start.11 = (f32[3,256,128]{2,1,0:T(8,128)S(1)}, f32[3,256,128]{2,1,0:T(8,128)S(1)}, u32[]{:S(2)}, u32[]{:S(2)}) collective-permute-start(f32[3,256,128]{2,1,0:T(8,128)S(1)} %get-tuple-element.66), channel_id=1, source_target_pairs={{0,12},{4,8},{8,4},{12,0},{16,28},{20,24},{24,20},{28,16},{1,13},{... | collective-permute-start | bytes 1179656 | tf_op jit(solution)/shard_map/ppermute | solution.py:583
  103.4 1.5 %collective-permute-start.7 = (f32[128,512]{1,0:T(8,128)S(1)}, f32[128,512]{1,0:T(8,128)S(1)}, u32[]{:S(2)}, u32[]{:S(2)}) collective-permute-start(f32[128,512]{1,0:T(8,128)S(1)} %kelvins.1.refs_0_), channel_id=1, source_target_pairs={{0,1},{1,0},{2,3},{3,2},{4,5},{5,4},{6,7},{7,6},{8,9},{9,8},{10,11... | collective-permute-start | bytes 786440 | tf_op jit(solution)/shard_map/ppermute | solution.py:583
  103.4 1.9 %collective-permute-start.8 = (f32[128,512]{1,0:T(8,128)S(1)}, f32[128,512]{1,0:T(8,128)S(1)}, u32[]{:S(2)}, u32[]{:S(2)}) collective-permute-start(f32[128,512]{1,0:T(8,128)S(1)} %collective-permute-done.6.refs_1_), channel_id=1, source_target_pairs={{0,1},{1,0},{2,3},{3,2},{4,5},{5,4},{6,7},{7,6},{8,9},{9,8},{10,11... | collective-permute-start | bytes 786440 | tf_op jit(solution)/shard_map/ppermute | solution.py:583

commit v12 on v11

--- a/solution.py
+++ b/solution.py
@@ -262,7 +262,7 @@
 
     row = lax.broadcasted_iota(jnp.int32, (8, 128), 0)
 
-    def one_slot(i, carry):
+    def of_slot(i):
         s = step * block + i
         label = labels[s]
         polar, turn_of = label % 4, (label // 4) % 8
@@ -271,9 +271,8 @@
         right, up = (turn_of < 2) | (turn_of > 5), turn_of < 4
         wide = (turn_of % 4 == 0) | (turn_of % 4 == 3)
         start, stride = jnp.where(forward, 0, depth - 1), jnp.where(forward, 1, -1)
-        side = jnp.where(forward, 0, 1)
         at_wall = jnp.where(forward, slab == 0, slab == slabs - 1)
-        c_self, ratio, warm = table[K_SELF, kind], table[K_RATIO, kind], table[K_HEAT, kind]
+        c_self = table[K_SELF, kind]
         c_y = table[jnp.where(wide, K_LARGE, K_SMALL), kind]
         c_z = table[jnp.where(wide, K_SMALL, K_LARGE), kind]
         wall = jnp.where(at_wall, 1.0, 0.0) * table[K_WALL, kind]
@@ -281,34 +280,47 @@
         at_edge = row == jnp.where(right, 0, 7)
         apply = lambda low, high: stencil(low, high, c_self, c_y, c_z, shift_y, shift_z, at_edge)
         xs = [start + stride * j for j in range(depth)]
-        layers = [(energy[i, x, :8, :], energy[i, x, 8:, :]) for x in xs]
-        last = []
+        return s, forward, kind, wall, apply, xs
+
+    def one_pair(pair, carry):
+        pair = [2 * pair, 2 * pair + 1]
+        slots_of = [of_slot(i) for i in pair]
+        layers = [[(energy[i, x, :8, :], energy[i, x, 8:, :]) for x in of[-1]] for i, of in zip(pair, slots_of)]
+        lasts = [[], []]
         for turn in range(ITERS):
-            total_low = total_high = wall
-            for j, x in enumerate(xs):
-                low, high = apply(*layers[j])
-                if turn == 0:
-                    low, high = low + sources[kind, x, :8, :], high + sources[kind, x, 8:, :]
-                else:
-                    low, high = low + warm * heat[x, :8, :], high + warm * heat[x, 8:, :]
-                total_low = ratio * total_low + low
-                total_high = ratio * total_high + high
-                layers[j] = (total_low, total_high)
-                density[turn, side, j, :8, :] += total_low
-                density[turn, side, j, 8:, :] += total_high
-                if turn == ITERS - 1:
-                    swept[i, x, :8, :] = total_low
-                    swept[i, x, 8:, :] = total_high
-            last.append((total_low, total_high))
-        turned = apply(*last[0])
-        at_low, at_high = rows_of(s)
-        values = (last[0], turned, apply(*turned), last[1], apply(*last[1]), last[2])
-        for plane, (low, high) in zip(planes, values):
-            plane[at_low, :] = low
-            plane[at_high, :] = high
+            for which, (s, forward, kind, wall, apply, xs) in enumerate(slots_of):
+                ratio = table[K_RATIO, kind]
+                warm = table[K_HEAT, kind] if turn else None
+                total_low = total_high = wall
+                for j, x in enumerate(xs):
+                    low, high = apply(*layers[which][j])
+                    if turn == 0:
+                        low, high = low + sources[kind, x, :8, :], high + sources[kind, x, 8:, :]
+                    else:
+                        low, high = low + warm * heat[x, :8, :], high + warm * heat[x, 8:, :]
+                    total_low = ratio * total_low + low
+                    total_high = ratio * total_high + high
+                    layers[which][j] = (total_low, total_high)
+                lasts[which].append((total_low, total_high))
+            for x in range(depth):
+                for half, here in enumerate((slice(0, 8), slice(8, 16))):
+                    values = [
+                        jnp.where(of[1], layer[x][half], layer[depth - 1 - x][half]) for of, layer in zip(slots_of, layers)
+                    ]
+                    density[turn, x, here, :] += values[0] + values[1]
+                    if turn == ITERS - 1:
+                        for i, value in zip(pair, values):
+                            swept[i, x, here, :] = value
+        for (s, _, _, _, apply, _), last in zip(slots_of, lasts):
+            turned = apply(*last[0])
+            at_low, at_high = rows_of(s)
+            values = (last[0], turned, apply(*turned), last[1], apply(*last[1]), last[2])
+            for plane, (low, high) in zip(planes, values):
+                plane[at_low, :] = low
+                plane[at_high, :] = high
         return carry
 
-    lax.fori_loop(0, block, one_slot, 0, unroll=2)
+    lax.fori_loop(0, block // 2, one_pair, 0)
 
     @pl.when(step == blocks - 1)
     def _():
@@ -318,7 +330,7 @@
                 faces[by][index] = plane[at, :]
         for turn in range(ITERS):
             for x in range(depth):
-                flat[turn, x * 16 : x * 16 + 16, :] = density[turn, 0, x] + density[turn, 1, depth - 1 - x]
+                flat[turn, x * 16 : x * 16 + 16, :] = density[turn, x]
         label = label_row[...]
         polar = label % 4
         kinds = 2 * (label // DIRS) + jnp.where((polar == 0) | (polar == 3), 0, 1)
@@ -605,7 +617,7 @@
         out_shape=[slot_shape, shape(depth, lanes)] + [shape(*face)] * group + [shape(*half)] * 2,
         scratch_shapes=[scratch(slots * width_y, width_z)] * 6
         + [
-            scratch(ITERS, 2, depth, width_y, width_z),
+            scratch(ITERS, depth, width_y, width_z),
             scratch(ITERS, cells, width_z),
             scratch(KINDS, depth, width_y, width_z),
             scratch(depth, width_y, width_z),
@@ -685,8 +697,10 @@
         summed,
         quarter,
     )
+    copies, entering = lax.optimization_barrier((copies, entering))
     gathered = lax.all_to_all(copies, "slab", 0, 0)
     entering = [entering[0]] + [swap(entering[index], "slab", index) for index in range(1, group)]
+    gathered, entering[1:3] = lax.optimization_barrier((gathered, entering[1:3]))
 
     pack_shape = shape(6 * KINDS + 4 * depth, lanes)
     (packed,) = call(

time: 124 us -> 128 us (1.032)
  waiting for transfers between devices: 38.8 us -> 51.5 us
  blocking collectives: 11.8 us -> 0 us
  starting transfers between devices: 21.2 us -> 25 us
    ppermute x12, waiting for transfers between devices: 38.8 us -> 51.5 us  [swap(): lax.ppermute(array, axis, [(i, i ^ by) for i in range(lax.axis_size(axis))])]
    all_to_all x1 -> x0, blocking collectives: 11.8 us -> none  [local(): gathered = lax.all_to_all(copies, 'slab', 0, 0)]
    all_to_all x0 -> x1, starting transfers between devices: none -> 3.68 us  [local(): gathered = lax.all_to_all(copies, 'slab', 0, 0)]
    unnamed x40 -> x44, local copies, waits for them, and re-layouts: 7.54 us -> 7.43 us
  transfers between devices with their start and end apart: 13 -> 14, of which waited for: 7 -> 8; matrix products, arithmetic and copies ran while one was open for 3% -> 2% of each run, Pallas kernels for 11% -> 9%
where the time goes in v12:
time: 128 us; the launch traced here: 127 us
  waiting for transfers between devices  51.5 us (40%)
  Pallas kernels  38.4 us (30%)
  starting transfers between devices  25 us (20%)
  local copies, waits for them, and re-layouts  7.81 us (6%)
  other arithmetic  3.36 us (3%)
    ppermute x12, waiting for transfers between devices, swap(): lax.ppermute(array, axis, [(i, i ^ by) for i in range(lax.axis_size(axis))])  51.5 us
    pallas_call x1, Pallas kernels, local(): pl.pallas_call(functools.partial(sweeps_kernel, (block, blocks, depth, wi...  16.8 us
    ppermute x12, starting transfers between devices, swap(): lax.ppermute(array, axis, [(i, i ^ by) for i in range(lax.axis_size(axis))])  15.2 us
    pallas_call x1, Pallas kernels, local(): pl.pallas_call(functools.partial(warm_kernel, (block, depth, width_y, wid...  8.74 us
    pallas_call x7, Pallas kernels, call(): pl.pallas_call(kernel, in_specs=in_specs, out_specs=[VMEM] * len(out_shap...  7.64 us
    unnamed x44, local copies, waits for them, and re-layouts  7.43 us
    all_to_all x1, starting transfers between devices, local(): summed = lax.all_to_all(parts, 'slab', 0, 0)  6.12 us
    pallas_call x1, Pallas kernels, local(): pl.pallas_call(functools.partial(inflow_kernel, (block, depth, own, group...  5.22 us
  transfers between devices with their start and end apart: 14, of which 8 were waited for; matrix products, arithmetic and copies ran while one was open for 2% of the time, Pallas kernels for 9%

profile of v12, /device:TPU:0, one launch (start us, length us, event | category | flops | bytes accessed | tf_op | source)
XLA Modules:
  0.0 127.0 jit_solution(10340148345583618116)
XLA Ops:
  0.6 0.0 copy-start.16
  0.6 0.0 copy-start.17
  0.7 0.0 copy-start.18
  0.7 0.0 copy-start.20
  0.7 0.0 copy-start.21
  0.7 0.0 copy-start.19
  0.7 0.6 pad_add_fusion.meta
  1.4 16.8 %sweeps.1 = (f32[64,8,16,128]{3,2,1,0:T(8,128)}, f32[8,512]{1,0:T(8,128)}, f32[3,256,128]{2,1,0:T(8,128)}, f32[3,256,128]{2,1,0:T(8,128)}, f32[3,256,128]{2,1,0:...) custom-call(s32[2]{0:T(128)} %pad_add_fusion.meta, s32[64]{0:T(128)} %labels.1, ...), custom_call_target="tpu_custom_call" | custom-call | tf_op jit(solution)/shard_map/sweeps/pallas_call | solution.py:612
  18.1 3.0 %collective-permute-start.2 = (f32[3,256,128]{2,1,0:T(8,128)}, f32[3,256,128]{2,1,0:T(8,128)S(1)}, u32[]{:S(2)}, u32[]{:S(2)}) collective-permute-start(f32[3,256,128]{2,1,0:T(8,128)} %get-tuple-element.47), channel_id=1, source_target_pairs={{0,4},{4,0},{8,12},{12,8},{16,20},{20,16},{24,28},{28,24},{1,5},{5... | collective-permute-start | bytes 1179656 | tf_op jit(solution)/shard_map/ppermute | solution.py:595
  21.2 1.6 %collective-permute-start.3 = (f32[3,256,128]{2,1,0:T(8,128)}, f32[3,256,128]{2,1,0:T(8,128)S(1)}, u32[]{:S(2)}, u32[]{:S(2)}) collective-permute-start(f32[3,256,128]{2,1,0:T(8,128)} %get-tuple-element.48), channel_id=1, source_target_pairs={{0,8},{4,12},{8,0},{12,4},{16,24},{20,28},{24,16},{28,20},{1,9},{5... | collective-permute-start | bytes 1179656 | tf_op jit(solution)/shard_map/ppermute | solution.py:595
  22.8 0.0 collective-permute-start.4
  22.8 0.0 collective-permute-start
  22.9 0.1 select_reduce_fusion
  23.0 0.6 fusion.20
  23.6 0.1 fusion.7
  23.8 1.4 %collective-permute-done.other = f32[2,3,64,512]{3,2,1,0:T(8,128)S(1)} collective-permute-done((f32[2,3,64,512]{3,2,1,0:T(8,128)}, f32[2,3,64,512]{3,2,1,0:T(8,128)S(1)}, u32[]{:S(2)}, u32[]{:S(2)}) %collective-permute-start) | collective-permute-done | bytes 786464 | tf_op jit(solution)/shard_map/ppermute | solution.py:595
  25.3 1.1 copy-done
  26.4 0.8 density_split.1
  27.2 1.9 %collective-permute-start.1 = (f32[1,3,64,512]{3,2,1,0:T(8,128)}, f32[1,3,64,512]{3,2,1,0:T(8,128)S(1)}, u32[]{:S(2)}, u32[]{:S(2)}) collective-permute-start(f32[1,3,64,512]{3,2,1,0:T(8,128)} %get-tuple-element.45), channel_id=1, source_target_pairs={{0,2},{1,3},{2,0},{3,1},{4,6},{5,7},{6,4},{7,5},{8,10},{9,11},{10,... | collective-permute-start | bytes 1179656 | tf_op jit(solution)/shard_map/ppermute | solution.py:595
  29.1 0.1 copy.14
  29.2 0.1 copy.15.kinds
  29.3 0.0 copy-done.6
  29.3 0.8 heat_matrices.1
  30.1 0.6 copy-done.4
  30.8 1.8 %pad_maximum_fusion.1.sums = f32[2]{0:T(128)} fusion(f32[1]{0:T(128)} %bitcast.36, f32[1]{0:T(128)} %bitcast.35), kind=kLoop, calls=%fused_computation.35 | loop fusion | flops 2 | bytes 16 | tf_op jit(solution)/shard_map/stack | solution.py:583
  32.6 0.0 collective-permute-done.2.refs_1_
  32.6 0.8 collective-permute-done.3.refs_2_
  33.4 6.8 %collective-permute-done.4.refs_3_ = f32[3,256,128]{2,1,0:T(8,128)S(1)} collective-permute-done((f32[3,256,128]{2,1,0:T(8,128)}, f32[3,256,128]{2,1,0:T(8,128)S(1)}, u32[]{:S(2)}, u32[]{:S(2)}) %collective-permute-start.4) | collective-permute-done | bytes 393248 | tf_op jit(solution)/shard_map/ppermute | solution.py:595
  40.2 0.0 copy-done.7
  40.2 1.0 copy-done.1
  41.2 1.2 compose.1
  42.4 0.8 copy-done.2
  43.1 0.0 collective-permute-done.1.other
  43.2 0.8 density_parts.1
  43.9 6.1 %all-to-all-start = ((f32[8,3,8,512]{3,2,1,0:T(8,128)}), f32[8,3,8,512]{3,2,1,0:T(8,128)S(1)}, u32[]{:S(2)}, u32[]{:S(2)}) async-start(f32[8,3,8,512]{3,2,1,0:T(8,128)} %density_parts.1), calls=%async_computation | async-start | bytes 786432 | tf_op jit(solution)/shard_map/all_to_all | solution.py:676
  50.1 2.9 %collective-permute-start.5 = (f32[3,256,128]{2,1,0:T(8,128)}, f32[3,256,128]{2,1,0:T(8,128)S(1)}, u32[]{:S(2)}, u32[]{:S(2)}) collective-permute-start(f32[3,256,128]{2,1,0:T(8,128)} %copy-done.2), channel_id=1, source_target_pairs={{0,16},{4,20},{8,24},{12,28},{16,0},{20,4},{24,8},{28,12},{1,17},{... | collective-permute-start | bytes 1179656 | tf_op jit(solution)/shard_map/ppermute | solution.py:595
  53.0 24.4 %collective-permute-done.5.refs_1_ = f32[3,256,128]{2,1,0:T(8,128)S(1)} collective-permute-done((f32[3,256,128]{2,1,0:T(8,128)}, f32[3,256,128]{2,1,0:T(8,128)S(1)}, u32[]{:S(2)}, u32[]{:S(2)}) %collective-permute-start.5) | collective-permute-done | bytes 393248 | tf_op jit(solution)/shard_map/ppermute | solution.py:595
  77.4 0.0 all-to-all-done.parts
  77.4 0.7 copy-done.9
  78.1 0.7 copy-done.10
  78.8 1.3 %density_totals.1 = (f32[8,2,8,512]{3,2,1,0:T(8,128)}, f32[8,512]{1,0:T(8,128)S(1)}) custom-call(f32[2]{0:T(128)S(1)} %copy-done.10, f32[8,3,8,512]{3,2,1,0:T(8,128)S(1)} %all-to-all-done.parts, f32[8,512]{1,0:T(8,128)S(1)} %copy-done.9), custom_call_target="tpu_custom_call" | custom-call | tf_op jit(solution)/shard_map/density_totals/pallas_call | solution.py:598
  80.1 1.0 copy-done.3
  81.1 1.4 %enter.1 = (f32[3,256,128]{2,1,0:T(8,128)S(1)}, f32[3,256,128]{2,1,0:T(8,128)S(1)}, f32[3,256,128]{2,1,0:T(8,128)S(1)}, f32[3,256,128]{2,1,0:T(8,128)S(1)}) custom-call(s32[2]{0:T(128)S(1)} %copy-done.6, f32[10,64]{1,0:T(8,128)S(1)} %stack.136.floats, s32[5,64]{1,0:T(8,128)S(1)} %stack.143.ints, f32[4,3,256,128]{3,2,1,0:T(8,128)S(1)} %get-tuple-element.64.effective, ...), custom_call_target="tpu_custom_call" | custom-call | tf_op jit(solution)/shard_map/enter/pallas_call | solution.py:598
  82.5 0.7 copy-done.12
  83.2 0.8 copy-done.13
  84.0 3.7 %all-to-all-start.1 = ((f32[8,2,8,512]{3,2,1,0:T(8,128)}), f32[8,2,8,512]{3,2,1,0:T(8,128)S(1)}, u32[]{:S(2)}, u32[]{:S(2)}) async-start(f32[8,2,8,512]{3,2,1,0:T(8,128)} %get-tuple-element.71), calls=%async_computation.1 | async-start | bytes 524288 | tf_op jit(solution)/shard_map/all_to_all | solution.py:701
  87.6 2.0 %collective-permute-start.6 = (f32[3,256,128]{2,1,0:T(8,128)}, f32[3,256,128]{2,1,0:T(8,128)S(1)}, u32[]{:S(2)}, u32[]{:S(2)}) collective-permute-start(f32[3,256,128]{2,1,0:T(8,128)} %copy-done.13), channel_id=1, source_target_pairs={{0,4},{4,0},{8,12},{12,8},{16,20},{20,16},{24,28},{28,24},{1,5},{5... | collective-permute-start | bytes 1179656 | tf_op jit(solution)/shard_map/ppermute | solution.py:595
  89.7 1.5 %collective-permute-start.7 = (f32[3,256,128]{2,1,0:T(8,128)}, f32[3,256,128]{2,1,0:T(8,128)S(1)}, u32[]{:S(2)}, u32[]{:S(2)}) collective-permute-start(f32[3,256,128]{2,1,0:T(8,128)} %copy-done.12), channel_id=1, source_target_pairs={{0,8},{4,12},{8,0},{12,4},{16,24},{20,28},{24,16},{28,20},{1,9},{5... | collective-permute-start | bytes 1179656 | tf_op jit(solution)/shard_map/ppermute | solution.py:595
  91.1 9.3 %collective-permute-done.6.refs_1_ = f32[3,256,128]{2,1,0:T(8,128)S(1)} collective-permute-done((f32[3,256,128]{2,1,0:T(8,128)}, f32[3,256,128]{2,1,0:T(8,128)S(1)}, u32[]{:S(2)}, u32[]{:S(2)}) %collective-permute-start.6) | collective-permute-done | bytes 393248 | tf_op jit(solution)/shard_map/ppermute | solution.py:595
  100.5 2.2 %collective-permute-done.7.refs_2_ = f32[3,256,128]{2,1,0:T(8,128)S(1)} collective-permute-done((f32[3,256,128]{2,1,0:T(8,128)}, f32[3,256,128]{2,1,0:T(8,128)S(1)}, u32[]{:S(2)}, u32[]{:S(2)}) %collective-permute-start.7) | collective-permute-done | bytes 393248 | tf_op jit(solution)/shard_map/ppermute | solution.py:595
  102.6 0.0 all-to-all-done.1.gathered
  102.6 0.0 copy-done.5
  102.6 1.4 %kelvins.1.refs_0_ = f32[128,512]{1,0:T(8,128)S(1)} custom-call(s32[2]{0:T(128)S(1)} %copy-done.6, f32[2]{0:T(128)S(1)} %copy-done.11, f32[8,2,8,512]{3,2,1,0:T(8,128)S(1)} %all-to-all-done.1.gathered, f32[8,512]{1,0:T(8,128)S(1)} %get-tuple-element.75.late, f32[144,128]{1,0:T(8,128)S(1)} %copy-done.5, f32[40,128]{1,0:T(8,128)S(1)} %copy-done.8), custom_call_target="tpu_custom_call" | custom-call | tf_op jit(solution)/shard_map/kelvins/pallas_call | solution.py:598
  104.0 1.6 %collective-permute-start.8 = (f32[128,512]{1,0:T(8,128)S(1)}, f32[128,512]{1,0:T(8,128)S(1)}, u32[]{:S(2)}, u32[]{:S(2)}) collective-permute-start(f32[128,512]{1,0:T(8,128)S(1)} %kelvins.1.refs_0_), channel_id=1, source_target_pairs={{0,2},{1,3},{2,0},{3,1},{4,6},{5,7},{6,4},{7,5},{8,10},{9,11},{10,... | collective-permute-start | bytes 786440 | tf_op jit(solution)/shard_map/ppermute | solution.py:595
  105.6 0.7 collective-permute-start.11
  106.3 0.0 collective-permute-start.9
  106.3 5.2 %collective-permute-done.8.refs_1_ = f32[128,512]{1,0:T(8,128)S(1)} collective-permute-done((f32[128,512]{1,0:T(8,128)S(1)}, f32[128,512]{1,0:T(8,128)S(1)}, u32[]{:S(2)}, u32[]{:S(2)}) %collective-permute-start.8) | collective-permute-done | bytes 262176 | tf_op jit(solution)/shard_map/ppermute | solution.py:595
  111.5 0.0 collective-permute-start.10
  111.5 0.1 copy.16.kinds
  111.6 0.0 collective-permute-done.9.refs_2_
  111.6 1.4 %collective-permute-done.10.refs_3_ = f32[128,512]{1,0:T(8,128)S(1)} collective-permute-done((f32[128,512]{1,0:T(8,128)S(1)}, f32[128,512]{1,0:T(8,128)S(1)}, u32[]{:S(2)}, u32[]{:S(2)}) %collective-permute-start.10) | collective-permute-done | bytes 262176 | tf_op jit(solution)/shard_map/ppermute | solution.py:595
  113.0 8.7 %warm.1 = (f32[64,8,16,128]{3,2,1,0:T(8,128)S(1)}, f32[128,128]{1,0:T(8,128)}) custom-call(s32[2]{0:T(128)S(1)} %copy-done.6, f32[10,64]{1,0:T(8,128)S(1)} %stack.136.floats, s32[5,64]{1,0:T(8,128)S(1)} %stack.143.ints, f32[6,16]{1,0:T(8,128)S(1)} %copy.16.kinds, f32[2]{0:T(128)S(1)} %copy-done.11, f32[64,8,16,128]{3,2,1,0:T(8,128)} %get-tuple-element.57.swept, ...), custom_call_target="tpu_custom_call" | custom-call | tf_op jit(solution)/shard_map/warm/pallas_call | solution.py:724
  121.8 0.0 collective-permute-done.11.refs_3_
  121.8 5.2 %inflow.1 = f32[64,8,16,128]{3,2,1,0:T(8,128)} custom-call(s32[2]{0:T(128)S(1)} %copy-done.6, f32[10,64]{1,0:T(8,128)S(1)} %stack.136.floats, s32[5,64]{1,0:T(8,128)S(1)} %stack.143.ints, f32[64,8,16,128]{3,2,1,0:T(8,128)S(1)} %get-tuple-element.78.warm, f32[3,256,128]{2,1,0:T(8,128)S(1)} %get-tuple-element.79.refs_0_, ...), custom_call_target="tpu_custom_call" | custom-call | tf_op jit(solution)/shard_map/inflow/pallas_call | solution.py:737
  (40 shorter events, 0.3 us)
Async XLA Ops:
  0.6 22.2 %copy-start.16 = (f32[8]{0:T(128)S(1)}, f32[8]{0:T(128)}, u32[]{:S(2)}) copy-start(f32[8]{0:T(128)} %refs_3_.1) | copy-start | bytes 100
  0.6 22.1 %copy-start.17 = (f32[8]{0:T(128)S(1)}, f32[8]{0:T(128)}, u32[]{:S(2)}) copy-start(f32[8]{0:T(128)} %refs_1_.1) | copy-start | bytes 100
  0.7 22.1 %copy-start.18 = (f32[8]{0:T(128)S(1)}, f32[8]{0:T(128)}, u32[]{:S(2)}) copy-start(f32[8]{0:T(128)} %refs_0_.1) | copy-start | bytes 100
  0.7 22.2 %copy-start.20 = (f32[8]{0:T(128)S(1)}, f32[8]{0:T(128)}, u32[]{:S(2)}) copy-start(f32[8]{0:T(128)} %refs_4_.1) | copy-start | bytes 100
  0.7 22.2 %copy-start.21 = (f32[8]{0:T(128)S(1)}, f32[8]{0:T(128)}, u32[]{:S(2)}) copy-start(f32[8]{0:T(128)} %refs_2_.1) | copy-start | bytes 100
  0.7 22.1 %copy-start.19 = (s32[64]{0:T(128)S(1)}, s32[64]{0:T(128)}, u32[]{:S(2)}) copy-start(s32[64]{0:T(128)} %labels.1) | copy-start | bytes 772
  1.4 27.9 %copy-start.6 = (s32[2]{0:T(128)S(1)}, s32[2]{0:T(128)}, u32[]{:S(2)}) copy-start(s32[2]{0:T(128)} %pad_add_fusion.meta) | copy-start | bytes 28
  18.1 14.4 %collective-permute-start.2 = (f32[3,256,128]{2,1,0:T(8,128)}, f32[3,256,128]{2,1,0:T(8,128)S(1)}, u32[]{:S(2)}, u32[]{:S(2)}) collective-permute-start(f32[3,256,128]{2,1,0:T(8,128)} %get-tuple-element.47), channel_id=1, source_target_pairs={{0,4},{4,0},{8,12},{12,8},{16,20},{20,16},{24,28},{28,24},{1,5},{5... | collective-permute-start | bytes 1179656 | tf_op jit(solution)/shard_map/ppermute | solution.py:595
  21.2 12.3 %collective-permute-start.3 = (f32[3,256,128]{2,1,0:T(8,128)}, f32[3,256,128]{2,1,0:T(8,128)S(1)}, u32[]{:S(2)}, u32[]{:S(2)}) collective-permute-start(f32[3,256,128]{2,1,0:T(8,128)} %get-tuple-element.48), channel_id=1, source_target_pairs={{0,8},{4,12},{8,0},{12,4},{16,24},{20,28},{24,16},{28,20},{1,9},{5... | collective-permute-start | bytes 1179656 | tf_op jit(solution)/shard_map/ppermute | solution.py:595
  22.8 17.4 %collective-permute-start.4 = (f32[3,256,128]{2,1,0:T(8,128)}, f32[3,256,128]{2,1,0:T(8,128)S(1)}, u32[]{:S(2)}, u32[]{:S(2)}) collective-permute-start(f32[3,256,128]{2,1,0:T(8,128)} %get-tuple-element.49), channel_id=1, source_target_pairs={{0,12},{4,8},{8,4},{12,0},{16,28},{20,24},{24,20},{28,16},{1,13},{... | collective-permute-start | bytes 1179656 | tf_op jit(solution)/shard_map/ppermute | solution.py:595
  22.8 2.5 %collective-permute-start = (f32[2,3,64,512]{3,2,1,0:T(8,128)}, f32[2,3,64,512]{3,2,1,0:T(8,128)S(1)}, u32[]{:S(2)}, u32[]{:S(2)}) collective-permute-start(f32[2,3,64,512]{3,2,1,0:T(8,128)} %get-tuple-element.44), channel_id=1, source_target_pairs={{0,1},{1,0},{2,3},{3,2},{4,5},{5,4},{6,7},{7,6},{8,9},{9,8},{10,11... | collective-permute-start | bytes 2359304 | tf_op jit(solution)/shard_map/ppermute | solution.py:595
  25.3 1.1 copy-start
  27.2 15.9 %collective-permute-start.1 = (f32[1,3,64,512]{3,2,1,0:T(8,128)}, f32[1,3,64,512]{3,2,1,0:T(8,128)S(1)}, u32[]{:S(2)}, u32[]{:S(2)}) collective-permute-start(f32[1,3,64,512]{3,2,1,0:T(8,128)} %get-tuple-element.45), channel_id=1, source_target_pairs={{0,2},{1,3},{2,0},{3,1},{4,6},{5,7},{6,4},{7,5},{8,10},{9,11},{10,... | collective-permute-start | bytes 1179656 | tf_op jit(solution)/shard_map/ppermute | solution.py:595
  29.2 1.5 %copy-start.14 = (f32[6,8,2]{0,2,1:T(2,128)}, f32[6,8,2]{0,2,1:T(2,128)S(1)}, u32[]{:S(2)}) copy-start(f32[6,8,2]{0,2,1:T(2,128)S(1)} %copy.14) | copy-start | bytes 1156
  30.1 0.6 copy-start.4
  30.7 9.5 %copy-start.7 = (f32[40,128]{1,0:T(8,128)}, f32[40,128]{1,0:T(8,128)S(1)}, u32[]{:S(2)}) copy-start(f32[40,128]{1,0:T(8,128)S(1)} %get-tuple-element.77.matrix_two) | copy-start | bytes 61444
  40.2 1.0 copy-start.1
  42.4 0.8 copy-start.2
  43.1 59.5 %copy-start.5 = (f32[144,128]{1,0:T(8,128)S(1)}, f32[144,128]{1,0:T(8,128)}, u32[]{:S(2)}) copy-start(f32[144,128]{1,0:T(8,128)} %copy-done.4) | copy-start | bytes 221188
  43.1 59.5 %copy-start.8 = (f32[40,128]{1,0:T(8,128)S(1)}, f32[40,128]{1,0:T(8,128)}, u32[]{:S(2)}) copy-start(f32[40,128]{1,0:T(8,128)} %copy-done.7) | copy-start | bytes 61444
  43.1 59.5 %copy-start.11 = (f32[2]{0:T(128)S(1)}, f32[2]{0:T(128)}, u32[]{:S(2)}) copy-start(f32[2]{0:T(128)} %pad_maximum_fusion.1.sums) | copy-start | bytes 28
  43.9 67.6 %copy-start.15 = (f32[6,8,2]{0,2,1:T(2,128)S(1)}, f32[6,8,2]{0,2,1:T(2,128)}, u32[]{:S(2)}) copy-start(f32[6,8,2]{0,2,1:T(2,128)} %copy-done.14) | copy-start | bytes 1156
  43.9 33.5 %all-to-all-start = ((f32[8,3,8,512]{3,2,1,0:T(8,128)}), f32[8,3,8,512]{3,2,1,0:T(8,128)S(1)}, u32[]{:S(2)}, u32[]{:S(2)}) async-start(f32[8,3,8,512]{3,2,1,0:T(8,128)} %density_parts.1), calls=%async_computation | async-start | bytes 786432 | tf_op jit(solution)/shard_map/all_to_all | solution.py:676
  50.1 27.3 %collective-permute-start.5 = (f32[3,256,128]{2,1,0:T(8,128)}, f32[3,256,128]{2,1,0:T(8,128)S(1)}, u32[]{:S(2)}, u32[]{:S(2)}) collective-permute-start(f32[3,256,128]{2,1,0:T(8,128)} %copy-done.2), channel_id=1, source_target_pairs={{0,16},{4,20},{8,24},{12,28},{16,0},{20,4},{24,8},{28,12},{1,17},{... | collective-permute-start | bytes 1179656 | tf_op jit(solution)/shard_map/ppermute | solution.py:595
  77.4 0.7 copy-start.9
  78.1 0.7 copy-start.10
  80.1 1.0 copy-start.3
  82.5 0.7 copy-start.12
  83.2 0.8 copy-start.13
  84.0 18.7 %all-to-all-start.1 = ((f32[8,2,8,512]{3,2,1,0:T(8,128)}), f32[8,2,8,512]{3,2,1,0:T(8,128)S(1)}, u32[]{:S(2)}, u32[]{:S(2)}) async-start(f32[8,2,8,512]{3,2,1,0:T(8,128)} %get-tuple-element.71), calls=%async_computation.1 | async-start | bytes 524288 | tf_op jit(solution)/shard_map/all_to_all | solution.py:701
  87.6 12.8 %collective-permute-start.6 = (f32[3,256,128]{2,1,0:T(8,128)}, f32[3,256,128]{2,1,0:T(8,128)S(1)}, u32[]{:S(2)}, u32[]{:S(2)}) collective-permute-start(f32[3,256,128]{2,1,0:T(8,128)} %copy-done.13), channel_id=1, source_target_pairs={{0,4},{4,0},{8,12},{12,8},{16,20},{20,16},{24,28},{28,24},{1,5},{5... | collective-permute-start | bytes 1179656 | tf_op jit(solution)/shard_map/ppermute | solution.py:595
  89.7 13.0 %collective-permute-start.7 = (f32[3,256,128]{2,1,0:T(8,128)}, f32[3,256,128]{2,1,0:T(8,128)S(1)}, u32[]{:S(2)}, u32[]{:S(2)}) collective-permute-start(f32[3,256,128]{2,1,0:T(8,128)} %copy-done.12), channel_id=1, source_target_pairs={{0,8},{4,12},{8,0},{12,4},{16,24},{20,28},{24,16},{28,20},{1,9},{5... | collective-permute-start | bytes 1179656 | tf_op jit(solution)/shard_map/ppermute | solution.py:595
  104.0 7.5 %collective-permute-start.8 = (f32[128,512]{1,0:T(8,128)S(1)}, f32[128,512]{1,0:T(8,128)S(1)}, u32[]{:S(2)}, u32[]{:S(2)}) collective-permute-start(f32[128,512]{1,0:T(8,128)S(1)} %kelvins.1.refs_0_), channel_id=1, source_target_pairs={{0,2},{1,3},{2,0},{3,1},{4,6},{5,7},{6,4},{7,5},{8,10},{9,11},{10,... | collective-permute-start | bytes 786440 | tf_op jit(solution)/shard_map/ppermute | solution.py:595
  105.6 16.1 %collective-permute-start.11 = (f32[3,256,128]{2,1,0:T(8,128)S(1)}, f32[3,256,128]{2,1,0:T(8,128)S(1)}, u32[]{:S(2)}, u32[]{:S(2)}) collective-permute-start(f32[3,256,128]{2,1,0:T(8,128)S(1)} %get-tuple-element.82), channel_id=1, source_target_pairs={{0,12},{4,8},{8,4},{12,0},{16,28},{20,24},{24,20},{28,16},{1,13},{... | collective-permute-start | bytes 1179656 | tf_op jit(solution)/shard_map/ppermute | solution.py:595
  106.3 5.2 %collective-permute-start.9 = (f32[128,512]{1,0:T(8,128)S(1)}, f32[128,512]{1,0:T(8,128)S(1)}, u32[]{:S(2)}, u32[]{:S(2)}) collective-permute-start(f32[128,512]{1,0:T(8,128)S(1)} %kelvins.1.refs_0_), channel_id=1, source_target_pairs={{0,1},{1,0},{2,3},{3,2},{4,5},{5,4},{6,7},{7,6},{8,9},{9,8},{10,11... | collective-permute-start | bytes 786440 | tf_op jit(solution)/shard_map/ppermute | solution.py:595
  111.5 1.5 %collective-permute-start.10 = (f32[128,512]{1,0:T(8,128)S(1)}, f32[128,512]{1,0:T(8,128)S(1)}, u32[]{:S(2)}, u32[]{:S(2)}) collective-permute-start(f32[128,512]{1,0:T(8,128)S(1)} %collective-permute-done.8.refs_1_), channel_id=1, source_target_pairs={{0,1},{1,0},{2,3},{3,2},{4,5},{5,4},{6,7},{7,6},{8,9},{9,8},{10,11... | collective-permute-start | bytes 786440 | tf_op jit(solution)/shard_map/ppermute | solution.py:595

commit v13 on v12

--- a/solution.py
+++ b/solution.py
@@ -406,7 +406,7 @@
 
 
 def compose_kernel(own, group, meta, floats, ints, *refs):
-    received, (composite, effective, ordered) = refs[:group], refs[group:]
+    received, (first, others, effective, ordered) = refs[:group], refs[group:]
     place = meta[SLAB] % group
     for by in range(group):
         ordered[place ^ by] = received[by][...]
@@ -422,8 +422,9 @@
             three = full * three + full_n * two + full_t * one + ordered[k, 2, at, :]
             two = full * two + full_n * one + ordered[k, 1, at, :]
             one = full * one + ordered[k, 0, at, :]
-        for index, value in enumerate((one, two, three)):
-            composite[index, at, :] = value
+        first[at, :] = one
+        others[0, at, :] = two
+        others[1, at, :] = three
         return carry
 
     lax.fori_loop(0, own, one_slot, 0, unroll=4)
@@ -431,12 +432,13 @@
 
 
 def enter_kernel(own, group, groups, depth, meta, floats, ints, effective, *refs):
-    composites, rest = refs[:groups], refs[groups:]
+    firsts, others, rest = refs[:groups], refs[groups : 2 * groups], refs[2 * groups :]
     outs, (ordered, entered) = rest[:group], rest[group:]
     slab = meta[SLAB]
     place, mine = slab % group, slab // group
     for by in range(groups):
-        ordered[mine ^ by] = composites[by][...]
+        ordered[mine ^ by, 0] = firsts[by][...]
+        ordered[mine ^ by, 1:] = others[by][...]
     span = depth * group
 
     def one_slot(i, carry):
@@ -657,37 +659,27 @@
         meta,
         kinds,
     )
-    composite, effective = call(
+    first, others, effective = call(
         functools.partial(compose_kernel, own, group),
         "compose",
         [SMEM] * 3 + [VMEM] * group,
-        [shape(*face), shape(group, *face)],
+        [shape(*face[1:]), shape(2, *face[1:]), shape(group, *face)],
         meta,
         floats,
         ints,
         *received,
         scratches=[scratch(group, *face)],
     )
-    other, composite, floats, ints, kinds, sums, first_matrix, second_matrix = lax.optimization_barrier(
-        (other, composite, floats, ints, kinds, sums, first_matrix, second_matrix)
-    )
-    composites = [composite] + [swap(composite, "slab", index * group) for index in range(1, groups)]
+    other, first, others, floats, ints, kinds, sums, first_matrix, second_matrix = lax.optimization_barrier(
+        (other, first, others, floats, ints, kinds, sums, first_matrix, second_matrix)
+    )
+    firsts, others = (
+        [value] + [swap(value, "slab", index * group) for index in range(1, groups)] for value in (first, others)
+    )
     (parts,) = call(functools.partial(parts_kernel, depth), "density_parts", [VMEM] * 2, [shape(*piece)], keep, other)
     summed = lax.all_to_all(parts, "slab", 0, 0)
-    summed, composites = lax.optimization_barrier((summed, composites))
-
-    entering = call(
-        functools.partial(enter_kernel, own, group, groups, depth),
-        "enter",
-        [SMEM] * 3 + [VMEM] * (1 + groups),
-        [shape(*face)] * group,
-        meta,
-        floats,
-        ints,
-        effective,
-        *composites,
-        scratches=[scratch(groups, *face), scratch(group, *face)],
-    )
+    summed, firsts = lax.optimization_barrier((summed, firsts))
+
     copies, late = call(
         totals_kernel,
         "density_totals",
@@ -697,10 +689,21 @@
         summed,
         quarter,
     )
-    copies, entering = lax.optimization_barrier((copies, entering))
     gathered = lax.all_to_all(copies, "slab", 0, 0)
+    entering = call(
+        functools.partial(enter_kernel, own, group, groups, depth),
+        "enter",
+        [SMEM] * 3 + [VMEM] * (1 + 2 * groups),
+        [shape(*face)] * group,
+        meta,
+        floats,
+        ints,
+        effective,
+        *firsts,
+        *others,
+        scratches=[scratch(groups, *face), scratch(group, *face)],
+    )
     entering = [entering[0]] + [swap(entering[index], "slab", index) for index in range(1, group)]
-    gathered, entering[1:3] = lax.optimization_barrier((gathered, entering[1:3]))
 
     pack_shape = shape(6 * KINDS + 4 * depth, lanes)
     (packed,) = call(

time: 128 us -> 122 us (0.953)
  waiting for transfers between devices: 51.5 us -> 39.7 us
  starting transfers between devices: 25 us -> 27.7 us
  local copies, waits for them, and re-layouts: 7.81 us -> 10 us
    ppermute x12 -> x13, waiting for transfers between devices: 51.5 us -> 27.2 us  [swap(): lax.ppermute(array, axis, [(i, i ^ by) for i in range(lax.axis_size(axis))])]
    all_to_all x1, waiting for transfers between devices: 0.01 us -> 12.5 us  [local(): gathered = lax.all_to_all(copies, 'slab', 0, 0)]
    ppermute x12 -> x13, starting transfers between devices: 15.2 us -> 17.9 us  [swap(): lax.ppermute(array, axis, [(i, i ^ by) for i in range(lax.axis_size(axis))])]
    unnamed x44 -> x46, local copies, waits for them, and re-layouts: 7.43 us -> 9.67 us
  transfers between devices with their start and end apart: 14 -> 15, of which waited for: 8 -> 8; matrix products, arithmetic and copies ran while one was open for 2% -> 3% of each run, Pallas kernels for 9% -> 13%
where the time goes in v13:
time: 122 us; the launch traced here: 121 us
  waiting for transfers between devices  39.7 us (33%)
  Pallas kernels  39.2 us (32%)
  starting transfers between devices  27.7 us (23%)
  local copies, waits for them, and re-layouts  10 us (8%)
  other arithmetic  3.41 us (3%)
    ppermute x13, waiting for transfers between devices, swap(): lax.ppermute(array, axis, [(i, i ^ by) for i in range(lax.axis_size(axis))])  27.2 us
    ppermute x13, starting transfers between devices, swap(): lax.ppermute(array, axis, [(i, i ^ by) for i in range(lax.axis_size(axis))])  17.9 us
    pallas_call x1, Pallas kernels, local(): pl.pallas_call(functools.partial(sweeps_kernel, (block, blocks, depth, wi...  16.8 us
    all_to_all x1, waiting for transfers between devices, local(): gathered = lax.all_to_all(copies, 'slab', 0, 0)  12.5 us
    unnamed x46, local copies, waits for them, and re-layouts  9.67 us
    pallas_call x1, Pallas kernels, local(): pl.pallas_call(functools.partial(warm_kernel, (block, depth, width_y, wid...  8.74 us
    pallas_call x7, Pallas kernels, call(): pl.pallas_call(kernel, in_specs=in_specs, out_specs=[VMEM] * len(out_shap...  8.51 us
    all_to_all x1, starting transfers between devices, local(): summed = lax.all_to_all(parts, 'slab', 0, 0)  6.12 us
  transfers between devices with their start and end apart: 15, of which 8 were waited for; matrix products, arithmetic and copies ran while one was open for 3% of the time, Pallas kernels for 13%

profile of v13, /device:TPU:0, one launch (start us, length us, event | category | flops | bytes accessed | tf_op | source)
XLA Modules:
  0.0 120.9 jit_solution(10431744072848299829)
XLA Ops:
  0.6 0.0 copy-start.19
  0.6 0.0 copy-start.18
  0.7 0.0 copy-start.22
  0.7 0.0 copy-start.17
  0.7 0.0 copy-start.21
  0.7 0.0 copy-start.20
  0.7 0.6 pad_add_fusion.meta
  1.3 16.8 %sweeps.1 = (f32[64,8,16,128]{3,2,1,0:T(8,128)}, f32[8,512]{1,0:T(8,128)}, f32[3,256,128]{2,1,0:T(8,128)}, f32[3,256,128]{2,1,0:T(8,128)}, f32[3,256,128]{2,1,0:...) custom-call(s32[2]{0:T(128)} %pad_add_fusion.meta, s32[64]{0:T(128)} %labels.1, ...), custom_call_target="tpu_custom_call" | custom-call | tf_op jit(solution)/shard_map/sweeps/pallas_call | solution.py:614
  18.0 3.0 %collective-permute-start.2 = (f32[3,256,128]{2,1,0:T(8,128)}, f32[3,256,128]{2,1,0:T(8,128)S(1)}, u32[]{:S(2)}, u32[]{:S(2)}) collective-permute-start(f32[3,256,128]{2,1,0:T(8,128)} %get-tuple-element.41), channel_id=1, source_target_pairs={{0,4},{4,0},{8,12},{12,8},{16,20},{20,16},{24,28},{28,24},{1,5},{5... | collective-permute-start | bytes 1179656 | tf_op jit(solution)/shard_map/ppermute | solution.py:597
  21.1 1.6 %collective-permute-start.3 = (f32[3,256,128]{2,1,0:T(8,128)}, f32[3,256,128]{2,1,0:T(8,128)S(1)}, u32[]{:S(2)}, u32[]{:S(2)}) collective-permute-start(f32[3,256,128]{2,1,0:T(8,128)} %get-tuple-element.42), channel_id=1, source_target_pairs={{0,8},{4,12},{8,0},{12,4},{16,24},{20,28},{24,16},{28,20},{1,9},{5... | collective-permute-start | bytes 1179656 | tf_op jit(solution)/shard_map/ppermute | solution.py:597
  22.6 0.0 collective-permute-start.4
  22.6 0.0 collective-permute-start
  22.7 0.1 select_reduce_fusion
  22.8 0.7 fusion.20
  23.5 0.1 fusion.7
  23.8 1.4 %collective-permute-done.other = f32[2,3,64,512]{3,2,1,0:T(8,128)S(1)} collective-permute-done((f32[2,3,64,512]{3,2,1,0:T(8,128)}, f32[2,3,64,512]{3,2,1,0:T(8,128)S(1)}, u32[]{:S(2)}, u32[]{:S(2)}) %collective-permute-start) | collective-permute-done | bytes 786464 | tf_op jit(solution)/shard_map/ppermute | solution.py:597
  25.1 1.1 copy-done
  26.3 0.8 density_split.1
  27.1 1.9 %collective-permute-start.1 = (f32[1,3,64,512]{3,2,1,0:T(8,128)}, f32[1,3,64,512]{3,2,1,0:T(8,128)S(1)}, u32[]{:S(2)}, u32[]{:S(2)}) collective-permute-start(f32[1,3,64,512]{3,2,1,0:T(8,128)} %get-tuple-element.39), channel_id=1, source_target_pairs={{0,2},{1,3},{2,0},{3,1},{4,6},{5,7},{6,4},{7,5},{8,10},{9,11},{10,... | collective-permute-start | bytes 1179656 | tf_op jit(solution)/shard_map/ppermute | solution.py:597
  29.0 0.1 copy.14
  29.1 0.1 copy.15.kinds
  29.2 0.8 heat_matrices.1
  30.0 0.6 copy-done.6
  30.7 1.9 %pad_maximum_fusion.1.sums = f32[2]{0:T(128)} fusion(f32[1]{0:T(128)} %bitcast.36, f32[1]{0:T(128)} %bitcast.35), kind=kLoop, calls=%fused_computation.35 | loop fusion | flops 2 | bytes 16 | tf_op jit(solution)/shard_map/stack | solution.py:585
  32.6 0.0 collective-permute-done.2.refs_1_
  32.6 0.7 collective-permute-done.3.refs_2_
  33.3 6.7 %collective-permute-done.4.refs_3_ = f32[3,256,128]{2,1,0:T(8,128)S(1)} collective-permute-done((f32[3,256,128]{2,1,0:T(8,128)}, f32[3,256,128]{2,1,0:T(8,128)S(1)}, u32[]{:S(2)}, u32[]{:S(2)}) %collective-permute-start.4) | collective-permute-done | bytes 393248 | tf_op jit(solution)/shard_map/ppermute | solution.py:597
  40.1 1.0 copy-done.1
  41.1 1.2 compose.1
  42.3 0.7 copy-done.2
  43.0 0.6 copy-done.4
  43.6 0.0 collective-permute-done.1.other
  43.6 0.8 density_parts.1
  44.4 6.1 %all-to-all-start = ((f32[8,3,8,512]{3,2,1,0:T(8,128)}), f32[8,3,8,512]{3,2,1,0:T(8,128)S(1)}, u32[]{:S(2)}, u32[]{:S(2)}) async-start(f32[8,3,8,512]{3,2,1,0:T(8,128)} %density_parts.1), calls=%async_computation | async-start | bytes 786432 | tf_op jit(solution)/shard_map/all_to_all | solution.py:680
  50.5 2.9 %collective-permute-start.5 = (f32[256,128]{1,0:T(8,128)}, f32[256,128]{1,0:T(8,128)S(1)}, u32[]{:S(2)}, u32[]{:S(2)}) collective-permute-start(f32[256,128]{1,0:T(8,128)} %copy-done.4), channel_id=1, source_target_pairs={{0,16},{4,20},{8,24},{12,28},{16,0},{20,4},{24,8},{28,12},{1,17},{... | collective-permute-start | bytes 393224 | tf_op jit(solution)/shard_map/ppermute | solution.py:597
  53.4 13.2 %collective-permute-done.5.refs_1_ = f32[256,128]{1,0:T(8,128)S(1)} collective-permute-done((f32[256,128]{1,0:T(8,128)}, f32[256,128]{1,0:T(8,128)S(1)}, u32[]{:S(2)}, u32[]{:S(2)}) %collective-permute-start.5) | collective-permute-done | bytes 131104 | tf_op jit(solution)/shard_map/ppermute | solution.py:597
  66.6 0.0 all-to-all-done.parts
  66.6 0.7 copy-done.11
  67.4 0.7 copy-done.12
  68.0 1.3 %density_totals.1 = (f32[8,2,8,512]{3,2,1,0:T(8,128)}, f32[8,512]{1,0:T(8,128)S(1)}) custom-call(f32[2]{0:T(128)S(1)} %copy-done.12, f32[8,3,8,512]{3,2,1,0:T(8,128)S(1)} %all-to-all-done.parts, f32[8,512]{1,0:T(8,128)S(1)} %copy-done.11), custom_call_target="tpu_custom_call" | custom-call | tf_op jit(solution)/shard_map/density_totals/pallas_call | solution.py:600
  69.3 3.7 %all-to-all-start.1 = ((f32[8,2,8,512]{3,2,1,0:T(8,128)}), f32[8,2,8,512]{3,2,1,0:T(8,128)S(1)}, u32[]{:S(2)}, u32[]{:S(2)}) async-start(f32[8,2,8,512]{3,2,1,0:T(8,128)} %get-tuple-element.58), calls=%async_computation.1 | async-start | bytes 524288 | tf_op jit(solution)/shard_map/all_to_all | solution.py:692
  73.0 2.9 %collective-permute-start.9 = (f32[2,256,128]{2,1,0:T(8,128)}, f32[2,256,128]{2,1,0:T(8,128)S(1)}, u32[]{:S(2)}, u32[]{:S(2)}) collective-permute-start(f32[2,256,128]{2,1,0:T(8,128)} %copy-done.2), channel_id=1, source_target_pairs={{0,16},{4,20},{8,24},{12,28},{16,0},{20,4},{24,8},{28,12},{1,17},{... | collective-permute-start | bytes 786440 | tf_op jit(solution)/shard_map/ppermute | solution.py:597
  75.9 12.5 %all-to-all-done.1.gathered = f32[8,2,8,512]{3,2,1,0:T(8,128)S(1)} async-done(((f32[8,2,8,512]{3,2,1,0:T(8,128)}), f32[8,2,8,512]{3,2,1,0:T(8,128)S(1)}, u32[]{:S(2)}, u32[]{:S(2)}) %all-to-all-start.1) | async-done | bytes 262176 | tf_op jit(solution)/shard_map/all_to_all | solution.py:692
  88.4 0.9 copy-done.7
  89.3 0.7 copy-done.10
  90.0 0.7 copy-done.13
  90.7 1.4 %kelvins.1.refs_0_ = f32[128,512]{1,0:T(8,128)S(1)} custom-call(s32[2]{0:T(128)S(1)} %copy-done.8, f32[2]{0:T(128)S(1)} %copy-done.13, f32[8,2,8,512]{3,2,1,0:T(8,128)S(1)} %all-to-all-done.1.gathered, f32[8,512]{1,0:T(8,128)S(1)} %get-tuple-element.59.late, f32[144,128]{1,0:T(8,128)S(1)} %copy-done.7, f32[40,128]{1,0:T(8,128)S(1)} %copy-done.10), custom_call_target="tpu_custom_call" | custom-call | tf_op jit(solution)/shard_map/kelvins/pallas_call | solution.py:600
  92.0 1.6 %collective-permute-start.6 = (f32[128,512]{1,0:T(8,128)S(1)}, f32[128,512]{1,0:T(8,128)S(1)}, u32[]{:S(2)}, u32[]{:S(2)}) collective-permute-start(f32[128,512]{1,0:T(8,128)S(1)} %kelvins.1.refs_0_), channel_id=1, source_target_pairs={{0,2},{1,3},{2,0},{3,1},{4,6},{5,7},{6,4},{7,5},{8,10},{9,11},{10,... | collective-permute-start | bytes 786440 | tf_op jit(solution)/shard_map/ppermute | solution.py:597
  93.6 0.0 collective-permute-done.9.refs_3_
  93.6 0.9 copy-done.3
  94.6 0.9 copy-done.5
  95.5 2.2 %enter.1 = (f32[3,256,128]{2,1,0:T(8,128)S(1)}, f32[3,256,128]{2,1,0:T(8,128)}, f32[3,256,128]{2,1,0:T(8,128)}, f32[3,256,128]{2,1,0:T(8,128)S(1)}) custom-call(s32[2]{0:T(128)S(1)} %copy-done.8, f32[10,64]{1,0:T(8,128)S(1)} %stack.136.floats, s32[5,64]{1,0:T(8,128)S(1)} %stack.143.ints, f32[4,3,256,128]{3,2,1,0:T(8,128)S(1)} %get-tuple-element.63.effective, ...), custom_call_target="tpu_custom_call" | custom-call | tf_op jit(solution)/shard_map/enter/pallas_call | solution.py:600
  97.7 1.4 %collective-permute-start.10 = (f32[3,256,128]{2,1,0:T(8,128)}, f32[3,256,128]{2,1,0:T(8,128)S(1)}, u32[]{:S(2)}, u32[]{:S(2)}) collective-permute-start(f32[3,256,128]{2,1,0:T(8,128)} %get-tuple-element.68), channel_id=1, source_target_pairs={{0,4},{4,0},{8,12},{12,8},{16,20},{20,16},{24,28},{28,24},{1,5},{5... | collective-permute-start | bytes 1179656 | tf_op jit(solution)/shard_map/ppermute | solution.py:597
  99.1 0.0 collective-permute-start.11
  99.1 2.1 %collective-permute-start.12 = (f32[3,256,128]{2,1,0:T(8,128)S(1)}, f32[3,256,128]{2,1,0:T(8,128)S(1)}, u32[]{:S(2)}, u32[]{:S(2)}) collective-permute-start(f32[3,256,128]{2,1,0:T(8,128)S(1)} %get-tuple-element.70), channel_id=1, source_target_pairs={{0,12},{4,8},{8,4},{12,0},{16,28},{20,24},{24,20},{28,16},{1,13},{... | collective-permute-start | bytes 1179656 | tf_op jit(solution)/shard_map/ppermute | solution.py:597
  101.2 0.0 collective-permute-start.7
  101.2 0.0 collective-permute-done.6.refs_1_
  101.2 0.5 collective-permute-start.8
  101.7 0.1 copy.16.kinds
  101.8 0.9 collective-permute-done.7.refs_2_
  102.7 0.4 collective-permute-done.8.refs_3_
  103.1 8.7 %warm.1 = (f32[64,8,16,128]{3,2,1,0:T(8,128)S(1)}, f32[128,128]{1,0:T(8,128)}) custom-call(s32[2]{0:T(128)S(1)} %copy-done.8, f32[10,64]{1,0:T(8,128)S(1)} %stack.136.floats, s32[5,64]{1,0:T(8,128)S(1)} %stack.143.ints, f32[6,16]{1,0:T(8,128)S(1)} %copy.16.kinds, f32[2]{0:T(128)S(1)} %copy-done.14, f32[64,8,16,128]{3,2,1,0:T(8,128)} %get-tuple-element.52.swept, ...), custom_call_target="tpu_custom_call" | custom-call | tf_op jit(solution)/shard_map/warm/pallas_call | solution.py:727
  111.9 3.9 %collective-permute-done.12.refs_3_ = f32[3,256,128]{2,1,0:T(8,128)S(1)} collective-permute-done((f32[3,256,128]{2,1,0:T(8,128)S(1)}, f32[3,256,128]{2,1,0:T(8,128)S(1)}, u32[]{:S(2)}, u32[]{:S(2)}) %collective-permute-start.12) | collective-permute-done | bytes 393248 | tf_op jit(solution)/shard_map/ppermute | solution.py:597
  115.7 5.2 %inflow.1 = f32[64,8,16,128]{3,2,1,0:T(8,128)} custom-call(s32[2]{0:T(128)S(1)} %copy-done.8, f32[10,64]{1,0:T(8,128)S(1)} %stack.136.floats, s32[5,64]{1,0:T(8,128)S(1)} %stack.143.ints, f32[64,8,16,128]{3,2,1,0:T(8,128)S(1)} %get-tuple-element.62.warm, f32[3,256,128]{2,1,0:T(8,128)S(1)} %get-tuple-element.67.refs_0_, ...), custom_call_target="tpu_custom_call" | custom-call | tf_op jit(solution)/shard_map/inflow/pallas_call | solution.py:740
  (44 shorter events, 0.4 us)
Async XLA Ops:
  0.6 22.0 %copy-start.19 = (f32[8]{0:T(128)S(1)}, f32[8]{0:T(128)}, u32[]{:S(2)}) copy-start(f32[8]{0:T(128)} %refs_0_.1) | copy-start | bytes 100
  0.6 22.0 %copy-start.18 = (f32[8]{0:T(128)S(1)}, f32[8]{0:T(128)}, u32[]{:S(2)}) copy-start(f32[8]{0:T(128)} %refs_1_.1) | copy-start | bytes 100
  0.7 22.1 %copy-start.22 = (f32[8]{0:T(128)S(1)}, f32[8]{0:T(128)}, u32[]{:S(2)}) copy-start(f32[8]{0:T(128)} %refs_2_.1) | copy-start | bytes 100
  0.7 22.1 %copy-start.17 = (f32[8]{0:T(128)S(1)}, f32[8]{0:T(128)}, u32[]{:S(2)}) copy-start(f32[8]{0:T(128)} %refs_3_.1) | copy-start | bytes 100
  0.7 22.1 %copy-start.21 = (f32[8]{0:T(128)S(1)}, f32[8]{0:T(128)}, u32[]{:S(2)}) copy-start(f32[8]{0:T(128)} %refs_4_.1) | copy-start | bytes 100
  0.7 22.0 %copy-start.20 = (s32[64]{0:T(128)S(1)}, s32[64]{0:T(128)}, u32[]{:S(2)}) copy-start(s32[64]{0:T(128)} %labels.1) | copy-start | bytes 772
  1.3 27.9 %copy-start.8 = (s32[2]{0:T(128)S(1)}, s32[2]{0:T(128)}, u32[]{:S(2)}) copy-start(s32[2]{0:T(128)} %pad_add_fusion.meta) | copy-start | bytes 28
  18.0 14.6 %collective-permute-start.2 = (f32[3,256,128]{2,1,0:T(8,128)}, f32[3,256,128]{2,1,0:T(8,128)S(1)}, u32[]{:S(2)}, u32[]{:S(2)}) collective-permute-start(f32[3,256,128]{2,1,0:T(8,128)} %get-tuple-element.41), channel_id=1, source_target_pairs={{0,4},{4,0},{8,12},{12,8},{16,20},{20,16},{24,28},{28,24},{1,5},{5... | collective-permute-start | bytes 1179656 | tf_op jit(solution)/shard_map/ppermute | solution.py:597
  21.1 12.3 %collective-permute-start.3 = (f32[3,256,128]{2,1,0:T(8,128)}, f32[3,256,128]{2,1,0:T(8,128)S(1)}, u32[]{:S(2)}, u32[]{:S(2)}) collective-permute-start(f32[3,256,128]{2,1,0:T(8,128)} %get-tuple-element.42), channel_id=1, source_target_pairs={{0,8},{4,12},{8,0},{12,4},{16,24},{20,28},{24,16},{28,20},{1,9},{5... | collective-permute-start | bytes 1179656 | tf_op jit(solution)/shard_map/ppermute | solution.py:597
  22.6 17.4 %collective-permute-start.4 = (f32[3,256,128]{2,1,0:T(8,128)}, f32[3,256,128]{2,1,0:T(8,128)S(1)}, u32[]{:S(2)}, u32[]{:S(2)}) collective-permute-start(f32[3,256,128]{2,1,0:T(8,128)} %get-tuple-element.43), channel_id=1, source_target_pairs={{0,12},{4,8},{8,4},{12,0},{16,28},{20,24},{24,20},{28,16},{1,13},{... | collective-permute-start | bytes 1179656 | tf_op jit(solution)/shard_map/ppermute | solution.py:597
  22.6 2.5 %collective-permute-start = (f32[2,3,64,512]{3,2,1,0:T(8,128)}, f32[2,3,64,512]{3,2,1,0:T(8,128)S(1)}, u32[]{:S(2)}, u32[]{:S(2)}) collective-permute-start(f32[2,3,64,512]{3,2,1,0:T(8,128)} %get-tuple-element.38), channel_id=1, source_target_pairs={{0,1},{1,0},{2,3},{3,2},{4,5},{5,4},{6,7},{7,6},{8,9},{9,8},{10,11... | collective-permute-start | bytes 2359304 | tf_op jit(solution)/shard_map/ppermute | solution.py:597
  25.1 1.1 copy-start
  27.1 16.5 %collective-permute-start.1 = (f32[1,3,64,512]{3,2,1,0:T(8,128)}, f32[1,3,64,512]{3,2,1,0:T(8,128)S(1)}, u32[]{:S(2)}, u32[]{:S(2)}) collective-permute-start(f32[1,3,64,512]{3,2,1,0:T(8,128)} %get-tuple-element.39), channel_id=1, source_target_pairs={{0,2},{1,3},{2,0},{3,1},{4,6},{5,7},{6,4},{7,5},{8,10},{9,11},{10,... | collective-permute-start | bytes 1179656 | tf_op jit(solution)/shard_map/ppermute | solution.py:597
  29.1 1.5 %copy-start.15 = (f32[6,8,2]{0,2,1:T(2,128)}, f32[6,8,2]{0,2,1:T(2,128)S(1)}, u32[]{:S(2)}) copy-start(f32[6,8,2]{0,2,1:T(2,128)S(1)} %copy.14) | copy-start | bytes 1156
  30.0 0.6 copy-start.6
  30.6 9.4 %copy-start.9 = (f32[40,128]{1,0:T(8,128)}, f32[40,128]{1,0:T(8,128)S(1)}, u32[]{:S(2)}) copy-start(f32[40,128]{1,0:T(8,128)S(1)} %get-tuple-element.61.matrix_two) | copy-start | bytes 61444
  40.1 1.0 copy-start.1
  42.3 0.7 copy-start.2
  43.0 0.6 copy-start.4
  43.6 59.5 %copy-start.14 = (f32[2]{0:T(128)S(1)}, f32[2]{0:T(128)}, u32[]{:S(2)}) copy-start(f32[2]{0:T(128)} %pad_maximum_fusion.1.sums) | copy-start | bytes 28
  44.4 57.3 %copy-start.16 = (f32[6,8,2]{0,2,1:T(2,128)S(1)}, f32[6,8,2]{0,2,1:T(2,128)}, u32[]{:S(2)}) copy-start(f32[6,8,2]{0,2,1:T(2,128)} %copy-done.15) | copy-start | bytes 1156
  44.4 22.2 %all-to-all-start = ((f32[8,3,8,512]{3,2,1,0:T(8,128)}), f32[8,3,8,512]{3,2,1,0:T(8,128)S(1)}, u32[]{:S(2)}, u32[]{:S(2)}) async-start(f32[8,3,8,512]{3,2,1,0:T(8,128)} %density_parts.1), calls=%async_computation | async-start | bytes 786432 | tf_op jit(solution)/shard_map/all_to_all | solution.py:680
  50.5 16.1 %collective-permute-start.5 = (f32[256,128]{1,0:T(8,128)}, f32[256,128]{1,0:T(8,128)S(1)}, u32[]{:S(2)}, u32[]{:S(2)}) collective-permute-start(f32[256,128]{1,0:T(8,128)} %copy-done.4), channel_id=1, source_target_pairs={{0,16},{4,20},{8,24},{12,28},{16,0},{20,4},{24,8},{28,12},{1,17},{... | collective-permute-start | bytes 393224 | tf_op jit(solution)/shard_map/ppermute | solution.py:597
  66.6 0.7 copy-start.11
  67.4 0.7 copy-start.12
  69.3 19.1 %all-to-all-start.1 = ((f32[8,2,8,512]{3,2,1,0:T(8,128)}), f32[8,2,8,512]{3,2,1,0:T(8,128)S(1)}, u32[]{:S(2)}, u32[]{:S(2)}) async-start(f32[8,2,8,512]{3,2,1,0:T(8,128)} %get-tuple-element.58), calls=%async_computation.1 | async-start | bytes 524288 | tf_op jit(solution)/shard_map/all_to_all | solution.py:692
  73.0 20.6 %collective-permute-start.9 = (f32[2,256,128]{2,1,0:T(8,128)}, f32[2,256,128]{2,1,0:T(8,128)S(1)}, u32[]{:S(2)}, u32[]{:S(2)}) collective-permute-start(f32[2,256,128]{2,1,0:T(8,128)} %copy-done.2), channel_id=1, source_target_pairs={{0,16},{4,20},{8,24},{12,28},{16,0},{20,4},{24,8},{28,12},{1,17},{... | collective-permute-start | bytes 786440 | tf_op jit(solution)/shard_map/ppermute | solution.py:597
  88.4 0.9 copy-start.7
  89.3 0.7 copy-start.10
  90.0 0.7 copy-start.13
  92.0 9.2 %collective-permute-start.6 = (f32[128,512]{1,0:T(8,128)S(1)}, f32[128,512]{1,0:T(8,128)S(1)}, u32[]{:S(2)}, u32[]{:S(2)}) collective-permute-start(f32[128,512]{1,0:T(8,128)S(1)} %kelvins.1.refs_0_), channel_id=1, source_target_pairs={{0,2},{1,3},{2,0},{3,1},{4,6},{5,7},{6,4},{7,5},{8,10},{9,11},{10,... | collective-permute-start | bytes 786440 | tf_op jit(solution)/shard_map/ppermute | solution.py:597
  93.6 1.0 copy-start.3
  94.6 0.9 copy-start.5
  97.7 14.1 %collective-permute-start.10 = (f32[3,256,128]{2,1,0:T(8,128)}, f32[3,256,128]{2,1,0:T(8,128)S(1)}, u32[]{:S(2)}, u32[]{:S(2)}) collective-permute-start(f32[3,256,128]{2,1,0:T(8,128)} %get-tuple-element.68), channel_id=1, source_target_pairs={{0,4},{4,0},{8,12},{12,8},{16,20},{20,16},{24,28},{28,24},{1,5},{5... | collective-permute-start | bytes 1179656 | tf_op jit(solution)/shard_map/ppermute | solution.py:597
  99.1 12.8 %collective-permute-start.11 = (f32[3,256,128]{2,1,0:T(8,128)}, f32[3,256,128]{2,1,0:T(8,128)S(1)}, u32[]{:S(2)}, u32[]{:S(2)}) collective-permute-start(f32[3,256,128]{2,1,0:T(8,128)} %get-tuple-element.69), channel_id=1, source_target_pairs={{0,8},{4,12},{8,0},{12,4},{16,24},{20,28},{24,16},{28,20},{1,9},{5... | collective-permute-start | bytes 1179656 | tf_op jit(solution)/shard_map/ppermute | solution.py:597
  99.1 16.6 %collective-permute-start.12 = (f32[3,256,128]{2,1,0:T(8,128)S(1)}, f32[3,256,128]{2,1,0:T(8,128)S(1)}, u32[]{:S(2)}, u32[]{:S(2)}) collective-permute-start(f32[3,256,128]{2,1,0:T(8,128)S(1)} %get-tuple-element.70), channel_id=1, source_target_pairs={{0,12},{4,8},{8,4},{12,0},{16,28},{20,24},{24,20},{28,16},{1,13},{... | collective-permute-start | bytes 1179656 | tf_op jit(solution)/shard_map/ppermute | solution.py:597
  101.2 1.5 %collective-permute-start.7 = (f32[128,512]{1,0:T(8,128)S(1)}, f32[128,512]{1,0:T(8,128)S(1)}, u32[]{:S(2)}, u32[]{:S(2)}) collective-permute-start(f32[128,512]{1,0:T(8,128)S(1)} %kelvins.1.refs_0_), channel_id=1, source_target_pairs={{0,1},{1,0},{2,3},{3,2},{4,5},{5,4},{6,7},{7,6},{8,9},{9,8},{10,11... | collective-permute-start | bytes 786440 | tf_op jit(solution)/shard_map/ppermute | solution.py:597
  101.2 1.9 %collective-permute-start.8 = (f32[128,512]{1,0:T(8,128)S(1)}, f32[128,512]{1,0:T(8,128)S(1)}, u32[]{:S(2)}, u32[]{:S(2)}) collective-permute-start(f32[128,512]{1,0:T(8,128)S(1)} %collective-permute-done.6.refs_1_), channel_id=1, source_target_pairs={{0,1},{1,0},{2,3},{3,2},{4,5},{5,4},{6,7},{7,6},{8,9},{9,8},{10,11... | collective-permute-start | bytes 786440 | tf_op jit(solution)/shard_map/ppermute | solution.py:597

commit v14 on v13

--- a/solution.py
+++ b/solution.py
@@ -262,7 +262,7 @@
 
     row = lax.broadcasted_iota(jnp.int32, (8, 128), 0)
 
-    def of_slot(i):
+    def one_slot(i, carry):
         s = step * block + i
         label = labels[s]
         polar, turn_of = label % 4, (label // 4) % 8
@@ -272,55 +272,48 @@
         wide = (turn_of % 4 == 0) | (turn_of % 4 == 3)
         start, stride = jnp.where(forward, 0, depth - 1), jnp.where(forward, 1, -1)
         at_wall = jnp.where(forward, slab == 0, slab == slabs - 1)
-        c_self = table[K_SELF, kind]
-        c_y = table[jnp.where(wide, K_LARGE, K_SMALL), kind]
-        c_z = table[jnp.where(wide, K_SMALL, K_LARGE), kind]
-        wall = jnp.where(at_wall, 1.0, 0.0) * table[K_WALL, kind]
-        shift_y, shift_z = jnp.where(right, 1, 7), jnp.where(up, 1, 127)
-        at_edge = row == jnp.where(right, 0, 7)
-        apply = lambda low, high: stencil(low, high, c_self, c_y, c_z, shift_y, shift_z, at_edge)
         xs = [start + stride * j for j in range(depth)]
-        return s, forward, kind, wall, apply, xs
-
-    def one_pair(pair, carry):
-        pair = [2 * pair, 2 * pair + 1]
-        slots_of = [of_slot(i) for i in pair]
-        layers = [[(energy[i, x, :8, :], energy[i, x, 8:, :]) for x in of[-1]] for i, of in zip(pair, slots_of)]
-        lasts = [[], []]
-        for turn in range(ITERS):
-            for which, (s, forward, kind, wall, apply, xs) in enumerate(slots_of):
-                ratio = table[K_RATIO, kind]
-                warm = table[K_HEAT, kind] if turn else None
+
+        def body(shift_y, shift_z):
+            c_self, ratio, warm = table[K_SELF, kind], table[K_RATIO, kind], table[K_HEAT, kind]
+            c_y = table[jnp.where(wide, K_LARGE, K_SMALL), kind]
+            c_z = table[jnp.where(wide, K_SMALL, K_LARGE), kind]
+            wall = jnp.where(at_wall, 1.0, 0.0) * table[K_WALL, kind]
+            at_edge = row == (0 if shift_y == 1 else 7)
+            apply = lambda low, high: stencil(low, high, c_self, c_y, c_z, shift_y, shift_z, at_edge)
+            layers = [(energy[i, x, :8, :], energy[i, x, 8:, :]) for x in xs]
+            last = []
+            for turn in range(ITERS):
                 total_low = total_high = wall
                 for j, x in enumerate(xs):
-                    low, high = apply(*layers[which][j])
+                    low, high = apply(*layers[j])
                     if turn == 0:
                         low, high = low + sources[kind, x, :8, :], high + sources[kind, x, 8:, :]
                     else:
                         low, high = low + warm * heat[x, :8, :], high + warm * heat[x, 8:, :]
                     total_low = ratio * total_low + low
                     total_high = ratio * total_high + high
-                    layers[which][j] = (total_low, total_high)
-                lasts[which].append((total_low, total_high))
-            for x in range(depth):
-                for half, here in enumerate((slice(0, 8), slice(8, 16))):
-                    values = [
-                        jnp.where(of[1], layer[x][half], layer[depth - 1 - x][half]) for of, layer in zip(slots_of, layers)
-                    ]
-                    density[turn, x, here, :] += values[0] + values[1]
-                    if turn == ITERS - 1:
-                        for i, value in zip(pair, values):
+                    layers[j] = (total_low, total_high)
+                last.append((total_low, total_high))
+                for x in range(depth):
+                    for half, here in enumerate((slice(0, 8), slice(8, 16))):
+                        value = jnp.where(forward, layers[x][half], layers[depth - 1 - x][half])
+                        density[turn, x, here, :] += value
+                        if turn == ITERS - 1:
                             swept[i, x, here, :] = value
-        for (s, _, _, _, apply, _), last in zip(slots_of, lasts):
             turned = apply(*last[0])
             at_low, at_high = rows_of(s)
             values = (last[0], turned, apply(*turned), last[1], apply(*last[1]), last[2])
             for plane, (low, high) in zip(planes, values):
                 plane[at_low, :] = low
                 plane[at_high, :] = high
+
+        for y_sign, shift_y in ((right, 1), (~right, 7)):
+            for z_sign, shift_z in ((up, 1), (~up, 127)):
+                pl.when(y_sign & z_sign)(functools.partial(body, shift_y, shift_z))
         return carry
 
-    lax.fori_loop(0, block // 2, one_pair, 0)
+    lax.fori_loop(0, block, one_slot, 0)
 
     @pl.when(step == blocks - 1)
     def _():
@@ -541,22 +534,25 @@
     lax.fori_loop(0, block, one_slot, 0, unroll=2)
 
 
-def inflow_kernel(sizes, meta, floats, ints, warm, *refs):
+def inflow_kernel(first, sizes, meta, floats, ints, warm, *refs):
     block, depth, own, group = sizes
-    received, (energy, ordered) = refs[:group], refs[group:]
+    received, (energy, ordered) = refs[:-2], refs[-2:]
     step = pl.program_id(0)
+    per_home = own // block
+    home = (meta[SLAB] % group) ^ (step // per_home + first)
 
     @pl.when(step == 0)
     def _():
-        for by in range(group):
-            ordered[(meta[SLAB] % group) ^ by] = received[by][...]
+        for index, ref in enumerate(received):
+            ordered[index] = ref[...]
 
     def one_slot(i, carry):
-        s = step * block + i
+        inside = (step % per_home) * block + i
+        s = home * own + inside
         start, stride = course(ints, s, depth)
         ratio = floats[RATIO, s]
-        at = pl.ds(pl.multiple_of((s % own) * 16, 16), 16)
-        one, two, three = (ordered[s // own, plane, at, :] for plane in range(ITERS))
+        at = pl.ds(pl.multiple_of(inside * 16, 16), 16)
+        one, two, three = (ordered[step // per_home, plane, at, :] for plane in range(ITERS))
         for j in range(depth):
             x = start + stride * j
             one = ratio * one
@@ -737,16 +733,32 @@
         compiler_params=PARAMS,
         name="warm",
     )(meta, floats, ints, kinds, sums, swept, *packs)
-    energy = pl.pallas_call(
-        functools.partial(inflow_kernel, (block, depth, own, group)),
-        grid=(blocks,),
-        in_specs=[SMEM] * 3 + [slot_block] + [whole(*face)] * group,
-        out_specs=slot_block,
-        out_shape=slot_shape,
-        scratch_shapes=[scratch(group, *face)],
-        compiler_params=PARAMS,
-        name="inflow",
-    )(meta, floats, ints, warm, *entering)
+    def add_inflow(first, received, energy):
+        per_home = own // block
+
+        def place(i, meta, floats, ints):
+            home = (meta[SLAB] % group) ^ (i // per_home + first)
+            return home * per_home + i % per_home, 0, 0, 0
+
+        home_block = pl.BlockSpec((block, depth, width_y, width_z), place)
+        face_block = pl.BlockSpec(face, lambda i, *_: (0, 0, 0))
+        return pl.pallas_call(
+            functools.partial(inflow_kernel, first, (block, depth, own, group)),
+            grid_spec=pltpu.PrefetchScalarGridSpec(
+                num_scalar_prefetch=3,
+                grid=(per_home * len(received),),
+                in_specs=[home_block] + [face_block] * len(received),
+                out_specs=home_block,
+                scratch_shapes=[scratch(len(received), *face)],
+            ),
+            out_shape=slot_shape,
+            input_output_aliases={3: 0},
+            compiler_params=PARAMS,
+            name=f"inflow_{first}",
+        )(meta, floats, ints, energy, *received)
+
+    energy = add_inflow(0, entering[:-1], warm)
+    energy = add_inflow(group - 1, entering[-1:], energy)
     return energy, kelvin.reshape(depth, width_y, width_z)
 
 

time: 122 us -> 132 us (1.082)
  Pallas kernels: 39.2 us -> 51.2 us
  waiting for transfers between devices: 39.7 us -> 35.7 us
  local copies, waits for them, and re-layouts: 10 us -> 12.2 us
    pallas_call x1, Pallas kernels: 16.8 us -> 25.3 us  [local(): pl.pallas_call(functools.partial(sweeps_kernel, (block, blocks, depth, wi...]
    pallas_call x1 -> x2, Pallas kernels: 5.19 us -> 9.55 us  [add_inflow(): pl.pallas_call(functools.partial(inflow_kernel, first, (block, depth, own...]
    ppermute x13, waiting for transfers between devices: 27.2 us -> 23.2 us  [swap(): lax.ppermute(array, axis, [(i, i ^ by) for i in range(lax.axis_size(axis))])]
    unnamed x46 -> x48, local copies, waits for them, and re-layouts: 9.67 us -> 11.9 us
  transfers between devices with their start and end apart: 15 -> 15, of which waited for: 8 -> 7; matrix products, arithmetic and copies ran while one was open for 3% -> 3% of each run, Pallas kernels for 13% -> 16%
where the time goes in v14:
time: 132 us; the launch traced here: 131 us
  Pallas kernels  51.2 us (39%)
  waiting for transfers between devices  35.7 us (27%)
  starting transfers between devices  27.8 us (21%)
  local copies, waits for them, and re-layouts  12.2 us (9%)
  other arithmetic  3.56 us (3%)
    pallas_call x1, Pallas kernels, local(): pl.pallas_call(functools.partial(sweeps_kernel, (block, blocks, depth, wi...  25.3 us
    ppermute x13, waiting for transfers between devices, swap(): lax.ppermute(array, axis, [(i, i ^ by) for i in range(lax.axis_size(axis))])  23.2 us
    ppermute x13, starting transfers between devices, swap(): lax.ppermute(array, axis, [(i, i ^ by) for i in range(lax.axis_size(axis))])  18 us
    all_to_all x1, waiting for transfers between devices, local(): gathered = lax.all_to_all(copies, 'slab', 0, 0)  12.5 us
    unnamed x48, local copies, waits for them, and re-layouts  11.9 us
    pallas_call x2, Pallas kernels, add_inflow(): pl.pallas_call(functools.partial(inflow_kernel, first, (block, depth, own...  9.55 us
    pallas_call x7, Pallas kernels, call(): pl.pallas_call(kernel, in_specs=in_specs, out_specs=[VMEM] * len(out_shap...  8.51 us
    pallas_call x1, Pallas kernels, local(): pl.pallas_call(functools.partial(warm_kernel, (block, depth, width_y, wid...  7.8 us
  transfers between devices with their start and end apart: 15, of which 7 were waited for; matrix products, arithmetic and copies ran while one was open for 3% of the time, Pallas kernels for 16%

profile of v14, /device:TPU:0, one launch (start us, length us, event | category | flops | bytes accessed | tf_op | source)
XLA Modules:
  0.0 131.3 jit_solution(16162802287165907214)
XLA Ops:
  0.6 0.0 copy-start.20
  0.6 0.0 copy-start.19
  0.7 0.0 copy-start.23
  0.7 0.0 copy-start.18
  0.7 0.0 copy-start.22
  0.7 0.0 copy-start.21
  0.7 0.6 pad_add_fusion.meta
  1.3 25.3 %sweeps.1 = (f32[64,8,16,128]{3,2,1,0:T(8,128)}, f32[8,512]{1,0:T(8,128)}, f32[3,256,128]{2,1,0:T(8,128)}, f32[3,256,128]{2,1,0:T(8,128)}, f32[3,256,128]{2,1,0:...) custom-call(s32[2]{0:T(128)} %pad_add_fusion.meta, s32[64]{0:T(128)} %labels.1, ...), custom_call_target="tpu_custom_call" | custom-call | tf_op jit(solution)/shard_map/sweeps/pallas_call | solution.py:610
  26.6 3.0 %collective-permute-start.2 = (f32[3,256,128]{2,1,0:T(8,128)}, f32[3,256,128]{2,1,0:T(8,128)S(1)}, u32[]{:S(2)}, u32[]{:S(2)}) collective-permute-start(f32[3,256,128]{2,1,0:T(8,128)} %get-tuple-element.41), channel_id=1, source_target_pairs={{0,4},{4,0},{8,12},{12,8},{16,20},{20,16},{24,28},{28,24},{1,5},{5... | collective-permute-start | bytes 1179656 | tf_op jit(solution)/shard_map/ppermute | solution.py:593
  29.6 1.6 %collective-permute-start.3 = (f32[3,256,128]{2,1,0:T(8,128)}, f32[3,256,128]{2,1,0:T(8,128)S(1)}, u32[]{:S(2)}, u32[]{:S(2)}) collective-permute-start(f32[3,256,128]{2,1,0:T(8,128)} %get-tuple-element.42), channel_id=1, source_target_pairs={{0,8},{4,12},{8,0},{12,4},{16,24},{20,28},{24,16},{28,20},{1,9},{5... | collective-permute-start | bytes 1179656 | tf_op jit(solution)/shard_map/ppermute | solution.py:593
  31.2 0.0 collective-permute-start.4
  31.2 0.0 collective-permute-start
  31.3 0.1 select_reduce_fusion
  31.4 0.7 fusion.20
  32.1 0.1 fusion.7
  32.4 1.3 %collective-permute-done.other = f32[2,3,64,512]{3,2,1,0:T(8,128)S(1)} collective-permute-done((f32[2,3,64,512]{3,2,1,0:T(8,128)}, f32[2,3,64,512]{3,2,1,0:T(8,128)S(1)}, u32[]{:S(2)}, u32[]{:S(2)}) %collective-permute-start) | collective-permute-done | bytes 786464 | tf_op jit(solution)/shard_map/ppermute | solution.py:593
  33.7 1.1 copy-done.1
  34.9 0.8 density_split.1
  35.7 1.9 %collective-permute-start.1 = (f32[1,3,64,512]{3,2,1,0:T(8,128)}, f32[1,3,64,512]{3,2,1,0:T(8,128)S(1)}, u32[]{:S(2)}, u32[]{:S(2)}) collective-permute-start(f32[1,3,64,512]{3,2,1,0:T(8,128)} %get-tuple-element.39), channel_id=1, source_target_pairs={{0,2},{1,3},{2,0},{3,1},{4,6},{5,7},{6,4},{7,5},{8,10},{9,11},{10,... | collective-permute-start | bytes 1179656 | tf_op jit(solution)/shard_map/ppermute | solution.py:593
  37.6 0.1 copy.16
  37.7 0.1 copy.17.kinds
  37.8 0.8 heat_matrices.1
  38.6 0.6 copy-done.7
  39.3 1.9 %pad_maximum_fusion.1.sums = f32[2]{0:T(128)} fusion(f32[1]{0:T(128)} %bitcast.36, f32[1]{0:T(128)} %bitcast.35), kind=kLoop, calls=%fused_computation.35 | loop fusion | flops 2 | bytes 16 | tf_op jit(solution)/shard_map/stack | solution.py:581
  41.3 0.0 collective-permute-done.2.refs_1_
  41.3 0.6 collective-permute-done.3.refs_2_
  41.9 6.8 %collective-permute-done.4.refs_3_ = f32[3,256,128]{2,1,0:T(8,128)S(1)} collective-permute-done((f32[3,256,128]{2,1,0:T(8,128)}, f32[3,256,128]{2,1,0:T(8,128)S(1)}, u32[]{:S(2)}, u32[]{:S(2)}) %collective-permute-start.4) | collective-permute-done | bytes 393248 | tf_op jit(solution)/shard_map/ppermute | solution.py:593
  48.7 1.0 copy-done.2
  49.7 1.2 compose.1
  50.9 0.7 copy-done.3
  51.6 0.6 copy-done.5
  52.2 0.0 collective-permute-done.1.other
  52.2 0.8 density_parts.1
  53.0 6.1 %all-to-all-start = ((f32[8,3,8,512]{3,2,1,0:T(8,128)}), f32[8,3,8,512]{3,2,1,0:T(8,128)S(1)}, u32[]{:S(2)}, u32[]{:S(2)}) async-start(f32[8,3,8,512]{3,2,1,0:T(8,128)} %density_parts.1), calls=%async_computation | async-start | bytes 786432 | tf_op jit(solution)/shard_map/all_to_all | solution.py:676
  59.1 2.9 %collective-permute-start.5 = (f32[256,128]{1,0:T(8,128)}, f32[256,128]{1,0:T(8,128)S(1)}, u32[]{:S(2)}, u32[]{:S(2)}) collective-permute-start(f32[256,128]{1,0:T(8,128)} %copy-done.5), channel_id=1, source_target_pairs={{0,16},{4,20},{8,24},{12,28},{16,0},{20,4},{24,8},{28,12},{1,17},{... | collective-permute-start | bytes 393224 | tf_op jit(solution)/shard_map/ppermute | solution.py:593
  62.0 13.2 %collective-permute-done.5.refs_1_ = f32[256,128]{1,0:T(8,128)S(1)} collective-permute-done((f32[256,128]{1,0:T(8,128)}, f32[256,128]{1,0:T(8,128)S(1)}, u32[]{:S(2)}, u32[]{:S(2)}) %collective-permute-start.5) | collective-permute-done | bytes 131104 | tf_op jit(solution)/shard_map/ppermute | solution.py:593
  75.2 0.0 all-to-all-done.parts
  75.2 0.7 copy-done.12
  76.0 0.7 copy-done.13
  76.6 1.3 density_totals.1
  77.9 3.7 %all-to-all-start.1 = ((f32[8,2,8,512]{3,2,1,0:T(8,128)}), f32[8,2,8,512]{3,2,1,0:T(8,128)S(1)}, u32[]{:S(2)}, u32[]{:S(2)}) async-start(f32[8,2,8,512]{3,2,1,0:T(8,128)} %get-tuple-element.58), calls=%async_computation.1 | async-start | bytes 524288 | tf_op jit(solution)/shard_map/all_to_all | solution.py:688
  81.6 2.9 %collective-permute-start.9 = (f32[2,256,128]{2,1,0:T(8,128)}, f32[2,256,128]{2,1,0:T(8,128)S(1)}, u32[]{:S(2)}, u32[]{:S(2)}) collective-permute-start(f32[2,256,128]{2,1,0:T(8,128)} %copy-done.3), channel_id=1, source_target_pairs={{0,16},{4,20},{8,24},{12,28},{16,0},{20,4},{24,8},{28,12},{1,17},{... | collective-permute-start | bytes 786440 | tf_op jit(solution)/shard_map/ppermute | solution.py:593
  84.5 12.5 %all-to-all-done.1.gathered = f32[8,2,8,512]{3,2,1,0:T(8,128)S(1)} async-done(((f32[8,2,8,512]{3,2,1,0:T(8,128)}), f32[8,2,8,512]{3,2,1,0:T(8,128)S(1)}, u32[]{:S(2)}, u32[]{:S(2)}) %all-to-all-start.1) | async-done | bytes 262176 | tf_op jit(solution)/shard_map/all_to_all | solution.py:688
  97.0 0.9 copy-done.8
  97.9 0.7 copy-done.11
  98.6 0.7 copy-done.14
  99.3 1.4 %kelvins.1.refs_0_ = f32[128,512]{1,0:T(8,128)S(1)} custom-call(s32[2]{0:T(128)S(1)} %copy-done.9, f32[2]{0:T(128)S(1)} %copy-done.14, f32[8,2,8,512]{3,2,1,0:T(8,128)S(1)} %all-to-all-done.1.gathered, f32[8,512]{1,0:T(8,128)S(1)} %get-tuple-element.59.late, f32[144,128]{1,0:T(8,128)S(1)} %copy-done.8, f32[40,128]{1,0:T(8,128)S(1)} %copy-done.11), custom_call_target="tpu_custom_call" | custom-call | tf_op jit(solution)/shard_map/kelvins/pallas_call | solution.py:596
  100.6 1.6 %collective-permute-start.6 = (f32[128,512]{1,0:T(8,128)S(1)}, f32[128,512]{1,0:T(8,128)S(1)}, u32[]{:S(2)}, u32[]{:S(2)}) collective-permute-start(f32[128,512]{1,0:T(8,128)S(1)} %kelvins.1.refs_0_), channel_id=1, source_target_pairs={{0,2},{1,3},{2,0},{3,1},{4,6},{5,7},{6,4},{7,5},{8,10},{9,11},{10,... | collective-permute-start | bytes 786440 | tf_op jit(solution)/shard_map/ppermute | solution.py:593
  102.2 0.0 collective-permute-done.9.refs_3_
  102.2 0.9 copy-done.4
  103.2 0.9 copy-done.6
  104.1 2.2 %enter.1 = (f32[3,256,128]{2,1,0:T(8,128)S(1)}, f32[3,256,128]{2,1,0:T(8,128)}, f32[3,256,128]{2,1,0:T(8,128)}, f32[3,256,128]{2,1,0:T(8,128)S(1)}) custom-call(s32[2]{0:T(128)S(1)} %copy-done.9, f32[10,64]{1,0:T(8,128)S(1)} %stack.136.floats, s32[5,64]{1,0:T(8,128)S(1)} %stack.143.ints, f32[4,3,256,128]{3,2,1,0:T(8,128)S(1)} %get-tuple-element.63.effective, ...), custom_call_target="tpu_custom_call" | custom-call | tf_op jit(solution)/shard_map/enter/pallas_call | solution.py:596
  106.3 1.4 %collective-permute-start.10 = (f32[3,256,128]{2,1,0:T(8,128)}, f32[3,256,128]{2,1,0:T(8,128)S(1)}, u32[]{:S(2)}, u32[]{:S(2)}) collective-permute-start(f32[3,256,128]{2,1,0:T(8,128)} %get-tuple-element.68), channel_id=1, source_target_pairs={{0,4},{4,0},{8,12},{12,8},{16,20},{20,16},{24,28},{28,24},{1,5},{5... | collective-permute-start | bytes 1179656 | tf_op jit(solution)/shard_map/ppermute | solution.py:593
  107.7 2.1 %collective-permute-start.12 = (f32[3,256,128]{2,1,0:T(8,128)S(1)}, f32[3,256,128]{2,1,0:T(8,128)S(1)}, u32[]{:S(2)}, u32[]{:S(2)}) collective-permute-start(f32[3,256,128]{2,1,0:T(8,128)S(1)} %get-tuple-element.70), channel_id=1, source_target_pairs={{0,12},{4,8},{8,4},{12,0},{16,28},{20,24},{24,20},{28,16},{1,13},{... | collective-permute-start | bytes 1179656 | tf_op jit(solution)/shard_map/ppermute | solution.py:593
  109.8 0.5 collective-permute-start.8
  110.3 0.1 copy.18.kinds
  110.4 0.9 collective-permute-done.7.refs_2_
  111.4 0.4 collective-permute-done.8.refs_3_
  111.7 2.2 %copy-done = f32[64,8,16,128]{3,2,1,0:T(8,128)S(1)} copy-done((f32[64,8,16,128]{3,2,1,0:T(8,128)S(1)}, f32[64,8,16,128]{3,2,1,0:T(8,128)}, u32[]{:S(2)}) %copy-start) | copy-done | bytes 4194328
  113.9 7.8 %warm.1 = (f32[64,8,16,128]{3,2,1,0:T(8,128)}, f32[128,128]{1,0:T(8,128)}) custom-call(s32[2]{0:T(128)S(1)} %copy-done.9, f32[10,64]{1,0:T(8,128)S(1)} %stack.136.floats, s32[5,64]{1,0:T(8,128)S(1)} %stack.143.ints, f32[6,16]{1,0:T(8,128)S(1)} %copy.18.kinds, f32[2]{0:T(128)S(1)} %copy-done.15, f32[64,8,16,128]{3,2,1,0:T(8,128)S(1)} %copy-done, ...), custom_call_target="tpu_custom_call" | custom-call | tf_op jit(solution)/shard_map/warm/pallas_call | solution.py:723
  121.7 0.0 collective-permute-done.10.refs_1_
  121.7 0.0 collective-permute-done.11.refs_2_
  121.7 6.5 %inflow_0.1.warm = f32[64,8,16,128]{3,2,1,0:T(8,128)} custom-call(s32[2]{0:T(128)S(1)} %copy-done.9, f32[10,64]{1,0:T(8,128)S(1)} %stack.136.floats, s32[5,64]{1,0:T(8,128)S(1)} %stack.143.ints, f32[64,8,16,128]{3,2,1,0:T(8,128)} %get-tuple-element.62.warm, f32[3,256,128]{2,1,0:T(8,128)S(1)} %get-tuple-element.67.refs_0_, ...), custom_call_target="tpu_custom_call", output_to_operand_aliasing={{}: (3, {})} | custom-call | tf_op jit(solution)/shard_map/inflow_0/pallas_call | solution.py:745
  128.2 3.0 %inflow_3.1 = f32[64,8,16,128]{3,2,1,0:T(8,128)} custom-call(s32[2]{0:T(128)S(1)} %copy-done.9, f32[10,64]{1,0:T(8,128)S(1)} %stack.136.floats, s32[5,64]{1,0:T(8,128)S(1)} %stack.143.ints, f32[64,8,16,128]{3,2,1,0:T(8,128)} %inflow_0.1.warm, f32[3,256,128]{2,1,0:T(8,128)S(1)} %collective-permute-done.12.refs_0_), custom_call_target="tpu_custom_call", output_to_operand_aliasing={{}: (3, {})} | custom-call | tf_op jit(solution)/shard_map/inflow_3/pallas_call | solution.py:745
  (47 shorter events, 0.4 us)
Async XLA Ops:
  0.6 30.6 %copy-start.20 = (f32[8]{0:T(128)S(1)}, f32[8]{0:T(128)}, u32[]{:S(2)}) copy-start(f32[8]{0:T(128)} %refs_0_.1) | copy-start | bytes 100
  0.6 30.6 %copy-start.19 = (f32[8]{0:T(128)S(1)}, f32[8]{0:T(128)}, u32[]{:S(2)}) copy-start(f32[8]{0:T(128)} %refs_1_.1) | copy-start | bytes 100
  0.7 30.6 %copy-start.23 = (f32[8]{0:T(128)S(1)}, f32[8]{0:T(128)}, u32[]{:S(2)}) copy-start(f32[8]{0:T(128)} %refs_2_.1) | copy-start | bytes 100
  0.7 30.6 %copy-start.18 = (f32[8]{0:T(128)S(1)}, f32[8]{0:T(128)}, u32[]{:S(2)}) copy-start(f32[8]{0:T(128)} %refs_3_.1) | copy-start | bytes 100
  0.7 30.6 %copy-start.22 = (f32[8]{0:T(128)S(1)}, f32[8]{0:T(128)}, u32[]{:S(2)}) copy-start(f32[8]{0:T(128)} %refs_4_.1) | copy-start | bytes 100
  0.7 30.5 %copy-start.21 = (s32[64]{0:T(128)S(1)}, s32[64]{0:T(128)}, u32[]{:S(2)}) copy-start(s32[64]{0:T(128)} %labels.1) | copy-start | bytes 772
  1.3 36.5 %copy-start.9 = (s32[2]{0:T(128)S(1)}, s32[2]{0:T(128)}, u32[]{:S(2)}) copy-start(s32[2]{0:T(128)} %pad_add_fusion.meta) | copy-start | bytes 28
  26.6 14.7 %collective-permute-start.2 = (f32[3,256,128]{2,1,0:T(8,128)}, f32[3,256,128]{2,1,0:T(8,128)S(1)}, u32[]{:S(2)}, u32[]{:S(2)}) collective-permute-start(f32[3,256,128]{2,1,0:T(8,128)} %get-tuple-element.41), channel_id=1, source_target_pairs={{0,4},{4,0},{8,12},{12,8},{16,20},{20,16},{24,28},{28,24},{1,5},{5... | collective-permute-start | bytes 1179656 | tf_op jit(solution)/shard_map/ppermute | solution.py:593
  29.6 12.3 %collective-permute-start.3 = (f32[3,256,128]{2,1,0:T(8,128)}, f32[3,256,128]{2,1,0:T(8,128)S(1)}, u32[]{:S(2)}, u32[]{:S(2)}) collective-permute-start(f32[3,256,128]{2,1,0:T(8,128)} %get-tuple-element.42), channel_id=1, source_target_pairs={{0,8},{4,12},{8,0},{12,4},{16,24},{20,28},{24,16},{28,20},{1,9},{5... | collective-permute-start | bytes 1179656 | tf_op jit(solution)/shard_map/ppermute | solution.py:593
  31.2 17.4 %collective-permute-start.4 = (f32[3,256,128]{2,1,0:T(8,128)}, f32[3,256,128]{2,1,0:T(8,128)S(1)}, u32[]{:S(2)}, u32[]{:S(2)}) collective-permute-start(f32[3,256,128]{2,1,0:T(8,128)} %get-tuple-element.43), channel_id=1, source_target_pairs={{0,12},{4,8},{8,4},{12,0},{16,28},{20,24},{24,20},{28,16},{1,13},{... | collective-permute-start | bytes 1179656 | tf_op jit(solution)/shard_map/ppermute | solution.py:593
  31.2 2.5 %collective-permute-start = (f32[2,3,64,512]{3,2,1,0:T(8,128)}, f32[2,3,64,512]{3,2,1,0:T(8,128)S(1)}, u32[]{:S(2)}, u32[]{:S(2)}) collective-permute-start(f32[2,3,64,512]{3,2,1,0:T(8,128)} %get-tuple-element.38), channel_id=1, source_target_pairs={{0,1},{1,0},{2,3},{3,2},{4,5},{5,4},{6,7},{7,6},{8,9},{9,8},{10,11... | collective-permute-start | bytes 2359304 | tf_op jit(solution)/shard_map/ppermute | solution.py:593
  33.7 1.1 copy-start.1
  35.7 16.5 %collective-permute-start.1 = (f32[1,3,64,512]{3,2,1,0:T(8,128)}, f32[1,3,64,512]{3,2,1,0:T(8,128)S(1)}, u32[]{:S(2)}, u32[]{:S(2)}) collective-permute-start(f32[1,3,64,512]{3,2,1,0:T(8,128)} %get-tuple-element.39), channel_id=1, source_target_pairs={{0,2},{1,3},{2,0},{3,1},{4,6},{5,7},{6,4},{7,5},{8,10},{9,11},{10,... | collective-permute-start | bytes 1179656 | tf_op jit(solution)/shard_map/ppermute | solution.py:593
  37.7 1.5 %copy-start.16 = (f32[6,8,2]{0,2,1:T(2,128)}, f32[6,8,2]{0,2,1:T(2,128)S(1)}, u32[]{:S(2)}) copy-start(f32[6,8,2]{0,2,1:T(2,128)S(1)} %copy.16) | copy-start | bytes 1156
  38.6 0.6 copy-start.7
  39.2 9.4 %copy-start.10 = (f32[40,128]{1,0:T(8,128)}, f32[40,128]{1,0:T(8,128)S(1)}, u32[]{:S(2)}) copy-start(f32[40,128]{1,0:T(8,128)S(1)} %get-tuple-element.61.matrix_two) | copy-start | bytes 61444
  48.7 1.0 copy-start.2
  50.9 0.7 copy-start.3
  51.6 0.6 copy-start.5
  52.2 59.5 %copy-start.15 = (f32[2]{0:T(128)S(1)}, f32[2]{0:T(128)}, u32[]{:S(2)}) copy-start(f32[2]{0:T(128)} %pad_maximum_fusion.1.sums) | copy-start | bytes 28
  53.0 57.3 %copy-start.17 = (f32[6,8,2]{0,2,1:T(2,128)S(1)}, f32[6,8,2]{0,2,1:T(2,128)}, u32[]{:S(2)}) copy-start(f32[6,8,2]{0,2,1:T(2,128)} %copy-done.16) | copy-start | bytes 1156
  53.0 22.2 %all-to-all-start = ((f32[8,3,8,512]{3,2,1,0:T(8,128)}), f32[8,3,8,512]{3,2,1,0:T(8,128)S(1)}, u32[]{:S(2)}, u32[]{:S(2)}) async-start(f32[8,3,8,512]{3,2,1,0:T(8,128)} %density_parts.1), calls=%async_computation | async-start | bytes 786432 | tf_op jit(solution)/shard_map/all_to_all | solution.py:676
  59.1 16.1 %collective-permute-start.5 = (f32[256,128]{1,0:T(8,128)}, f32[256,128]{1,0:T(8,128)S(1)}, u32[]{:S(2)}, u32[]{:S(2)}) collective-permute-start(f32[256,128]{1,0:T(8,128)} %copy-done.5), channel_id=1, source_target_pairs={{0,16},{4,20},{8,24},{12,28},{16,0},{20,4},{24,8},{28,12},{1,17},{... | collective-permute-start | bytes 393224 | tf_op jit(solution)/shard_map/ppermute | solution.py:593
  75.2 0.7 copy-start.12
  76.0 0.7 copy-start.13
  77.9 19.1 %all-to-all-start.1 = ((f32[8,2,8,512]{3,2,1,0:T(8,128)}), f32[8,2,8,512]{3,2,1,0:T(8,128)S(1)}, u32[]{:S(2)}, u32[]{:S(2)}) async-start(f32[8,2,8,512]{3,2,1,0:T(8,128)} %get-tuple-element.58), calls=%async_computation.1 | async-start | bytes 524288 | tf_op jit(solution)/shard_map/all_to_all | solution.py:688
  81.6 20.7 %collective-permute-start.9 = (f32[2,256,128]{2,1,0:T(8,128)}, f32[2,256,128]{2,1,0:T(8,128)S(1)}, u32[]{:S(2)}, u32[]{:S(2)}) collective-permute-start(f32[2,256,128]{2,1,0:T(8,128)} %copy-done.3), channel_id=1, source_target_pairs={{0,16},{4,20},{8,24},{12,28},{16,0},{20,4},{24,8},{28,12},{1,17},{... | collective-permute-start | bytes 786440 | tf_op jit(solution)/shard_map/ppermute | solution.py:593
  97.0 0.9 copy-start.8
  97.9 0.7 copy-start.11
  98.6 0.7 copy-start.14
  100.6 9.2 %collective-permute-start.6 = (f32[128,512]{1,0:T(8,128)S(1)}, f32[128,512]{1,0:T(8,128)S(1)}, u32[]{:S(2)}, u32[]{:S(2)}) collective-permute-start(f32[128,512]{1,0:T(8,128)S(1)} %kelvins.1.refs_0_), channel_id=1, source_target_pairs={{0,2},{1,3},{2,0},{3,1},{4,6},{5,7},{6,4},{7,5},{8,10},{9,11},{10,... | collective-permute-start | bytes 786440 | tf_op jit(solution)/shard_map/ppermute | solution.py:593
  102.2 1.0 copy-start.4
  103.2 0.9 copy-start.6
  106.3 15.4 %collective-permute-start.10 = (f32[3,256,128]{2,1,0:T(8,128)}, f32[3,256,128]{2,1,0:T(8,128)S(1)}, u32[]{:S(2)}, u32[]{:S(2)}) collective-permute-start(f32[3,256,128]{2,1,0:T(8,128)} %get-tuple-element.68), channel_id=1, source_target_pairs={{0,4},{4,0},{8,12},{12,8},{16,20},{20,16},{24,28},{28,24},{1,5},{5... | collective-permute-start | bytes 1179656 | tf_op jit(solution)/shard_map/ppermute | solution.py:593
  107.7 14.0 %collective-permute-start.11 = (f32[3,256,128]{2,1,0:T(8,128)}, f32[3,256,128]{2,1,0:T(8,128)S(1)}, u32[]{:S(2)}, u32[]{:S(2)}) collective-permute-start(f32[3,256,128]{2,1,0:T(8,128)} %get-tuple-element.69), channel_id=1, source_target_pairs={{0,8},{4,12},{8,0},{12,4},{16,24},{20,28},{24,16},{28,20},{1,9},{5... | collective-permute-start | bytes 1179656 | tf_op jit(solution)/shard_map/ppermute | solution.py:593
  107.7 20.5 %collective-permute-start.12 = (f32[3,256,128]{2,1,0:T(8,128)S(1)}, f32[3,256,128]{2,1,0:T(8,128)S(1)}, u32[]{:S(2)}, u32[]{:S(2)}) collective-permute-start(f32[3,256,128]{2,1,0:T(8,128)S(1)} %get-tuple-element.70), channel_id=1, source_target_pairs={{0,12},{4,8},{8,4},{12,0},{16,28},{20,24},{24,20},{28,16},{1,13},{... | collective-permute-start | bytes 1179656 | tf_op jit(solution)/shard_map/ppermute | solution.py:593
  109.8 1.5 %collective-permute-start.7 = (f32[128,512]{1,0:T(8,128)S(1)}, f32[128,512]{1,0:T(8,128)S(1)}, u32[]{:S(2)}, u32[]{:S(2)}) collective-permute-start(f32[128,512]{1,0:T(8,128)S(1)} %kelvins.1.refs_0_), channel_id=1, source_target_pairs={{0,1},{1,0},{2,3},{3,2},{4,5},{5,4},{6,7},{7,6},{8,9},{9,8},{10,11... | collective-permute-start | bytes 786440 | tf_op jit(solution)/shard_map/ppermute | solution.py:593
  109.8 1.9 %collective-permute-start.8 = (f32[128,512]{1,0:T(8,128)S(1)}, f32[128,512]{1,0:T(8,128)S(1)}, u32[]{:S(2)}, u32[]{:S(2)}) collective-permute-start(f32[128,512]{1,0:T(8,128)S(1)} %collective-permute-done.6.refs_1_), channel_id=1, source_target_pairs={{0,1},{1,0},{2,3},{3,2},{4,5},{5,4},{6,7},{7,6},{8,9},{9,8},{10,11... | collective-permute-start | bytes 786440 | tf_op jit(solution)/shard_map/ppermute | solution.py:593
  111.7 2.2 %copy-start = (f32[64,8,16,128]{3,2,1,0:T(8,128)S(1)}, f32[64,8,16,128]{3,2,1,0:T(8,128)}, u32[]{:S(2)}) copy-start(f32[64,8,16,128]{3,2,1,0:T(8,128)} %get-tuple-element.52.swept) | copy-start | bytes 12582916

commit v15 on v13

--- a/solution.py
+++ b/solution.py
@@ -320,7 +320,7 @@
                 plane[at_high, :] = high
         return carry
 
-    lax.fori_loop(0, block // 2, one_pair, 0)
+    lax.fori_loop(0, block // 2, one_pair, 0, unroll=2)
 
     @pl.when(step == blocks - 1)
     def _():
@@ -603,7 +603,7 @@
             out_specs=[VMEM] * len(out_shapes),
             out_shape=out_shapes,
             scratch_shapes=list(scratches),
-            compiler_params=PARAMS,
+            compiler_params=LARGE if name in ("density_parts", "density_totals", "enter", "kelvins") else PARAMS,
             name=name,
         )(*args)
 

time: 122 us -> 122 us (level)
  waiting for transfers between devices: 39.7 us -> 37.1 us
  Pallas kernels: 39.2 us -> 41 us
    pallas_call x7, Pallas kernels: 8.51 us -> 11.7 us  [call(): pl.pallas_call(kernel, in_specs=in_specs, out_specs=[VMEM] * len(out_shap...]
    ppermute x13, waiting for transfers between devices: 27.2 us -> 24.6 us  [swap(): lax.ppermute(array, axis, [(i, i ^ by) for i in range(lax.axis_size(axis))])]
    pallas_call x1, Pallas kernels: 16.8 us -> 15.3 us  [local(): pl.pallas_call(functools.partial(sweeps_kernel, (block, blocks, depth, wi...]
    unnamed x46 -> x56, local copies, waits for them, and re-layouts: 9.67 us -> 10.6 us
  transfers between devices with their start and end apart: 15 -> 15, of which waited for: 8 -> 6; matrix products, arithmetic and copies ran while one was open for 3% -> 3% of each run, Pallas kernels for 13% -> 14%
where the time goes in v15:
time: 122 us; the launch traced here: 121 us
  Pallas kernels  41 us (34%)
  waiting for transfers between devices  37.1 us (30%)
  starting transfers between devices  27.5 us (23%)
  local copies, waits for them, and re-layouts  11 us (9%)
  other arithmetic  3.49 us (3%)
    ppermute x13, waiting for transfers between devices, swap(): lax.ppermute(array, axis, [(i, i ^ by) for i in range(lax.axis_size(axis))])  24.6 us
    ppermute x13, starting transfers between devices, swap(): lax.ppermute(array, axis, [(i, i ^ by) for i in range(lax.axis_size(axis))])  17.8 us
    pallas_call x1, Pallas kernels, local(): pl.pallas_call(functools.partial(sweeps_kernel, (block, blocks, depth, wi...  15.3 us
    all_to_all x1, waiting for transfers between devices, local(): gathered = lax.all_to_all(copies, 'slab', 0, 0)  12.5 us
    pallas_call x7, Pallas kernels, call(): pl.pallas_call(kernel, in_specs=in_specs, out_specs=[VMEM] * len(out_shap...  11.7 us
    unnamed x56, local copies, waits for them, and re-layouts  10.6 us
    pallas_call x1, Pallas kernels, local(): pl.pallas_call(functools.partial(warm_kernel, (block, depth, width_y, wid...  8.79 us
    all_to_all x1, starting transfers between devices, local(): summed = lax.all_to_all(parts, 'slab', 0, 0)  5.99 us
  transfers between devices with their start and end apart: 15, of which 6 were waited for; matrix products, arithmetic and copies ran while one was open for 3% of the time, Pallas kernels for 14%

profile of v15, /device:TPU:0, one launch (start us, length us, event | category | flops | bytes accessed | tf_op | source)
XLA Modules:
  0.0 120.9 jit_solution(13061367156628798466)
XLA Ops:
  0.6 0.0 copy-start.24
  0.6 0.0 copy-start.23
  0.7 0.0 copy-start.27
  0.7 0.0 copy-start.22
  0.7 0.0 copy-start.26
  0.7 0.0 copy-start.25
  0.7 0.6 pad_add_fusion.meta
  1.3 15.3 %sweeps.1 = (f32[64,8,16,128]{3,2,1,0:T(8,128)}, f32[8,512]{1,0:T(8,128)}, f32[3,256,128]{2,1,0:T(8,128)}, f32[3,256,128]{2,1,0:T(8,128)}, f32[3,256,128]{2,1,0:...) custom-call(s32[2]{0:T(128)} %pad_add_fusion.meta, s32[64]{0:T(128)} %labels.1, ...), custom_call_target="tpu_custom_call" | custom-call | tf_op jit(solution)/shard_map/sweeps/pallas_call | solution.py:614
  16.6 3.0 %collective-permute-start.2 = (f32[3,256,128]{2,1,0:T(8,128)}, f32[3,256,128]{2,1,0:T(8,128)S(1)}, u32[]{:S(2)}, u32[]{:S(2)}) collective-permute-start(f32[3,256,128]{2,1,0:T(8,128)} %get-tuple-element.41), channel_id=1, source_target_pairs={{0,4},{4,0},{8,12},{12,8},{16,20},{20,16},{24,28},{28,24},{1,5},{5... | collective-permute-start | bytes 1179656 | tf_op jit(solution)/shard_map/ppermute | solution.py:597
  19.6 1.6 %collective-permute-start.3 = (f32[3,256,128]{2,1,0:T(8,128)}, f32[3,256,128]{2,1,0:T(8,128)S(1)}, u32[]{:S(2)}, u32[]{:S(2)}) collective-permute-start(f32[3,256,128]{2,1,0:T(8,128)} %get-tuple-element.42), channel_id=1, source_target_pairs={{0,8},{4,12},{8,0},{12,4},{16,24},{20,28},{24,16},{28,20},{1,9},{5... | collective-permute-start | bytes 1179656 | tf_op jit(solution)/shard_map/ppermute | solution.py:597
  21.2 0.0 collective-permute-start.4
  21.3 0.1 select_reduce_fusion
  21.4 0.7 fusion.20
  22.1 0.1 fusion.7
  22.3 1.4 %collective-permute-done.other = f32[2,3,64,512]{3,2,1,0:T(8,128)S(1)} collective-permute-done((f32[2,3,64,512]{3,2,1,0:T(8,128)}, f32[2,3,64,512]{3,2,1,0:T(8,128)S(1)}, u32[]{:S(2)}, u32[]{:S(2)}) %collective-permute-start) | collective-permute-done | bytes 786464 | tf_op jit(solution)/shard_map/ppermute | solution.py:597
  23.7 1.1 copy-done.2
  24.8 0.1 density_split.1
  24.9 0.7 copy-done.5
  25.7 1.9 %collective-permute-start.1 = (f32[1,3,64,512]{3,2,1,0:T(8,128)S(1)}, f32[1,3,64,512]{3,2,1,0:T(8,128)S(1)}, u32[]{:S(2)}, u32[]{:S(2)}) collective-permute-start(f32[1,3,64,512]{3,2,1,0:T(8,128)S(1)} %get-tuple-element.39), channel_id=1, source_target_pairs={{0,2},{1,3},{2,0},{3,1},{4,6},{5,7},{6,4},{7,5},{8,10},{9,11},{10,... | collective-permute-start | bytes 1179656 | tf_op jit(solution)/shard_map/ppermute | solution.py:597
  27.5 0.1 copy.14
  27.6 0.1 copy.15.kinds
  27.7 0.8 heat_matrices.1
  28.5 0.6 copy-done.12
  29.2 0.6 copy-done.15
  29.9 1.9 %pad_maximum_fusion.1.sums = f32[2]{0:T(128)} fusion(f32[1]{0:T(128)} %bitcast.36, f32[1]{0:T(128)} %bitcast.35), kind=kLoop, calls=%fused_computation.35 | loop fusion | flops 2 | bytes 16 | tf_op jit(solution)/shard_map/stack | solution.py:585
  31.8 0.0 collective-permute-done.2.refs_1_
  31.8 0.0 collective-permute-done.3.refs_2_
  31.9 6.7 %collective-permute-done.4.refs_3_ = f32[3,256,128]{2,1,0:T(8,128)S(1)} collective-permute-done((f32[3,256,128]{2,1,0:T(8,128)}, f32[3,256,128]{2,1,0:T(8,128)S(1)}, u32[]{:S(2)}, u32[]{:S(2)}) %collective-permute-start.4) | collective-permute-done | bytes 393248 | tf_op jit(solution)/shard_map/ppermute | solution.py:597
  38.6 1.0 copy-done.4
  39.6 1.2 compose.1
  40.8 1.2 copy-done
  42.0 0.8 copy-done.19
  42.8 1.9 %density_parts.1 = f32[8,3,8,512]{3,2,1,0:T(8,128)} custom-call(f32[1,3,64,512]{3,2,1,0:T(8,128)} %copy-done.5, f32[1,3,64,512]{3,2,1,0:T(8,128)} %copy-done.19), custom_call_target="tpu_custom_call" | custom-call | tf_op jit(solution)/shard_map/density_parts/pallas_call | solution.py:600
  44.7 6.0 %all-to-all-start = ((f32[8,3,8,512]{3,2,1,0:T(8,128)}), f32[8,3,8,512]{3,2,1,0:T(8,128)S(1)}, u32[]{:S(2)}, u32[]{:S(2)}) async-start(f32[8,3,8,512]{3,2,1,0:T(8,128)} %density_parts.1), calls=%async_computation | async-start | bytes 786432 | tf_op jit(solution)/shard_map/all_to_all | solution.py:680
  50.7 2.9 %collective-permute-start.5 = (f32[256,128]{1,0:T(8,128)S(1)}, f32[256,128]{1,0:T(8,128)S(1)}, u32[]{:S(2)}, u32[]{:S(2)}) collective-permute-start(f32[256,128]{1,0:T(8,128)S(1)} %get-tuple-element.64.refs_0_), channel_id=1, source_target_pairs={{0,16},{4,20},{8,24},{12,28},{16,0},{20,4},{24,8},{28,12},{1,17},{... | collective-permute-start | bytes 393224 | tf_op jit(solution)/shard_map/ppermute | solution.py:597
  53.6 13.2 %collective-permute-done.5.refs_1_ = f32[256,128]{1,0:T(8,128)S(1)} collective-permute-done((f32[256,128]{1,0:T(8,128)S(1)}, f32[256,128]{1,0:T(8,128)S(1)}, u32[]{:S(2)}, u32[]{:S(2)}) %collective-permute-start.5) | collective-permute-done | bytes 131104 | tf_op jit(solution)/shard_map/ppermute | solution.py:597
  66.7 0.0 all-to-all-done.parts
  66.8 0.8 copy-done.17
  67.5 1.8 %density_totals.1 = (f32[8,2,8,512]{3,2,1,0:T(8,128)}, f32[8,512]{1,0:T(8,128)}) custom-call(f32[2]{0:T(128)} %pad_maximum_fusion.1.sums, f32[8,3,8,512]{3,2,1,0:T(8,128)} %copy-done.17, f32[8,512]{1,0:T(8,128)} %get-tuple-element.57.before), custom_call_target="tpu_custom_call" | custom-call | tf_op jit(solution)/shard_map/density_totals/pallas_call | solution.py:600
  69.3 3.7 %all-to-all-start.1 = ((f32[8,2,8,512]{3,2,1,0:T(8,128)}), f32[8,2,8,512]{3,2,1,0:T(8,128)S(1)}, u32[]{:S(2)}, u32[]{:S(2)}) async-start(f32[8,2,8,512]{3,2,1,0:T(8,128)} %get-tuple-element.58), calls=%async_computation.1 | async-start | bytes 524288 | tf_op jit(solution)/shard_map/all_to_all | solution.py:692
  73.0 2.9 %collective-permute-start.9 = (f32[2,256,128]{2,1,0:T(8,128)S(1)}, f32[2,256,128]{2,1,0:T(8,128)S(1)}, u32[]{:S(2)}, u32[]{:S(2)}) collective-permute-start(f32[2,256,128]{2,1,0:T(8,128)S(1)} %get-tuple-element.66.refs_2_), channel_id=1, source_target_pairs={{0,16},{4,20},{8,24},{12,28},{16,0},{20,4},{24,8},{28,12},{1,17},{... | collective-permute-start | bytes 786440 | tf_op jit(solution)/shard_map/ppermute | solution.py:597
  75.9 12.5 %all-to-all-done.1.gathered = f32[8,2,8,512]{3,2,1,0:T(8,128)S(1)} async-done(((f32[8,2,8,512]{3,2,1,0:T(8,128)}), f32[8,2,8,512]{3,2,1,0:T(8,128)S(1)}, u32[]{:S(2)}, u32[]{:S(2)}) %all-to-all-start.1) | async-done | bytes 262176 | tf_op jit(solution)/shard_map/all_to_all | solution.py:692
  88.4 0.7 copy-done.18
  89.1 2.5 %kelvins.1.refs_0_ = f32[128,512]{1,0:T(8,128)} custom-call(s32[2]{0:T(128)} %pad_add_fusion.meta, f32[2]{0:T(128)} %pad_maximum_fusion.1.sums, f32[8,2,8,512]{3,2,1,0:T(8,128)} %copy-done.18, f32[8,512]{1,0:T(8,128)} %get-tuple-element.59.late, f32[144,128]{1,0:T(8,128)} %copy-done.12, f32[40,128]{1,0:T(8,128)} %copy-done.15), custom_call_target="tpu_custom_call" | custom-call | tf_op jit(solution)/shard_map/kelvins/pallas_call | solution.py:600
  91.6 1.5 %collective-permute-start.6 = (f32[128,512]{1,0:T(8,128)}, f32[128,512]{1,0:T(8,128)S(1)}, u32[]{:S(2)}, u32[]{:S(2)}) collective-permute-start(f32[128,512]{1,0:T(8,128)} %kelvins.1.refs_0_), channel_id=1, source_target_pairs={{0,2},{1,3},{2,0},{3,1},{4,6},{5,7},{6,4},{7,5},{8,10},{9,11},{10,... | collective-permute-start | bytes 786440 | tf_op jit(solution)/shard_map/ppermute | solution.py:597
  93.1 0.0 collective-permute-done.9.refs_3_
  93.1 0.7 copy-done.20
  93.8 3.4 %enter.1 = (f32[3,256,128]{2,1,0:T(8,128)}, f32[3,256,128]{2,1,0:T(8,128)}, f32[3,256,128]{2,1,0:T(8,128)}, f32[3,256,128]{2,1,0:T(8,128)}) custom-call(s32[2]{0:T(128)} %pad_add_fusion.meta, f32[10,64]{1,0:T(8,128)} %copy-done.7, s32[5,64]{1,0:T(8,128)} %copy-done.10, f32[4,3,256,128]{3,2,1,0:T(8,128)} %copy-done, f32[256,128]{1,0:T(8,128)} %copy-done.9, ...), custom_call_target="tpu_custom_call" | custom-call | tf_op jit(solution)/shard_map/enter/pallas_call | solution.py:600
  97.2 1.4 %collective-permute-start.10 = (f32[3,256,128]{2,1,0:T(8,128)}, f32[3,256,128]{2,1,0:T(8,128)S(1)}, u32[]{:S(2)}, u32[]{:S(2)}) collective-permute-start(f32[3,256,128]{2,1,0:T(8,128)} %get-tuple-element.68), channel_id=1, source_target_pairs={{0,4},{4,0},{8,12},{12,8},{16,20},{20,16},{24,28},{28,24},{1,5},{5... | collective-permute-start | bytes 1179656 | tf_op jit(solution)/shard_map/ppermute | solution.py:597
  98.6 0.0 collective-permute-start.11
  98.6 2.1 %collective-permute-start.12 = (f32[3,256,128]{2,1,0:T(8,128)}, f32[3,256,128]{2,1,0:T(8,128)S(1)}, u32[]{:S(2)}, u32[]{:S(2)}) collective-permute-start(f32[3,256,128]{2,1,0:T(8,128)} %get-tuple-element.70), channel_id=1, source_target_pairs={{0,12},{4,8},{8,4},{12,0},{16,28},{20,24},{24,20},{28,16},{1,13},{... | collective-permute-start | bytes 1179656 | tf_op jit(solution)/shard_map/ppermute | solution.py:597
  100.7 0.0 collective-permute-start.7
  100.7 0.0 collective-permute-done.6.refs_1_
  100.7 0.5 collective-permute-start.8
  101.2 0.1 copy.16.kinds
  101.3 1.5 %collective-permute-done.7.refs_2_ = f32[128,512]{1,0:T(8,128)S(1)} collective-permute-done((f32[128,512]{1,0:T(8,128)}, f32[128,512]{1,0:T(8,128)S(1)}, u32[]{:S(2)}, u32[]{:S(2)}) %collective-permute-start.7) | collective-permute-done | bytes 262176 | tf_op jit(solution)/shard_map/ppermute | solution.py:597
  102.8 0.0 collective-permute-done.8.refs_3_
  102.8 0.9 copy-done.1
  103.7 0.7 copy-done.8
  104.4 0.7 copy-done.11
  105.1 8.8 %warm.1 = (f32[64,8,16,128]{3,2,1,0:T(8,128)S(1)}, f32[128,128]{1,0:T(8,128)}) custom-call(s32[2]{0:T(128)S(1)} %copy-done.14, f32[10,64]{1,0:T(8,128)S(1)} %copy-done.8, s32[5,64]{1,0:T(8,128)S(1)} %copy-done.11, f32[6,16]{1,0:T(8,128)S(1)} %copy.16.kinds, f32[2]{0:T(128)S(1)} %copy-done.16, f32[64,8,16,128]{3,2,1,0:T(8,128)} %get-tuple-element.52.swept, ...), custom_call_target="tpu_custom_call" | custom-call | tf_op jit(solution)/shard_map/warm/pallas_call | solution.py:727
  113.9 0.0 collective-permute-done.10.refs_1_
  113.9 1.8 %collective-permute-done.12.refs_3_ = f32[3,256,128]{2,1,0:T(8,128)S(1)} collective-permute-done((f32[3,256,128]{2,1,0:T(8,128)}, f32[3,256,128]{2,1,0:T(8,128)S(1)}, u32[]{:S(2)}, u32[]{:S(2)}) %collective-permute-start.12) | collective-permute-done | bytes 393248 | tf_op jit(solution)/shard_map/ppermute | solution.py:597
  115.7 5.2 %inflow.1 = f32[64,8,16,128]{3,2,1,0:T(8,128)} custom-call(s32[2]{0:T(128)S(1)} %copy-done.14, f32[10,64]{1,0:T(8,128)S(1)} %copy-done.8, s32[5,64]{1,0:T(8,128)S(1)} %copy-done.11, f32[64,8,16,128]{3,2,1,0:T(8,128)S(1)} %get-tuple-element.62.warm, f32[3,256,128]{2,1,0:T(8,128)S(1)} %copy-done.3, f32[3,256,128]{2,1,0:T(8,128)S(1)} %collective-permute-done.10.refs_1_, ...), custom_call_target="tpu_custom_call" | custom-call | tf_op jit(solution)/shard_map/inflow/pallas_call | solution.py:740
  (54 shorter events, 0.4 us)
Async XLA Ops:
  0.6 20.6 %copy-start.24 = (f32[8]{0:T(128)S(1)}, f32[8]{0:T(128)}, u32[]{:S(2)}) copy-start(f32[8]{0:T(128)} %refs_0_.1) | copy-start | bytes 100
  0.6 20.6 %copy-start.23 = (f32[8]{0:T(128)S(1)}, f32[8]{0:T(128)}, u32[]{:S(2)}) copy-start(f32[8]{0:T(128)} %refs_1_.1) | copy-start | bytes 100
  0.7 20.6 %copy-start.27 = (f32[8]{0:T(128)S(1)}, f32[8]{0:T(128)}, u32[]{:S(2)}) copy-start(f32[8]{0:T(128)} %refs_2_.1) | copy-start | bytes 100
  0.7 20.6 %copy-start.22 = (f32[8]{0:T(128)S(1)}, f32[8]{0:T(128)}, u32[]{:S(2)}) copy-start(f32[8]{0:T(128)} %refs_3_.1) | copy-start | bytes 100
  0.7 20.6 %copy-start.26 = (f32[8]{0:T(128)S(1)}, f32[8]{0:T(128)}, u32[]{:S(2)}) copy-start(f32[8]{0:T(128)} %refs_4_.1) | copy-start | bytes 100
  0.7 20.5 %copy-start.25 = (s32[64]{0:T(128)S(1)}, s32[64]{0:T(128)}, u32[]{:S(2)}) copy-start(s32[64]{0:T(128)} %labels.1) | copy-start | bytes 772
  1.3 26.5 %copy-start.13 = (s32[2]{0:T(128)S(1)}, s32[2]{0:T(128)}, u32[]{:S(2)}) copy-start(s32[2]{0:T(128)} %pad_add_fusion.meta) | copy-start | bytes 28
  16.6 15.2 %collective-permute-start.2 = (f32[3,256,128]{2,1,0:T(8,128)}, f32[3,256,128]{2,1,0:T(8,128)S(1)}, u32[]{:S(2)}, u32[]{:S(2)}) collective-permute-start(f32[3,256,128]{2,1,0:T(8,128)} %get-tuple-element.41), channel_id=1, source_target_pairs={{0,4},{4,0},{8,12},{12,8},{16,20},{20,16},{24,28},{28,24},{1,5},{5... | collective-permute-start | bytes 1179656 | tf_op jit(solution)/shard_map/ppermute | solution.py:597
  19.6 12.3 %collective-permute-start.3 = (f32[3,256,128]{2,1,0:T(8,128)}, f32[3,256,128]{2,1,0:T(8,128)S(1)}, u32[]{:S(2)}, u32[]{:S(2)}) collective-permute-start(f32[3,256,128]{2,1,0:T(8,128)} %get-tuple-element.42), channel_id=1, source_target_pairs={{0,8},{4,12},{8,0},{12,4},{16,24},{20,28},{24,16},{28,20},{1,9},{5... | collective-permute-start | bytes 1179656 | tf_op jit(solution)/shard_map/ppermute | solution.py:597
  21.2 17.4 %collective-permute-start.4 = (f32[3,256,128]{2,1,0:T(8,128)}, f32[3,256,128]{2,1,0:T(8,128)S(1)}, u32[]{:S(2)}, u32[]{:S(2)}) collective-permute-start(f32[3,256,128]{2,1,0:T(8,128)} %get-tuple-element.43), channel_id=1, source_target_pairs={{0,12},{4,8},{8,4},{12,0},{16,28},{20,24},{24,20},{28,16},{1,13},{... | collective-permute-start | bytes 1179656 | tf_op jit(solution)/shard_map/ppermute | solution.py:597
  21.2 2.5 %collective-permute-start = (f32[2,3,64,512]{3,2,1,0:T(8,128)}, f32[2,3,64,512]{3,2,1,0:T(8,128)S(1)}, u32[]{:S(2)}, u32[]{:S(2)}) collective-permute-start(f32[2,3,64,512]{3,2,1,0:T(8,128)} %get-tuple-element.38), channel_id=1, source_target_pairs={{0,1},{1,0},{2,3},{3,2},{4,5},{5,4},{6,7},{7,6},{8,9},{9,8},{10,11... | collective-permute-start | bytes 2359304 | tf_op jit(solution)/shard_map/ppermute | solution.py:597
  23.7 1.1 copy-start.2
  24.9 0.8 copy-start.5
  25.7 77.1 %copy-start.14 = (s32[2]{0:T(128)S(1)}, s32[2]{0:T(128)}, u32[]{:S(2)}) copy-start(s32[2]{0:T(128)} %pad_add_fusion.meta) | copy-start | bytes 28
  25.7 16.3 %collective-permute-start.1 = (f32[1,3,64,512]{3,2,1,0:T(8,128)S(1)}, f32[1,3,64,512]{3,2,1,0:T(8,128)S(1)}, u32[]{:S(2)}, u32[]{:S(2)}) collective-permute-start(f32[1,3,64,512]{3,2,1,0:T(8,128)S(1)} %get-tuple-element.39), channel_id=1, source_target_pairs={{0,2},{1,3},{2,0},{3,1},{4,6},{5,7},{6,4},{7,5},{8,10},{9,11},{10,... | collective-permute-start | bytes 1179656 | tf_op jit(solution)/shard_map/ppermute | solution.py:597
  28.5 0.6 copy-start.12
  29.2 0.6 copy-start.15
  29.8 63.3 %copy-start.10 = (s32[5,64]{1,0:T(8,128)}, s32[5,64]{1,0:T(8,128)S(1)}, u32[]{:S(2)}) copy-start(s32[5,64]{1,0:T(8,128)S(1)} %stack.143.ints) | copy-start | bytes 3844
  29.9 63.2 %copy-start.7 = (f32[10,64]{1,0:T(8,128)}, f32[10,64]{1,0:T(8,128)S(1)}, u32[]{:S(2)}) copy-start(f32[10,64]{1,0:T(8,128)S(1)} %stack.136.floats) | copy-start | bytes 7684
  31.8 71.0 %copy-start.16 = (f32[2]{0:T(128)S(1)}, f32[2]{0:T(128)}, u32[]{:S(2)}) copy-start(f32[2]{0:T(128)} %pad_maximum_fusion.1.sums) | copy-start | bytes 28
  38.6 1.0 copy-start.4
  40.8 1.2 copy-start
  42.0 51.2 %copy-start.6 = (f32[2,256,128]{2,1,0:T(8,128)}, f32[2,256,128]{2,1,0:T(8,128)S(1)}, u32[]{:S(2)}) copy-start(f32[2,256,128]{2,1,0:T(8,128)S(1)} %get-tuple-element.66.refs_2_) | copy-start | bytes 786436
  42.0 51.2 %copy-start.9 = (f32[256,128]{1,0:T(8,128)}, f32[256,128]{1,0:T(8,128)S(1)}, u32[]{:S(2)}) copy-start(f32[256,128]{1,0:T(8,128)S(1)} %get-tuple-element.64.refs_0_) | copy-start | bytes 393220
  42.0 0.8 copy-start.19
  44.7 22.1 %all-to-all-start = ((f32[8,3,8,512]{3,2,1,0:T(8,128)}), f32[8,3,8,512]{3,2,1,0:T(8,128)S(1)}, u32[]{:S(2)}, u32[]{:S(2)}) async-start(f32[8,3,8,512]{3,2,1,0:T(8,128)} %density_parts.1), calls=%async_computation | async-start | bytes 786432 | tf_op jit(solution)/shard_map/all_to_all | solution.py:680
  50.7 16.1 %collective-permute-start.5 = (f32[256,128]{1,0:T(8,128)S(1)}, f32[256,128]{1,0:T(8,128)S(1)}, u32[]{:S(2)}, u32[]{:S(2)}) collective-permute-start(f32[256,128]{1,0:T(8,128)S(1)} %get-tuple-element.64.refs_0_), channel_id=1, source_target_pairs={{0,16},{4,20},{8,24},{12,28},{16,0},{20,4},{24,8},{28,12},{1,17},{... | collective-permute-start | bytes 393224 | tf_op jit(solution)/shard_map/ppermute | solution.py:597
  66.7 26.4 %copy-start.21 = (f32[256,128]{1,0:T(8,128)}, f32[256,128]{1,0:T(8,128)S(1)}, u32[]{:S(2)}) copy-start(f32[256,128]{1,0:T(8,128)S(1)} %collective-permute-done.5.refs_1_) | copy-start | bytes 393220
  66.8 0.8 copy-start.17
  69.3 19.1 %all-to-all-start.1 = ((f32[8,2,8,512]{3,2,1,0:T(8,128)}), f32[8,2,8,512]{3,2,1,0:T(8,128)S(1)}, u32[]{:S(2)}, u32[]{:S(2)}) async-start(f32[8,2,8,512]{3,2,1,0:T(8,128)} %get-tuple-element.58), calls=%async_computation.1 | async-start | bytes 524288 | tf_op jit(solution)/shard_map/all_to_all | solution.py:692
  73.0 20.1 %collective-permute-start.9 = (f32[2,256,128]{2,1,0:T(8,128)S(1)}, f32[2,256,128]{2,1,0:T(8,128)S(1)}, u32[]{:S(2)}, u32[]{:S(2)}) collective-permute-start(f32[2,256,128]{2,1,0:T(8,128)S(1)} %get-tuple-element.66.refs_2_), channel_id=1, source_target_pairs={{0,16},{4,20},{8,24},{12,28},{16,0},{20,4},{24,8},{28,12},{1,17},{... | collective-permute-start | bytes 786440 | tf_op jit(solution)/shard_map/ppermute | solution.py:597
  88.4 0.7 copy-start.18
  91.6 9.1 %collective-permute-start.6 = (f32[128,512]{1,0:T(8,128)}, f32[128,512]{1,0:T(8,128)S(1)}, u32[]{:S(2)}, u32[]{:S(2)}) collective-permute-start(f32[128,512]{1,0:T(8,128)} %kelvins.1.refs_0_), channel_id=1, source_target_pairs={{0,2},{1,3},{2,0},{3,1},{4,6},{5,7},{6,4},{7,5},{8,10},{9,11},{10,... | collective-permute-start | bytes 786440 | tf_op jit(solution)/shard_map/ppermute | solution.py:597
  93.1 0.7 copy-start.20
  97.2 16.7 %collective-permute-start.10 = (f32[3,256,128]{2,1,0:T(8,128)}, f32[3,256,128]{2,1,0:T(8,128)S(1)}, u32[]{:S(2)}, u32[]{:S(2)}) collective-permute-start(f32[3,256,128]{2,1,0:T(8,128)} %get-tuple-element.68), channel_id=1, source_target_pairs={{0,4},{4,0},{8,12},{12,8},{16,20},{20,16},{24,28},{28,24},{1,5},{5... | collective-permute-start | bytes 1179656 | tf_op jit(solution)/shard_map/ppermute | solution.py:597
  98.6 15.3 %collective-permute-start.11 = (f32[3,256,128]{2,1,0:T(8,128)}, f32[3,256,128]{2,1,0:T(8,128)S(1)}, u32[]{:S(2)}, u32[]{:S(2)}) collective-permute-start(f32[3,256,128]{2,1,0:T(8,128)} %get-tuple-element.69), channel_id=1, source_target_pairs={{0,8},{4,12},{8,0},{12,4},{16,24},{20,28},{24,16},{28,20},{1,9},{5... | collective-permute-start | bytes 1179656 | tf_op jit(solution)/shard_map/ppermute | solution.py:597
  98.6 17.1 %collective-permute-start.12 = (f32[3,256,128]{2,1,0:T(8,128)}, f32[3,256,128]{2,1,0:T(8,128)S(1)}, u32[]{:S(2)}, u32[]{:S(2)}) collective-permute-start(f32[3,256,128]{2,1,0:T(8,128)} %get-tuple-element.70), channel_id=1, source_target_pairs={{0,12},{4,8},{8,4},{12,0},{16,28},{20,24},{24,20},{28,16},{1,13},{... | collective-permute-start | bytes 1179656 | tf_op jit(solution)/shard_map/ppermute | solution.py:597
  100.7 2.0 %collective-permute-start.7 = (f32[128,512]{1,0:T(8,128)}, f32[128,512]{1,0:T(8,128)S(1)}, u32[]{:S(2)}, u32[]{:S(2)}) collective-permute-start(f32[128,512]{1,0:T(8,128)} %kelvins.1.refs_0_), channel_id=1, source_target_pairs={{0,1},{1,0},{2,3},{3,2},{4,5},{5,4},{6,7},{7,6},{8,9},{9,8},{10,11... | collective-permute-start | bytes 786440 | tf_op jit(solution)/shard_map/ppermute | solution.py:597
  100.7 2.0 %collective-permute-start.8 = (f32[128,512]{1,0:T(8,128)S(1)}, f32[128,512]{1,0:T(8,128)S(1)}, u32[]{:S(2)}, u32[]{:S(2)}) collective-permute-start(f32[128,512]{1,0:T(8,128)S(1)} %collective-permute-done.6.refs_1_), channel_id=1, source_target_pairs={{0,1},{1,0},{2,3},{3,2},{4,5},{5,4},{6,7},{7,6},{8,9},{9,8},{10,11... | collective-permute-start | bytes 786440 | tf_op jit(solution)/shard_map/ppermute | solution.py:597
  102.8 1.0 copy-start.1
  103.7 0.7 copy-start.8
  104.4 0.7 copy-start.11
  105.1 10.6 %copy-start.3 = (f32[3,256,128]{2,1,0:T(8,128)S(1)}, f32[3,256,128]{2,1,0:T(8,128)}, u32[]{:S(2)}) copy-start(f32[3,256,128]{2,1,0:T(8,128)} %get-tuple-element.67.refs_0_) | copy-start | bytes 1179652

commit v16 on v15

--- a/solution.py
+++ b/solution.py
@@ -603,7 +603,7 @@
             out_specs=[VMEM] * len(out_shapes),
             out_shape=out_shapes,
             scratch_shapes=list(scratches),
-            compiler_params=LARGE if name in ("density_parts", "density_totals", "enter", "kelvins") else PARAMS,
+            compiler_params=PARAMS,
             name=name,
         )(*args)
 

time: 122 us -> 120 us (0.984)
  Pallas kernels: 41 us -> 37.7 us
  waiting for transfers between devices: 37.1 us -> 39.6 us
    pallas_call x7, Pallas kernels: 11.7 us -> 8.51 us  [call(): pl.pallas_call(kernel, in_specs=in_specs, out_specs=[VMEM] * len(out_shap...]
    ppermute x13, waiting for transfers between devices: 24.6 us -> 27.2 us  [swap(): lax.ppermute(array, axis, [(i, i ^ by) for i in range(lax.axis_size(axis))])]
    unnamed x56 -> x46, local copies, waits for them, and re-layouts: 10.6 us -> 9.67 us
  transfers between devices with their start and end apart: 15 -> 15, of which waited for: 6 -> 8; matrix products, arithmetic and copies ran while one was open for 3% -> 3% of each run, Pallas kernels for 14% -> 13%
where the time goes in v16:
time: 120 us; the launch traced here: 119 us
  waiting for transfers between devices  39.6 us (33%)
  Pallas kernels  37.7 us (31%)
  starting transfers between devices  27.8 us (23%)
  local copies, waits for them, and re-layouts  10 us (8%)
  other arithmetic  3.41 us (3%)
    ppermute x13, waiting for transfers between devices, swap(): lax.ppermute(array, axis, [(i, i ^ by) for i in range(lax.axis_size(axis))])  27.2 us
    ppermute x13, starting transfers between devices, swap(): lax.ppermute(array, axis, [(i, i ^ by) for i in range(lax.axis_size(axis))])  17.9 us
    pallas_call x1, Pallas kernels, local(): pl.pallas_call(functools.partial(sweeps_kernel, (block, blocks, depth, wi...  15.3 us
    all_to_all x1, waiting for transfers between devices, local(): gathered = lax.all_to_all(copies, 'slab', 0, 0)  12.5 us
    unnamed x46, local copies, waits for them, and re-layouts  9.67 us
    pallas_call x1, Pallas kernels, local(): pl.pallas_call(functools.partial(warm_kernel, (block, depth, width_y, wid...  8.74 us
    pallas_call x7, Pallas kernels, call(): pl.pallas_call(kernel, in_specs=in_specs, out_specs=[VMEM] * len(out_shap...  8.51 us
    all_to_all x1, starting transfers between devices, local(): summed = lax.all_to_all(parts, 'slab', 0, 0)  6.12 us
  transfers between devices with their start and end apart: 15, of which 8 were waited for; matrix products, arithmetic and copies ran while one was open for 3% of the time, Pallas kernels for 13%

profile of v16, /device:TPU:0, one launch (start us, length us, event | category | flops | bytes accessed | tf_op | source)
XLA Modules:
  0.0 119.4 jit_solution(14919302333081603094)
XLA Ops:
  0.6 0.0 copy-start.19
  0.6 0.0 copy-start.18
  0.7 0.0 copy-start.22
  0.7 0.0 copy-start.17
  0.7 0.0 copy-start.21
  0.7 0.0 copy-start.20
  0.7 0.6 pad_add_fusion.meta
  1.3 15.3 %sweeps.1 = (f32[64,8,16,128]{3,2,1,0:T(8,128)}, f32[8,512]{1,0:T(8,128)}, f32[3,256,128]{2,1,0:T(8,128)}, f32[3,256,128]{2,1,0:T(8,128)}, f32[3,256,128]{2,1,0:...) custom-call(s32[2]{0:T(128)} %pad_add_fusion.meta, s32[64]{0:T(128)} %labels.1, ...), custom_call_target="tpu_custom_call" | custom-call | tf_op jit(solution)/shard_map/sweeps/pallas_call | solution.py:614
  16.5 3.0 %collective-permute-start.2 = (f32[3,256,128]{2,1,0:T(8,128)}, f32[3,256,128]{2,1,0:T(8,128)S(1)}, u32[]{:S(2)}, u32[]{:S(2)}) collective-permute-start(f32[3,256,128]{2,1,0:T(8,128)} %get-tuple-element.41), channel_id=1, source_target_pairs={{0,4},{4,0},{8,12},{12,8},{16,20},{20,16},{24,28},{28,24},{1,5},{5... | collective-permute-start | bytes 1179656 | tf_op jit(solution)/shard_map/ppermute | solution.py:597
  19.6 1.6 %collective-permute-start.3 = (f32[3,256,128]{2,1,0:T(8,128)}, f32[3,256,128]{2,1,0:T(8,128)S(1)}, u32[]{:S(2)}, u32[]{:S(2)}) collective-permute-start(f32[3,256,128]{2,1,0:T(8,128)} %get-tuple-element.42), channel_id=1, source_target_pairs={{0,8},{4,12},{8,0},{12,4},{16,24},{20,28},{24,16},{28,20},{1,9},{5... | collective-permute-start | bytes 1179656 | tf_op jit(solution)/shard_map/ppermute | solution.py:597
  21.2 0.0 collective-permute-start.4
  21.2 0.0 collective-permute-start
  21.3 0.1 select_reduce_fusion
  21.4 0.7 fusion.20
  22.0 0.1 fusion.7
  22.3 1.4 %collective-permute-done.other = f32[2,3,64,512]{3,2,1,0:T(8,128)S(1)} collective-permute-done((f32[2,3,64,512]{3,2,1,0:T(8,128)}, f32[2,3,64,512]{3,2,1,0:T(8,128)S(1)}, u32[]{:S(2)}, u32[]{:S(2)}) %collective-permute-start) | collective-permute-done | bytes 786464 | tf_op jit(solution)/shard_map/ppermute | solution.py:597
  23.7 1.1 copy-done
  24.8 0.8 density_split.1
  25.6 1.9 %collective-permute-start.1 = (f32[1,3,64,512]{3,2,1,0:T(8,128)}, f32[1,3,64,512]{3,2,1,0:T(8,128)S(1)}, u32[]{:S(2)}, u32[]{:S(2)}) collective-permute-start(f32[1,3,64,512]{3,2,1,0:T(8,128)} %get-tuple-element.39), channel_id=1, source_target_pairs={{0,2},{1,3},{2,0},{3,1},{4,6},{5,7},{6,4},{7,5},{8,10},{9,11},{10,... | collective-permute-start | bytes 1179656 | tf_op jit(solution)/shard_map/ppermute | solution.py:597
  27.5 0.1 copy.14
  27.6 0.1 copy.15.kinds
  27.7 0.8 heat_matrices.1
  28.5 0.6 copy-done.6
  29.2 1.9 %pad_maximum_fusion.1.sums = f32[2]{0:T(128)} fusion(f32[1]{0:T(128)} %bitcast.36, f32[1]{0:T(128)} %bitcast.35), kind=kLoop, calls=%fused_computation.35 | loop fusion | flops 2 | bytes 16 | tf_op jit(solution)/shard_map/stack | solution.py:585
  31.1 0.0 collective-permute-done.2.refs_1_
  31.1 0.7 collective-permute-done.3.refs_2_
  31.8 6.8 %collective-permute-done.4.refs_3_ = f32[3,256,128]{2,1,0:T(8,128)S(1)} collective-permute-done((f32[3,256,128]{2,1,0:T(8,128)}, f32[3,256,128]{2,1,0:T(8,128)S(1)}, u32[]{:S(2)}, u32[]{:S(2)}) %collective-permute-start.4) | collective-permute-done | bytes 393248 | tf_op jit(solution)/shard_map/ppermute | solution.py:597
  38.6 1.0 copy-done.1
  39.6 1.2 compose.1
  40.8 0.7 copy-done.2
  41.5 0.6 copy-done.4
  42.1 0.0 collective-permute-done.1.other
  42.1 0.8 density_parts.1
  42.9 6.1 %all-to-all-start = ((f32[8,3,8,512]{3,2,1,0:T(8,128)}), f32[8,3,8,512]{3,2,1,0:T(8,128)S(1)}, u32[]{:S(2)}, u32[]{:S(2)}) async-start(f32[8,3,8,512]{3,2,1,0:T(8,128)} %density_parts.1), calls=%async_computation | async-start | bytes 786432 | tf_op jit(solution)/shard_map/all_to_all | solution.py:680
  49.0 2.9 %collective-permute-start.5 = (f32[256,128]{1,0:T(8,128)}, f32[256,128]{1,0:T(8,128)S(1)}, u32[]{:S(2)}, u32[]{:S(2)}) collective-permute-start(f32[256,128]{1,0:T(8,128)} %copy-done.4), channel_id=1, source_target_pairs={{0,16},{4,20},{8,24},{12,28},{16,0},{20,4},{24,8},{28,12},{1,17},{... | collective-permute-start | bytes 393224 | tf_op jit(solution)/shard_map/ppermute | solution.py:597
  52.0 13.2 %collective-permute-done.5.refs_1_ = f32[256,128]{1,0:T(8,128)S(1)} collective-permute-done((f32[256,128]{1,0:T(8,128)}, f32[256,128]{1,0:T(8,128)S(1)}, u32[]{:S(2)}, u32[]{:S(2)}) %collective-permute-start.5) | collective-permute-done | bytes 131104 | tf_op jit(solution)/shard_map/ppermute | solution.py:597
  65.1 0.0 all-to-all-done.parts
  65.1 0.7 copy-done.11
  65.9 0.7 copy-done.12
  66.5 1.3 %density_totals.1 = (f32[8,2,8,512]{3,2,1,0:T(8,128)}, f32[8,512]{1,0:T(8,128)S(1)}) custom-call(f32[2]{0:T(128)S(1)} %copy-done.12, f32[8,3,8,512]{3,2,1,0:T(8,128)S(1)} %all-to-all-done.parts, f32[8,512]{1,0:T(8,128)S(1)} %copy-done.11), custom_call_target="tpu_custom_call" | custom-call | tf_op jit(solution)/shard_map/density_totals/pallas_call | solution.py:600
  67.8 3.7 %all-to-all-start.1 = ((f32[8,2,8,512]{3,2,1,0:T(8,128)}), f32[8,2,8,512]{3,2,1,0:T(8,128)S(1)}, u32[]{:S(2)}, u32[]{:S(2)}) async-start(f32[8,2,8,512]{3,2,1,0:T(8,128)} %get-tuple-element.58), calls=%async_computation.1 | async-start | bytes 524288 | tf_op jit(solution)/shard_map/all_to_all | solution.py:692
  71.5 2.9 %collective-permute-start.9 = (f32[2,256,128]{2,1,0:T(8,128)}, f32[2,256,128]{2,1,0:T(8,128)S(1)}, u32[]{:S(2)}, u32[]{:S(2)}) collective-permute-start(f32[2,256,128]{2,1,0:T(8,128)} %copy-done.2), channel_id=1, source_target_pairs={{0,16},{4,20},{8,24},{12,28},{16,0},{20,4},{24,8},{28,12},{1,17},{... | collective-permute-start | bytes 786440 | tf_op jit(solution)/shard_map/ppermute | solution.py:597
  74.4 12.5 %all-to-all-done.1.gathered = f32[8,2,8,512]{3,2,1,0:T(8,128)S(1)} async-done(((f32[8,2,8,512]{3,2,1,0:T(8,128)}), f32[8,2,8,512]{3,2,1,0:T(8,128)S(1)}, u32[]{:S(2)}, u32[]{:S(2)}) %all-to-all-start.1) | async-done | bytes 262176 | tf_op jit(solution)/shard_map/all_to_all | solution.py:692
  86.9 0.9 copy-done.7
  87.8 0.7 copy-done.10
  88.5 0.7 copy-done.13
  89.2 1.4 %kelvins.1.refs_0_ = f32[128,512]{1,0:T(8,128)S(1)} custom-call(s32[2]{0:T(128)S(1)} %copy-done.8, f32[2]{0:T(128)S(1)} %copy-done.13, f32[8,2,8,512]{3,2,1,0:T(8,128)S(1)} %all-to-all-done.1.gathered, f32[8,512]{1,0:T(8,128)S(1)} %get-tuple-element.59.late, f32[144,128]{1,0:T(8,128)S(1)} %copy-done.7, f32[40,128]{1,0:T(8,128)S(1)} %copy-done.10), custom_call_target="tpu_custom_call" | custom-call | tf_op jit(solution)/shard_map/kelvins/pallas_call | solution.py:600
  90.5 1.6 %collective-permute-start.6 = (f32[128,512]{1,0:T(8,128)S(1)}, f32[128,512]{1,0:T(8,128)S(1)}, u32[]{:S(2)}, u32[]{:S(2)}) collective-permute-start(f32[128,512]{1,0:T(8,128)S(1)} %kelvins.1.refs_0_), channel_id=1, source_target_pairs={{0,2},{1,3},{2,0},{3,1},{4,6},{5,7},{6,4},{7,5},{8,10},{9,11},{10,... | collective-permute-start | bytes 786440 | tf_op jit(solution)/shard_map/ppermute | solution.py:597
  92.1 0.0 collective-permute-done.9.refs_3_
  92.2 0.9 copy-done.3
  93.1 0.9 copy-done.5
  94.0 2.2 %enter.1 = (f32[3,256,128]{2,1,0:T(8,128)S(1)}, f32[3,256,128]{2,1,0:T(8,128)}, f32[3,256,128]{2,1,0:T(8,128)}, f32[3,256,128]{2,1,0:T(8,128)S(1)}) custom-call(s32[2]{0:T(128)S(1)} %copy-done.8, f32[10,64]{1,0:T(8,128)S(1)} %stack.136.floats, s32[5,64]{1,0:T(8,128)S(1)} %stack.143.ints, f32[4,3,256,128]{3,2,1,0:T(8,128)S(1)} %get-tuple-element.63.effective, ...), custom_call_target="tpu_custom_call" | custom-call | tf_op jit(solution)/shard_map/enter/pallas_call | solution.py:600
  96.2 1.4 %collective-permute-start.10 = (f32[3,256,128]{2,1,0:T(8,128)}, f32[3,256,128]{2,1,0:T(8,128)S(1)}, u32[]{:S(2)}, u32[]{:S(2)}) collective-permute-start(f32[3,256,128]{2,1,0:T(8,128)} %get-tuple-element.68), channel_id=1, source_target_pairs={{0,4},{4,0},{8,12},{12,8},{16,20},{20,16},{24,28},{28,24},{1,5},{5... | collective-permute-start | bytes 1179656 | tf_op jit(solution)/shard_map/ppermute | solution.py:597
  97.6 0.0 collective-permute-start.11
  97.6 2.1 %collective-permute-start.12 = (f32[3,256,128]{2,1,0:T(8,128)S(1)}, f32[3,256,128]{2,1,0:T(8,128)S(1)}, u32[]{:S(2)}, u32[]{:S(2)}) collective-permute-start(f32[3,256,128]{2,1,0:T(8,128)S(1)} %get-tuple-element.70), channel_id=1, source_target_pairs={{0,12},{4,8},{8,4},{12,0},{16,28},{20,24},{24,20},{28,16},{1,13},{... | collective-permute-start | bytes 1179656 | tf_op jit(solution)/shard_map/ppermute | solution.py:597
  99.7 0.0 collective-permute-start.7
  99.7 0.0 collective-permute-done.6.refs_1_
  99.7 0.5 collective-permute-start.8
  100.3 0.1 copy.16.kinds
  100.3 0.9 collective-permute-done.7.refs_2_
  101.3 0.4 collective-permute-done.8.refs_3_
  101.6 8.7 %warm.1 = (f32[64,8,16,128]{3,2,1,0:T(8,128)S(1)}, f32[128,128]{1,0:T(8,128)}) custom-call(s32[2]{0:T(128)S(1)} %copy-done.8, f32[10,64]{1,0:T(8,128)S(1)} %stack.136.floats, s32[5,64]{1,0:T(8,128)S(1)} %stack.143.ints, f32[6,16]{1,0:T(8,128)S(1)} %copy.16.kinds, f32[2]{0:T(128)S(1)} %copy-done.14, f32[64,8,16,128]{3,2,1,0:T(8,128)} %get-tuple-element.52.swept, ...), custom_call_target="tpu_custom_call" | custom-call | tf_op jit(solution)/shard_map/warm/pallas_call | solution.py:727
  110.4 3.8 %collective-permute-done.12.refs_3_ = f32[3,256,128]{2,1,0:T(8,128)S(1)} collective-permute-done((f32[3,256,128]{2,1,0:T(8,128)S(1)}, f32[3,256,128]{2,1,0:T(8,128)S(1)}, u32[]{:S(2)}, u32[]{:S(2)}) %collective-permute-start.12) | collective-permute-done | bytes 393248 | tf_op jit(solution)/shard_map/ppermute | solution.py:597
  114.2 5.2 %inflow.1 = f32[64,8,16,128]{3,2,1,0:T(8,128)} custom-call(s32[2]{0:T(128)S(1)} %copy-done.8, f32[10,64]{1,0:T(8,128)S(1)} %stack.136.floats, s32[5,64]{1,0:T(8,128)S(1)} %stack.143.ints, f32[64,8,16,128]{3,2,1,0:T(8,128)S(1)} %get-tuple-element.62.warm, f32[3,256,128]{2,1,0:T(8,128)S(1)} %get-tuple-element.67.refs_0_, ...), custom_call_target="tpu_custom_call" | custom-call | tf_op jit(solution)/shard_map/inflow/pallas_call | solution.py:740
  (44 shorter events, 0.4 us)
Async XLA Ops:
  0.6 20.6 %copy-start.19 = (f32[8]{0:T(128)S(1)}, f32[8]{0:T(128)}, u32[]{:S(2)}) copy-start(f32[8]{0:T(128)} %refs_0_.1) | copy-start | bytes 100
  0.6 20.6 %copy-start.18 = (f32[8]{0:T(128)S(1)}, f32[8]{0:T(128)}, u32[]{:S(2)}) copy-start(f32[8]{0:T(128)} %refs_1_.1) | copy-start | bytes 100
  0.7 20.6 %copy-start.22 = (f32[8]{0:T(128)S(1)}, f32[8]{0:T(128)}, u32[]{:S(2)}) copy-start(f32[8]{0:T(128)} %refs_2_.1) | copy-start | bytes 100
  0.7 20.6 %copy-start.17 = (f32[8]{0:T(128)S(1)}, f32[8]{0:T(128)}, u32[]{:S(2)}) copy-start(f32[8]{0:T(128)} %refs_3_.1) | copy-start | bytes 100
  0.7 20.6 %copy-start.21 = (f32[8]{0:T(128)S(1)}, f32[8]{0:T(128)}, u32[]{:S(2)}) copy-start(f32[8]{0:T(128)} %refs_4_.1) | copy-start | bytes 100
  0.7 20.5 %copy-start.20 = (s32[64]{0:T(128)S(1)}, s32[64]{0:T(128)}, u32[]{:S(2)}) copy-start(s32[64]{0:T(128)} %labels.1) | copy-start | bytes 772
  1.3 26.4 %copy-start.8 = (s32[2]{0:T(128)S(1)}, s32[2]{0:T(128)}, u32[]{:S(2)}) copy-start(s32[2]{0:T(128)} %pad_add_fusion.meta) | copy-start | bytes 28
  16.5 14.6 %collective-permute-start.2 = (f32[3,256,128]{2,1,0:T(8,128)}, f32[3,256,128]{2,1,0:T(8,128)S(1)}, u32[]{:S(2)}, u32[]{:S(2)}) collective-permute-start(f32[3,256,128]{2,1,0:T(8,128)} %get-tuple-element.41), channel_id=1, source_target_pairs={{0,4},{4,0},{8,12},{12,8},{16,20},{20,16},{24,28},{28,24},{1,5},{5... | collective-permute-start | bytes 1179656 | tf_op jit(solution)/shard_map/ppermute | solution.py:597
  19.6 12.3 %collective-permute-start.3 = (f32[3,256,128]{2,1,0:T(8,128)}, f32[3,256,128]{2,1,0:T(8,128)S(1)}, u32[]{:S(2)}, u32[]{:S(2)}) collective-permute-start(f32[3,256,128]{2,1,0:T(8,128)} %get-tuple-element.42), channel_id=1, source_target_pairs={{0,8},{4,12},{8,0},{12,4},{16,24},{20,28},{24,16},{28,20},{1,9},{5... | collective-permute-start | bytes 1179656 | tf_op jit(solution)/shard_map/ppermute | solution.py:597
  21.2 17.4 %collective-permute-start.4 = (f32[3,256,128]{2,1,0:T(8,128)}, f32[3,256,128]{2,1,0:T(8,128)S(1)}, u32[]{:S(2)}, u32[]{:S(2)}) collective-permute-start(f32[3,256,128]{2,1,0:T(8,128)} %get-tuple-element.43), channel_id=1, source_target_pairs={{0,12},{4,8},{8,4},{12,0},{16,28},{20,24},{24,20},{28,16},{1,13},{... | collective-permute-start | bytes 1179656 | tf_op jit(solution)/shard_map/ppermute | solution.py:597
  21.2 2.5 %collective-permute-start = (f32[2,3,64,512]{3,2,1,0:T(8,128)}, f32[2,3,64,512]{3,2,1,0:T(8,128)S(1)}, u32[]{:S(2)}, u32[]{:S(2)}) collective-permute-start(f32[2,3,64,512]{3,2,1,0:T(8,128)} %get-tuple-element.38), channel_id=1, source_target_pairs={{0,1},{1,0},{2,3},{3,2},{4,5},{5,4},{6,7},{7,6},{8,9},{9,8},{10,11... | collective-permute-start | bytes 2359304 | tf_op jit(solution)/shard_map/ppermute | solution.py:597
  23.7 1.1 copy-start
  25.6 16.5 %collective-permute-start.1 = (f32[1,3,64,512]{3,2,1,0:T(8,128)}, f32[1,3,64,512]{3,2,1,0:T(8,128)S(1)}, u32[]{:S(2)}, u32[]{:S(2)}) collective-permute-start(f32[1,3,64,512]{3,2,1,0:T(8,128)} %get-tuple-element.39), channel_id=1, source_target_pairs={{0,2},{1,3},{2,0},{3,1},{4,6},{5,7},{6,4},{7,5},{8,10},{9,11},{10,... | collective-permute-start | bytes 1179656 | tf_op jit(solution)/shard_map/ppermute | solution.py:597
  27.6 1.5 %copy-start.15 = (f32[6,8,2]{0,2,1:T(2,128)}, f32[6,8,2]{0,2,1:T(2,128)S(1)}, u32[]{:S(2)}) copy-start(f32[6,8,2]{0,2,1:T(2,128)S(1)} %copy.14) | copy-start | bytes 1156
  28.5 0.6 copy-start.6
  29.1 9.4 %copy-start.9 = (f32[40,128]{1,0:T(8,128)}, f32[40,128]{1,0:T(8,128)S(1)}, u32[]{:S(2)}) copy-start(f32[40,128]{1,0:T(8,128)S(1)} %get-tuple-element.61.matrix_two) | copy-start | bytes 61444
  38.6 1.0 copy-start.1
  40.8 0.7 copy-start.2
  41.5 0.6 copy-start.4
  42.1 59.5 %copy-start.14 = (f32[2]{0:T(128)S(1)}, f32[2]{0:T(128)}, u32[]{:S(2)}) copy-start(f32[2]{0:T(128)} %pad_maximum_fusion.1.sums) | copy-start | bytes 28
  42.9 57.3 %copy-start.16 = (f32[6,8,2]{0,2,1:T(2,128)S(1)}, f32[6,8,2]{0,2,1:T(2,128)}, u32[]{:S(2)}) copy-start(f32[6,8,2]{0,2,1:T(2,128)} %copy-done.15) | copy-start | bytes 1156
  42.9 22.2 %all-to-all-start = ((f32[8,3,8,512]{3,2,1,0:T(8,128)}), f32[8,3,8,512]{3,2,1,0:T(8,128)S(1)}, u32[]{:S(2)}, u32[]{:S(2)}) async-start(f32[8,3,8,512]{3,2,1,0:T(8,128)} %density_parts.1), calls=%async_computation | async-start | bytes 786432 | tf_op jit(solution)/shard_map/all_to_all | solution.py:680
  49.0 16.1 %collective-permute-start.5 = (f32[256,128]{1,0:T(8,128)}, f32[256,128]{1,0:T(8,128)S(1)}, u32[]{:S(2)}, u32[]{:S(2)}) collective-permute-start(f32[256,128]{1,0:T(8,128)} %copy-done.4), channel_id=1, source_target_pairs={{0,16},{4,20},{8,24},{12,28},{16,0},{20,4},{24,8},{28,12},{1,17},{... | collective-permute-start | bytes 393224 | tf_op jit(solution)/shard_map/ppermute | solution.py:597
  65.1 0.7 copy-start.11
  65.9 0.7 copy-start.12
  67.8 19.1 %all-to-all-start.1 = ((f32[8,2,8,512]{3,2,1,0:T(8,128)}), f32[8,2,8,512]{3,2,1,0:T(8,128)S(1)}, u32[]{:S(2)}, u32[]{:S(2)}) async-start(f32[8,2,8,512]{3,2,1,0:T(8,128)} %get-tuple-element.58), calls=%async_computation.1 | async-start | bytes 524288 | tf_op jit(solution)/shard_map/all_to_all | solution.py:692
  71.5 20.6 %collective-permute-start.9 = (f32[2,256,128]{2,1,0:T(8,128)}, f32[2,256,128]{2,1,0:T(8,128)S(1)}, u32[]{:S(2)}, u32[]{:S(2)}) collective-permute-start(f32[2,256,128]{2,1,0:T(8,128)} %copy-done.2), channel_id=1, source_target_pairs={{0,16},{4,20},{8,24},{12,28},{16,0},{20,4},{24,8},{28,12},{1,17},{... | collective-permute-start | bytes 786440 | tf_op jit(solution)/shard_map/ppermute | solution.py:597
  86.9 0.9 copy-start.7
  87.8 0.7 copy-start.10
  88.5 0.7 copy-start.13
  90.5 9.2 %collective-permute-start.6 = (f32[128,512]{1,0:T(8,128)S(1)}, f32[128,512]{1,0:T(8,128)S(1)}, u32[]{:S(2)}, u32[]{:S(2)}) collective-permute-start(f32[128,512]{1,0:T(8,128)S(1)} %kelvins.1.refs_0_), channel_id=1, source_target_pairs={{0,2},{1,3},{2,0},{3,1},{4,6},{5,7},{6,4},{7,5},{8,10},{9,11},{10,... | collective-permute-start | bytes 786440 | tf_op jit(solution)/shard_map/ppermute | solution.py:597
  92.1 1.0 copy-start.3
  93.1 0.9 copy-start.5
  96.2 14.1 %collective-permute-start.10 = (f32[3,256,128]{2,1,0:T(8,128)}, f32[3,256,128]{2,1,0:T(8,128)S(1)}, u32[]{:S(2)}, u32[]{:S(2)}) collective-permute-start(f32[3,256,128]{2,1,0:T(8,128)} %get-tuple-element.68), channel_id=1, source_target_pairs={{0,4},{4,0},{8,12},{12,8},{16,20},{20,16},{24,28},{28,24},{1,5},{5... | collective-permute-start | bytes 1179656 | tf_op jit(solution)/shard_map/ppermute | solution.py:597
  97.6 12.8 %collective-permute-start.11 = (f32[3,256,128]{2,1,0:T(8,128)}, f32[3,256,128]{2,1,0:T(8,128)S(1)}, u32[]{:S(2)}, u32[]{:S(2)}) collective-permute-start(f32[3,256,128]{2,1,0:T(8,128)} %get-tuple-element.69), channel_id=1, source_target_pairs={{0,8},{4,12},{8,0},{12,4},{16,24},{20,28},{24,16},{28,20},{1,9},{5... | collective-permute-start | bytes 1179656 | tf_op jit(solution)/shard_map/ppermute | solution.py:597
  97.6 16.6 %collective-permute-start.12 = (f32[3,256,128]{2,1,0:T(8,128)S(1)}, f32[3,256,128]{2,1,0:T(8,128)S(1)}, u32[]{:S(2)}, u32[]{:S(2)}) collective-permute-start(f32[3,256,128]{2,1,0:T(8,128)S(1)} %get-tuple-element.70), channel_id=1, source_target_pairs={{0,12},{4,8},{8,4},{12,0},{16,28},{20,24},{24,20},{28,16},{1,13},{... | collective-permute-start | bytes 1179656 | tf_op jit(solution)/shard_map/ppermute | solution.py:597
  99.7 1.5 %collective-permute-start.7 = (f32[128,512]{1,0:T(8,128)S(1)}, f32[128,512]{1,0:T(8,128)S(1)}, u32[]{:S(2)}, u32[]{:S(2)}) collective-permute-start(f32[128,512]{1,0:T(8,128)S(1)} %kelvins.1.refs_0_), channel_id=1, source_target_pairs={{0,1},{1,0},{2,3},{3,2},{4,5},{5,4},{6,7},{7,6},{8,9},{9,8},{10,11... | collective-permute-start | bytes 786440 | tf_op jit(solution)/shard_map/ppermute | solution.py:597
  99.7 1.9 %collective-permute-start.8 = (f32[128,512]{1,0:T(8,128)S(1)}, f32[128,512]{1,0:T(8,128)S(1)}, u32[]{:S(2)}, u32[]{:S(2)}) collective-permute-start(f32[128,512]{1,0:T(8,128)S(1)} %collective-permute-done.6.refs_1_), channel_id=1, source_target_pairs={{0,1},{1,0},{2,3},{3,2},{4,5},{5,4},{6,7},{7,6},{8,9},{9,8},{10,11... | collective-permute-start | bytes 786440 | tf_op jit(solution)/shard_map/ppermute | solution.py:597

commit v17 on v16

--- a/solution.py
+++ b/solution.py
@@ -320,7 +320,7 @@
                 plane[at_high, :] = high
         return carry
 
-    lax.fori_loop(0, block // 2, one_pair, 0, unroll=2)
+    lax.fori_loop(0, block // 2, one_pair, 0, unroll=4)
 
     @pl.when(step == blocks - 1)
     def _():

time: 120 us -> 120 us (level)
  no operation moved by 1% of the time
where the time goes in v17:
time: 120 us; the launch traced here: 119 us
  waiting for transfers between devices  39.7 us (33%)
  Pallas kernels  37 us (31%)
  starting transfers between devices  27.7 us (23%)
  local copies, waits for them, and re-layouts  10 us (8%)
  other arithmetic  3.41 us (3%)
    ppermute x13, waiting for transfers between devices, swap(): lax.ppermute(array, axis, [(i, i ^ by) for i in range(lax.axis_size(axis))])  27.2 us
    ppermute x13, starting transfers between devices, swap(): lax.ppermute(array, axis, [(i, i ^ by) for i in range(lax.axis_size(axis))])  17.9 us
    pallas_call x1, Pallas kernels, local(): pl.pallas_call(functools.partial(sweeps_kernel, (block, blocks, depth, wi...  14.6 us
    all_to_all x1, waiting for transfers between devices, local(): gathered = lax.all_to_all(copies, 'slab', 0, 0)  12.5 us
    unnamed x46, local copies, waits for them, and re-layouts  9.67 us
    pallas_call x1, Pallas kernels, local(): pl.pallas_call(functools.partial(warm_kernel, (block, depth, width_y, wid...  8.74 us
    pallas_call x7, Pallas kernels, call(): pl.pallas_call(kernel, in_specs=in_specs, out_specs=[VMEM] * len(out_shap...  8.52 us
    all_to_all x1, starting transfers between devices, local(): summed = lax.all_to_all(parts, 'slab', 0, 0)  6.12 us
  transfers between devices with their start and end apart: 15, of which 8 were waited for; matrix products, arithmetic and copies ran while one was open for 3% of the time, Pallas kernels for 13%

profile of v17, /device:TPU:0, one launch (start us, length us, event | category | flops | bytes accessed | tf_op | source)
XLA Modules:
  0.0 118.7 jit_solution(15070918365304944529)
XLA Ops:
  0.6 0.0 copy-start.19
  0.6 0.0 copy-start.18
  0.7 0.0 copy-start.22
  0.7 0.0 copy-start.17
  0.7 0.0 copy-start.21
  0.7 0.0 copy-start.20
  0.7 0.6 pad_add_fusion.meta
  1.3 14.6 %sweeps.1 = (f32[64,8,16,128]{3,2,1,0:T(8,128)}, f32[8,512]{1,0:T(8,128)}, f32[3,256,128]{2,1,0:T(8,128)}, f32[3,256,128]{2,1,0:T(8,128)}, f32[3,256,128]{2,1,0:...) custom-call(s32[2]{0:T(128)} %pad_add_fusion.meta, s32[64]{0:T(128)} %labels.1, ...), custom_call_target="tpu_custom_call" | custom-call | tf_op jit(solution)/shard_map/sweeps/pallas_call | solution.py:614
  15.9 3.0 %collective-permute-start.2 = (f32[3,256,128]{2,1,0:T(8,128)}, f32[3,256,128]{2,1,0:T(8,128)S(1)}, u32[]{:S(2)}, u32[]{:S(2)}) collective-permute-start(f32[3,256,128]{2,1,0:T(8,128)} %get-tuple-element.41), channel_id=1, source_target_pairs={{0,4},{4,0},{8,12},{12,8},{16,20},{20,16},{24,28},{28,24},{1,5},{5... | collective-permute-start | bytes 1179656 | tf_op jit(solution)/shard_map/ppermute | solution.py:597
  18.9 1.6 %collective-permute-start.3 = (f32[3,256,128]{2,1,0:T(8,128)}, f32[3,256,128]{2,1,0:T(8,128)S(1)}, u32[]{:S(2)}, u32[]{:S(2)}) collective-permute-start(f32[3,256,128]{2,1,0:T(8,128)} %get-tuple-element.42), channel_id=1, source_target_pairs={{0,8},{4,12},{8,0},{12,4},{16,24},{20,28},{24,16},{28,20},{1,9},{5... | collective-permute-start | bytes 1179656 | tf_op jit(solution)/shard_map/ppermute | solution.py:597
  20.5 0.0 collective-permute-start.4
  20.5 0.0 collective-permute-start
  20.6 0.1 select_reduce_fusion
  20.7 0.7 fusion.20
  21.3 0.1 fusion.7
  21.6 1.4 %collective-permute-done.other = f32[2,3,64,512]{3,2,1,0:T(8,128)S(1)} collective-permute-done((f32[2,3,64,512]{3,2,1,0:T(8,128)}, f32[2,3,64,512]{3,2,1,0:T(8,128)S(1)}, u32[]{:S(2)}, u32[]{:S(2)}) %collective-permute-start) | collective-permute-done | bytes 786464 | tf_op jit(solution)/shard_map/ppermute | solution.py:597
  23.0 1.1 copy-done
  24.1 0.8 density_split.1
  24.9 1.9 %collective-permute-start.1 = (f32[1,3,64,512]{3,2,1,0:T(8,128)}, f32[1,3,64,512]{3,2,1,0:T(8,128)S(1)}, u32[]{:S(2)}, u32[]{:S(2)}) collective-permute-start(f32[1,3,64,512]{3,2,1,0:T(8,128)} %get-tuple-element.39), channel_id=1, source_target_pairs={{0,2},{1,3},{2,0},{3,1},{4,6},{5,7},{6,4},{7,5},{8,10},{9,11},{10,... | collective-permute-start | bytes 1179656 | tf_op jit(solution)/shard_map/ppermute | solution.py:597
  26.8 0.1 copy.14
  26.9 0.1 copy.15.kinds
  27.0 0.8 heat_matrices.1
  27.8 0.6 copy-done.6
  28.5 1.9 %pad_maximum_fusion.1.sums = f32[2]{0:T(128)} fusion(f32[1]{0:T(128)} %bitcast.36, f32[1]{0:T(128)} %bitcast.35), kind=kLoop, calls=%fused_computation.35 | loop fusion | flops 2 | bytes 16 | tf_op jit(solution)/shard_map/stack | solution.py:585
  30.4 0.0 collective-permute-done.2.refs_1_
  30.4 0.7 collective-permute-done.3.refs_2_
  31.1 6.8 %collective-permute-done.4.refs_3_ = f32[3,256,128]{2,1,0:T(8,128)S(1)} collective-permute-done((f32[3,256,128]{2,1,0:T(8,128)}, f32[3,256,128]{2,1,0:T(8,128)S(1)}, u32[]{:S(2)}, u32[]{:S(2)}) %collective-permute-start.4) | collective-permute-done | bytes 393248 | tf_op jit(solution)/shard_map/ppermute | solution.py:597
  37.9 1.0 copy-done.1
  38.9 1.2 compose.1
  40.1 0.7 copy-done.2
  40.8 0.6 copy-done.4
  41.5 0.0 collective-permute-done.1.other
  41.5 0.8 density_parts.1
  42.2 6.1 %all-to-all-start = ((f32[8,3,8,512]{3,2,1,0:T(8,128)}), f32[8,3,8,512]{3,2,1,0:T(8,128)S(1)}, u32[]{:S(2)}, u32[]{:S(2)}) async-start(f32[8,3,8,512]{3,2,1,0:T(8,128)} %density_parts.1), calls=%async_computation | async-start | bytes 786432 | tf_op jit(solution)/shard_map/all_to_all | solution.py:680
  48.4 2.9 %collective-permute-start.5 = (f32[256,128]{1,0:T(8,128)}, f32[256,128]{1,0:T(8,128)S(1)}, u32[]{:S(2)}, u32[]{:S(2)}) collective-permute-start(f32[256,128]{1,0:T(8,128)} %copy-done.4), channel_id=1, source_target_pairs={{0,16},{4,20},{8,24},{12,28},{16,0},{20,4},{24,8},{28,12},{1,17},{... | collective-permute-start | bytes 393224 | tf_op jit(solution)/shard_map/ppermute | solution.py:597
  51.3 13.2 %collective-permute-done.5.refs_1_ = f32[256,128]{1,0:T(8,128)S(1)} collective-permute-done((f32[256,128]{1,0:T(8,128)}, f32[256,128]{1,0:T(8,128)S(1)}, u32[]{:S(2)}, u32[]{:S(2)}) %collective-permute-start.5) | collective-permute-done | bytes 131104 | tf_op jit(solution)/shard_map/ppermute | solution.py:597
  64.5 0.0 all-to-all-done.parts
  64.5 0.7 copy-done.11
  65.2 0.7 copy-done.12
  65.9 1.3 %density_totals.1 = (f32[8,2,8,512]{3,2,1,0:T(8,128)}, f32[8,512]{1,0:T(8,128)S(1)}) custom-call(f32[2]{0:T(128)S(1)} %copy-done.12, f32[8,3,8,512]{3,2,1,0:T(8,128)S(1)} %all-to-all-done.parts, f32[8,512]{1,0:T(8,128)S(1)} %copy-done.11), custom_call_target="tpu_custom_call" | custom-call | tf_op jit(solution)/shard_map/density_totals/pallas_call | solution.py:600
  67.2 3.7 %all-to-all-start.1 = ((f32[8,2,8,512]{3,2,1,0:T(8,128)}), f32[8,2,8,512]{3,2,1,0:T(8,128)S(1)}, u32[]{:S(2)}, u32[]{:S(2)}) async-start(f32[8,2,8,512]{3,2,1,0:T(8,128)} %get-tuple-element.58), calls=%async_computation.1 | async-start | bytes 524288 | tf_op jit(solution)/shard_map/all_to_all | solution.py:692
  70.8 2.9 %collective-permute-start.9 = (f32[2,256,128]{2,1,0:T(8,128)}, f32[2,256,128]{2,1,0:T(8,128)S(1)}, u32[]{:S(2)}, u32[]{:S(2)}) collective-permute-start(f32[2,256,128]{2,1,0:T(8,128)} %copy-done.2), channel_id=1, source_target_pairs={{0,16},{4,20},{8,24},{12,28},{16,0},{20,4},{24,8},{28,12},{1,17},{... | collective-permute-start | bytes 786440 | tf_op jit(solution)/shard_map/ppermute | solution.py:597
  73.8 12.5 %all-to-all-done.1.gathered = f32[8,2,8,512]{3,2,1,0:T(8,128)S(1)} async-done(((f32[8,2,8,512]{3,2,1,0:T(8,128)}), f32[8,2,8,512]{3,2,1,0:T(8,128)S(1)}, u32[]{:S(2)}, u32[]{:S(2)}) %all-to-all-start.1) | async-done | bytes 262176 | tf_op jit(solution)/shard_map/all_to_all | solution.py:692
  86.2 0.9 copy-done.7
  87.1 0.7 copy-done.10
  87.8 0.7 copy-done.13
  88.5 1.4 %kelvins.1.refs_0_ = f32[128,512]{1,0:T(8,128)S(1)} custom-call(s32[2]{0:T(128)S(1)} %copy-done.8, f32[2]{0:T(128)S(1)} %copy-done.13, f32[8,2,8,512]{3,2,1,0:T(8,128)S(1)} %all-to-all-done.1.gathered, f32[8,512]{1,0:T(8,128)S(1)} %get-tuple-element.59.late, f32[144,128]{1,0:T(8,128)S(1)} %copy-done.7, f32[40,128]{1,0:T(8,128)S(1)} %copy-done.10), custom_call_target="tpu_custom_call" | custom-call | tf_op jit(solution)/shard_map/kelvins/pallas_call | solution.py:600
  89.9 1.6 %collective-permute-start.6 = (f32[128,512]{1,0:T(8,128)S(1)}, f32[128,512]{1,0:T(8,128)S(1)}, u32[]{:S(2)}, u32[]{:S(2)}) collective-permute-start(f32[128,512]{1,0:T(8,128)S(1)} %kelvins.1.refs_0_), channel_id=1, source_target_pairs={{0,2},{1,3},{2,0},{3,1},{4,6},{5,7},{6,4},{7,5},{8,10},{9,11},{10,... | collective-permute-start | bytes 786440 | tf_op jit(solution)/shard_map/ppermute | solution.py:597
  91.5 0.0 collective-permute-done.9.refs_3_
  91.5 0.9 copy-done.3
  92.4 0.9 copy-done.5
  93.3 2.2 %enter.1 = (f32[3,256,128]{2,1,0:T(8,128)S(1)}, f32[3,256,128]{2,1,0:T(8,128)}, f32[3,256,128]{2,1,0:T(8,128)}, f32[3,256,128]{2,1,0:T(8,128)S(1)}) custom-call(s32[2]{0:T(128)S(1)} %copy-done.8, f32[10,64]{1,0:T(8,128)S(1)} %stack.136.floats, s32[5,64]{1,0:T(8,128)S(1)} %stack.143.ints, f32[4,3,256,128]{3,2,1,0:T(8,128)S(1)} %get-tuple-element.63.effective, ...), custom_call_target="tpu_custom_call" | custom-call | tf_op jit(solution)/shard_map/enter/pallas_call | solution.py:600
  95.6 1.4 %collective-permute-start.10 = (f32[3,256,128]{2,1,0:T(8,128)}, f32[3,256,128]{2,1,0:T(8,128)S(1)}, u32[]{:S(2)}, u32[]{:S(2)}) collective-permute-start(f32[3,256,128]{2,1,0:T(8,128)} %get-tuple-element.68), channel_id=1, source_target_pairs={{0,4},{4,0},{8,12},{12,8},{16,20},{20,16},{24,28},{28,24},{1,5},{5... | collective-permute-start | bytes 1179656 | tf_op jit(solution)/shard_map/ppermute | solution.py:597
  96.9 0.0 collective-permute-start.11
  96.9 2.1 %collective-permute-start.12 = (f32[3,256,128]{2,1,0:T(8,128)S(1)}, f32[3,256,128]{2,1,0:T(8,128)S(1)}, u32[]{:S(2)}, u32[]{:S(2)}) collective-permute-start(f32[3,256,128]{2,1,0:T(8,128)S(1)} %get-tuple-element.70), channel_id=1, source_target_pairs={{0,12},{4,8},{8,4},{12,0},{16,28},{20,24},{24,20},{28,16},{1,13},{... | collective-permute-start | bytes 1179656 | tf_op jit(solution)/shard_map/ppermute | solution.py:597
  99.0 0.0 collective-permute-start.7
  99.0 0.0 collective-permute-done.6.refs_1_
  99.1 0.5 collective-permute-start.8
  99.6 0.1 copy.16.kinds
  99.6 0.9 collective-permute-done.7.refs_2_
  100.6 0.4 collective-permute-done.8.refs_3_
  101.0 8.7 %warm.1 = (f32[64,8,16,128]{3,2,1,0:T(8,128)S(1)}, f32[128,128]{1,0:T(8,128)}) custom-call(s32[2]{0:T(128)S(1)} %copy-done.8, f32[10,64]{1,0:T(8,128)S(1)} %stack.136.floats, s32[5,64]{1,0:T(8,128)S(1)} %stack.143.ints, f32[6,16]{1,0:T(8,128)S(1)} %copy.16.kinds, f32[2]{0:T(128)S(1)} %copy-done.14, f32[64,8,16,128]{3,2,1,0:T(8,128)} %get-tuple-element.52.swept, ...), custom_call_target="tpu_custom_call" | custom-call | tf_op jit(solution)/shard_map/warm/pallas_call | solution.py:727
  109.7 3.8 %collective-permute-done.12.refs_3_ = f32[3,256,128]{2,1,0:T(8,128)S(1)} collective-permute-done((f32[3,256,128]{2,1,0:T(8,128)S(1)}, f32[3,256,128]{2,1,0:T(8,128)S(1)}, u32[]{:S(2)}, u32[]{:S(2)}) %collective-permute-start.12) | collective-permute-done | bytes 393248 | tf_op jit(solution)/shard_map/ppermute | solution.py:597
  113.6 5.2 %inflow.1 = f32[64,8,16,128]{3,2,1,0:T(8,128)} custom-call(s32[2]{0:T(128)S(1)} %copy-done.8, f32[10,64]{1,0:T(8,128)S(1)} %stack.136.floats, s32[5,64]{1,0:T(8,128)S(1)} %stack.143.ints, f32[64,8,16,128]{3,2,1,0:T(8,128)S(1)} %get-tuple-element.62.warm, f32[3,256,128]{2,1,0:T(8,128)S(1)} %get-tuple-element.67.refs_0_, ...), custom_call_target="tpu_custom_call" | custom-call | tf_op jit(solution)/shard_map/inflow/pallas_call | solution.py:740
  (44 shorter events, 0.4 us)
Async XLA Ops:
  0.6 19.9 %copy-start.19 = (f32[8]{0:T(128)S(1)}, f32[8]{0:T(128)}, u32[]{:S(2)}) copy-start(f32[8]{0:T(128)} %refs_0_.1) | copy-start | bytes 100
  0.6 19.9 %copy-start.18 = (f32[8]{0:T(128)S(1)}, f32[8]{0:T(128)}, u32[]{:S(2)}) copy-start(f32[8]{0:T(128)} %refs_1_.1) | copy-start | bytes 100
  0.7 19.9 %copy-start.22 = (f32[8]{0:T(128)S(1)}, f32[8]{0:T(128)}, u32[]{:S(2)}) copy-start(f32[8]{0:T(128)} %refs_2_.1) | copy-start | bytes 100
  0.7 19.9 %copy-start.17 = (f32[8]{0:T(128)S(1)}, f32[8]{0:T(128)}, u32[]{:S(2)}) copy-start(f32[8]{0:T(128)} %refs_3_.1) | copy-start | bytes 100
  0.7 19.9 %copy-start.21 = (f32[8]{0:T(128)S(1)}, f32[8]{0:T(128)}, u32[]{:S(2)}) copy-start(f32[8]{0:T(128)} %refs_4_.1) | copy-start | bytes 100
  0.7 19.8 %copy-start.20 = (s32[64]{0:T(128)S(1)}, s32[64]{0:T(128)}, u32[]{:S(2)}) copy-start(s32[64]{0:T(128)} %labels.1) | copy-start | bytes 772
  1.3 25.7 %copy-start.8 = (s32[2]{0:T(128)S(1)}, s32[2]{0:T(128)}, u32[]{:S(2)}) copy-start(s32[2]{0:T(128)} %pad_add_fusion.meta) | copy-start | bytes 28
  15.9 14.6 %collective-permute-start.2 = (f32[3,256,128]{2,1,0:T(8,128)}, f32[3,256,128]{2,1,0:T(8,128)S(1)}, u32[]{:S(2)}, u32[]{:S(2)}) collective-permute-start(f32[3,256,128]{2,1,0:T(8,128)} %get-tuple-element.41), channel_id=1, source_target_pairs={{0,4},{4,0},{8,12},{12,8},{16,20},{20,16},{24,28},{28,24},{1,5},{5... | collective-permute-start | bytes 1179656 | tf_op jit(solution)/shard_map/ppermute | solution.py:597
  18.9 12.2 %collective-permute-start.3 = (f32[3,256,128]{2,1,0:T(8,128)}, f32[3,256,128]{2,1,0:T(8,128)S(1)}, u32[]{:S(2)}, u32[]{:S(2)}) collective-permute-start(f32[3,256,128]{2,1,0:T(8,128)} %get-tuple-element.42), channel_id=1, source_target_pairs={{0,8},{4,12},{8,0},{12,4},{16,24},{20,28},{24,16},{28,20},{1,9},{5... | collective-permute-start | bytes 1179656 | tf_op jit(solution)/shard_map/ppermute | solution.py:597
  20.5 17.4 %collective-permute-start.4 = (f32[3,256,128]{2,1,0:T(8,128)}, f32[3,256,128]{2,1,0:T(8,128)S(1)}, u32[]{:S(2)}, u32[]{:S(2)}) collective-permute-start(f32[3,256,128]{2,1,0:T(8,128)} %get-tuple-element.43), channel_id=1, source_target_pairs={{0,12},{4,8},{8,4},{12,0},{16,28},{20,24},{24,20},{28,16},{1,13},{... | collective-permute-start | bytes 1179656 | tf_op jit(solution)/shard_map/ppermute | solution.py:597
  20.5 2.5 %collective-permute-start = (f32[2,3,64,512]{3,2,1,0:T(8,128)}, f32[2,3,64,512]{3,2,1,0:T(8,128)S(1)}, u32[]{:S(2)}, u32[]{:S(2)}) collective-permute-start(f32[2,3,64,512]{3,2,1,0:T(8,128)} %get-tuple-element.38), channel_id=1, source_target_pairs={{0,1},{1,0},{2,3},{3,2},{4,5},{5,4},{6,7},{7,6},{8,9},{9,8},{10,11... | collective-permute-start | bytes 2359304 | tf_op jit(solution)/shard_map/ppermute | solution.py:597
  23.0 1.1 copy-start
  24.9 16.5 %collective-permute-start.1 = (f32[1,3,64,512]{3,2,1,0:T(8,128)}, f32[1,3,64,512]{3,2,1,0:T(8,128)S(1)}, u32[]{:S(2)}, u32[]{:S(2)}) collective-permute-start(f32[1,3,64,512]{3,2,1,0:T(8,128)} %get-tuple-element.39), channel_id=1, source_target_pairs={{0,2},{1,3},{2,0},{3,1},{4,6},{5,7},{6,4},{7,5},{8,10},{9,11},{10,... | collective-permute-start | bytes 1179656 | tf_op jit(solution)/shard_map/ppermute | solution.py:597
  26.9 1.5 %copy-start.15 = (f32[6,8,2]{0,2,1:T(2,128)}, f32[6,8,2]{0,2,1:T(2,128)S(1)}, u32[]{:S(2)}) copy-start(f32[6,8,2]{0,2,1:T(2,128)S(1)} %copy.14) | copy-start | bytes 1156
  27.8 0.6 copy-start.6
  28.5 9.4 %copy-start.9 = (f32[40,128]{1,0:T(8,128)}, f32[40,128]{1,0:T(8,128)S(1)}, u32[]{:S(2)}) copy-start(f32[40,128]{1,0:T(8,128)S(1)} %get-tuple-element.61.matrix_two) | copy-start | bytes 61444
  37.9 1.0 copy-start.1
  40.1 0.7 copy-start.2
  40.8 0.6 copy-start.4
  41.5 59.5 %copy-start.14 = (f32[2]{0:T(128)S(1)}, f32[2]{0:T(128)}, u32[]{:S(2)}) copy-start(f32[2]{0:T(128)} %pad_maximum_fusion.1.sums) | copy-start | bytes 28
  42.2 57.3 %copy-start.16 = (f32[6,8,2]{0,2,1:T(2,128)S(1)}, f32[6,8,2]{0,2,1:T(2,128)}, u32[]{:S(2)}) copy-start(f32[6,8,2]{0,2,1:T(2,128)} %copy-done.15) | copy-start | bytes 1156
  42.2 22.2 %all-to-all-start = ((f32[8,3,8,512]{3,2,1,0:T(8,128)}), f32[8,3,8,512]{3,2,1,0:T(8,128)S(1)}, u32[]{:S(2)}, u32[]{:S(2)}) async-start(f32[8,3,8,512]{3,2,1,0:T(8,128)} %density_parts.1), calls=%async_computation | async-start | bytes 786432 | tf_op jit(solution)/shard_map/all_to_all | solution.py:680
  48.4 16.1 %collective-permute-start.5 = (f32[256,128]{1,0:T(8,128)}, f32[256,128]{1,0:T(8,128)S(1)}, u32[]{:S(2)}, u32[]{:S(2)}) collective-permute-start(f32[256,128]{1,0:T(8,128)} %copy-done.4), channel_id=1, source_target_pairs={{0,16},{4,20},{8,24},{12,28},{16,0},{20,4},{24,8},{28,12},{1,17},{... | collective-permute-start | bytes 393224 | tf_op jit(solution)/shard_map/ppermute | solution.py:597
  64.5 0.7 copy-start.11
  65.2 0.7 copy-start.12
  67.2 19.1 %all-to-all-start.1 = ((f32[8,2,8,512]{3,2,1,0:T(8,128)}), f32[8,2,8,512]{3,2,1,0:T(8,128)S(1)}, u32[]{:S(2)}, u32[]{:S(2)}) async-start(f32[8,2,8,512]{3,2,1,0:T(8,128)} %get-tuple-element.58), calls=%async_computation.1 | async-start | bytes 524288 | tf_op jit(solution)/shard_map/all_to_all | solution.py:692
  70.8 20.6 %collective-permute-start.9 = (f32[2,256,128]{2,1,0:T(8,128)}, f32[2,256,128]{2,1,0:T(8,128)S(1)}, u32[]{:S(2)}, u32[]{:S(2)}) collective-permute-start(f32[2,256,128]{2,1,0:T(8,128)} %copy-done.2), channel_id=1, source_target_pairs={{0,16},{4,20},{8,24},{12,28},{16,0},{20,4},{24,8},{28,12},{1,17},{... | collective-permute-start | bytes 786440 | tf_op jit(solution)/shard_map/ppermute | solution.py:597
  86.2 0.9 copy-start.7
  87.1 0.7 copy-start.10
  87.8 0.7 copy-start.13
  89.9 9.2 %collective-permute-start.6 = (f32[128,512]{1,0:T(8,128)S(1)}, f32[128,512]{1,0:T(8,128)S(1)}, u32[]{:S(2)}, u32[]{:S(2)}) collective-permute-start(f32[128,512]{1,0:T(8,128)S(1)} %kelvins.1.refs_0_), channel_id=1, source_target_pairs={{0,2},{1,3},{2,0},{3,1},{4,6},{5,7},{6,4},{7,5},{8,10},{9,11},{10,... | collective-permute-start | bytes 786440 | tf_op jit(solution)/shard_map/ppermute | solution.py:597
  91.5 1.0 copy-start.3
  92.4 0.9 copy-start.5
  95.6 14.1 %collective-permute-start.10 = (f32[3,256,128]{2,1,0:T(8,128)}, f32[3,256,128]{2,1,0:T(8,128)S(1)}, u32[]{:S(2)}, u32[]{:S(2)}) collective-permute-start(f32[3,256,128]{2,1,0:T(8,128)} %get-tuple-element.68), channel_id=1, source_target_pairs={{0,4},{4,0},{8,12},{12,8},{16,20},{20,16},{24,28},{28,24},{1,5},{5... | collective-permute-start | bytes 1179656 | tf_op jit(solution)/shard_map/ppermute | solution.py:597
  96.9 12.8 %collective-permute-start.11 = (f32[3,256,128]{2,1,0:T(8,128)}, f32[3,256,128]{2,1,0:T(8,128)S(1)}, u32[]{:S(2)}, u32[]{:S(2)}) collective-permute-start(f32[3,256,128]{2,1,0:T(8,128)} %get-tuple-element.69), channel_id=1, source_target_pairs={{0,8},{4,12},{8,0},{12,4},{16,24},{20,28},{24,16},{28,20},{1,9},{5... | collective-permute-start | bytes 1179656 | tf_op jit(solution)/shard_map/ppermute | solution.py:597
  96.9 16.6 %collective-permute-start.12 = (f32[3,256,128]{2,1,0:T(8,128)S(1)}, f32[3,256,128]{2,1,0:T(8,128)S(1)}, u32[]{:S(2)}, u32[]{:S(2)}) collective-permute-start(f32[3,256,128]{2,1,0:T(8,128)S(1)} %get-tuple-element.70), channel_id=1, source_target_pairs={{0,12},{4,8},{8,4},{12,0},{16,28},{20,24},{24,20},{28,16},{1,13},{... | collective-permute-start | bytes 1179656 | tf_op jit(solution)/shard_map/ppermute | solution.py:597
  99.0 1.5 %collective-permute-start.7 = (f32[128,512]{1,0:T(8,128)S(1)}, f32[128,512]{1,0:T(8,128)S(1)}, u32[]{:S(2)}, u32[]{:S(2)}) collective-permute-start(f32[128,512]{1,0:T(8,128)S(1)} %kelvins.1.refs_0_), channel_id=1, source_target_pairs={{0,1},{1,0},{2,3},{3,2},{4,5},{5,4},{6,7},{7,6},{8,9},{9,8},{10,11... | collective-permute-start | bytes 786440 | tf_op jit(solution)/shard_map/ppermute | solution.py:597
  99.1 1.9 %collective-permute-start.8 = (f32[128,512]{1,0:T(8,128)S(1)}, f32[128,512]{1,0:T(8,128)S(1)}, u32[]{:S(2)}, u32[]{:S(2)}) collective-permute-start(f32[128,512]{1,0:T(8,128)S(1)} %collective-permute-done.6.refs_1_), channel_id=1, source_target_pairs={{0,1},{1,0},{2,3},{3,2},{4,5},{5,4},{6,7},{7,6},{8,9},{9,8},{10,11... | collective-permute-start | bytes 786440 | tf_op jit(solution)/shard_map/ppermute | solution.py:597
